TPU v7x, 32 devices: a whole 2x2x4 slice. The times are simulated.
32 devices in a mesh: groups: 2 (over x), expert: 16 (over z, y, core), mp: 1.
Axes of the slice: x: 2, y: 2, z: 4, core: 2. Of those that a mesh axis runs over, the one named last changes fastest.
Arguments:
- tokens: bfloat16 [2048, 2560], P(('groups', 'expert'), 'mp'), parts along dimension 0, may hold values from -6 to 6
- routes: int32 [2048, 6], P('groups'), parts along dimension 0, may hold values from 0 to 15, all different within a row; in each aligned block of 64 rows (0 to 63, 64 to 127, ...) at most 48 rows name the same one
- quant_gate: bfloat16 [32, 2560, 768], P('expert', None, 'mp'), may hold values from -6 to 6
- quant_up: bfloat16 [32, 2560, 768], P('expert', None, 'mp'), may hold values from -6 to 6
- gate_scales: float32 [32, 20, 6], P(None, None, 'mp'), may hold values from 0.5 to 2
- up_scales: float32 [32, 20, 6], P(None, None, 'mp'), may hold values from 0.5 to 2
- cluster_ids: int32 [32, 1], replicated, may hold values from 0 to 15
- frequency: float32 [32], replicated, may hold values from 0.1 to 10
Outputs:
- merged_gate: bfloat16 [32, 2560, 768], P(('groups', 'expert'), None, 'mp'), parts along dimension 0
- merged_up: bfloat16 [32, 2560, 768], P(('groups', 'expert'), None, 'mp'), parts along dimension 0
- hidden_out: bfloat16 [2048, 6, 768], P(('groups', 'expert'), None, 'mp'), parts along dimension 0
There are 2 independent parts, one for each index of `groups`. A program takes and returns all parts, laid end to end along the dimension named above; an argument that names none is the same for every part. Nothing has to cross between parts.
Inputs may be any that keep to these rules, and one draw needn't show every extreme that they name: `routes`: in each aligned block of 64 tokens (the tokens of one device) no merged expert is named by more than 48 tokens, and some merged expert is named by exactly 48; the 6 ids of one token differ. `cluster_ids`: every merged expert has at least one source expert.
All inputs are finite; a program needn't handle non-finite values.
Results may differ from a plain program's by a relative error of at most 0.0058.
Values may be sent and summed in bfloat16 or wider, within the bound.
No kernel may reach another device: no remote copies, remote signals or barrier semaphores. Data moves between devices by JAX's collectives and lax.ppermute only.
A program may use at most 128 MiB of HBM per device.

v0:
```python
import math

import jax
import jax.numpy as jnp
from jax import lax
from jax.sharding import PartitionSpec as P

D = 2560
BLOCK = 128


def combine_weights(cluster_ids, frequency, merged_count):
    member = (
        cluster_ids[:, 0][None, :] == jnp.arange(merged_count, dtype=jnp.int32)[:, None]
    ).astype(jnp.float32)
    weighted = member * frequency[None, :]
    return weighted / jnp.sum(weighted, axis=1, keepdims=True)


def merge_rows(moved, scales, cluster_blend, row_start):
    source_count, count_of_rows, width = moved.shape
    column_blocks = scales.shape[2]
    row_blocks = scales.shape[1]
    row_index = row_start + jnp.arange(count_of_rows, dtype=jnp.int32)
    selector = (
        (row_index // BLOCK)[:, None] == jnp.arange(row_blocks, dtype=jnp.int32)[None, :]
    ).astype(jnp.float32)
    row_scales = jnp.einsum("ebg,wb->ewg", scales, selector, precision=lax.Precision.HIGHEST)
    coefficient = cluster_blend[:, :, None, None] * row_scales[None, :, :, :]
    blocked = moved.reshape(
        source_count, count_of_rows, column_blocks, width // column_blocks
    ).astype(jnp.float32)
    reduced_sum = jnp.einsum(
        "mewg,ewgy->mwgy", coefficient, blocked, precision=lax.Precision.HIGHEST
    )
    return reduced_sum.reshape(cluster_blend.shape[0], count_of_rows, width).astype(jnp.bfloat16)


def route_slots(routes, merged_count, tok_dev):
    experts = jnp.arange(merged_count, dtype=jnp.int32)
    hit_table = jnp.sum((routes[:, :, None] == experts).astype(jnp.int32), axis=1)
    hit_table = hit_table.reshape(-1, tok_dev, merged_count)
    position_lookup = jnp.cumsum(hit_table, axis=1) - hit_table
    return (hit_table, position_lookup)


def shards(tokens, routes, quant_gate, quant_up, gate_scales, up_scales, cluster_ids, frequency):
    expert_count = lax.axis_size("expert")
    own_index = lax.axis_index("expert")
    tok_dev = tokens.shape[0]
    top_count = routes.shape[1]
    capacity = min(tok_dev, 2 * tok_dev * top_count // expert_count)
    factor = 1.0 / math.sqrt(D)
    cluster_blend = combine_weights(cluster_ids, frequency, expert_count)
    moved_gate, moved_up = (
        lax.all_to_all(quant_gate, "expert", split_axis=1, concat_axis=0, tiled=True),
        lax.all_to_all(quant_up, "expert", split_axis=1, concat_axis=0, tiled=True),
    )
    row_start = own_index * moved_gate.shape[1]
    part_gate = merge_rows(moved_gate, gate_scales, cluster_blend, row_start)
    part_up = merge_rows(moved_up, up_scales, cluster_blend, row_start)
    merged_gate, merged_up = (
        lax.all_to_all(part_gate, "expert", split_axis=0, concat_axis=1, tiled=True),
        lax.all_to_all(part_up, "expert", split_axis=0, concat_axis=1, tiled=True),
    )
    hit_table, position_lookup = route_slots(routes, expert_count, tok_dev)
    positions = jnp.arange(capacity, dtype=jnp.int32)
    everyone = lax.all_gather(tokens, "expert", axis=0, tiled=True)
    column_hits = lax.dynamic_index_in_dim(hit_table, own_index, 2, keepdims=False)
    column_slots = lax.dynamic_index_in_dim(position_lookup, own_index, 2, keepdims=False)
    placing = (
        (column_hits[:, None, :] == 1) & (column_slots[:, None, :] == positions[None, :, None])
    ).astype(jnp.bfloat16)
    grouped = everyone.reshape(expert_count, tok_dev, everyone.shape[1])
    arrived = jnp.einsum(
        "jct,jtd->jcd", placing, grouped, preferred_element_type=jnp.float32
    ).astype(jnp.bfloat16)
    arrived = lax.all_gather(arrived, "mp", axis=2, tiled=True)
    flattened = arrived.reshape(expert_count * capacity, arrived.shape[2])
    gate_value = jnp.dot(flattened, merged_gate[0], preferred_element_type=jnp.float32) * factor
    up_projection_value = (
        jnp.dot(flattened, merged_up[0], preferred_element_type=jnp.float32) * factor
    )
    hidden = (jax.nn.silu(gate_value) * up_projection_value).astype(jnp.bfloat16)
    hidden = hidden.reshape(expert_count, capacity, hidden.shape[1])
    returned = lax.all_to_all(hidden, "expert", split_axis=0, concat_axis=0, tiled=True)
    experts = jnp.arange(expert_count, dtype=jnp.int32)
    local_routes = lax.dynamic_slice_in_dim(routes, own_index * tok_dev, tok_dev, 0)
    own_slots = lax.dynamic_index_in_dim(position_lookup, own_index, 0, keepdims=False)
    chosen = local_routes[:, :, None] == experts
    slot_of = jnp.sum(jnp.where(chosen, own_slots[:, None, :], 0), axis=2)
    picking = (chosen[:, :, :, None] & (slot_of[:, :, None, None] == positions)).astype(
        jnp.bfloat16
    )
    picking = picking.reshape(tok_dev * top_count, expert_count * capacity)
    gathered_rows = returned.reshape(expert_count * capacity, returned.shape[2])
    output = jnp.dot(picking, gathered_rows, preferred_element_type=jnp.float32).astype(
        jnp.bfloat16
    )
    return (merged_gate, merged_up, output.reshape(tok_dev, top_count, gathered_rows.shape[1]))


def solution(mesh):
    return jax.shard_map(
        shards,
        mesh=mesh,
        in_specs=(
            P(("groups", "expert"), "mp"),
            P("groups", None),
            P("expert", None, "mp"),
            P("expert", None, "mp"),
            P(None, None, "mp"),
            P(None, None, "mp"),
            P(),
            P(),
        ),
        out_specs=(
            P(("groups", "expert"), None, "mp"),
            P(("groups", "expert"), None, "mp"),
            P(("groups", "expert"), None, "mp"),
        ),
        check_vma=False,
    )
```

profile of v0, /device:TPU:0, one launch (start us, length us, event | category | flops | bytes accessed | tf_op | source)
XLA Modules:
  0.0 648.1 jit_solution(12521342591237097695)
XLA Ops:
  7.2 15.6 %copy.44 = bf16[2,2560,768]{2,0,1:T(2,128)(2,1)} copy(bf16[2,2560,768]{2,1,0:T(8,128)(2,1)} %param.10) | data formatting | bytes 15728640 | tf_op args[2]
  22.8 7.4 %all-to-all-start = ((bf16[2,2560,768]{2,0,1:T(2,128)(2,1)}), bf16[2,2560,768]{2,0,1:T(2,128)(2,1)}, u32[]{:S(2)}, u32[]{:S(2)}) async-start(bf16[2,2560,768]{2,0,1:T(2,128)(2,1)} %copy.44), calls=%async_computation | async-start | bytes 15728640 | tf_op jit(solution)/shard_map/all_to_all | solution.py:56
  30.2 15.6 %copy.49 = bf16[2,2560,768]{2,0,1:T(2,128)(2,1)} copy(bf16[2,2560,768]{2,1,0:T(8,128)(2,1)} %param.11) | data formatting | bytes 15728640 | tf_op args[3]
  45.9 126.0 %all-to-all-done = bf16[2,2560,768]{2,0,1:T(2,128)(2,1)} async-done(((bf16[2,2560,768]{2,0,1:T(2,128)(2,1)}), bf16[2,2560,768]{2,0,1:T(2,128)(2,1)}, u32[]{:S(2)}, u32[]{:S(2)}) %all-to-all-start) | async-done | bytes 7864352 | tf_op jit(solution)/shard_map/all_to_all | solution.py:56
  171.8 34.4 %all-to-all-start.2 = ((bf16[2,2560,768]{2,0,1:T(2,128)(2,1)}), bf16[2,2560,768]{2,0,1:T(2,128)(2,1)}, u32[]{:S(2)}, u32[]{:S(2)}) async-start(bf16[2,2560,768]{2,0,1:T(2,128)(2,1)} %copy.49), calls=%async_computation.2 | async-start | bytes 15728640 | tf_op jit(solution)/shard_map/all_to_all | solution.py:57
  207.1 7.9 %copy.69 = bf16[2,16,160,768]{3,2,0,1:T(8,128)(2,1)} copy(bf16[2,16,160,768]{3,0,2,1:T(2,128)(2,1)} %bitcast.3) | data formatting | bytes 15728640 | tf_op jit(solution)/shard_map/all_to_all | solution.py:56
  215.0 16.8 %reshape.153 = bf16[32,160,6,128]{3,2,1,0:T(8,128)(2,1)} reshape(bf16[16,2,160,768]{3,2,1,0:T(8,128)(2,1)} %bitcast.51) | data formatting | bytes 15728640 | tf_op jit(solution)/shard_map/reshape | solution.py:30
  231.8 10.3 %convert_bitcast_fusion.1 = bf16[16,160,6,128]{3,0,2,1:T(8,128)(2,1)S(1)} fusion(bf16[32,160,6,128]{3,2,1,0:T(8,128)(2,1)} %reshape.153, f32[32,160,6]{0,2,1:T(8,128)S(1)} %copy.43, f32[16,32]{1,0:T(8,128)S(1)} %select_divide_fusion), kind=kOutput, calls=%fused_computation.11 | convolution fusion | flops 757432320 | bytes 11921408 | tf_op jit(solution)/shard_map/mewg,ewgy->mwgy/dot_general | solution.py:33
  245.7 9.3 %convert_element_type.39 = bf16[16,160,768]{2,1,0:T(8,128)(2,1)} reshape(bf16[16,160,6,128]{3,2,1,0:T(8,128)(2,1)} %copy.47) | data formatting | bytes 7864320 | tf_op jit(solution)/shard_map/convert_element_type | solution.py:36
  255.0 92.8 %all-to-all-done.2 = bf16[2,2560,768]{2,0,1:T(2,128)(2,1)} async-done(((bf16[2,2560,768]{2,0,1:T(2,128)(2,1)}), bf16[2,2560,768]{2,0,1:T(2,128)(2,1)}, u32[]{:S(2)}, u32[]{:S(2)}) %all-to-all-start.2) | async-done | bytes 7864352 | tf_op jit(solution)/shard_map/all_to_all | solution.py:57
  347.9 34.4 %all-to-all-start.1 = ((bf16[16,160,768]{2,1,0:T(8,128)(2,1)}), bf16[16,160,768]{2,1,0:T(8,128)(2,1)}, u32[]{:S(2)}, u32[]{:S(2)}) async-start(bf16[16,160,768]{2,1,0:T(8,128)(2,1)} %convert_element_type.39), calls=%async_computation.1 | async-start | bytes 7864320 | tf_op jit(solution)/shard_map/all_to_all | solution.py:63
  383.6 8.0 %copy.68 = bf16[2,16,160,768]{3,2,0,1:T(8,128)(2,1)} copy(bf16[2,16,160,768]{3,0,2,1:T(2,128)(2,1)} %bitcast.8) | data formatting | bytes 15728640 | tf_op jit(solution)/shard_map/all_to_all | solution.py:57
  391.6 16.8 %reshape.154 = bf16[32,160,6,128]{3,2,1,0:T(8,128)(2,1)} reshape(bf16[16,2,160,768]{3,2,1,0:T(8,128)(2,1)} %bitcast.52) | data formatting | bytes 15728640 | tf_op jit(solution)/shard_map/reshape | solution.py:30
  408.4 10.3 %convert_bitcast_fusion = bf16[16,160,6,128]{3,0,2,1:T(8,128)(2,1)S(1)} fusion(bf16[32,160,6,128]{3,2,1,0:T(8,128)(2,1)} %reshape.154, f32[32,160,6]{0,2,1:T(8,128)S(1)} %copy.48, f32[16,32]{1,0:T(8,128)S(1)} %select_divide_fusion), kind=kOutput, calls=%fused_computation.9 | convolution fusion | flops 757432320 | bytes 11921408 | tf_op jit(solution)/shard_map/mewg,ewgy->mwgy/dot_general | solution.py:33
  422.4 9.3 %convert_element_type.42 = bf16[16,160,768]{2,1,0:T(8,128)(2,1)} reshape(bf16[16,160,6,128]{3,2,1,0:T(8,128)(2,1)} %copy.52) | data formatting | bytes 7864320 | tf_op jit(solution)/shard_map/convert_element_type | solution.py:36
  431.6 55.3 %all-to-all-done.1 = bf16[16,160,768]{2,1,0:T(8,128)(2,1)} async-done(((bf16[16,160,768]{2,1,0:T(8,128)(2,1)}), bf16[16,160,768]{2,1,0:T(8,128)(2,1)}, u32[]{:S(2)}, u32[]{:S(2)}) %all-to-all-start.1) | async-done | bytes 3932192 | tf_op jit(solution)/shard_map/all_to_all | solution.py:63
  487.0 18.6 %all-to-all-start.3 = ((bf16[16,160,768]{2,1,0:T(8,128)(2,1)}), bf16[16,160,768]{2,1,0:T(8,128)(2,1)}, u32[]{:S(2)}, u32[]{:S(2)}) async-start(bf16[16,160,768]{2,1,0:T(8,128)(2,1)} %convert_element_type.42), calls=%async_computation.3 | async-start | bytes 7864320 | tf_op jit(solution)/shard_map/all_to_all | solution.py:64
  506.1 6.3 fusion.28
  518.5 6.7 %fusion.29 = f32[768,768]{1,0:T(8,128)} fusion(bf16[768,2560]{1,0:T(8,128)(2,1)S(1)} %bitcast.54, bf16[2560,768]{1,0:T(8,128)(2,1)} %bitcast.17), kind=kOutput, calls=%fused_computation.46 | convolution fusion | flops 3019898880 | bytes 10223616 | tf_op jit(solution)/shard_map/dot_general | solution.py:80
  525.3 53.5 %all-to-all-done.3 = bf16[16,160,768]{2,1,0:T(8,128)(2,1)} async-done(((bf16[16,160,768]{2,1,0:T(8,128)(2,1)}), bf16[16,160,768]{2,1,0:T(8,128)(2,1)}, u32[]{:S(2)}, u32[]{:S(2)}) %all-to-all-start.3) | async-done | bytes 3932192 | tf_op jit(solution)/shard_map/all_to_all | solution.py:64
  578.7 8.5 %multiply_convert_fusion = bf16[768,768]{1,0:T(8,128)(2,1)} fusion(f32[768,768]{1,0:T(8,128)} %fusion.29, bf16[768,2560]{1,0:T(8,128)(2,1)} %bitcast.55, bf16[2560,768]{1,0:T(8,128)(2,1)} %bitcast.18), kind=kOutput, calls=%fused_computation.15 | convolution fusion | flops 3024617472 | bytes 11403264 | tf_op jit(solution)/shard_map/dot_general | solution.py:82
  587.2 18.6 %all-to-all-start.4 = ((bf16[16,48,768]{2,1,0:T(8,128)(2,1)}), bf16[16,48,768]{2,1,0:T(8,128)(2,1)S(1)}, u32[]{:S(2)}, u32[]{:S(2)}) async-start(bf16[16,48,768]{2,1,0:T(8,128)(2,1)} %bitcast.19), calls=%async_computation.4 | async-start | bytes 2359296 | tf_op jit(solution)/shard_map/all_to_all | solution.py:86
  610.1 20.8 %all-to-all-done.4 = bf16[16,48,768]{2,1,0:T(8,128)(2,1)S(1)} async-done(((bf16[16,48,768]{2,1,0:T(8,128)(2,1)}), bf16[16,48,768]{2,1,0:T(8,128)(2,1)S(1)}, u32[]{:S(2)}, u32[]{:S(2)}) %all-to-all-start.4) | async-done | bytes 1179680 | tf_op jit(solution)/shard_map/all_to_all | solution.py:86
  632.7 4.3 copy.73
  (46 shorter events, 26.3 us)
Async XLA Ops:
  7.2 199.1 %copy-start = (f32[32,20,6]{0,1,2:T(8,128)S(1)}, f32[32,20,6]{0,1,2:T(8,128)}, u32[]{:S(2)}) copy-start(f32[32,20,6]{0,1,2:T(8,128)} %param.12) | copy-start | bytes 46084
  22.8 149.0 %all-to-all-start = ((bf16[2,2560,768]{2,0,1:T(2,128)(2,1)}), bf16[2,2560,768]{2,0,1:T(2,128)(2,1)}, u32[]{:S(2)}, u32[]{:S(2)}) async-start(bf16[2,2560,768]{2,0,1:T(2,128)(2,1)} %copy.44), calls=%async_computation | async-start | bytes 15728640 | tf_op jit(solution)/shard_map/all_to_all | solution.py:56
  45.9 161.0 %copy-start.5 = (f32[32]{0:T(128)S(1)}, f32[32]{0:T(128)}, u32[]{:S(2)}) copy-start(f32[32]{0:T(128)} %param.15) | copy-start | bytes 388
  45.9 161.1 %copy-start.6 = (s32[32,1]{0,1:T(1,128)S(1)}, s32[32,1]{0,1:T(1,128)}, u32[]{:S(2)}) copy-start(s32[32,1]{0,1:T(1,128)} %param.14) | copy-start | bytes 388
  171.8 176.0 %all-to-all-start.2 = ((bf16[2,2560,768]{2,0,1:T(2,128)(2,1)}), bf16[2,2560,768]{2,0,1:T(2,128)(2,1)}, u32[]{:S(2)}, u32[]{:S(2)}) async-start(bf16[2,2560,768]{2,0,1:T(2,128)(2,1)} %copy.49), calls=%async_computation.2 | async-start | bytes 15728640 | tf_op jit(solution)/shard_map/all_to_all | solution.py:57
  255.0 128.0 %copy-start.3 = (f32[32,20,6]{0,1,2:T(8,128)S(1)}, f32[32,20,6]{0,1,2:T(8,128)}, u32[]{:S(2)}) copy-start(f32[32,20,6]{0,1,2:T(8,128)} %param.13) | copy-start | bytes 46084
  347.9 139.1 %all-to-all-start.1 = ((bf16[16,160,768]{2,1,0:T(8,128)(2,1)}), bf16[16,160,768]{2,1,0:T(8,128)(2,1)}, u32[]{:S(2)}, u32[]{:S(2)}) async-start(bf16[16,160,768]{2,1,0:T(8,128)(2,1)} %convert_element_type.39), calls=%async_computation.1 | async-start | bytes 7864320 | tf_op jit(solution)/shard_map/all_to_all | solution.py:63
  382.3 130.7 %all-gather.2.cloned.1.call-start = ((), (), s32[]{:S(2)}) async-start(), calls=%async_computation.5 | async-start | bytes 5570560 | tf_op jit(solution)/shard_map/all_gather | solution.py:68
  431.6 74.0 %copy-start.4 = (s32[1024,6]{0,1:T(8,128)S(1)}, s32[1024,6]{0,1:T(8,128)}, u32[]{:S(2)}) copy-start(s32[1024,6]{0,1:T(8,128)} %param.9) | copy-start | bytes 73732
  487.0 91.8 %all-to-all-start.3 = ((bf16[16,160,768]{2,1,0:T(8,128)(2,1)}), bf16[16,160,768]{2,1,0:T(8,128)(2,1)}, u32[]{:S(2)}, u32[]{:S(2)}) async-start(bf16[16,160,768]{2,1,0:T(8,128)(2,1)} %convert_element_type.42), calls=%async_computation.3 | async-start | bytes 7864320 | tf_op jit(solution)/shard_map/all_to_all | solution.py:64
  516.6 1.9 copy-start.2
  587.2 43.7 %all-to-all-start.4 = ((bf16[16,48,768]{2,1,0:T(8,128)(2,1)}), bf16[16,48,768]{2,1,0:T(8,128)(2,1)S(1)}, u32[]{:S(2)}, u32[]{:S(2)}) async-start(bf16[16,48,768]{2,1,0:T(8,128)(2,1)} %bitcast.19), calls=%async_computation.4 | async-start | bytes 2359296 | tf_op jit(solution)/shard_map/all_to_all | solution.py:86
  632.7 8.6 %copy-start.1 = (f32[32,20,6]{0,1,2:T(8,128)S(1)}, f32[32,20,6]{0,1,2:T(8,128)}, u32[]{:S(2)}) copy-start(f32[32,20,6]{0,1,2:T(8,128)} %param.12) | copy-start | bytes 46084
Sparse Core Ops, SparseCore 0:
  385.4 97.2 all-gather.1
where the time goes:
time: 652 us; the launch traced here: 648 us
  waiting for transfers between devices  349 us (54%)
  local copies, waits for them, and re-layouts  121 us (19%)
  starting transfers between devices  114 us (17%)
  matrix products  40.6 us (6%)
  between operations  14.3 us (2%)
  other arithmetic  9.32 us (1%)
    all_to_all x1, waiting for transfers between devices, shards(): lax.all_to_all(quant_gate, 'expert', split_axis=1, concat_axis=0, tiled=T...  126 us
    all_to_all x1, waiting for transfers between devices, shards(): lax.all_to_all(quant_up, 'expert', split_axis=1, concat_axis=0, tiled=True)  92.8 us
    all_to_all x1, waiting for transfers between devices, shards(): lax.all_to_all(part_gate, 'expert', split_axis=0, concat_axis=1, tiled=True)  55.3 us
    all_to_all x1, waiting for transfers between devices, shards(): lax.all_to_all(part_up, 'expert', split_axis=0, concat_axis=1, tiled=True)  53.5 us
    unnamed x19, local copies, waits for them, and re-layouts  42.7 us
    all_to_all x1, starting transfers between devices, shards(): lax.all_to_all(quant_up, 'expert', split_axis=1, concat_axis=0, tiled=True)  34.4 us
    all_to_all x1, starting transfers between devices, shards(): lax.all_to_all(part_gate, 'expert', split_axis=0, concat_axis=1, tiled=True)  34.4 us
    reshape x2, local copies, waits for them, and re-layouts, merge_rows(): moved.reshape(source_count, count_of_rows, column_blocks, width // column...  33.6 us
  transfers between devices with their start and end apart: 6, of which 5 were waited for; matrix products, arithmetic and copies ran while one was open for 21% of the time, Pallas kernels for 0%

commit v1 on v0

v1 whole, which is shorter than its diff:
```python
import math

import jax
import jax.numpy as jnp
from jax import lax
from jax.experimental import pallas as pl
from jax.experimental.pallas import tpu as pltpu
from jax.sharding import PartitionSpec as P

D = 2560
BLOCK = 128
PLANES = 4
VMEM_LIMIT = 48 * 1024 * 1024


def cluster_weights(cluster_ids, frequency):
    ids = cluster_ids[:, 0]
    same = (ids[:, None] == ids[None, :]).astype(jnp.float32)
    return frequency / jnp.sum(same * frequency[None, :], axis=1)


def pack(info, gate, up, after, column, plane):
    sources, depth, _ = gate.shape
    rows = depth // plane

    def kernel(info_ref, gate_ref, up_ref, after_ref, *rest):
        outs, sems = rest[:plane], rest[plane]
        place = info_ref[0]

        def move(source):
            copies = [
                pltpu.make_async_copy(
                    source.at[
                        :,
                        pl.ds(pl.multiple_of((place ^ shift) * rows, 16), rows),
                        pl.ds(column * BLOCK, BLOCK),
                    ],
                    outs[shift],
                    sems.at[shift],
                )
                for shift in range(plane)
            ]
            for copy in copies:
                copy.start()
            for copy in copies:
                copy.wait()

        @pl.when(info_ref[2] == 0)
        def _():
            move(gate_ref)

        @pl.when(info_ref[2] != 0)
        def _():
            move(up_ref)

    any_spec = pl.BlockSpec(memory_space=pl.ANY)
    return pl.pallas_call(
        kernel,
        out_shape=[jax.ShapeDtypeStruct((sources, rows, BLOCK), gate.dtype)] * plane,
        in_specs=[pl.BlockSpec(memory_space=pltpu.SMEM)] + [any_spec] * 3,
        out_specs=[any_spec] * plane,
        scratch_shapes=[pltpu.SemaphoreType.DMA((plane,))],
        cost_estimate=pl.CostEstimate(
            flops=0, bytes_accessed=4 * sources * depth * BLOCK, transcendentals=0
        ),
        name="pack",
    )(info, gate, up, after)


def merge(info, ids, weights, scales, near, far, received, column, scale_blocks):
    plane, sources, rows, width = near.shape
    step = math.gcd(rows, BLOCK)
    row_blocks, column_blocks = scale_blocks

    def kernel(info_ref, ids_ref, weights_ref, scales_ref, near_ref, far_ref, *rest):
        total = rest[-1]
        place, inner = info_ref[0], info_ref[1]
        outer = jnp.where(inner == 1, 0, PLANES - 1)
        other_outer = PLANES - 1 - outer
        other_inner = PLANES - 1 - inner
        to_inner, to_outer = (
            (inner, outer) if received is not None else (other_inner, other_outer)
        )
        row_block = (place * rows + pl.program_id(0) * step) // BLOCK

        @pl.when(info_ref[3] == 1)
        def _():
            if received is None:
                total[...] = jnp.zeros_like(total)
            else:
                total[...] = rest[0][...].astype(jnp.float32)
            for block, held in ((near_ref, inner), (far_ref, outer)):
                for shift in range(plane):
                    for number in range(sources):
                        source = (held * plane + (place ^ shift)) * sources + number
                        target = ids_ref[source]
                        target_plane = target // plane
                        slot = (target % plane) ^ place

                        @pl.when((target_plane == to_inner) | (target_plane == to_outer))
                        def _():
                            scale = scales_ref[
                                (source * row_blocks + row_block) * column_blocks + column
                            ]
                            index = jnp.where(target_plane == to_outer, plane, 0) + slot
                            total[index] += block[shift, number].astype(jnp.float32) * (
                                weights_ref[source] * scale
                            )

            if received is None:
                rest[0][...] = total[...].astype(jnp.bfloat16)
            else:
                rest[1][...] = total[:plane].astype(jnp.bfloat16)
                rest[2][...] = total[plane:].astype(jnp.bfloat16)

    smem = pl.BlockSpec(memory_space=pltpu.SMEM)
    stack = pl.BlockSpec((plane, sources, step, width), lambda i: (0, 0, i, 0))
    both = pl.BlockSpec((2 * plane, step, width), lambda i: (0, i, 0))
    one = pl.BlockSpec((plane, step, width), lambda i: (0, i, 0))
    if received is None:
        operands, in_specs = (), []
        out_shape = jax.ShapeDtypeStruct((2 * plane, rows, width), jnp.bfloat16)
        out_specs = both
    else:
        operands, in_specs = (received,), [both]
        out_shape = [jax.ShapeDtypeStruct((plane, rows, width), jnp.bfloat16)] * 2
        out_specs = [one, one]
    return pl.pallas_call(
        kernel,
        grid=(rows // step,),
        out_shape=out_shape,
        in_specs=[smem] * 4 + [stack, stack] + in_specs,
        out_specs=out_specs,
        scratch_shapes=[pltpu.VMEM((2 * plane, step, width), jnp.float32)],
        compiler_params=pltpu.CompilerParams(vmem_limit_bytes=VMEM_LIMIT),
        cost_estimate=pl.CostEstimate(
            flops=4 * near.size, bytes_accessed=8 * near.size, transcendentals=0
        ),
        name="merge",
    )(info, ids, weights, scales, near, far, *operands)


def run_chunk(info, grouped, own, partner, outputs, column, shape):
    plane, rows, width = own.shape
    depth, full = shape
    count = grouped.shape[0]
    factor = 1.0 / math.sqrt(D)

    def kernel(info_ref, grouped_ref, own_ref, partner_ref, *rest):
        gate_out, up_out, hidden_ref, whole, sems, out_sems = rest[len(outputs) :]
        place = info_ref[0]

        def load(pieces, start, base):
            return [
                pltpu.make_async_copy(
                    pieces.at[shift],
                    whole.at[
                        pl.ds(pl.multiple_of((place ^ shift) * rows, 16), rows),
                        pl.ds(start, width),
                    ],
                    sems.at[base + shift],
                )
                for shift in range(plane)
            ]

        def fill(gate, up):
            copies = load(gate, 0, 0) + load(up, width, plane)
            for copy in copies:
                copy.start()
            for copy in copies:
                copy.wait()

        @pl.when(info_ref[2] == 0)
        def _():
            fill(own_ref, partner_ref)

        @pl.when(info_ref[2] != 0)
        def _():
            fill(partner_ref, own_ref)

        stores = [
            pltpu.make_async_copy(
                whole.at[:, pl.ds(index * width, width)],
                out.at[0, :, pl.ds(column * width, width)],
                out_sems.at[index],
            )
            for index, out in enumerate((gate_out, up_out))
        ]
        for store in stores:
            store.start()
        values = jnp.dot(grouped_ref[...], whole[...], preferred_element_type=jnp.float32)
        gate_value = values[:, :width] * factor
        up_value = values[:, width:] * factor
        hidden_ref[...] = (gate_value / (1.0 + jnp.exp(-gate_value)) * up_value).astype(
            jnp.bfloat16
        )
        for store in stores:
            store.wait()

    any_spec = pl.BlockSpec(memory_space=pl.ANY)
    weights = jax.ShapeDtypeStruct((1, depth, full), jnp.bfloat16)
    return pl.pallas_call(
        kernel,
        out_shape=[weights, weights, jax.ShapeDtypeStruct((count, width), jnp.bfloat16)],
        in_specs=[
            pl.BlockSpec(memory_space=pltpu.SMEM),
            pl.BlockSpec(memory_space=pltpu.VMEM),
            any_spec,
            any_spec,
        ]
        + [any_spec] * len(outputs),
        out_specs=[any_spec, any_spec, pl.BlockSpec(memory_space=pltpu.VMEM)],
        scratch_shapes=[
            pltpu.VMEM((depth, 2 * width), jnp.bfloat16),
            pltpu.SemaphoreType.DMA((2 * plane,)),
            pltpu.SemaphoreType.DMA((2,)),
        ],
        input_output_aliases={4 + index: index for index in range(len(outputs))},
        compiler_params=pltpu.CompilerParams(vmem_limit_bytes=VMEM_LIMIT),
        cost_estimate=pl.CostEstimate(
            flops=4 * count * depth * width,
            bytes_accessed=2 * (grouped.size + 4 * depth * width),
            transcendentals=count * width,
        ),
        name="run_chunk",
    )(info, grouped, own, partner, *outputs)


def route_slots(routes, merged_count, tok_dev):
    experts = jnp.arange(merged_count, dtype=jnp.int32)
    hit_table = jnp.sum((routes[:, :, None] == experts).astype(jnp.int32), axis=1)
    hit_table = hit_table.reshape(-1, tok_dev, merged_count)
    position_lookup = jnp.cumsum(hit_table, axis=1) - hit_table
    return (hit_table, position_lookup)


def shards(tokens, routes, quant_gate, quant_up, gate_scales, up_scales, cluster_ids, frequency):
    expert_count = lax.axis_size("expert")
    own_index = lax.axis_index("expert")
    group_count = lax.axis_size("groups")
    half = lax.axis_index("groups") % 2
    plane = expert_count // PLANES
    place, level = own_index % plane, own_index // plane
    is_inner = (level == 1) | (level == 2)
    depth, full = quant_gate.shape[1:]
    chunks = full // BLOCK
    tok_dev = tokens.shape[0]
    top_count = routes.shape[1]
    capacity = min(tok_dev, 2 * tok_dev * top_count // expert_count)

    def wires(pairs):
        return [(a * plane + p, b * plane + p) for a, b in pairs for p in range(plane)]

    inward = wires([(0, 1), (3, 2)])
    across = wires([(1, 2), (2, 1)])
    outward = wires([(1, 0), (2, 3)])
    within = {
        shift: [(i, i // plane * plane + (i % plane ^ shift)) for i in range(expert_count)]
        for shift in range(1, plane)
    }
    partners = [(g, g ^ 1) for g in range(group_count)]

    def swap_within(pieces):
        return [pieces[0]] + [
            lax.ppermute(pieces[shift], "expert", within[shift]) for shift in range(1, plane)
        ]

    info = jnp.stack([place, level, half, is_inner.astype(jnp.int32)]).astype(jnp.int32)
    ids = cluster_ids[:, 0]
    weights = cluster_weights(cluster_ids, frequency)
    scales = jnp.where(half == 0, gate_scales, up_scales)
    scale_blocks = scales.shape[1:]
    scales = scales.reshape(-1)

    hit_table, position_lookup = route_slots(routes, expert_count, tok_dev)
    positions = jnp.arange(capacity, dtype=jnp.int32)
    everyone = lax.all_gather(tokens, "expert", axis=0, tiled=True)
    column_hits = lax.dynamic_index_in_dim(hit_table, own_index, 2, keepdims=False)
    column_slots = lax.dynamic_index_in_dim(position_lookup, own_index, 2, keepdims=False)
    placing = (
        (column_hits[:, None, :] == 1) & (column_slots[:, None, :] == positions[None, :, None])
    ).astype(jnp.bfloat16)
    spread = everyone.reshape(expert_count, tok_dev, everyone.shape[1])
    arrived = jnp.einsum(
        "jct,jtd->jcd", placing, spread, preferred_element_type=jnp.float32
    ).astype(jnp.bfloat16)
    arrived = lax.all_gather(arrived, "mp", axis=2, tiled=True)
    grouped = arrived.reshape(expert_count * capacity, arrived.shape[2])

    experts = jnp.arange(expert_count, dtype=jnp.int32)
    local_routes = lax.dynamic_slice_in_dim(routes, own_index * tok_dev, tok_dev, 0)
    own_slots = lax.dynamic_index_in_dim(position_lookup, own_index, 0, keepdims=False)
    chosen = local_routes[:, :, None] == experts
    slot_of = jnp.sum(jnp.where(chosen, own_slots[:, None, :], 0), axis=2)
    picking = (chosen[:, :, :, None] & (slot_of[:, :, None, None] == positions)).astype(
        jnp.bfloat16
    )
    picking = picking.reshape(tok_dev * top_count, expert_count * capacity)

    arrivals = []
    hiddens = []
    outputs = ()
    for column in range(chunks):
        after = arrivals[column - 2] if column >= 2 else info
        pieces = pack(info, quant_gate, quant_up, after, column, plane)
        near = jnp.stack(swap_within(pieces))
        far = lax.ppermute(near, "expert", inward)
        arrivals.append(far)
        partial = merge(info, ids, weights, scales, near, far, None, column, scale_blocks)
        received = lax.ppermute(partial, "expert", across)
        to_inner, to_outer = merge(
            info, ids, weights, scales, near, far, received, column, scale_blocks
        )
        mine = jnp.where(is_inner, to_inner, lax.ppermute(to_outer, "expert", outward))
        own = jnp.stack(swap_within([mine[shift] for shift in range(plane)]))
        partner = lax.ppermute(own, "groups", partners)
        *outputs, hidden = run_chunk(
            info, grouped, own, partner, tuple(outputs), column, (depth, full)
        )
        hiddens.append(hidden.reshape(expert_count, capacity, BLOCK))

    cut = max(1, chunks - 2)
    finished = []
    for batch in (hiddens[:cut], hiddens[cut:]):
        hidden = jnp.concatenate(batch, axis=2)
        returned = lax.all_to_all(hidden, "expert", split_axis=0, concat_axis=0, tiled=True)
        rows = returned.reshape(expert_count * capacity, returned.shape[2])
        finished.append(
            jnp.dot(picking, rows, preferred_element_type=jnp.float32).astype(jnp.bfloat16)
        )
    output = jnp.concatenate(finished, axis=1)
    merged_gate, merged_up = outputs
    return (merged_gate, merged_up, output.reshape(tok_dev, top_count, full))


def solution(mesh):
    return jax.shard_map(
        shards,
        mesh=mesh,
        in_specs=(
            P(("groups", "expert"), "mp"),
            P("groups", None),
            P("expert", None, "mp"),
            P("expert", None, "mp"),
            P(None, None, "mp"),
            P(None, None, "mp"),
            P(),
            P(),
        ),
        out_specs=(
            P(("groups", "expert"), None, "mp"),
            P(("groups", "expert"), None, "mp"),
            P(("groups", "expert"), None, "mp"),
        ),
        check_vma=False,
    )
```

time: 652 us -> 652 us (level)
  Pallas kernels: 0 us -> 309 us
  waiting for transfers between devices: 349 us -> 187 us
  local copies, waits for them, and re-layouts: 121 us -> 23 us
  matrix products: 40.6 us -> 4.55 us
  starting transfers between devices: 114 us -> 86 us
  other arithmetic: 9.32 us -> 25.4 us
    all_to_all x4 -> x0, waiting for transfers between devices: 328 us -> none  [the longest x1 126 us: shards(): lax.all_to_all(quant_gate, 'expert', split_axis=1, concat_axis=0, tiled=T...]
    pallas_call x0 -> x24, Pallas kernels: none -> 309 us  [the longest x6 249 us: pack(): pl.pallas_call(kernel, out_shape=[jax.ShapeDtypeStruct((sources, rows, BL...]
    ppermute x0 -> x60, waiting for transfers between devices: none -> 163 us  [the longest x6 44.7 us: shards(): partner = lax.ppermute(own, 'groups', partners)]
    all_to_all x4 -> x0, starting transfers between devices: 94.9 us -> none  [the longest x1 34.4 us: shards(): lax.all_to_all(quant_up, 'expert', split_axis=1, concat_axis=0, tiled=True)]
    ppermute x0 -> x60, starting transfers between devices: none -> 76.8 us  [the longest x6 28 us: shards(): far = lax.ppermute(near, 'expert', inward)]
    dot_general x8 -> x3, matrix products: 40.6 us -> 4.55 us  [the longest x1 3.75 us: shards(): jnp.einsum('jct,jtd->jcd', placing, spread, preferred_element_type=jnp.fl...]
    reshape x3 -> x2, local copies, waits for them, and re-layouts: 33.8 us -> 0.39 us  [the longest x1 0.2 us: shards(): scales = scales.reshape(-1)]
    unnamed x19 -> x113, local copies, waits for them, and re-layouts: 42.7 us -> 16.3 us
  transfers between devices with their start and end apart: 6 -> 63, of which waited for: 5 -> 27; matrix products, arithmetic and copies ran while one was open for 21% -> 5% of each run, Pallas kernels for 0% -> 47%
where the time goes in v1:
time: 652 us; the launch traced here: 650 us
  Pallas kernels  309 us (47%)
  waiting for transfers between devices  187 us (29%)
  starting transfers between devices  86 us (13%)
  other arithmetic  25.4 us (4%)
  local copies, waits for them, and re-layouts  23 us (4%)
  between operations  15.1 us (2%)
    pallas_call x6, Pallas kernels, pack(): pl.pallas_call(kernel, out_shape=[jax.ShapeDtypeStruct((sources, rows, BL...  249 us
    ppermute x6, waiting for transfers between devices, shards(): partner = lax.ppermute(own, 'groups', partners)  44.7 us
    ppermute x6, waiting for transfers between devices, shards(): lax.ppermute(to_outer, 'expert', outward)  43.7 us
    pallas_call x12, Pallas kernels, merge(): pl.pallas_call(kernel, grid=(rows // step,), out_shape=out_shape, in_spec...  42 us
    ppermute x36, waiting for transfers between devices, swap_within(): lax.ppermute(pieces[shift], 'expert', within[shift])  38.8 us
    ppermute x6, waiting for transfers between devices, shards(): far = lax.ppermute(near, 'expert', inward)  35.3 us
    ppermute x6, starting transfers between devices, shards(): far = lax.ppermute(near, 'expert', inward)  28 us
    ppermute x36, starting transfers between devices, swap_within(): lax.ppermute(pieces[shift], 'expert', within[shift])  24.9 us
  transfers between devices with their start and end apart: 63, of which 27 were waited for; matrix products, arithmetic and copies ran while one was open for 5% of the time, Pallas kernels for 47%

profile of v1, /device:TPU:0, one launch (start us, length us, event | category | flops | bytes accessed | tf_op | source)
XLA Modules:
  0.0 650.3 jit_solution(10755027163333308391)
XLA Ops:
  8.5 41.5 %pack.6 = (bf16[2,640,128]{2,1,0:T(8,128)(2,1)}, bf16[2,640,128]{2,1,0:T(8,128)(2,1)}, bf16[2,640,128]{2,1,0:T(8,128)(2,1)}, bf16[2,640,128]{2,1,0:T(8,128)(2,1)}) custom-call(s32[4]{0:T(128)} %pad_add_fusion.info_ref.after_ref, bf16[2,2560,768]{2,1,0:T(8,128)(2,1)} %gate_ref.11, bf16[2,2560,768]{2,1,0:T(8,128)(2,1)} %up_ref.11, s32[4]{0:T(128)} %pad_add_fusion.info_ref.after_ref), custom_call_target="tpu_custom_call" | custom-call | bytes 2621440 | tf_op jit(solution)/shard_map/pack/pallas_call | solution.py:57
  53.2 41.6 %pack.9 = (bf16[2,640,128]{2,1,0:T(8,128)(2,1)}, bf16[2,640,128]{2,1,0:T(8,128)(2,1)}, bf16[2,640,128]{2,1,0:T(8,128)(2,1)}, bf16[2,640,128]{2,1,0:T(8,128)(2,1)}) custom-call(s32[4]{0:T(128)} %pad_add_fusion.info_ref.after_ref, bf16[2,2560,768]{2,1,0:T(8,128)(2,1)} %gate_ref.11, bf16[2,2560,768]{2,1,0:T(8,128)(2,1)} %up_ref.11, s32[4]{0:T(128)} %pad_add_fusion.info_ref.after_ref), custom_call_target="tpu_custom_call" | custom-call | bytes 2621440 | tf_op jit(solution)/shard_map/pack/pallas_call | solution.py:57
  100.7 5.1 collective-permute-done.19
  105.9 5.9 collective-permute-done.20
  116.4 13.3 %collective-permute-done.3.after_ref.far_ref = bf16[4,2,640,128]{3,2,1,0:T(8,128)(2,1)S(1)} collective-permute-done((bf16[4,2,640,128]{3,2,1,0:T(8,128)(2,1)S(1)}, bf16[4,2,640,128]{3,2,1,0:T(8,128)(2,1)S(1)}, u32[]{:S(2)}, u32[]{:S(2)}) %collective-permute-start.3) | collective-permute-done | bytes 1310752 | tf_op jit(solution)/shard_map/ppermute | solution.py:307
  130.8 41.5 %pack.7 = (bf16[2,640,128]{2,1,0:T(8,128)(2,1)}, bf16[2,640,128]{2,1,0:T(8,128)(2,1)}, bf16[2,640,128]{2,1,0:T(8,128)(2,1)}, bf16[2,640,128]{2,1,0:T(8,128)(2,1)}) custom-call(s32[4]{0:T(128)} %pad_add_fusion.info_ref.after_ref, bf16[2,2560,768]{2,1,0:T(8,128)(2,1)} %gate_ref.11, bf16[2,2560,768]{2,1,0:T(8,128)(2,1)} %up_ref.11, ...), custom_call_target="tpu_custom_call" | custom-call | bytes 2621440 | tf_op jit(solution)/shard_map/pack/pallas_call | solution.py:57
  175.3 41.5 %pack.10 = (bf16[2,640,128]{2,1,0:T(8,128)(2,1)}, bf16[2,640,128]{2,1,0:T(8,128)(2,1)}, bf16[2,640,128]{2,1,0:T(8,128)(2,1)}, bf16[2,640,128]{2,1,0:T(8,128)(2,1)}) custom-call(s32[4]{0:T(128)} %pad_add_fusion.info_ref.after_ref, bf16[2,2560,768]{2,1,0:T(8,128)(2,1)} %gate_ref.11, bf16[2,2560,768]{2,1,0:T(8,128)(2,1)} %up_ref.11, ...), custom_call_target="tpu_custom_call" | custom-call | bytes 2621440 | tf_op jit(solution)/shard_map/pack/pallas_call | solution.py:57
  228.0 5.6 collective-permute-done.24
  256.1 41.5 %pack.8 = (bf16[2,640,128]{2,1,0:T(8,128)(2,1)}, bf16[2,640,128]{2,1,0:T(8,128)(2,1)}, bf16[2,640,128]{2,1,0:T(8,128)(2,1)}, bf16[2,640,128]{2,1,0:T(8,128)(2,1)}) custom-call(s32[4]{0:T(128)} %pad_add_fusion.info_ref.after_ref, bf16[2,2560,768]{2,1,0:T(8,128)(2,1)} %gate_ref.11, bf16[2,2560,768]{2,1,0:T(8,128)(2,1)} %up_ref.11, bf16[4,2,640,128]{3,2,1,0:T(8,128)(2,1)} %copy-done), custom_call_target="tpu_custom_call" | custom-call | bytes 2621440 | tf_op jit(solution)/shard_map/pack/pallas_call | solution.py:57
  300.4 41.5 %pack.11 = (bf16[2,640,128]{2,1,0:T(8,128)(2,1)}, bf16[2,640,128]{2,1,0:T(8,128)(2,1)}, bf16[2,640,128]{2,1,0:T(8,128)(2,1)}, bf16[2,640,128]{2,1,0:T(8,128)(2,1)}) custom-call(s32[4]{0:T(128)} %pad_add_fusion.info_ref.after_ref, bf16[2,2560,768]{2,1,0:T(8,128)(2,1)} %gate_ref.11, bf16[2,2560,768]{2,1,0:T(8,128)(2,1)} %up_ref.11, ...), custom_call_target="tpu_custom_call" | custom-call | bytes 2621440 | tf_op jit(solution)/shard_map/pack/pallas_call | solution.py:57
  352.4 7.3 %collective-permute-start.11 = (bf16[4,2,640,128]{3,2,1,0:T(8,128)(2,1)S(1)}, bf16[4,2,640,128]{3,2,1,0:T(8,128)(2,1)S(1)}, u32[]{:S(2)}, u32[]{:S(2)}) collective-permute-start(bf16[4,2,640,128]{3,2,1,0:T(8,128)(2,1)S(1)} %pad_maximum_fusion.2.near_ref), channel_id=1, source_target_pairs={{0,4},{1,5},{2,6},{3,7},{12,8},{13,9},{14,10},{15,11},{16,20},{17,... | collective-permute-start | bytes 3932168 | tf_op jit(solution)/shard_map/ppermute | solution.py:307
  379.0 9.6 %collective-permute-done.55 = bf16[4,640,128]{2,1,0:T(8,128)(2,1)S(1)} collective-permute-done((bf16[4,640,128]{2,1,0:T(8,128)(2,1)}, bf16[4,640,128]{2,1,0:T(8,128)(2,1)S(1)}, u32[]{:S(2)}, u32[]{:S(2)}) %collective-permute-start.55) | collective-permute-done | bytes 655392 | tf_op jit(solution)/shard_map/ppermute | solution.py:314
  394.9 21.5 %collective-permute-done.29.far_ref = bf16[4,2,640,128]{3,2,1,0:T(8,128)(2,1)S(1)} collective-permute-done((bf16[4,2,640,128]{3,2,1,0:T(8,128)(2,1)S(1)}, bf16[4,2,640,128]{3,2,1,0:T(8,128)(2,1)S(1)}, u32[]{:S(2)}, u32[]{:S(2)}) %collective-permute-start.29) | collective-permute-done | bytes 1310752 | tf_op jit(solution)/shard_map/ppermute | solution.py:307
  442.4 6.3 fusion.11
  466.1 5.5 collective-permute-done.37
  471.5 14.0 %collective-permute-done.43 = bf16[4,640,128]{2,1,0:T(8,128)(2,1)} collective-permute-done((bf16[4,640,128]{2,1,0:T(8,128)(2,1)}, bf16[4,640,128]{2,1,0:T(8,128)(2,1)}, u32[]{:S(2)}, u32[]{:S(2)}) %collective-permute-start.43) | collective-permute-done | bytes 655392 | tf_op jit(solution)/shard_map/ppermute | solution.py:314
  500.2 14.1 %collective-permute-done.31 = bf16[4,640,128]{2,1,0:T(8,128)(2,1)S(1)} collective-permute-done((bf16[4,640,128]{2,1,0:T(8,128)(2,1)S(1)}, bf16[4,640,128]{2,1,0:T(8,128)(2,1)S(1)}, u32[]{:S(2)}, u32[]{:S(2)}) %collective-permute-start.31) | collective-permute-done | bytes 655392 | tf_op jit(solution)/shard_map/ppermute | solution.py:314
  545.8 10.3 %collective-permute-done.47.partner_ref = bf16[4,640,128]{2,1,0:T(8,128)(2,1)} collective-permute-done((bf16[4,640,128]{2,1,0:T(8,128)(2,1)S(1)}, bf16[4,640,128]{2,1,0:T(8,128)(2,1)}, u32[]{:S(2)}, u32[]{:S(2)}) %collective-permute-start.47) | collective-permute-done | bytes 655392 | tf_op jit(solution)/shard_map/ppermute | solution.py:316
  559.1 10.9 %collective-permute-done.41.partner_ref = bf16[4,640,128]{2,1,0:T(8,128)(2,1)} collective-permute-done((bf16[4,640,128]{2,1,0:T(8,128)(2,1)S(1)}, bf16[4,640,128]{2,1,0:T(8,128)(2,1)}, u32[]{:S(2)}, u32[]{:S(2)}) %collective-permute-start.41) | collective-permute-done | bytes 655392 | tf_op jit(solution)/shard_map/ppermute | solution.py:316
  573.2 10.9 %collective-permute-done.35.partner_ref = bf16[4,640,128]{2,1,0:T(8,128)(2,1)} collective-permute-done((bf16[4,640,128]{2,1,0:T(8,128)(2,1)S(1)}, bf16[4,640,128]{2,1,0:T(8,128)(2,1)}, u32[]{:S(2)}, u32[]{:S(2)}) %collective-permute-start.35) | collective-permute-done | bytes 655392 | tf_op jit(solution)/shard_map/ppermute | solution.py:316
  587.2 10.7 %collective-permute-done.17.partner_ref = bf16[4,640,128]{2,1,0:T(8,128)(2,1)} collective-permute-done((bf16[4,640,128]{2,1,0:T(8,128)(2,1)S(1)}, bf16[4,640,128]{2,1,0:T(8,128)(2,1)}, u32[]{:S(2)}, u32[]{:S(2)}) %collective-permute-start.17) | collective-permute-done | bytes 655392 | tf_op jit(solution)/shard_map/ppermute | solution.py:316
  601.9 5.5 all-to-all-start.1
  608.3 11.2 %all-to-all-done.1 = bf16[16,48,256]{2,1,0:T(8,128)(2,1)S(1)} async-done(((bf16[16,48,256]{2,1,0:T(8,128)(2,1)}), bf16[16,48,256]{2,1,0:T(8,128)(2,1)S(1)}, u32[]{:S(2)}, u32[]{:S(2)}) %all-to-all-start.1) | async-done | bytes 393248 | tf_op jit(solution)/shard_map/all_to_all | solution.py:326
  628.8 13.0 %all-to-all-done = bf16[16,48,512]{2,1,0:T(8,128)(2,1)S(1)} async-done(((bf16[16,48,512]{2,1,0:T(8,128)(2,1)}), bf16[16,48,512]{2,1,0:T(8,128)(2,1)S(1)}, u32[]{:S(2)}, u32[]{:S(2)}) %all-to-all-start) | async-done | bytes 786464 | tf_op jit(solution)/shard_map/all_to_all | solution.py:326
  (290 shorter events, 205.2 us)
Async XLA Ops:
  7.2 527.1 %all-gather.2.cloned.1.call-start = ((), (), s32[]{:S(2)}) async-start(), calls=%async_computation.2 | async-start | bytes 5570560 | tf_op jit(solution)/shard_map/all_gather | solution.py:277
  50.1 46.8 %collective-permute-start = (bf16[2,640,128]{2,1,0:T(8,128)(2,1)}, bf16[2,640,128]{2,1,0:T(8,128)(2,1)S(1)}, u32[]{:S(2)}, u32[]{:S(2)}) collective-permute-start(bf16[2,640,128]{2,1,0:T(8,128)(2,1)} %get-tuple-element.58), channel_id=1, source_target_pairs={{0,1},{1,0},{2,3},{3,2},{4,5},{5,4},{6,7},{7,6},{8,9},{9,8},{10,11... | collective-permute-start | bytes 983048 | tf_op jit(solution)/shard_map/ppermute | solution.py:265
  50.6 46.3 %collective-permute-start.1 = (bf16[2,640,128]{2,1,0:T(8,128)(2,1)}, bf16[2,640,128]{2,1,0:T(8,128)(2,1)S(1)}, u32[]{:S(2)}, u32[]{:S(2)}) collective-permute-start(bf16[2,640,128]{2,1,0:T(8,128)(2,1)} %get-tuple-element.59), channel_id=1, source_target_pairs={{0,2},{1,3},{2,0},{3,1},{4,6},{5,7},{6,4},{7,5},{8,10},{9,11},{10,... | collective-permute-start | bytes 983048 | tf_op jit(solution)/shard_map/ppermute | solution.py:265
  53.2 43.7 %collective-permute-start.2 = (bf16[2,640,128]{2,1,0:T(8,128)(2,1)}, bf16[2,640,128]{2,1,0:T(8,128)(2,1)S(1)}, u32[]{:S(2)}, u32[]{:S(2)}) collective-permute-start(bf16[2,640,128]{2,1,0:T(8,128)(2,1)} %get-tuple-element.60), channel_id=1, source_target_pairs={{0,3},{1,2},{2,1},{3,0},{4,7},{5,6},{6,5},{7,4},{8,11},{9,10},{10,... | collective-permute-start | bytes 983048 | tf_op jit(solution)/shard_map/ppermute | solution.py:265
  113.0 61.3 %collective-permute-start.21 = (bf16[4,2,640,128]{3,2,1,0:T(8,128)(2,1)}, bf16[4,2,640,128]{3,2,1,0:T(8,128)(2,1)S(1)}, u32[]{:S(2)}, u32[]{:S(2)}) collective-permute-start(bf16[4,2,640,128]{3,2,1,0:T(8,128)(2,1)} %pad_maximum_fusion.3.near_ref), channel_id=1, source_target_pairs={{0,4},{1,5},{2,6},{3,7},{12,8},{13,9},{14,10},{15,11},{16,20},{17,... | collective-permute-start | bytes 3932168 | tf_op jit(solution)/shard_map/ppermute | solution.py:307
  172.3 46.5 %collective-permute-start.4 = (bf16[2,640,128]{2,1,0:T(8,128)(2,1)}, bf16[2,640,128]{2,1,0:T(8,128)(2,1)S(1)}, u32[]{:S(2)}, u32[]{:S(2)}) collective-permute-start(bf16[2,640,128]{2,1,0:T(8,128)(2,1)} %get-tuple-element.62), channel_id=1, source_target_pairs={{0,1},{1,0},{2,3},{3,2},{4,5},{5,4},{6,7},{7,6},{8,9},{9,8},{10,11... | collective-permute-start | bytes 983048 | tf_op jit(solution)/shard_map/ppermute | solution.py:265
  172.4 46.4 %collective-permute-start.5 = (bf16[2,640,128]{2,1,0:T(8,128)(2,1)}, bf16[2,640,128]{2,1,0:T(8,128)(2,1)S(1)}, u32[]{:S(2)}, u32[]{:S(2)}) collective-permute-start(bf16[2,640,128]{2,1,0:T(8,128)(2,1)} %get-tuple-element.63), channel_id=1, source_target_pairs={{0,2},{1,3},{2,0},{3,1},{4,6},{5,7},{6,4},{7,5},{8,10},{9,11},{10,... | collective-permute-start | bytes 983048 | tf_op jit(solution)/shard_map/ppermute | solution.py:265
  174.0 44.8 %collective-permute-start.6 = (bf16[2,640,128]{2,1,0:T(8,128)(2,1)}, bf16[2,640,128]{2,1,0:T(8,128)(2,1)}, u32[]{:S(2)}, u32[]{:S(2)}) collective-permute-start(bf16[2,640,128]{2,1,0:T(8,128)(2,1)} %get-tuple-element.64), channel_id=1, source_target_pairs={{0,3},{1,2},{2,1},{3,0},{4,7},{5,6},{6,5},{7,4},{8,11},{9,10},{10,... | collective-permute-start | bytes 983048 | tf_op jit(solution)/shard_map/ppermute | solution.py:265
  235.9 63.4 %collective-permute-start.25 = (bf16[4,2,640,128]{3,2,1,0:T(8,128)(2,1)}, bf16[4,2,640,128]{3,2,1,0:T(8,128)(2,1)S(1)}, u32[]{:S(2)}, u32[]{:S(2)}) collective-permute-start(bf16[4,2,640,128]{3,2,1,0:T(8,128)(2,1)} %pad_maximum_fusion.4.near_ref), channel_id=1, source_target_pairs={{0,4},{1,5},{2,6},{3,7},{12,8},{13,9},{14,10},{15,11},{16,20},{17,... | collective-permute-start | bytes 3932168 | tf_op jit(solution)/shard_map/ppermute | solution.py:307
  246.9 95.0 %collective-permute-start.48 = (bf16[8,640,128]{2,1,0:T(8,128)(2,1)}, bf16[8,640,128]{2,1,0:T(8,128)(2,1)}, u32[]{:S(2)}, u32[]{:S(2)}) collective-permute-start(bf16[8,640,128]{2,1,0:T(8,128)(2,1)} %merge.20), channel_id=1, source_target_pairs={{4,8},{5,9},{6,10},{7,11},{8,4},{9,5},{10,6},{11,7},{20,24},{21,25... | collective-permute-start | bytes 3932168 | tf_op jit(solution)/shard_map/ppermute | solution.py:310
  252.6 112.1 %collective-permute-start.54 = (bf16[8,640,128]{2,1,0:T(8,128)(2,1)}, bf16[8,640,128]{2,1,0:T(8,128)(2,1)}, u32[]{:S(2)}, u32[]{:S(2)}) collective-permute-start(bf16[8,640,128]{2,1,0:T(8,128)(2,1)} %merge.22), channel_id=1, source_target_pairs={{4,8},{5,9},{6,10},{7,11},{8,4},{9,5},{10,6},{11,7},{20,24},{21,25... | collective-permute-start | bytes 3932168 | tf_op jit(solution)/shard_map/ppermute | solution.py:310
  297.6 44.6 %collective-permute-start.8 = (bf16[2,640,128]{2,1,0:T(8,128)(2,1)}, bf16[2,640,128]{2,1,0:T(8,128)(2,1)S(1)}, u32[]{:S(2)}, u32[]{:S(2)}) collective-permute-start(bf16[2,640,128]{2,1,0:T(8,128)(2,1)} %get-tuple-element.66), channel_id=1, source_target_pairs={{0,1},{1,0},{2,3},{3,2},{4,5},{5,4},{6,7},{7,6},{8,9},{9,8},{10,11... | collective-permute-start | bytes 983048 | tf_op jit(solution)/shard_map/ppermute | solution.py:265
  297.7 45.5 %collective-permute-start.9 = (bf16[2,640,128]{2,1,0:T(8,128)(2,1)}, bf16[2,640,128]{2,1,0:T(8,128)(2,1)S(1)}, u32[]{:S(2)}, u32[]{:S(2)}) collective-permute-start(bf16[2,640,128]{2,1,0:T(8,128)(2,1)} %get-tuple-element.67), channel_id=1, source_target_pairs={{0,2},{1,3},{2,0},{3,1},{4,6},{5,7},{6,4},{7,5},{8,10},{9,11},{10,... | collective-permute-start | bytes 983048 | tf_op jit(solution)/shard_map/ppermute | solution.py:265
  299.3 50.6 %collective-permute-start.10 = (bf16[2,640,128]{2,1,0:T(8,128)(2,1)}, bf16[2,640,128]{2,1,0:T(8,128)(2,1)}, u32[]{:S(2)}, u32[]{:S(2)}) collective-permute-start(bf16[2,640,128]{2,1,0:T(8,128)(2,1)} %get-tuple-element.68), channel_id=1, source_target_pairs={{0,3},{1,2},{2,1},{3,0},{4,7},{5,6},{6,5},{7,4},{8,11},{9,10},{10,... | collective-permute-start | bytes 983048 | tf_op jit(solution)/shard_map/ppermute | solution.py:265
  360.0 56.3 %collective-permute-start.29 = (bf16[4,2,640,128]{3,2,1,0:T(8,128)(2,1)S(1)}, bf16[4,2,640,128]{3,2,1,0:T(8,128)(2,1)S(1)}, u32[]{:S(2)}, u32[]{:S(2)}) collective-permute-start(bf16[4,2,640,128]{3,2,1,0:T(8,128)(2,1)S(1)} %pad_maximum_fusion.5.near_ref), channel_id=1, source_target_pairs={{0,4},{1,5},{2,6},{3,7},{12,8},{13,9},{14,10},{15,11},{16,20},{17,... | collective-permute-start | bytes 3932168 | tf_op jit(solution)/shard_map/ppermute | solution.py:307
  374.3 50.2 %collective-permute-start.36 = (bf16[8,640,128]{2,1,0:T(8,128)(2,1)S(1)}, bf16[8,640,128]{2,1,0:T(8,128)(2,1)S(1)}, u32[]{:S(2)}, u32[]{:S(2)}) collective-permute-start(bf16[8,640,128]{2,1,0:T(8,128)(2,1)S(1)} %merge.16), channel_id=1, source_target_pairs={{4,8},{5,9},{6,10},{7,11},{8,4},{9,5},{10,6},{11,7},{20,24},{21,25... | collective-permute-start | bytes 3932168 | tf_op jit(solution)/shard_map/ppermute | solution.py:310
  378.2 47.7 %collective-permute-start.42 = (bf16[8,640,128]{2,1,0:T(8,128)(2,1)S(1)}, bf16[8,640,128]{2,1,0:T(8,128)(2,1)S(1)}, u32[]{:S(2)}, u32[]{:S(2)}) collective-permute-start(bf16[8,640,128]{2,1,0:T(8,128)(2,1)S(1)} %merge.18), channel_id=1, source_target_pairs={{4,8},{5,9},{6,10},{7,11},{8,4},{9,5},{10,6},{11,7},{20,24},{21,25... | collective-permute-start | bytes 3932168 | tf_op jit(solution)/shard_map/ppermute | solution.py:310
  393.1 63.7 %collective-permute-start.12 = (bf16[8,640,128]{2,1,0:T(8,128)(2,1)}, bf16[8,640,128]{2,1,0:T(8,128)(2,1)}, u32[]{:S(2)}, u32[]{:S(2)}) collective-permute-start(bf16[8,640,128]{2,1,0:T(8,128)(2,1)} %merge.12), channel_id=1, source_target_pairs={{4,8},{5,9},{6,10},{7,11},{8,4},{9,5},{10,6},{11,7},{20,24},{21,25... | collective-permute-start | bytes 3932168 | tf_op jit(solution)/shard_map/ppermute | solution.py:310
  419.4 42.1 %collective-permute-start.30 = (bf16[8,640,128]{2,1,0:T(8,128)(2,1)}, bf16[8,640,128]{2,1,0:T(8,128)(2,1)}, u32[]{:S(2)}, u32[]{:S(2)}) collective-permute-start(bf16[8,640,128]{2,1,0:T(8,128)(2,1)} %merge.14), channel_id=1, source_target_pairs={{4,8},{5,9},{6,10},{7,11},{8,4},{9,5},{10,6},{11,7},{20,24},{21,25... | collective-permute-start | bytes 3932168 | tf_op jit(solution)/shard_map/ppermute | solution.py:310
  441.0 44.5 %collective-permute-start.43 = (bf16[4,640,128]{2,1,0:T(8,128)(2,1)}, bf16[4,640,128]{2,1,0:T(8,128)(2,1)}, u32[]{:S(2)}, u32[]{:S(2)}) collective-permute-start(bf16[4,640,128]{2,1,0:T(8,128)(2,1)} %get-tuple-element.88), channel_id=1, source_target_pairs={{4,0},{5,1},{6,2},{7,3},{8,12},{9,13},{10,14},{11,15},{20,16},{21,... | collective-permute-start | bytes 1966088 | tf_op jit(solution)/shard_map/ppermute | solution.py:314
  464.8 49.5 %collective-permute-start.31 = (bf16[4,640,128]{2,1,0:T(8,128)(2,1)S(1)}, bf16[4,640,128]{2,1,0:T(8,128)(2,1)S(1)}, u32[]{:S(2)}, u32[]{:S(2)}) collective-permute-start(bf16[4,640,128]{2,1,0:T(8,128)(2,1)S(1)} %get-tuple-element.84), channel_id=1, source_target_pairs={{4,0},{5,1},{6,2},{7,3},{8,12},{9,13},{10,14},{11,15},{20,16},{21,... | collective-permute-start | bytes 1966088 | tf_op jit(solution)/shard_map/ppermute | solution.py:314
  489.1 44.0 %collective-permute-start.59 = (bf16[4,640,128]{2,1,0:T(8,128)(2,1)S(1)}, bf16[4,640,128]{2,1,0:T(8,128)(2,1)S(1)}, u32[]{:S(2)}, u32[]{:S(2)}) collective-permute-start(bf16[4,640,128]{2,1,0:T(8,128)(2,1)S(1)} %pad_maximum_fusion.12.own_ref), channel_id=1, source_target_pairs={{0,16},{16,0},{1,17},{17,1},{2,18},{18,2},{3,19},{19,3},{4,20},{20... | collective-permute-start | bytes 1966088 | tf_op jit(solution)/shard_map/ppermute | solution.py:316
  531.3 52.8 %collective-permute-start.35 = (bf16[4,640,128]{2,1,0:T(8,128)(2,1)S(1)}, bf16[4,640,128]{2,1,0:T(8,128)(2,1)}, u32[]{:S(2)}, u32[]{:S(2)}) collective-permute-start(bf16[4,640,128]{2,1,0:T(8,128)(2,1)S(1)} %pad_maximum_fusion.8.own_ref), channel_id=1, source_target_pairs={{0,16},{16,0},{1,17},{17,1},{2,18},{18,2},{3,19},{19,3},{4,20},{20... | collective-permute-start | bytes 1966088 | tf_op jit(solution)/shard_map/ppermute | solution.py:316
  533.9 64.1 %collective-permute-start.17 = (bf16[4,640,128]{2,1,0:T(8,128)(2,1)S(1)}, bf16[4,640,128]{2,1,0:T(8,128)(2,1)}, u32[]{:S(2)}, u32[]{:S(2)}) collective-permute-start(bf16[4,640,128]{2,1,0:T(8,128)(2,1)S(1)} %pad_maximum_fusion.7.own_ref), channel_id=1, source_target_pairs={{0,16},{16,0},{1,17},{17,1},{2,18},{18,2},{3,19},{19,3},{4,20},{20... | collective-permute-start | bytes 1966088 | tf_op jit(solution)/shard_map/ppermute | solution.py:316
  (95 other events, 1193.8 us)
Sparse Core Ops, SparseCore 0:
  10.3 60.2 all-gather.1

commit v2 on v1

--- a/solution.py
+++ b/solution.py
@@ -24,26 +24,33 @@
     rows = depth // plane
 
     def kernel(info_ref, gate_ref, up_ref, after_ref, *rest):
-        outs, sems = rest[:plane], rest[plane]
+        outs, held, in_sems, out_sems = rest[:plane], *rest[plane:]
         place = info_ref[0]
 
         def move(source):
-            copies = [
+            loads = [
                 pltpu.make_async_copy(
                     source.at[
                         :,
                         pl.ds(pl.multiple_of((place ^ shift) * rows, 16), rows),
                         pl.ds(column * BLOCK, BLOCK),
                     ],
-                    outs[shift],
-                    sems.at[shift],
+                    held.at[shift],
+                    in_sems.at[shift],
                 )
                 for shift in range(plane)
             ]
-            for copy in copies:
-                copy.start()
-            for copy in copies:
-                copy.wait()
+            stores = [
+                pltpu.make_async_copy(held.at[shift], outs[shift], out_sems.at[shift])
+                for shift in range(plane)
+            ]
+            for load in loads:
+                load.start()
+            for load, store in zip(loads, stores):
+                load.wait()
+                store.start()
+            for store in stores:
+                store.wait()
 
         @pl.when(info_ref[2] == 0)
         def _():
@@ -59,7 +66,12 @@
         out_shape=[jax.ShapeDtypeStruct((sources, rows, BLOCK), gate.dtype)] * plane,
         in_specs=[pl.BlockSpec(memory_space=pltpu.SMEM)] + [any_spec] * 3,
         out_specs=[any_spec] * plane,
-        scratch_shapes=[pltpu.SemaphoreType.DMA((plane,))],
+        scratch_shapes=[
+            pltpu.VMEM((plane, sources, rows, BLOCK), gate.dtype),
+            pltpu.SemaphoreType.DMA((plane,)),
+            pltpu.SemaphoreType.DMA((plane,)),
+        ],
+        compiler_params=pltpu.CompilerParams(vmem_limit_bytes=VMEM_LIMIT),
         cost_estimate=pl.CostEstimate(
             flops=0, bytes_accessed=4 * sources * depth * BLOCK, transcendentals=0
         ),

time: 652 us -> 498 us (0.76)
  Pallas kernels: 309 us -> 66.4 us
  waiting for transfers between devices: 187 us -> 290 us
  local copies, waits for them, and re-layouts: 23 us -> 16 us
    pallas_call x6, Pallas kernels: 249 us -> 12.3 us  [pack(): pl.pallas_call(kernel, out_shape=[jax.ShapeDtypeStruct((sources, rows, BL...]
    ppermute x6, waiting for transfers between devices: 35.3 us -> 103 us  [shards(): far = lax.ppermute(near, 'expert', inward)]
    ppermute x36, waiting for transfers between devices: 38.8 us -> 65.5 us  [swap_within(): lax.ppermute(pieces[shift], 'expert', within[shift])]
    ppermute x6, waiting for transfers between devices: 43.7 us -> 51.6 us  [shards(): lax.ppermute(to_outer, 'expert', outward)]
    unnamed x113 -> x79, local copies, waits for them, and re-layouts: 16.3 us -> 9.33 us
  transfers between devices with their start and end apart: 63 -> 63, of which waited for: 27 -> 34; matrix products, arithmetic and copies ran while one was open for 5% -> 7% of each run, Pallas kernels for 47% -> 13%
where the time goes in v2:
time: 498 us; the launch traced here: 496 us
  waiting for transfers between devices  290 us (58%)
  starting transfers between devices  80.6 us (16%)
  Pallas kernels  66.4 us (13%)
  other arithmetic  23 us (5%)
  local copies, waits for them, and re-layouts  16 us (3%)
  between operations  15 us (3%)
    ppermute x6, waiting for transfers between devices, shards(): far = lax.ppermute(near, 'expert', inward)  103 us
    ppermute x36, waiting for transfers between devices, swap_within(): lax.ppermute(pieces[shift], 'expert', within[shift])  65.5 us
    ppermute x6, waiting for transfers between devices, shards(): lax.ppermute(to_outer, 'expert', outward)  51.6 us
    ppermute x6, waiting for transfers between devices, shards(): partner = lax.ppermute(own, 'groups', partners)  44.7 us
    pallas_call x12, Pallas kernels, merge(): pl.pallas_call(kernel, grid=(rows // step,), out_shape=out_shape, in_spec...  36.5 us
    ppermute x6, starting transfers between devices, shards(): far = lax.ppermute(near, 'expert', inward)  25.8 us
    all_to_all x2, waiting for transfers between devices, shards(): lax.all_to_all(hidden, 'expert', split_axis=0, concat_axis=0, tiled=True)  24.2 us
    ppermute x36, starting transfers between devices, swap_within(): lax.ppermute(pieces[shift], 'expert', within[shift])  23 us
  transfers between devices with their start and end apart: 63, of which 34 were waited for; matrix products, arithmetic and copies ran while one was open for 7% of the time, Pallas kernels for 13%

profile of v2, /device:TPU:0, one launch (start us, length us, event | category | flops | bytes accessed | tf_op | source)
XLA Modules:
  0.0 495.8 jit_solution(5606829066403568782)
XLA Ops:
  21.7 10.0 %collective-permute-done.2 = bf16[2,640,128]{2,1,0:T(8,128)(2,1)S(1)} collective-permute-done((bf16[2,640,128]{2,1,0:T(8,128)(2,1)S(1)}, bf16[2,640,128]{2,1,0:T(8,128)(2,1)S(1)}, u32[]{:S(2)}, u32[]{:S(2)}) %collective-permute-start.2) | collective-permute-done | bytes 327712 | tf_op jit(solution)/shard_map/ppermute | solution.py:277
  39.3 8.0 %collective-permute-done.20 = bf16[2,640,128]{2,1,0:T(8,128)(2,1)S(1)} collective-permute-done((bf16[2,640,128]{2,1,0:T(8,128)(2,1)S(1)}, bf16[2,640,128]{2,1,0:T(8,128)(2,1)S(1)}, u32[]{:S(2)}, u32[]{:S(2)}) %collective-permute-start.20) | collective-permute-done | bytes 327712 | tf_op jit(solution)/shard_map/ppermute | solution.py:277
  50.9 35.0 %collective-permute-done.3.after_ref.far_ref = bf16[4,2,640,128]{3,2,1,0:T(8,128)(2,1)S(1)} collective-permute-done((bf16[4,2,640,128]{3,2,1,0:T(8,128)(2,1)S(1)}, bf16[4,2,640,128]{3,2,1,0:T(8,128)(2,1)S(1)}, u32[]{:S(2)}, u32[]{:S(2)}) %collective-permute-start.3) | collective-permute-done | bytes 1310752 | tf_op jit(solution)/shard_map/ppermute | solution.py:319
  89.9 23.9 %collective-permute-done.21.after_ref.far_ref = bf16[4,2,640,128]{3,2,1,0:T(8,128)(2,1)S(1)} collective-permute-done((bf16[4,2,640,128]{3,2,1,0:T(8,128)(2,1)S(1)}, bf16[4,2,640,128]{3,2,1,0:T(8,128)(2,1)S(1)}, u32[]{:S(2)}, u32[]{:S(2)}) %collective-permute-start.21) | collective-permute-done | bytes 1310752 | tf_op jit(solution)/shard_map/ppermute | solution.py:319
  120.1 4.5 collective-permute-start.7
  126.6 6.1 %collective-permute-done.24 = bf16[2,640,128]{2,1,0:T(8,128)(2,1)} collective-permute-done((bf16[2,640,128]{2,1,0:T(8,128)(2,1)S(1)}, bf16[2,640,128]{2,1,0:T(8,128)(2,1)}, u32[]{:S(2)}, u32[]{:S(2)}) %collective-permute-start.24) | collective-permute-done | bytes 327712 | tf_op jit(solution)/shard_map/ppermute | solution.py:277
  135.0 4.5 collective-permute-start.25
  157.4 24.0 %collective-permute-done.25.after_ref.far_ref = bf16[4,2,640,128]{3,2,1,0:T(8,128)(2,1)S(1)} collective-permute-done((bf16[4,2,640,128]{3,2,1,0:T(8,128)(2,1)}, bf16[4,2,640,128]{3,2,1,0:T(8,128)(2,1)S(1)}, u32[]{:S(2)}, u32[]{:S(2)}) %collective-permute-start.25) | collective-permute-done | bytes 1310752 | tf_op jit(solution)/shard_map/ppermute | solution.py:319
  192.9 5.5 %collective-permute-start.11 = (bf16[4,2,640,128]{3,2,1,0:T(8,128)(2,1)S(1)}, bf16[4,2,640,128]{3,2,1,0:T(8,128)(2,1)S(1)}, u32[]{:S(2)}, u32[]{:S(2)}) collective-permute-start(bf16[4,2,640,128]{3,2,1,0:T(8,128)(2,1)S(1)} %pad_maximum_fusion.2.near_ref), channel_id=1, source_target_pairs={{0,4},{1,5},{2,6},{3,7},{12,8},{13,9},{14,10},{15,11},{16,20},{17,... | collective-permute-start | bytes 3932168 | tf_op jit(solution)/shard_map/ppermute | solution.py:319
  198.5 7.0 %collective-permute-done.28 = bf16[2,640,128]{2,1,0:T(8,128)(2,1)S(1)} collective-permute-done((bf16[2,640,128]{2,1,0:T(8,128)(2,1)S(1)}, bf16[2,640,128]{2,1,0:T(8,128)(2,1)S(1)}, u32[]{:S(2)}, u32[]{:S(2)}) %collective-permute-start.28) | collective-permute-done | bytes 327712 | tf_op jit(solution)/shard_map/ppermute | solution.py:277
  205.6 4.4 collective-permute-start.29
  223.1 8.6 %collective-permute-done.55 = bf16[4,640,128]{2,1,0:T(8,128)(2,1)} collective-permute-done((bf16[4,640,128]{2,1,0:T(8,128)(2,1)S(1)}, bf16[4,640,128]{2,1,0:T(8,128)(2,1)}, u32[]{:S(2)}, u32[]{:S(2)}) %collective-permute-start.55) | collective-permute-done | bytes 655392 | tf_op jit(solution)/shard_map/ppermute | solution.py:326
  238.1 16.5 %collective-permute-done.29.far_ref = bf16[4,2,640,128]{3,2,1,0:T(8,128)(2,1)S(1)} collective-permute-done((bf16[4,2,640,128]{3,2,1,0:T(8,128)(2,1)S(1)}, bf16[4,2,640,128]{3,2,1,0:T(8,128)(2,1)S(1)}, u32[]{:S(2)}, u32[]{:S(2)}) %collective-permute-start.29) | collective-permute-done | bytes 1310752 | tf_op jit(solution)/shard_map/ppermute | solution.py:319
  280.7 6.3 %fusion.11 = s32[16,64,16]{2,0,1:T(8,128)S(1)} fusion(s32[16,64,16]{2,0,1:T(8,128)S(1)} %copy-done.29), kind=kOutput, calls=%fused_computation.66 | output fusion | flops 1032192 | bytes 131072 | tf_op jit(solution)/shard_map/jit(cumsum)/reduce_window_sum | solution.py:245
  304.4 13.2 %collective-permute-done.37 = bf16[4,640,128]{2,1,0:T(8,128)(2,1)} collective-permute-done((bf16[4,640,128]{2,1,0:T(8,128)(2,1)}, bf16[4,640,128]{2,1,0:T(8,128)(2,1)}, u32[]{:S(2)}, u32[]{:S(2)}) %collective-permute-start.37) | collective-permute-done | bytes 655392 | tf_op jit(solution)/shard_map/ppermute | solution.py:326
  317.7 14.0 %collective-permute-done.43 = bf16[4,640,128]{2,1,0:T(8,128)(2,1)} collective-permute-done((bf16[4,640,128]{2,1,0:T(8,128)(2,1)}, bf16[4,640,128]{2,1,0:T(8,128)(2,1)}, u32[]{:S(2)}, u32[]{:S(2)}) %collective-permute-start.43) | collective-permute-done | bytes 655392 | tf_op jit(solution)/shard_map/ppermute | solution.py:326
  345.3 14.1 %collective-permute-done.31 = bf16[4,640,128]{2,1,0:T(8,128)(2,1)S(1)} collective-permute-done((bf16[4,640,128]{2,1,0:T(8,128)(2,1)S(1)}, bf16[4,640,128]{2,1,0:T(8,128)(2,1)S(1)}, u32[]{:S(2)}, u32[]{:S(2)}) %collective-permute-start.31) | collective-permute-done | bytes 655392 | tf_op jit(solution)/shard_map/ppermute | solution.py:326
  390.9 10.3 %collective-permute-done.47.partner_ref = bf16[4,640,128]{2,1,0:T(8,128)(2,1)} collective-permute-done((bf16[4,640,128]{2,1,0:T(8,128)(2,1)S(1)}, bf16[4,640,128]{2,1,0:T(8,128)(2,1)}, u32[]{:S(2)}, u32[]{:S(2)}) %collective-permute-start.47) | collective-permute-done | bytes 655392 | tf_op jit(solution)/shard_map/ppermute | solution.py:328
  404.3 10.9 %collective-permute-done.41.partner_ref = bf16[4,640,128]{2,1,0:T(8,128)(2,1)} collective-permute-done((bf16[4,640,128]{2,1,0:T(8,128)(2,1)S(1)}, bf16[4,640,128]{2,1,0:T(8,128)(2,1)}, u32[]{:S(2)}, u32[]{:S(2)}) %collective-permute-start.41) | collective-permute-done | bytes 655392 | tf_op jit(solution)/shard_map/ppermute | solution.py:328
  418.3 10.9 %collective-permute-done.35.partner_ref = bf16[4,640,128]{2,1,0:T(8,128)(2,1)} collective-permute-done((bf16[4,640,128]{2,1,0:T(8,128)(2,1)S(1)}, bf16[4,640,128]{2,1,0:T(8,128)(2,1)}, u32[]{:S(2)}, u32[]{:S(2)}) %collective-permute-start.35) | collective-permute-done | bytes 655392 | tf_op jit(solution)/shard_map/ppermute | solution.py:328
  432.3 10.7 %collective-permute-done.17.partner_ref = bf16[4,640,128]{2,1,0:T(8,128)(2,1)} collective-permute-done((bf16[4,640,128]{2,1,0:T(8,128)(2,1)S(1)}, bf16[4,640,128]{2,1,0:T(8,128)(2,1)}, u32[]{:S(2)}, u32[]{:S(2)}) %collective-permute-start.17) | collective-permute-done | bytes 655392 | tf_op jit(solution)/shard_map/ppermute | solution.py:328
  447.0 5.8 %all-to-all-start.1 = ((bf16[16,48,256]{2,1,0:T(8,128)(2,1)}), bf16[16,48,256]{2,1,0:T(8,128)(2,1)S(1)}, u32[]{:S(2)}, u32[]{:S(2)}) async-start(bf16[16,48,256]{2,1,0:T(8,128)(2,1)} %pad_maximum_fusion.14), calls=%async_computation.1 | async-start | bytes 786432 | tf_op jit(solution)/shard_map/all_to_all | solution.py:338
  453.8 11.2 %all-to-all-done.1 = bf16[16,48,256]{2,1,0:T(8,128)(2,1)S(1)} async-done(((bf16[16,48,256]{2,1,0:T(8,128)(2,1)}), bf16[16,48,256]{2,1,0:T(8,128)(2,1)S(1)}, u32[]{:S(2)}, u32[]{:S(2)}) %all-to-all-start.1) | async-done | bytes 393248 | tf_op jit(solution)/shard_map/all_to_all | solution.py:338
  474.3 13.0 %all-to-all-done = bf16[16,48,512]{2,1,0:T(8,128)(2,1)S(1)} async-done(((bf16[16,48,512]{2,1,0:T(8,128)(2,1)}), bf16[16,48,512]{2,1,0:T(8,128)(2,1)S(1)}, u32[]{:S(2)}, u32[]{:S(2)}) %all-to-all-start) | async-done | bytes 786464 | tf_op jit(solution)/shard_map/all_to_all | solution.py:338
  (256 shorter events, 202.4 us)
Async XLA Ops:
  7.2 372.2 %all-gather.2.cloned.1.call-start = ((), (), s32[]{:S(2)}) async-start(), calls=%async_computation.2 | async-start | bytes 5570560 | tf_op jit(solution)/shard_map/all_gather | solution.py:289
  17.5 29.8 %collective-permute-start.20 = (bf16[2,640,128]{2,1,0:T(8,128)(2,1)S(1)}, bf16[2,640,128]{2,1,0:T(8,128)(2,1)S(1)}, u32[]{:S(2)}, u32[]{:S(2)}) collective-permute-start(bf16[2,640,128]{2,1,0:T(8,128)(2,1)S(1)} %get-tuple-element.74), channel_id=1, source_target_pairs={{0,3},{1,2},{2,1},{3,0},{4,7},{5,6},{6,5},{7,4},{8,11},{9,10},{10,... | collective-permute-start | bytes 983048 | tf_op jit(solution)/shard_map/ppermute | solution.py:277
  31.9 53.9 %collective-permute-start.3 = (bf16[4,2,640,128]{3,2,1,0:T(8,128)(2,1)S(1)}, bf16[4,2,640,128]{3,2,1,0:T(8,128)(2,1)S(1)}, u32[]{:S(2)}, u32[]{:S(2)}) collective-permute-start(bf16[4,2,640,128]{3,2,1,0:T(8,128)(2,1)S(1)} %pad_maximum_fusion.near_ref), channel_id=1, source_target_pairs={{0,4},{1,5},{2,6},{3,7},{12,8},{13,9},{14,10},{15,11},{16,20},{17,... | collective-permute-start | bytes 3932168 | tf_op jit(solution)/shard_map/ppermute | solution.py:319
  47.5 66.3 %collective-permute-start.21 = (bf16[4,2,640,128]{3,2,1,0:T(8,128)(2,1)S(1)}, bf16[4,2,640,128]{3,2,1,0:T(8,128)(2,1)S(1)}, u32[]{:S(2)}, u32[]{:S(2)}) collective-permute-start(bf16[4,2,640,128]{3,2,1,0:T(8,128)(2,1)S(1)} %pad_maximum_fusion.3.near_ref), channel_id=1, source_target_pairs={{0,4},{1,5},{2,6},{3,7},{12,8},{13,9},{14,10},{15,11},{16,20},{17,... | collective-permute-start | bytes 3932168 | tf_op jit(solution)/shard_map/ppermute | solution.py:319
  120.1 33.8 %collective-permute-start.7 = (bf16[4,2,640,128]{3,2,1,0:T(8,128)(2,1)}, bf16[4,2,640,128]{3,2,1,0:T(8,128)(2,1)S(1)}, u32[]{:S(2)}, u32[]{:S(2)}) collective-permute-start(bf16[4,2,640,128]{3,2,1,0:T(8,128)(2,1)} %pad_maximum_fusion.1.near_ref), channel_id=1, source_target_pairs={{0,4},{1,5},{2,6},{3,7},{12,8},{13,9},{14,10},{15,11},{16,20},{17,... | collective-permute-start | bytes 3932168 | tf_op jit(solution)/shard_map/ppermute | solution.py:319
  135.0 46.4 %collective-permute-start.25 = (bf16[4,2,640,128]{3,2,1,0:T(8,128)(2,1)}, bf16[4,2,640,128]{3,2,1,0:T(8,128)(2,1)S(1)}, u32[]{:S(2)}, u32[]{:S(2)}) collective-permute-start(bf16[4,2,640,128]{3,2,1,0:T(8,128)(2,1)} %pad_maximum_fusion.4.near_ref), channel_id=1, source_target_pairs={{0,4},{1,5},{2,6},{3,7},{12,8},{13,9},{14,10},{15,11},{16,20},{17,... | collective-permute-start | bytes 3932168 | tf_op jit(solution)/shard_map/ppermute | solution.py:319
  144.1 40.1 %collective-permute-start.48 = (bf16[8,640,128]{2,1,0:T(8,128)(2,1)S(1)}, bf16[8,640,128]{2,1,0:T(8,128)(2,1)S(1)}, u32[]{:S(2)}, u32[]{:S(2)}) collective-permute-start(bf16[8,640,128]{2,1,0:T(8,128)(2,1)S(1)} %merge.20), channel_id=1, source_target_pairs={{4,8},{5,9},{6,10},{7,11},{8,4},{9,5},{10,6},{11,7},{20,24},{21,25... | collective-permute-start | bytes 3932168 | tf_op jit(solution)/shard_map/ppermute | solution.py:322
  148.0 62.0 %collective-permute-start.54 = (bf16[8,640,128]{2,1,0:T(8,128)(2,1)}, bf16[8,640,128]{2,1,0:T(8,128)(2,1)}, u32[]{:S(2)}, u32[]{:S(2)}) collective-permute-start(bf16[8,640,128]{2,1,0:T(8,128)(2,1)} %merge.22), channel_id=1, source_target_pairs={{4,8},{5,9},{6,10},{7,11},{8,4},{9,5},{10,6},{11,7},{20,24},{21,25... | collective-permute-start | bytes 3932168 | tf_op jit(solution)/shard_map/ppermute | solution.py:322
  191.4 31.0 %collective-permute-start.49 = (bf16[4,640,128]{2,1,0:T(8,128)(2,1)S(1)}, bf16[4,640,128]{2,1,0:T(8,128)(2,1)}, u32[]{:S(2)}, u32[]{:S(2)}) collective-permute-start(bf16[4,640,128]{2,1,0:T(8,128)(2,1)S(1)} %get-tuple-element.90), channel_id=1, source_target_pairs={{4,0},{5,1},{6,2},{7,3},{8,12},{9,13},{10,14},{11,15},{20,16},{21,... | collective-permute-start | bytes 1966088 | tf_op jit(solution)/shard_map/ppermute | solution.py:326
  192.9 40.3 %collective-permute-start.11 = (bf16[4,2,640,128]{3,2,1,0:T(8,128)(2,1)S(1)}, bf16[4,2,640,128]{3,2,1,0:T(8,128)(2,1)S(1)}, u32[]{:S(2)}, u32[]{:S(2)}) collective-permute-start(bf16[4,2,640,128]{3,2,1,0:T(8,128)(2,1)S(1)} %pad_maximum_fusion.2.near_ref), channel_id=1, source_target_pairs={{0,4},{1,5},{2,6},{3,7},{12,8},{13,9},{14,10},{15,11},{16,20},{17,... | collective-permute-start | bytes 3932168 | tf_op jit(solution)/shard_map/ppermute | solution.py:319
  205.6 49.0 %collective-permute-start.29 = (bf16[4,2,640,128]{3,2,1,0:T(8,128)(2,1)S(1)}, bf16[4,2,640,128]{3,2,1,0:T(8,128)(2,1)S(1)}, u32[]{:S(2)}, u32[]{:S(2)}) collective-permute-start(bf16[4,2,640,128]{3,2,1,0:T(8,128)(2,1)S(1)} %pad_maximum_fusion.5.near_ref), channel_id=1, source_target_pairs={{0,4},{1,5},{2,6},{3,7},{12,8},{13,9},{14,10},{15,11},{16,20},{17,... | collective-permute-start | bytes 3932168 | tf_op jit(solution)/shard_map/ppermute | solution.py:319
  218.5 44.3 %collective-permute-start.36 = (bf16[8,640,128]{2,1,0:T(8,128)(2,1)}, bf16[8,640,128]{2,1,0:T(8,128)(2,1)S(1)}, u32[]{:S(2)}, u32[]{:S(2)}) collective-permute-start(bf16[8,640,128]{2,1,0:T(8,128)(2,1)} %merge.16), channel_id=1, source_target_pairs={{4,8},{5,9},{6,10},{7,11},{8,4},{9,5},{10,6},{11,7},{20,24},{21,25... | collective-permute-start | bytes 3932168 | tf_op jit(solution)/shard_map/ppermute | solution.py:322
  222.4 41.8 %collective-permute-start.42 = (bf16[8,640,128]{2,1,0:T(8,128)(2,1)S(1)}, bf16[8,640,128]{2,1,0:T(8,128)(2,1)S(1)}, u32[]{:S(2)}, u32[]{:S(2)}) collective-permute-start(bf16[8,640,128]{2,1,0:T(8,128)(2,1)S(1)} %merge.18), channel_id=1, source_target_pairs={{4,8},{5,9},{6,10},{7,11},{8,4},{9,5},{10,6},{11,7},{20,24},{21,25... | collective-permute-start | bytes 3932168 | tf_op jit(solution)/shard_map/ppermute | solution.py:322
  236.3 58.9 %collective-permute-start.12 = (bf16[8,640,128]{2,1,0:T(8,128)(2,1)}, bf16[8,640,128]{2,1,0:T(8,128)(2,1)}, u32[]{:S(2)}, u32[]{:S(2)}) collective-permute-start(bf16[8,640,128]{2,1,0:T(8,128)(2,1)} %merge.12), channel_id=1, source_target_pairs={{4,8},{5,9},{6,10},{7,11},{8,4},{9,5},{10,6},{11,7},{20,24},{21,25... | collective-permute-start | bytes 3932168 | tf_op jit(solution)/shard_map/ppermute | solution.py:322
  257.7 42.2 %collective-permute-start.30 = (bf16[8,640,128]{2,1,0:T(8,128)(2,1)}, bf16[8,640,128]{2,1,0:T(8,128)(2,1)}, u32[]{:S(2)}, u32[]{:S(2)}) collective-permute-start(bf16[8,640,128]{2,1,0:T(8,128)(2,1)} %merge.14), channel_id=1, source_target_pairs={{4,8},{5,9},{6,10},{7,11},{8,4},{9,5},{10,6},{11,7},{20,24},{21,25... | collective-permute-start | bytes 3932168 | tf_op jit(solution)/shard_map/ppermute | solution.py:322
  278.1 39.5 %collective-permute-start.37 = (bf16[4,640,128]{2,1,0:T(8,128)(2,1)}, bf16[4,640,128]{2,1,0:T(8,128)(2,1)}, u32[]{:S(2)}, u32[]{:S(2)}) collective-permute-start(bf16[4,640,128]{2,1,0:T(8,128)(2,1)} %get-tuple-element.86), channel_id=1, source_target_pairs={{4,0},{5,1},{6,2},{7,3},{8,12},{9,13},{10,14},{11,15},{20,16},{21,... | collective-permute-start | bytes 1966088 | tf_op jit(solution)/shard_map/ppermute | solution.py:326
  279.4 52.3 %collective-permute-start.43 = (bf16[4,640,128]{2,1,0:T(8,128)(2,1)}, bf16[4,640,128]{2,1,0:T(8,128)(2,1)}, u32[]{:S(2)}, u32[]{:S(2)}) collective-permute-start(bf16[4,640,128]{2,1,0:T(8,128)(2,1)} %get-tuple-element.88), channel_id=1, source_target_pairs={{4,0},{5,1},{6,2},{7,3},{8,12},{9,13},{10,14},{11,15},{20,16},{21,... | collective-permute-start | bytes 1966088 | tf_op jit(solution)/shard_map/ppermute | solution.py:326
  298.6 46.7 %collective-permute-start.13 = (bf16[4,640,128]{2,1,0:T(8,128)(2,1)S(1)}, bf16[4,640,128]{2,1,0:T(8,128)(2,1)S(1)}, u32[]{:S(2)}, u32[]{:S(2)}) collective-permute-start(bf16[4,640,128]{2,1,0:T(8,128)(2,1)S(1)} %get-tuple-element.70), channel_id=1, source_target_pairs={{4,0},{5,1},{6,2},{7,3},{8,12},{9,13},{10,14},{11,15},{20,16},{21,... | collective-permute-start | bytes 1966088 | tf_op jit(solution)/shard_map/ppermute | solution.py:326
  303.1 56.3 %collective-permute-start.31 = (bf16[4,640,128]{2,1,0:T(8,128)(2,1)S(1)}, bf16[4,640,128]{2,1,0:T(8,128)(2,1)S(1)}, u32[]{:S(2)}, u32[]{:S(2)}) collective-permute-start(bf16[4,640,128]{2,1,0:T(8,128)(2,1)S(1)} %get-tuple-element.84), channel_id=1, source_target_pairs={{4,0},{5,1},{6,2},{7,3},{8,12},{9,13},{10,14},{11,15},{20,16},{21,... | collective-permute-start | bytes 1966088 | tf_op jit(solution)/shard_map/ppermute | solution.py:326
  335.2 42.8 %collective-permute-start.59 = (bf16[4,640,128]{2,1,0:T(8,128)(2,1)S(1)}, bf16[4,640,128]{2,1,0:T(8,128)(2,1)S(1)}, u32[]{:S(2)}, u32[]{:S(2)}) collective-permute-start(bf16[4,640,128]{2,1,0:T(8,128)(2,1)S(1)} %pad_maximum_fusion.12.own_ref), channel_id=1, source_target_pairs={{0,16},{16,0},{1,17},{17,1},{2,18},{18,2},{3,19},{19,3},{4,20},{20... | collective-permute-start | bytes 1966088 | tf_op jit(solution)/shard_map/ppermute | solution.py:328
  371.0 30.2 %collective-permute-start.47 = (bf16[4,640,128]{2,1,0:T(8,128)(2,1)S(1)}, bf16[4,640,128]{2,1,0:T(8,128)(2,1)}, u32[]{:S(2)}, u32[]{:S(2)}) collective-permute-start(bf16[4,640,128]{2,1,0:T(8,128)(2,1)S(1)} %pad_maximum_fusion.10.own_ref), channel_id=1, source_target_pairs={{0,16},{16,0},{1,17},{17,1},{2,18},{18,2},{3,19},{19,3},{4,20},{20... | collective-permute-start | bytes 1966088 | tf_op jit(solution)/shard_map/ppermute | solution.py:328
  373.8 41.4 %collective-permute-start.41 = (bf16[4,640,128]{2,1,0:T(8,128)(2,1)S(1)}, bf16[4,640,128]{2,1,0:T(8,128)(2,1)}, u32[]{:S(2)}, u32[]{:S(2)}) collective-permute-start(bf16[4,640,128]{2,1,0:T(8,128)(2,1)S(1)} %pad_maximum_fusion.9.own_ref), channel_id=1, source_target_pairs={{0,16},{16,0},{1,17},{17,1},{2,18},{18,2},{3,19},{19,3},{4,20},{20... | collective-permute-start | bytes 1966088 | tf_op jit(solution)/shard_map/ppermute | solution.py:328
  376.4 52.8 %collective-permute-start.35 = (bf16[4,640,128]{2,1,0:T(8,128)(2,1)S(1)}, bf16[4,640,128]{2,1,0:T(8,128)(2,1)}, u32[]{:S(2)}, u32[]{:S(2)}) collective-permute-start(bf16[4,640,128]{2,1,0:T(8,128)(2,1)S(1)} %pad_maximum_fusion.8.own_ref), channel_id=1, source_target_pairs={{0,16},{16,0},{1,17},{17,1},{2,18},{18,2},{3,19},{19,3},{4,20},{20... | collective-permute-start | bytes 1966088 | tf_op jit(solution)/shard_map/ppermute | solution.py:328
  378.8 64.2 %collective-permute-start.17 = (bf16[4,640,128]{2,1,0:T(8,128)(2,1)S(1)}, bf16[4,640,128]{2,1,0:T(8,128)(2,1)}, u32[]{:S(2)}, u32[]{:S(2)}) collective-permute-start(bf16[4,640,128]{2,1,0:T(8,128)(2,1)S(1)} %pad_maximum_fusion.7.own_ref), channel_id=1, source_target_pairs={{0,16},{16,0},{1,17},{17,1},{2,18},{18,2},{3,19},{19,3},{4,20},{20... | collective-permute-start | bytes 1966088 | tf_op jit(solution)/shard_map/ppermute | solution.py:328
  (78 other events, 895.2 us)
Sparse Core Ops, SparseCore 0:
  10.3 75.7 all-gather.1

commit v3 on v2

v3 whole, which is shorter than its diff:
```python
import math
import random

import jax
import jax.numpy as jnp
from jax import lax
from jax.experimental import pallas as pl
from jax.experimental.pallas import tpu as pltpu
from jax.sharding import PartitionSpec as P

D = 2560
BLOCK = 128
PLANES = 4
TOKEN = jax.ShapeDtypeStruct((8, 128), jnp.float32)
ANY = pl.BlockSpec(memory_space=pl.ANY)
SMEM = pl.BlockSpec(memory_space=pltpu.SMEM)
VMEM = pl.BlockSpec(memory_space=pltpu.VMEM)
VMEM_LIMIT = 48 * 1024 * 1024


def cluster_weights(cluster_ids, frequency):
    ids = cluster_ids[:, 0]
    same = (ids[:, None] == ids[None, :]).astype(jnp.float32)
    return frequency / jnp.sum(same * frequency[None, :], axis=1)


def step_call(kernel, token, operands, in_specs, out_shape, out_specs, cost, **options):
    count = len(operands)

    def ordered(*refs):
        kernel(*refs[:count], *refs[count + 1 : count + 1 + len(out_shape)], *refs[count + 2 + len(out_shape) :])

    *results, token = pl.pallas_call(
        ordered,
        out_shape=[*out_shape, TOKEN],
        in_specs=[*in_specs, ANY],
        out_specs=[*out_specs, ANY],
        compiler_params=pltpu.CompilerParams(vmem_limit_bytes=VMEM_LIMIT),
        cost_estimate=pl.CostEstimate(flops=cost[0], bytes_accessed=cost[1], transcendentals=0),
        **options,
    )(*operands, token)
    return results, token


def pack(token, info, gate, up, start, width, plane):
    sources, depth, _ = gate.shape
    rows = depth // plane

    def kernel(info_ref, gate_ref, up_ref, *rest):
        outs, held, in_sems, out_sems = rest[:plane], *rest[plane:]
        place = info_ref[0]

        def move(source):
            loads = [
                pltpu.make_async_copy(
                    source.at[
                        :,
                        pl.ds(pl.multiple_of((place ^ shift) * rows, 16), rows),
                        pl.ds(start, width),
                    ],
                    held.at[shift],
                    in_sems.at[shift],
                )
                for shift in range(plane)
            ]
            stores = [
                pltpu.make_async_copy(held.at[shift], outs[shift], out_sems.at[shift])
                for shift in range(plane)
            ]
            for load in loads:
                load.start()
            for load, store in zip(loads, stores):
                load.wait()
                store.start()
            for store in stores:
                store.wait()

        @pl.when(info_ref[2] == 0)
        def _():
            move(gate_ref)

        @pl.when(info_ref[2] != 0)
        def _():
            move(up_ref)

    return step_call(
        kernel,
        token,
        (info, gate, up),
        [SMEM, ANY, ANY],
        [jax.ShapeDtypeStruct((sources, rows, width), gate.dtype)] * plane,
        [ANY] * plane,
        (0, 4 * sources * depth * width),
        scratch_shapes=[
            pltpu.VMEM((plane, sources, rows, width), gate.dtype),
            pltpu.SemaphoreType.DMA((plane,)),
            pltpu.SemaphoreType.DMA((plane,)),
        ],
        name="pack",
    )


def stack(token, pieces):
    plane = len(pieces)

    def kernel(*refs):
        for shift in range(plane):
            refs[plane][shift] = refs[shift][...]

    (whole,), token = step_call(
        kernel,
        token,
        tuple(pieces),
        [VMEM] * plane,
        [jax.ShapeDtypeStruct((plane,) + pieces[0].shape, pieces[0].dtype)],
        [VMEM],
        (0, 4 * plane * pieces[0].size),
        name="stack",
    )
    return whole, token


def hold(token, value, earlier):
    def kernel(*refs):
        pass

    (value,), token = step_call(
        kernel,
        token,
        (value, *earlier),
        [ANY] * (1 + len(earlier)),
        [jax.ShapeDtypeStruct(value.shape, value.dtype)],
        [ANY],
        (0, 0),
        input_output_aliases={0: 0},
        name="hold",
    )
    return value, token


def merge(token, info, ids, weights, scales, near, far, received, start, scale_blocks):
    plane, sources, rows, width = near.shape
    step = math.gcd(rows, BLOCK)
    row_blocks, column_blocks = scale_blocks
    first = start // BLOCK

    def kernel(info_ref, ids_ref, weights_ref, scales_ref, near_ref, far_ref, *rest):
        total = rest[-1]
        place, inner = info_ref[0], info_ref[1]
        outer = jnp.where(inner == 1, 0, PLANES - 1)
        to_inner = inner if received is not None else PLANES - 1 - inner
        to_outer = outer if received is not None else PLANES - 1 - outer
        row_block = (place * rows + pl.program_id(0) * step) // BLOCK

        @pl.when(info_ref[3] == 1)
        def _():
            if received is None:
                total[...] = jnp.zeros_like(total)
            else:
                total[...] = rest[0][...].astype(jnp.float32)
            for block, held in ((near_ref, inner), (far_ref, outer)):
                for shift in range(plane):
                    for number in range(sources):
                        source = (held * plane + (place ^ shift)) * sources + number
                        target = ids_ref[source]
                        target_plane = target // plane
                        slot = (target % plane) ^ place

                        @pl.when((target_plane == to_inner) | (target_plane == to_outer))
                        def _():
                            index = jnp.where(target_plane == to_outer, plane, 0) + slot
                            base = (source * row_blocks + row_block) * column_blocks + first
                            for part in range(width // BLOCK):
                                lanes = pl.ds(part * BLOCK, BLOCK)
                                factor = weights_ref[source] * scales_ref[base + part]
                                total[index, :, lanes] += (
                                    block[shift, number, :, lanes].astype(jnp.float32) * factor
                                )

            if received is None:
                rest[0][...] = total[...].astype(jnp.bfloat16)
            else:
                rest[1][...] = total[:plane].astype(jnp.bfloat16)
                rest[2][...] = total[plane:].astype(jnp.bfloat16)

    pieces = pl.BlockSpec((plane, sources, step, width), lambda i: (0, 0, i, 0))
    both = pl.BlockSpec((2 * plane, step, width), lambda i: (0, i, 0))
    one = pl.BlockSpec((plane, step, width), lambda i: (0, i, 0))
    if received is None:
        extra, extra_specs = (), []
        out_shape = [jax.ShapeDtypeStruct((2 * plane, rows, width), jnp.bfloat16)]
        out_specs = [both]
    else:
        extra, extra_specs = (received,), [both]
        out_shape = [jax.ShapeDtypeStruct((plane, rows, width), jnp.bfloat16)] * 2
        out_specs = [one, one]
    return step_call(
        kernel,
        token,
        (info, ids, weights, scales, near, far, *extra),
        [SMEM] * 4 + [pieces, pieces] + extra_specs,
        out_shape,
        out_specs,
        (4 * near.size, 8 * near.size),
        grid=(rows // step,),
        scratch_shapes=[pltpu.VMEM((2 * plane, step, width), jnp.float32)],
        name="merge",
    )


def choose(token, info, inside, outside):
    plane, rows, width = inside.shape

    def kernel(info_ref, inside_ref, outside_ref, *rest):
        outs, sems = rest[:plane], rest[plane]

        def move(source):
            copies = [
                pltpu.make_async_copy(source.at[shift], outs[shift], sems.at[shift])
                for shift in range(plane)
            ]
            for copy in copies:
                copy.start()
            for copy in copies:
                copy.wait()

        @pl.when(info_ref[3] == 1)
        def _():
            move(inside_ref)

        @pl.when(info_ref[3] != 1)
        def _():
            move(outside_ref)

    return step_call(
        kernel,
        token,
        (info, inside, outside),
        [SMEM, ANY, ANY],
        [jax.ShapeDtypeStruct((rows, width), inside.dtype)] * plane,
        [VMEM] * plane,
        (0, 4 * inside.size),
        scratch_shapes=[pltpu.SemaphoreType.DMA((plane,))],
        name="choose",
    )


def run_chunk(token, info, grouped, own, partner, outputs, start, shape, blocks):
    plane, rows, width = own.shape
    depth, full = shape
    count = grouped.shape[0]
    each = count // len(blocks)
    factor = 1.0 / math.sqrt(D)

    def kernel(info_ref, grouped_ref, own_ref, partner_ref, *rest):
        gate_out, up_out, hidden_ref, whole, sems, out_sems = rest[len(outputs) :]
        place = info_ref[0]

        def load(pieces, column, base):
            return [
                pltpu.make_async_copy(
                    pieces.at[shift],
                    whole.at[
                        pl.ds(pl.multiple_of((place ^ shift) * rows, 16), rows),
                        pl.ds(column, width),
                    ],
                    sems.at[base + shift],
                )
                for shift in range(plane)
            ]

        def fill(gate, up):
            copies = load(gate, 0, 0) + load(up, width, plane)
            for copy in copies:
                copy.start()
            for copy in copies:
                copy.wait()

        @pl.when(info_ref[2] == 0)
        def _():
            fill(own_ref, partner_ref)

        @pl.when(info_ref[2] != 0)
        def _():
            fill(partner_ref, own_ref)

        stores = [
            pltpu.make_async_copy(
                whole.at[:, pl.ds(index * width, width)],
                out.at[0, :, pl.ds(start, width)],
                out_sems.at[index],
            )
            for index, out in enumerate((gate_out, up_out))
        ]
        for store in stores:
            store.start()
        values = jnp.dot(grouped_ref[...], whole[...], preferred_element_type=jnp.float32)
        gate_value = values[:, :width] * factor
        up_value = values[:, width:] * factor
        hidden = (gate_value / (1.0 + jnp.exp(-gate_value)) * up_value).astype(jnp.bfloat16)
        for index, block in enumerate(blocks):
            hidden_ref[block] = hidden[index * each : (index + 1) * each]
        for store in stores:
            store.wait()

    weights = jax.ShapeDtypeStruct((1, depth, full), jnp.bfloat16)
    return step_call(
        kernel,
        token,
        (info, grouped, own, partner, *outputs),
        [SMEM, VMEM, ANY, ANY] + [ANY] * len(outputs),
        [weights, weights, jax.ShapeDtypeStruct((len(blocks), each, width), jnp.bfloat16)],
        [ANY, ANY, VMEM],
        (4 * count * depth * width, 2 * (grouped.size + 4 * depth * width)),
        scratch_shapes=[
            pltpu.VMEM((depth, 2 * width), jnp.bfloat16),
            pltpu.SemaphoreType.DMA((2 * plane,)),
            pltpu.SemaphoreType.DMA((2,)),
        ],
        input_output_aliases={4 + index: index for index in range(len(outputs))},
        name="run_chunk",
    )


STEPS = {
    "run": (("x", "run before"), (2.0, 1.2), None),
    "join": (("e",), (1.0, 0.7), ("x", 12.0, "x")),
    "choose": (("d",), (3.0, 0.8), ("e", 7.0, "y")),
    "finish": (("m",), (3.0, 3.0), ("d", 13.0, "out")),
    "partial": (("a",), (4.0, 2.2), ("m", 25.0, "middle")),
    "send": (("stack", "a before"), (1.5, 0.0), ("a", 25.0, "in")),
    "stack": (("b",), (1.0, 1.0), None),
    "pack": (("stack before",), (5.0, 1.0), ("b", 13.0, "y")),
}
LATENCY = 1.5
TRIES = 1500


def play(widths, delay):
    ready = {}
    links = {}
    now = 0.0
    order = []
    left = [(name, chunk) for name in STEPS for chunk in range(len(widths))]
    while left:
        best = None
        for name, chunk in left:
            needs = []
            for need in STEPS[name][0]:
                if not need.endswith(" before"):
                    needs.append((need, chunk))
                elif chunk > 0:
                    needs.append((need[: -len(" before")], chunk - 1))
            if all(need in ready for need in needs):
                begin = max([now] + [ready[need] for need in needs])
                rank = begin + delay[(name, chunk)]
                if best is None or rank < best[0]:
                    best = (rank, begin, name, chunk)
        _, begin, name, chunk = best
        _, (fixed, each), sent = STEPS[name]
        now = begin + fixed + each * widths[chunk]
        ready[(name, chunk)] = now
        if sent is not None:
            what, cost, link = sent
            links[link] = max(now, links.get(link, 0.0)) + cost * widths[chunk]
            ready[(what, chunk)] = links[link] + LATENCY
        left.remove((name, chunk))
        order.append((name, chunk))
    return now, order


def plan(widths):
    draw = random.Random(0)
    steps = [(name, chunk) for name in STEPS for chunk in range(len(widths))]
    best = None
    for attempt in range(TRIES):
        if attempt == 0 or draw.random() < 0.3:
            delay = {step: draw.uniform(-15.0, 15.0) + 3.0 * step[1] for step in steps}
        else:
            delay = dict(best[2])
            for _ in range(draw.randint(1, 3)):
                delay[draw.choice(steps)] += draw.gauss(0.0, 10.0)
        end, order = play(widths, delay)
        if best is None or end < best[0]:
            best = (end, order, delay)
    return best[1]


def route_slots(routes, merged_count, tok_dev):
    experts = jnp.arange(merged_count, dtype=jnp.int32)
    hit_table = jnp.sum((routes[:, :, None] == experts).astype(jnp.int32), axis=1)
    hit_table = hit_table.reshape(-1, tok_dev, merged_count)
    position_lookup = jnp.cumsum(hit_table, axis=1) - hit_table
    return (hit_table, position_lookup)


def chunk_widths(blocks):
    if blocks < 4:
        return [1] * blocks
    return [1, 2] + [1] * (blocks - 3)


def shards(tokens, routes, quant_gate, quant_up, gate_scales, up_scales, cluster_ids, frequency):
    expert_count = lax.axis_size("expert")
    own_index = lax.axis_index("expert")
    group_count = lax.axis_size("groups")
    half = lax.axis_index("groups") % 2
    plane = expert_count // PLANES
    place, level = own_index % plane, own_index // plane
    is_inner = (level == 1) | (level == 2)
    depth, full = quant_gate.shape[1:]
    tok_dev = tokens.shape[0]
    top_count = routes.shape[1]
    capacity = min(tok_dev, 2 * tok_dev * top_count // expert_count)

    def wires(pairs):
        return [(a * plane + p, b * plane + p) for a, b in pairs for p in range(plane)]

    inward = wires([(0, 1), (3, 2)])
    across = wires([(1, 2), (2, 1)])
    outward = wires([(1, 0), (2, 3)])
    within = {
        shift: [(i, i // plane * plane + (i % plane ^ shift)) for i in range(expert_count)]
        for shift in range(1, plane)
    }
    partners = [(g, g ^ 1) for g in range(group_count)]

    def swap_within(pieces):
        return [pieces[0]] + [
            lax.ppermute(pieces[shift], "expert", within[shift]) for shift in range(1, plane)
        ]

    info = jnp.stack([place, level, half, is_inner.astype(jnp.int32)]).astype(jnp.int32)
    ids = cluster_ids[:, 0]
    weights = cluster_weights(cluster_ids, frequency)
    scales = jnp.where(half == 0, gate_scales, up_scales)
    scale_blocks = scales.shape[1:]
    scales = scales.reshape(-1)

    blocks = [z * plane + p for p in range(plane) for z in range(PLANES)]
    by_line = [[z * plane + p for z in range(PLANES)] for p in range(plane)]
    by_plane = [[z * plane + p for p in range(plane)] for z in range(PLANES)]
    everyone = lax.all_gather(tokens, "expert", axis=0, tiled=True, axis_index_groups=by_line)
    everyone = lax.all_gather(everyone, "expert", axis=0, tiled=True, axis_index_groups=by_plane)
    spread = everyone.reshape(expert_count, tok_dev, everyone.shape[1])
    hit_table, position_lookup = route_slots(routes, expert_count, tok_dev)
    positions = jnp.arange(capacity, dtype=jnp.int32)

    def in_blocks(table):
        column = lax.dynamic_index_in_dim(table, own_index, 2, keepdims=False)
        column = column.reshape(PLANES, plane, tok_dev).transpose(1, 0, 2)
        return column.reshape(expert_count, 1, tok_dev)

    placing = (
        (in_blocks(hit_table) == 1) & (in_blocks(position_lookup) == positions[None, :, None])
    ).astype(jnp.bfloat16)
    arrived = jnp.einsum(
        "jct,jtd->jcd", placing, spread, preferred_element_type=jnp.float32
    ).astype(jnp.bfloat16)
    arrived = lax.all_gather(arrived, "mp", axis=2, tiled=True)
    grouped = arrived.reshape(expert_count * capacity, arrived.shape[2])

    experts = jnp.arange(expert_count, dtype=jnp.int32)
    local_routes = lax.dynamic_slice_in_dim(routes, own_index * tok_dev, tok_dev, 0)
    own_slots = lax.dynamic_index_in_dim(position_lookup, own_index, 0, keepdims=False)
    chosen = local_routes[:, :, None] == experts
    slot_of = jnp.sum(jnp.where(chosen, own_slots[:, None, :], 0), axis=2)
    picking = (chosen[:, :, :, None] & (slot_of[:, :, None, None] == positions)).astype(
        jnp.bfloat16
    )
    picking = picking.reshape(tok_dev * top_count, expert_count * capacity)

    widths = chunk_widths(full // BLOCK)
    starts = [BLOCK * sum(widths[:chunk]) for chunk in range(len(widths))]
    token = jnp.zeros(TOKEN.shape, TOKEN.dtype)
    held, near, far, received, inside, outside, mine, own, partner, hiddens = (
        {} for _ in range(10)
    )
    outputs = ()
    for name, c in plan(widths):
        start, width = starts[c], widths[c] * BLOCK
        if name == "pack":
            pieces, token = pack(token, info, quant_gate, quant_up, start, width, plane)
            held[c] = swap_within(pieces)
        elif name == "stack":
            near[c], token = stack(token, held[c])
        elif name == "send":
            near[c], token = hold(token, near[c], [far[c - 1]] if c else [])
            far[c] = lax.ppermute(near[c], "expert", inward)
        elif name == "partial":
            (partial,), token = merge(
                token, info, ids, weights, scales, near[c], far[c], None, start, scale_blocks
            )
            received[c] = lax.ppermute(partial, "expert", across)
        elif name == "finish":
            (inside[c], outward_rows), token = merge(
                token, info, ids, weights, scales, near[c], far[c], received[c], start, scale_blocks
            )
            outside[c] = lax.ppermute(outward_rows, "expert", outward)
        elif name == "choose":
            pieces, token = choose(token, info, inside[c], outside[c])
            mine[c] = swap_within(pieces)
        elif name == "join":
            own[c], token = stack(token, mine[c])
            partner[c] = lax.ppermute(own[c], "groups", partners)
        else:
            (*outputs, hiddens[c]), token = run_chunk(
                token, info, grouped, own[c], partner[c], outputs, start, (depth, full), blocks
            )

    last = len(widths) - 1
    finished = []
    for batch in (range(last), range(last, last + 1)):
        hidden = jnp.concatenate([hiddens[c] for c in batch], axis=2)
        returned = lax.all_to_all(hidden, "expert", split_axis=0, concat_axis=0, tiled=True)
        rows = returned.reshape(expert_count * capacity, returned.shape[2])
        finished.append(
            jnp.dot(picking, rows, preferred_element_type=jnp.float32).astype(jnp.bfloat16)
        )
    output = jnp.concatenate(finished, axis=1)
    merged_gate, merged_up = outputs
    return (merged_gate, merged_up, output.reshape(tok_dev, top_count, full))


def solution(mesh):
    return jax.shard_map(
        shards,
        mesh=mesh,
        in_specs=(
            P(("groups", "expert"), "mp"),
            P("groups", None),
            P("expert", None, "mp"),
            P("expert", None, "mp"),
            P(None, None, "mp"),
            P(None, None, "mp"),
            P(),
            P(),
        ),
        out_specs=(
            P(("groups", "expert"), None, "mp"),
            P(("groups", "expert"), None, "mp"),
            P(("groups", "expert"), None, "mp"),
        ),
        check_vma=False,
    )
```

time: 498 us -> 443 us (0.89)
  waiting for transfers between devices: 290 us -> 246 us
  other arithmetic: 23 us -> 6.01 us
  local copies, waits for them, and re-layouts: 16 us -> 28.1 us
  starting transfers between devices: 80.6 us -> 70.4 us
    ppermute x24 -> x20, waiting for transfers between devices: 200 us -> 102 us  [the longest x5 46.1 us: shards(): far[c] = lax.ppermute(near[c], 'expert', inward)]
    ppermute x36 -> x30, waiting for transfers between devices: 65.5 us -> 120 us  [swap_within(): lax.ppermute(pieces[shift], 'expert', within[shift])]
    unnamed x79 -> x75, local copies, waits for them, and re-layouts: 9.33 us -> 19.7 us
    ppermute x24 -> x20, starting transfers between devices: 48.1 us -> 38.6 us  [the longest x5 19.7 us: shards(): far[c] = lax.ppermute(near[c], 'expert', inward)]
    another operation x12 -> x0, other arithmetic: 7.94 us -> none  [the longest x6 5.3 us: shards(): near = jnp.stack(swap_within(pieces))]
    another operation x1, other arithmetic: 6.33 us -> 1.11 us  [route_slots(): position_lookup = jnp.cumsum(hit_table, axis=1) - hit_table]
    pallas_call x24 -> x40, Pallas kernels: 66.4 us -> 71.2 us  [step_call(): pl.pallas_call(ordered, out_shape=[*out_shape, TOKEN], in_specs=[*in_spec...]
    ppermute x36 -> x30, starting transfers between devices: 23 us -> 21.6 us  [swap_within(): lax.ppermute(pieces[shift], 'expert', within[shift])]
  transfers between devices with their start and end apart: 63 -> 54, of which waited for: 34 -> 34; matrix products, arithmetic and copies ran while one was open for 7% -> 4% of each run, Pallas kernels for 13% -> 14%
where the time goes in v3:
time: 443 us; the launch traced here: 441 us
  waiting for transfers between devices  246 us (56%)
  Pallas kernels  71.2 us (16%)
  starting transfers between devices  70.4 us (16%)
  local copies, waits for them, and re-layouts  28.1 us (6%)
  between operations  14.9 us (3%)
  other arithmetic  6.01 us (1%)
  matrix products  4.59 us (1%)
    ppermute x30, waiting for transfers between devices, swap_within(): lax.ppermute(pieces[shift], 'expert', within[shift])  120 us
    pallas_call x40, Pallas kernels, step_call(): pl.pallas_call(ordered, out_shape=[*out_shape, TOKEN], in_specs=[*in_spec...  71.2 us
    ppermute x5, waiting for transfers between devices, shards(): far[c] = lax.ppermute(near[c], 'expert', inward)  46.1 us
    ppermute x5, waiting for transfers between devices, shards(): partner[c] = lax.ppermute(own[c], 'groups', partners)  34 us
    all_to_all x2, waiting for transfers between devices, shards(): lax.all_to_all(hidden, 'expert', split_axis=0, concat_axis=0, tiled=True)  23.9 us
    ppermute x5, waiting for transfers between devices, shards(): outside[c] = lax.ppermute(outward_rows, 'expert', outward)  21.6 us
    ppermute x30, starting transfers between devices, swap_within(): lax.ppermute(pieces[shift], 'expert', within[shift])  21.6 us
    unnamed x75, local copies, waits for them, and re-layouts  19.7 us
  transfers between devices with their start and end apart: 54, of which 34 were waited for; matrix products, arithmetic and copies ran while one was open for 4% of the time, Pallas kernels for 14%

profile of v3, /device:TPU:0, one launch (start us, length us, event | category | flops | bytes accessed | tf_op | source)
XLA Modules:
  0.0 441.1 jit_solution(2362519150622215588)
XLA Ops:
  12.6 8.5 %collective-permute-done.1.refs_2_ = bf16[2,640,128]{2,1,0:T(8,128)(2,1)S(1)} collective-permute-done((bf16[2,640,128]{2,1,0:T(8,128)(2,1)S(1)}, bf16[2,640,128]{2,1,0:T(8,128)(2,1)S(1)}, u32[]{:S(2)}, u32[]{:S(2)}) %collective-permute-start.1) | collective-permute-done | bytes 327712 | tf_op jit(solution)/shard_map/ppermute | solution.py:430
  21.1 6.5 %collective-permute-done.2.refs_3_ = bf16[2,640,128]{2,1,0:T(8,128)(2,1)S(1)} collective-permute-done((bf16[2,640,128]{2,1,0:T(8,128)(2,1)S(1)}, bf16[2,640,128]{2,1,0:T(8,128)(2,1)S(1)}, u32[]{:S(2)}, u32[]{:S(2)}) %collective-permute-start.2) | collective-permute-done | bytes 327712 | tf_op jit(solution)/shard_map/ppermute | solution.py:430
  38.2 15.5 %collective-permute-done.5.refs_2_ = bf16[2,640,256]{2,1,0:T(8,128)(2,1)S(1)} collective-permute-done((bf16[2,640,256]{2,1,0:T(8,128)(2,1)}, bf16[2,640,256]{2,1,0:T(8,128)(2,1)S(1)}, u32[]{:S(2)}, u32[]{:S(2)}) %collective-permute-start.5) | collective-permute-done | bytes 655392 | tf_op jit(solution)/shard_map/ppermute | solution.py:430
  53.7 13.1 %collective-permute-done.6.refs_3_ = bf16[2,640,256]{2,1,0:T(8,128)(2,1)S(1)} collective-permute-done((bf16[2,640,256]{2,1,0:T(8,128)(2,1)}, bf16[2,640,256]{2,1,0:T(8,128)(2,1)S(1)}, u32[]{:S(2)}, u32[]{:S(2)}) %collective-permute-start.6) | collective-permute-done | bytes 655392 | tf_op jit(solution)/shard_map/ppermute | solution.py:430
  68.5 16.1 %collective-permute-done.3.refs_1_.refs_5_ = bf16[4,2,640,128]{3,2,1,0:T(8,128)(2,1)S(1)} collective-permute-done((bf16[4,2,640,128]{3,2,1,0:T(8,128)(2,1)S(1)}, bf16[4,2,640,128]{3,2,1,0:T(8,128)(2,1)S(1)}, u32[]{:S(2)}, u32[]{:S(2)}) %collective-permute-start.3) | collective-permute-done | bytes 1310752 | tf_op jit(solution)/shard_map/ppermute | solution.py:489
  104.3 8.1 %collective-permute-done.10.refs_3_ = bf16[2,640,128]{2,1,0:T(8,128)(2,1)S(1)} collective-permute-done((bf16[2,640,128]{2,1,0:T(8,128)(2,1)}, bf16[2,640,128]{2,1,0:T(8,128)(2,1)S(1)}, u32[]{:S(2)}, u32[]{:S(2)}) %collective-permute-start.10) | collective-permute-done | bytes 327712 | tf_op jit(solution)/shard_map/ppermute | solution.py:430
  112.4 13.4 %collective-permute-done.9.refs_2_ = bf16[2,640,128]{2,1,0:T(8,128)(2,1)S(1)} collective-permute-done((bf16[2,640,128]{2,1,0:T(8,128)(2,1)}, bf16[2,640,128]{2,1,0:T(8,128)(2,1)S(1)}, u32[]{:S(2)}, u32[]{:S(2)}) %collective-permute-start.9) | collective-permute-done | bytes 327712 | tf_op jit(solution)/shard_map/ppermute | solution.py:430
  131.8 13.2 %collective-permute-done.12.refs_5_.refs_1_ = bf16[4,2,640,256]{3,2,1,0:T(8,128)(2,1)S(1)} collective-permute-done((bf16[4,2,640,256]{3,2,1,0:T(8,128)(2,1)}, bf16[4,2,640,256]{3,2,1,0:T(8,128)(2,1)S(1)}, u32[]{:S(2)}, u32[]{:S(2)}) %collective-permute-start.12) | collective-permute-done | bytes 2621472 | tf_op jit(solution)/shard_map/ppermute | solution.py:489
  155.9 5.7 %collective-permute-start.23 = (bf16[4,2,640,128]{3,2,1,0:T(8,128)(2,1)S(1)}, bf16[4,2,640,128]{3,2,1,0:T(8,128)(2,1)S(1)}, u32[]{:S(2)}, u32[]{:S(2)}) collective-permute-start(bf16[4,2,640,128]{3,2,1,0:T(8,128)(2,1)S(1)} %get-tuple-element.176.refs_4_), channel_id=1, source_target_pairs={{0,4},{1,5},{2,6},{3,7},{12,8},{13,9},{14,10},{15,11},{16,20},{17,... | collective-permute-start | bytes 3932168 | tf_op jit(solution)/shard_map/ppermute | solution.py:489
  163.6 5.2 %collective-permute-done.14.refs_2_ = bf16[640,128]{1,0:T(8,128)(2,1)S(1)} collective-permute-done((bf16[640,128]{1,0:T(8,128)(2,1)S(1)}, bf16[640,128]{1,0:T(8,128)(2,1)S(1)}, u32[]{:S(2)}, u32[]{:S(2)}) %collective-permute-start.14) | collective-permute-done | bytes 163872 | tf_op jit(solution)/shard_map/ppermute | solution.py:430
  176.3 8.9 %collective-permute-done.17.refs_2_ = bf16[2,640,128]{2,1,0:T(8,128)(2,1)S(1)} collective-permute-done((bf16[2,640,128]{2,1,0:T(8,128)(2,1)S(1)}, bf16[2,640,128]{2,1,0:T(8,128)(2,1)S(1)}, u32[]{:S(2)}, u32[]{:S(2)}) %collective-permute-start.17) | collective-permute-done | bytes 327712 | tf_op jit(solution)/shard_map/ppermute | solution.py:430
  185.2 5.6 %collective-permute-done.18.refs_3_ = bf16[2,640,128]{2,1,0:T(8,128)(2,1)S(1)} collective-permute-done((bf16[2,640,128]{2,1,0:T(8,128)(2,1)S(1)}, bf16[2,640,128]{2,1,0:T(8,128)(2,1)S(1)}, u32[]{:S(2)}, u32[]{:S(2)}) %collective-permute-start.18) | collective-permute-done | bytes 327712 | tf_op jit(solution)/shard_map/ppermute | solution.py:430
  205.8 5.3 %collective-permute-done.21.refs_3_ = bf16[2,640,128]{2,1,0:T(8,128)(2,1)S(1)} collective-permute-done((bf16[2,640,128]{2,1,0:T(8,128)(2,1)S(1)}, bf16[2,640,128]{2,1,0:T(8,128)(2,1)S(1)}, u32[]{:S(2)}, u32[]{:S(2)}) %collective-permute-start.21) | collective-permute-done | bytes 327712 | tf_op jit(solution)/shard_map/ppermute | solution.py:430
  211.2 12.1 %collective-permute-done.24.refs_1_.refs_5_ = bf16[4,2,640,128]{3,2,1,0:T(8,128)(2,1)S(1)} collective-permute-done((bf16[4,2,640,128]{3,2,1,0:T(8,128)(2,1)S(1)}, bf16[4,2,640,128]{3,2,1,0:T(8,128)(2,1)S(1)}, u32[]{:S(2)}, u32[]{:S(2)}) %collective-permute-start.24) | collective-permute-done | bytes 1310752 | tf_op jit(solution)/shard_map/ppermute | solution.py:489
  232.3 14.5 %collective-permute-done.26.refs_2_ = bf16[4,640,256]{2,1,0:T(8,128)(2,1)S(1)} collective-permute-done((bf16[4,640,256]{2,1,0:T(8,128)(2,1)S(1)}, bf16[4,640,256]{2,1,0:T(8,128)(2,1)S(1)}, u32[]{:S(2)}, u32[]{:S(2)}) %collective-permute-start.26) | collective-permute-done | bytes 1310752 | tf_op jit(solution)/shard_map/ppermute | solution.py:499
  272.1 6.1 %collective-permute-done.32.refs_3_ = bf16[640,256]{1,0:T(8,128)(2,1)S(1)} collective-permute-done((bf16[640,256]{1,0:T(8,128)(2,1)S(1)}, bf16[640,256]{1,0:T(8,128)(2,1)S(1)}, u32[]{:S(2)}, u32[]{:S(2)}) %collective-permute-start.32) | collective-permute-done | bytes 327712 | tf_op jit(solution)/shard_map/ppermute | solution.py:430
  286.2 5.1 %collective-permute-done.35.refs_2_ = bf16[640,128]{1,0:T(8,128)(2,1)S(1)} collective-permute-done((bf16[640,128]{1,0:T(8,128)(2,1)S(1)}, bf16[640,128]{1,0:T(8,128)(2,1)S(1)}, u32[]{:S(2)}, u32[]{:S(2)}) %collective-permute-start.35) | collective-permute-done | bytes 163872 | tf_op jit(solution)/shard_map/ppermute | solution.py:430
  337.8 7.3 %collective-permute-done.49.refs_3_ = bf16[4,640,128]{2,1,0:T(8,128)(2,1)} collective-permute-done((bf16[4,640,128]{2,1,0:T(8,128)(2,1)}, bf16[4,640,128]{2,1,0:T(8,128)(2,1)}, u32[]{:S(2)}, u32[]{:S(2)}) %collective-permute-start.49) | collective-permute-done | bytes 655392 | tf_op jit(solution)/shard_map/ppermute | solution.py:505
  354.0 5.2 %collective-permute-done.47.refs_3_ = bf16[4,640,128]{2,1,0:T(8,128)(2,1)} collective-permute-done((bf16[4,640,128]{2,1,0:T(8,128)(2,1)S(1)}, bf16[4,640,128]{2,1,0:T(8,128)(2,1)}, u32[]{:S(2)}, u32[]{:S(2)}) %collective-permute-start.47) | collective-permute-done | bytes 655392 | tf_op jit(solution)/shard_map/ppermute | solution.py:505
  362.2 10.9 %collective-permute-done.46.refs_3_ = bf16[4,640,128]{2,1,0:T(8,128)(2,1)} collective-permute-done((bf16[4,640,128]{2,1,0:T(8,128)(2,1)}, bf16[4,640,128]{2,1,0:T(8,128)(2,1)}, u32[]{:S(2)}, u32[]{:S(2)}) %collective-permute-start.46) | collective-permute-done | bytes 655392 | tf_op jit(solution)/shard_map/ppermute | solution.py:505
  376.3 10.6 %collective-permute-done.45.refs_3_ = bf16[4,640,128]{2,1,0:T(8,128)(2,1)} collective-permute-done((bf16[4,640,128]{2,1,0:T(8,128)(2,1)}, bf16[4,640,128]{2,1,0:T(8,128)(2,1)}, u32[]{:S(2)}, u32[]{:S(2)}) %collective-permute-start.45) | collective-permute-done | bytes 655392 | tf_op jit(solution)/shard_map/ppermute | solution.py:505
  391.7 6.2 %all-to-all-start.1 = ((bf16[16,48,128]{2,1,0:T(8,128)(2,1)}), bf16[16,48,128]{2,1,0:T(8,128)(2,1)S(1)}, u32[]{:S(2)}, u32[]{:S(2)}) async-start(bf16[16,48,128]{2,1,0:T(8,128)(2,1)} %get-tuple-element.250), calls=%async_computation.1 | async-start | bytes 393216 | tf_op jit(solution)/shard_map/all_to_all | solution.py:515
  399.0 7.9 %all-to-all-done.1 = bf16[16,48,128]{2,1,0:T(8,128)(2,1)S(1)} async-done(((bf16[16,48,128]{2,1,0:T(8,128)(2,1)}), bf16[16,48,128]{2,1,0:T(8,128)(2,1)S(1)}, u32[]{:S(2)}, u32[]{:S(2)}) %all-to-all-start.1) | async-done | bytes 196640 | tf_op jit(solution)/shard_map/all_to_all | solution.py:515
  416.4 16.0 %all-to-all-done = bf16[16,48,640]{2,1,0:T(8,128)(2,1)S(1)} async-done(((bf16[16,48,640]{2,1,0:T(8,128)(2,1)}), bf16[16,48,640]{2,1,0:T(8,128)(2,1)S(1)}, u32[]{:S(2)}, u32[]{:S(2)}) %all-to-all-start) | async-done | bytes 983072 | tf_op jit(solution)/shard_map/all_to_all | solution.py:515
  (232 shorter events, 199.1 us)
Async XLA Ops:
  7.2 94.9 %all-gather.3.cloned.1.call-start = ((), (), s32[]{:S(2)}) async-start(), calls=%async_computation.2 | async-start | bytes 1638400 | tf_op jit(solution)/shard_map/all_gather | solution.py:443
  32.1 52.5 %collective-permute-start.3 = (bf16[4,2,640,128]{3,2,1,0:T(8,128)(2,1)S(1)}, bf16[4,2,640,128]{3,2,1,0:T(8,128)(2,1)S(1)}, u32[]{:S(2)}, u32[]{:S(2)}) collective-permute-start(bf16[4,2,640,128]{3,2,1,0:T(8,128)(2,1)S(1)} %get-tuple-element.135.refs_4_), channel_id=1, source_target_pairs={{0,4},{1,5},{2,6},{3,7},{12,8},{13,9},{14,10},{15,11},{16,20},{17,... | collective-permute-start | bytes 3932168 | tf_op jit(solution)/shard_map/ppermute | solution.py:489
  35.8 298.3 %all-gather.5.cloned.1.call-start = ((), (), s32[]{:S(2)}) async-start(), calls=%async_computation.3 | async-start | bytes 6553600 | tf_op jit(solution)/shard_map/all_gather | solution.py:444
  37.5 29.4 %collective-permute-start.6 = (bf16[2,640,256]{2,1,0:T(8,128)(2,1)}, bf16[2,640,256]{2,1,0:T(8,128)(2,1)S(1)}, u32[]{:S(2)}, u32[]{:S(2)}) collective-permute-start(bf16[2,640,256]{2,1,0:T(8,128)(2,1)} %copy-done.24), channel_id=1, source_target_pairs={{0,3},{1,2},{2,1},{3,0},{4,7},{5,6},{6,5},{7,4},{8,11},{9,10},{10,... | collective-permute-start | bytes 1966088 | tf_op jit(solution)/shard_map/ppermute | solution.py:430
  85.7 59.2 %collective-permute-start.12 = (bf16[4,2,640,256]{3,2,1,0:T(8,128)(2,1)}, bf16[4,2,640,256]{3,2,1,0:T(8,128)(2,1)S(1)}, u32[]{:S(2)}, u32[]{:S(2)}) collective-permute-start(bf16[4,2,640,256]{3,2,1,0:T(8,128)(2,1)} %get-tuple-element.154.refs_4_), channel_id=1, source_target_pairs={{0,4},{1,5},{2,6},{3,7},{12,8},{13,9},{14,10},{15,11},{16,20},{17,... | collective-permute-start | bytes 7864328 | tf_op jit(solution)/shard_map/ppermute | solution.py:489
  100.3 25.6 %collective-permute-start.7 = (bf16[8,640,128]{2,1,0:T(8,128)(2,1)}, bf16[8,640,128]{2,1,0:T(8,128)(2,1)}, u32[]{:S(2)}, u32[]{:S(2)}) collective-permute-start(bf16[8,640,128]{2,1,0:T(8,128)(2,1)} %get-tuple-element.145), channel_id=1, source_target_pairs={{4,8},{5,9},{6,10},{7,11},{8,4},{9,5},{10,6},{11,7},{20,24},{21,25... | collective-permute-start | bytes 3932168 | tf_op jit(solution)/shard_map/ppermute | solution.py:494
  103.6 22.2 %collective-permute-start.9 = (bf16[2,640,128]{2,1,0:T(8,128)(2,1)}, bf16[2,640,128]{2,1,0:T(8,128)(2,1)S(1)}, u32[]{:S(2)}, u32[]{:S(2)}) collective-permute-start(bf16[2,640,128]{2,1,0:T(8,128)(2,1)} %copy-done.27), channel_id=1, source_target_pairs={{0,2},{1,3},{2,0},{3,1},{4,6},{5,7},{6,4},{7,5},{8,10},{9,11},{10,... | collective-permute-start | bytes 983048 | tf_op jit(solution)/shard_map/ppermute | solution.py:430
  130.5 22.2 %collective-permute-start.11 = (bf16[4,640,128]{2,1,0:T(8,128)(2,1)S(1)}, bf16[4,640,128]{2,1,0:T(8,128)(2,1)S(1)}, u32[]{:S(2)}, u32[]{:S(2)}) collective-permute-start(bf16[4,640,128]{2,1,0:T(8,128)(2,1)S(1)} %get-tuple-element.153), channel_id=1, source_target_pairs={{4,0},{5,1},{6,2},{7,3},{8,12},{9,13},{10,14},{11,15},{20,16},{21,... | collective-permute-start | bytes 1966088 | tf_op jit(solution)/shard_map/ppermute | solution.py:499
  150.5 47.6 %collective-permute-start.22 = (bf16[8,640,256]{2,1,0:T(8,128)(2,1)S(1)}, bf16[8,640,256]{2,1,0:T(8,128)(2,1)}, u32[]{:S(2)}, u32[]{:S(2)}) collective-permute-start(bf16[8,640,256]{2,1,0:T(8,128)(2,1)S(1)} %get-tuple-element.175), channel_id=1, source_target_pairs={{4,8},{5,9},{6,10},{7,11},{8,4},{9,5},{10,6},{11,7},{20,24},{21,25... | collective-permute-start | bytes 7864328 | tf_op jit(solution)/shard_map/ppermute | solution.py:494
  155.9 37.1 %collective-permute-start.23 = (bf16[4,2,640,128]{3,2,1,0:T(8,128)(2,1)S(1)}, bf16[4,2,640,128]{3,2,1,0:T(8,128)(2,1)S(1)}, u32[]{:S(2)}, u32[]{:S(2)}) collective-permute-start(bf16[4,2,640,128]{3,2,1,0:T(8,128)(2,1)S(1)} %get-tuple-element.176.refs_4_), channel_id=1, source_target_pairs={{0,4},{1,5},{2,6},{3,7},{12,8},{13,9},{14,10},{15,11},{16,20},{17,... | collective-permute-start | bytes 3932168 | tf_op jit(solution)/shard_map/ppermute | solution.py:489
  193.0 30.3 %collective-permute-start.24 = (bf16[4,2,640,128]{3,2,1,0:T(8,128)(2,1)S(1)}, bf16[4,2,640,128]{3,2,1,0:T(8,128)(2,1)S(1)}, u32[]{:S(2)}, u32[]{:S(2)}) collective-permute-start(bf16[4,2,640,128]{3,2,1,0:T(8,128)(2,1)S(1)} %get-tuple-element.183.refs_4_), channel_id=1, source_target_pairs={{0,4},{1,5},{2,6},{3,7},{12,8},{13,9},{14,10},{15,11},{16,20},{17,... | collective-permute-start | bytes 3932168 | tf_op jit(solution)/shard_map/ppermute | solution.py:489
  198.1 32.8 %collective-permute-start.27 = (bf16[8,640,128]{2,1,0:T(8,128)(2,1)S(1)}, bf16[8,640,128]{2,1,0:T(8,128)(2,1)S(1)}, u32[]{:S(2)}, u32[]{:S(2)}) collective-permute-start(bf16[8,640,128]{2,1,0:T(8,128)(2,1)S(1)} %get-tuple-element.188), channel_id=1, source_target_pairs={{4,8},{5,9},{6,10},{7,11},{8,4},{9,5},{10,6},{11,7},{20,24},{21,25... | collective-permute-start | bytes 3932168 | tf_op jit(solution)/shard_map/ppermute | solution.py:494
  203.4 43.4 %collective-permute-start.26 = (bf16[4,640,256]{2,1,0:T(8,128)(2,1)S(1)}, bf16[4,640,256]{2,1,0:T(8,128)(2,1)S(1)}, u32[]{:S(2)}, u32[]{:S(2)}) collective-permute-start(bf16[4,640,256]{2,1,0:T(8,128)(2,1)S(1)} %get-tuple-element.187), channel_id=1, source_target_pairs={{4,0},{5,1},{6,2},{7,3},{8,12},{9,13},{10,14},{11,15},{20,16},{21,... | collective-permute-start | bytes 3932168 | tf_op jit(solution)/shard_map/ppermute | solution.py:499
  223.3 32.8 %collective-permute-start.25 = (bf16[4,2,640,128]{3,2,1,0:T(8,128)(2,1)S(1)}, bf16[4,2,640,128]{3,2,1,0:T(8,128)(2,1)S(1)}, u32[]{:S(2)}, u32[]{:S(2)}) collective-permute-start(bf16[4,2,640,128]{3,2,1,0:T(8,128)(2,1)S(1)} %get-tuple-element.185.refs_4_), channel_id=1, source_target_pairs={{0,4},{1,5},{2,6},{3,7},{12,8},{13,9},{14,10},{15,11},{16,20},{17,... | collective-permute-start | bytes 3932168 | tf_op jit(solution)/shard_map/ppermute | solution.py:489
  230.2 33.0 %collective-permute-start.33 = (bf16[8,640,128]{2,1,0:T(8,128)(2,1)}, bf16[8,640,128]{2,1,0:T(8,128)(2,1)S(1)}, u32[]{:S(2)}, u32[]{:S(2)}) collective-permute-start(bf16[8,640,128]{2,1,0:T(8,128)(2,1)} %copy-done.23), channel_id=1, source_target_pairs={{4,8},{5,9},{6,10},{7,11},{8,4},{9,5},{10,6},{11,7},{20,24},{21,25... | collective-permute-start | bytes 3932168 | tf_op jit(solution)/shard_map/ppermute | solution.py:494
  259.2 34.9 %collective-permute-start.28 = (bf16[8,640,128]{2,1,0:T(8,128)(2,1)}, bf16[8,640,128]{2,1,0:T(8,128)(2,1)S(1)}, u32[]{:S(2)}, u32[]{:S(2)}) collective-permute-start(bf16[8,640,128]{2,1,0:T(8,128)(2,1)} %get-tuple-element.193), channel_id=1, source_target_pairs={{4,8},{5,9},{6,10},{7,11},{8,4},{9,5},{10,6},{11,7},{20,24},{21,25... | collective-permute-start | bytes 3932168 | tf_op jit(solution)/shard_map/ppermute | solution.py:494
  259.9 22.7 %collective-permute-start.29 = (bf16[4,640,128]{2,1,0:T(8,128)(2,1)S(1)}, bf16[4,640,128]{2,1,0:T(8,128)(2,1)S(1)}, u32[]{:S(2)}, u32[]{:S(2)}) collective-permute-start(bf16[4,640,128]{2,1,0:T(8,128)(2,1)S(1)} %get-tuple-element.195), channel_id=1, source_target_pairs={{4,0},{5,1},{6,2},{7,3},{8,12},{9,13},{10,14},{11,15},{20,16},{21,... | collective-permute-start | bytes 1966088 | tf_op jit(solution)/shard_map/ppermute | solution.py:499
  267.2 35.1 %collective-permute-start.38 = (bf16[4,640,128]{2,1,0:T(8,128)(2,1)}, bf16[4,640,128]{2,1,0:T(8,128)(2,1)}, u32[]{:S(2)}, u32[]{:S(2)}) collective-permute-start(bf16[4,640,128]{2,1,0:T(8,128)(2,1)} %get-tuple-element.213), channel_id=1, source_target_pairs={{4,0},{5,1},{6,2},{7,3},{8,12},{9,13},{10,14},{11,15},{20,16},{21,... | collective-permute-start | bytes 1966088 | tf_op jit(solution)/shard_map/ppermute | solution.py:499
  299.3 49.0 %collective-permute-start.48 = (bf16[4,640,256]{2,1,0:T(8,128)(2,1)S(1)}, bf16[4,640,256]{2,1,0:T(8,128)(2,1)S(1)}, u32[]{:S(2)}, u32[]{:S(2)}) collective-permute-start(bf16[4,640,256]{2,1,0:T(8,128)(2,1)S(1)} %get-tuple-element.229.refs_2_), channel_id=1, source_target_pairs={{0,16},{16,0},{1,17},{17,1},{2,18},{18,2},{3,19},{19,3},{4,20},{20... | collective-permute-start | bytes 3932168 | tf_op jit(solution)/shard_map/ppermute | solution.py:505
  308.3 36.7 %collective-permute-start.49 = (bf16[4,640,128]{2,1,0:T(8,128)(2,1)}, bf16[4,640,128]{2,1,0:T(8,128)(2,1)}, u32[]{:S(2)}, u32[]{:S(2)}) collective-permute-start(bf16[4,640,128]{2,1,0:T(8,128)(2,1)} %get-tuple-element.230.refs_2_), channel_id=1, source_target_pairs={{0,16},{16,0},{1,17},{17,1},{2,18},{18,2},{3,19},{19,3},{4,20},{20... | collective-permute-start | bytes 1966088 | tf_op jit(solution)/shard_map/ppermute | solution.py:505
  325.7 33.4 %collective-permute-start.47 = (bf16[4,640,128]{2,1,0:T(8,128)(2,1)S(1)}, bf16[4,640,128]{2,1,0:T(8,128)(2,1)}, u32[]{:S(2)}, u32[]{:S(2)}) collective-permute-start(bf16[4,640,128]{2,1,0:T(8,128)(2,1)S(1)} %get-tuple-element.228.refs_2_), channel_id=1, source_target_pairs={{0,16},{16,0},{1,17},{17,1},{2,18},{18,2},{3,19},{19,3},{4,20},{20... | collective-permute-start | bytes 1966088 | tf_op jit(solution)/shard_map/ppermute | solution.py:505
  328.3 44.9 %collective-permute-start.46 = (bf16[4,640,128]{2,1,0:T(8,128)(2,1)}, bf16[4,640,128]{2,1,0:T(8,128)(2,1)}, u32[]{:S(2)}, u32[]{:S(2)}) collective-permute-start(bf16[4,640,128]{2,1,0:T(8,128)(2,1)} %copy-done.14), channel_id=1, source_target_pairs={{0,16},{16,0},{1,17},{17,1},{2,18},{18,2},{3,19},{19,3},{4,20},{20... | collective-permute-start | bytes 1966088 | tf_op jit(solution)/shard_map/ppermute | solution.py:505
  332.9 54.0 %collective-permute-start.45 = (bf16[4,640,128]{2,1,0:T(8,128)(2,1)}, bf16[4,640,128]{2,1,0:T(8,128)(2,1)}, u32[]{:S(2)}, u32[]{:S(2)}) collective-permute-start(bf16[4,640,128]{2,1,0:T(8,128)(2,1)} %get-tuple-element.226.refs_2_), channel_id=1, source_target_pairs={{0,16},{16,0},{1,17},{17,1},{2,18},{18,2},{3,19},{19,3},{4,20},{20... | collective-permute-start | bytes 1966088 | tf_op jit(solution)/shard_map/ppermute | solution.py:505
  406.9 25.5 %all-to-all-start = ((bf16[16,48,640]{2,1,0:T(8,128)(2,1)}), bf16[16,48,640]{2,1,0:T(8,128)(2,1)S(1)}, u32[]{:S(2)}, u32[]{:S(2)}) async-start(bf16[16,48,640]{2,1,0:T(8,128)(2,1)} %pad_maximum_fusion), calls=%async_computation | async-start | bytes 1966080 | tf_op jit(solution)/shard_map/all_to_all | solution.py:515
  (67 other events, 515.8 us)
Sparse Core Ops, SparseCore 0:
  35.9 49.3 all-gather.2
  102.2 46.7 all-gather.4

commit v4 on v3

v4 whole, which is shorter than its diff:
```python
import math
import random

import jax
import jax.numpy as jnp
from jax import lax
from jax.experimental import pallas as pl
from jax.experimental.pallas import tpu as pltpu
from jax.sharding import PartitionSpec as P

D = 2560
BLOCK = 128
PLANES = 4
TOKEN = jax.ShapeDtypeStruct((8, 128), jnp.float32)
ANY = pl.BlockSpec(memory_space=pl.ANY)
SMEM = pl.BlockSpec(memory_space=pltpu.SMEM)
VMEM = pl.BlockSpec(memory_space=pltpu.VMEM)
VMEM_LIMIT = 60 * 1024 * 1024


def cluster_weights(cluster_ids, frequency):
    ids = cluster_ids[:, 0]
    same = (ids[:, None] == ids[None, :]).astype(jnp.float32)
    return frequency / jnp.sum(same * frequency[None, :], axis=1)


def step_call(kernel, token, operands, in_specs, out_shape, out_specs, cost, **options):
    count = len(operands)

    def ordered(*refs):
        kernel(*refs[:count], *refs[count + 1 : count + 1 + len(out_shape)], *refs[count + 2 + len(out_shape) :])

    *results, token = pl.pallas_call(
        ordered,
        out_shape=[*out_shape, TOKEN],
        in_specs=[*in_specs, ANY],
        out_specs=[*out_specs, ANY],
        compiler_params=pltpu.CompilerParams(vmem_limit_bytes=VMEM_LIMIT),
        cost_estimate=pl.CostEstimate(flops=cost[0], bytes_accessed=cost[1], transcendentals=0),
        **options,
    )(*operands, token)
    return results, token


def pack(token, info, gate, up, start, width, plane):
    sources, depth, _ = gate.shape
    rows = depth // plane

    def kernel(info_ref, gate_ref, up_ref, *rest):
        outs, held, in_sems, out_sems = rest[:plane], *rest[plane:]
        place = info_ref[0]

        def move(source):
            loads = [
                pltpu.make_async_copy(
                    source.at[
                        :,
                        pl.ds(pl.multiple_of((place ^ shift) * rows, 16), rows),
                        pl.ds(start, width),
                    ],
                    held.at[shift],
                    in_sems.at[shift],
                )
                for shift in range(plane)
            ]
            stores = [
                pltpu.make_async_copy(held.at[shift], outs[shift], out_sems.at[shift])
                for shift in range(plane)
            ]
            for load in loads:
                load.start()
            for load, store in zip(loads, stores):
                load.wait()
                store.start()
            for store in stores:
                store.wait()

        @pl.when(info_ref[2] == 0)
        def _():
            move(gate_ref)

        @pl.when(info_ref[2] != 0)
        def _():
            move(up_ref)

    return step_call(
        kernel,
        token,
        (info, gate, up),
        [SMEM, ANY, ANY],
        [jax.ShapeDtypeStruct((sources, rows, width), gate.dtype)] * plane,
        [ANY] * plane,
        (0, 4 * sources * depth * width),
        scratch_shapes=[
            pltpu.VMEM((plane, sources, rows, width), gate.dtype),
            pltpu.SemaphoreType.DMA((plane,)),
            pltpu.SemaphoreType.DMA((plane,)),
        ],
        name="pack",
    )


def merge(token, info, ids, weights, scales, near, far, received, start, scale_blocks):
    plane = len(near)
    sources, rows, width = near[0].shape
    step = math.gcd(rows, BLOCK)
    row_blocks, column_blocks = scale_blocks
    first = start // BLOCK

    def kernel(info_ref, ids_ref, weights_ref, scales_ref, *rest):
        blocks, rest, total = rest[: 2 * plane], rest[2 * plane : -1], rest[-1]
        place, inner = info_ref[0], info_ref[1]
        outer = jnp.where(inner == 1, 0, PLANES - 1)
        to_inner = inner if received is not None else PLANES - 1 - inner
        to_outer = outer if received is not None else PLANES - 1 - outer
        row_block = (place * rows + pl.program_id(0) * step) // BLOCK

        @pl.when(info_ref[3] == 1)
        def _():
            if received is None:
                total[...] = jnp.zeros_like(total)
            else:
                total[...] = rest[0][...].astype(jnp.float32)
            for index, block in enumerate(blocks):
                held = inner if index < plane else outer
                for number in range(sources):
                    source = (held * plane + (place ^ (index % plane))) * sources + number
                    target = ids_ref[source]
                    target_plane = target // plane
                    slot = (target % plane) ^ place

                    @pl.when((target_plane == to_inner) | (target_plane == to_outer))
                    def _():
                        into = jnp.where(target_plane == to_outer, plane, 0) + slot
                        base = (source * row_blocks + row_block) * column_blocks + first
                        for part in range(width // BLOCK):
                            lanes = pl.ds(part * BLOCK, BLOCK)
                            factor = weights_ref[source] * scales_ref[base + part]
                            total[into, :, lanes] += (
                                block[number, :, lanes].astype(jnp.float32) * factor
                            )

            if received is None:
                rest[0][...] = total[...].astype(jnp.bfloat16)
            else:
                for index in range(2 * plane):
                    rest[1 + index][...] = total[index].astype(jnp.bfloat16)

    pieces = pl.BlockSpec((sources, step, width), lambda i: (0, i, 0))
    both = pl.BlockSpec((2 * plane, step, width), lambda i: (0, i, 0))
    one = pl.BlockSpec((step, width), lambda i: (i, 0))
    if received is None:
        extra, extra_specs = (), []
        out_shape = [jax.ShapeDtypeStruct((2 * plane, rows, width), jnp.bfloat16)]
        out_specs = [both]
    else:
        extra, extra_specs = (received,), [both]
        out_shape = [jax.ShapeDtypeStruct((rows, width), jnp.bfloat16)] * (2 * plane)
        out_specs = [one] * (2 * plane)
    size = plane * near[0].size
    return step_call(
        kernel,
        token,
        (info, ids, weights, scales, *near, *far, *extra),
        [SMEM] * 4 + [pieces] * (2 * plane) + extra_specs,
        out_shape,
        out_specs,
        (4 * size, 8 * size),
        grid=(rows // step,),
        scratch_shapes=[pltpu.VMEM((2 * plane, step, width), jnp.float32)],
        name="merge",
    )


def join(token, info, inside, outside):
    plane = len(inside)
    rows, width = inside[0].shape

    def kernel(info_ref, *rest):
        out, sems = rest[2 * plane :]

        def move(sources):
            copies = [
                pltpu.make_async_copy(sources[shift], out.at[shift], sems.at[shift])
                for shift in range(plane)
            ]
            for copy in copies:
                copy.start()
            for copy in copies:
                copy.wait()

        @pl.when(info_ref[3] == 1)
        def _():
            move(rest[:plane])

        @pl.when(info_ref[3] != 1)
        def _():
            move(rest[plane : 2 * plane])

    (own,), token = step_call(
        kernel,
        token,
        (info, *inside, *outside),
        [SMEM] + [ANY] * (2 * plane),
        [jax.ShapeDtypeStruct((plane, rows, width), inside[0].dtype)],
        [VMEM],
        (0, 4 * plane * rows * width),
        scratch_shapes=[pltpu.SemaphoreType.DMA((plane,))],
        name="join",
    )
    return own, token


def pair(token, tokens, other):
    def kernel(tokens_ref, other_ref, out_ref):
        out_ref[0] = tokens_ref[...]
        out_ref[1] = other_ref[...]

    (both,), token = step_call(
        kernel,
        token,
        (tokens, other),
        [VMEM, VMEM],
        [jax.ShapeDtypeStruct((2,) + tokens.shape, tokens.dtype)],
        [VMEM],
        (0, 8 * tokens.size),
        name="pair",
    )
    return both, token


def line(token, info, tokens, other, crossed, forwarded):
    def kernel(info_ref, tokens_ref, other_ref, crossed_ref, forwarded_ref, out_ref):
        level = info_ref[1]
        low = level < PLANES // 2
        out_ref[level] = tokens_ref[...]
        out_ref[level ^ 1] = other_ref[...]

        def put(pair_ref):
            out_ref[jnp.where(low, 2, 1)] = pair_ref[0]
            out_ref[jnp.where(low, 3, 0)] = pair_ref[1]

        @pl.when(info_ref[3] == 1)
        def _():
            put(crossed_ref)

        @pl.when(info_ref[3] != 1)
        def _():
            put(forwarded_ref)

    (whole,), token = step_call(
        kernel,
        token,
        (info, tokens, other, crossed, forwarded),
        [SMEM] + [VMEM] * 4,
        [jax.ShapeDtypeStruct((PLANES,) + tokens.shape, tokens.dtype)],
        [VMEM],
        (0, 16 * tokens.size),
        name="line",
    )
    return whole, token


def dispatch(token, placing, lines):
    count, capacity, tok_dev = placing.shape
    width = lines[0].shape[2]

    def kernel(placing_ref, *rest):
        out_ref = rest[len(lines)]
        for block in range(count):
            rows = rest[block // PLANES][block % PLANES]
            out_ref[block * capacity : (block + 1) * capacity] = jnp.dot(
                placing_ref[block], rows, preferred_element_type=jnp.float32
            ).astype(jnp.bfloat16)

    (grouped,), token = step_call(
        kernel,
        token,
        (placing, *lines),
        [VMEM] * (1 + len(lines)),
        [jax.ShapeDtypeStruct((count * capacity, width), jnp.bfloat16)],
        [VMEM],
        (2 * count * capacity * tok_dev * width, 4 * count * tok_dev * width),
        name="dispatch",
    )
    return grouped, token


def run_chunk(token, info, grouped, own, partner, outputs, start, shape, devices):
    plane, rows, width = own.shape
    depth, full = shape
    count = grouped.shape[0]
    each = count // devices
    factor = 1.0 / math.sqrt(D)

    def kernel(info_ref, grouped_ref, own_ref, partner_ref, *rest):
        gate_out, up_out, hidden_ref, whole, sems, out_sems = rest[len(outputs) :]
        place = info_ref[0]

        def load(pieces, column, base):
            return [
                pltpu.make_async_copy(
                    pieces.at[shift],
                    whole.at[
                        pl.ds(pl.multiple_of((place ^ shift) * rows, 16), rows),
                        pl.ds(column, width),
                    ],
                    sems.at[base + shift],
                )
                for shift in range(plane)
            ]

        def fill(gate, up):
            copies = load(gate, 0, 0) + load(up, width, plane)
            for copy in copies:
                copy.start()
            for copy in copies:
                copy.wait()

        @pl.when(info_ref[2] == 0)
        def _():
            fill(own_ref, partner_ref)

        @pl.when(info_ref[2] != 0)
        def _():
            fill(partner_ref, own_ref)

        stores = [
            pltpu.make_async_copy(
                whole.at[:, pl.ds(index * width, width)],
                out.at[0, :, pl.ds(start, width)],
                out_sems.at[index],
            )
            for index, out in enumerate((gate_out, up_out))
        ]
        for store in stores:
            store.start()
        values = jnp.dot(grouped_ref[...], whole[...], preferred_element_type=jnp.float32)
        gate_value = values[:, :width] * factor
        up_value = values[:, width:] * factor
        hidden = (gate_value / (1.0 + jnp.exp(-gate_value)) * up_value).astype(jnp.bfloat16)
        for index in range(devices):
            device = (index % PLANES) * plane + (place ^ (index // PLANES))
            hidden_ref[device] = hidden[index * each : (index + 1) * each]
        for store in stores:
            store.wait()

    weights = jax.ShapeDtypeStruct((1, depth, full), jnp.bfloat16)
    return step_call(
        kernel,
        token,
        (info, grouped, own, partner, *outputs),
        [SMEM, VMEM, ANY, ANY] + [ANY] * len(outputs),
        [weights, weights, jax.ShapeDtypeStruct((devices, each, width), jnp.bfloat16)],
        [ANY, ANY, VMEM],
        (4 * count * depth * width, 2 * (grouped.size + 4 * depth * width)),
        scratch_shapes=[
            pltpu.VMEM((depth, 2 * width), jnp.bfloat16),
            pltpu.SemaphoreType.DMA((2 * plane,)),
            pltpu.SemaphoreType.DMA((2,)),
        ],
        input_output_aliases={4 + index: index for index in range(len(outputs))},
        name="run_chunk",
    )


STEPS = {
    "pair": (("t1",), (3.0, 0.0), (("t2", 13.0, "middle"),)),
    "line": (("t3",), (4.0, 0.0), (("t4", 40.0, "y"),)),
    "dispatch": (("t4",), (6.0, 0.0), ()),
    "pack": (("pack before",), (8.0, 0.6), (("a", 25.0, "in"), ("b", 13.0, "y"))),
    "partial": (("a", "b"), (5.0, 1.5), (("m", 25.0, "middle"),)),
    "finish": (("m",), (8.0, 2.0), (("d", 13.0, "out"), ("e", 13.0, "y"))),
    "join": (("d", "e"), (2.5, 0.5), (("x", 12.0, "x"),)),
    "run": (("x", "dispatch", "run before"), (2.0, 1.5), ()),
}
ONCE = ("pair", "line", "dispatch")
LATENCY = 2.0
RETURN = 30.0
TRIES = 2500


def needs_of(name, chunk):
    needs = []
    for need in STEPS[name][0]:
        if need in ONCE or need[0] == "t":
            needs.append((need, 0))
        elif not need.endswith(" before"):
            needs.append((need, chunk))
        elif chunk > 0:
            needs.append((need[: -len(" before")], chunk - 1))
    return needs


def advance(now, until, links, done):
    while now < until:
        left = [min(load.values()) * len(load) for load in links.values() if load]
        span = min(left + [until - now])
        for load in links.values():
            for key in load:
                load[key] -= span / len(load)
        for load in links.values():
            for key in [key for key, rest in load.items() if rest <= 1e-6]:
                del load[key]
                done[key] = now + span + LATENCY
        now += span
    return now


def play(widths, order):
    links = {"in": {}, "middle": {}, "out": {}, "y": {}, "x": {}}
    done = {("t1", 0): 8.0}
    clock = 0.0
    now = 0.0
    for name, chunk in order:
        for need in needs_of(name, chunk):
            if need == ("t3", 0):
                need = ("t2", 0)
                extra = 16.0
            else:
                extra = 0.0
            while need not in done:
                clock = advance(clock, clock + 1.0, links, done)
            now = max(now, done[need] + extra)
        _, (fixed, each), sent = STEPS[name]
        width = 1 if name in ONCE else widths[chunk]
        now += fixed + each * width
        clock = advance(clock, max(clock, now), links, done)
        done[(name, chunk)] = now
        for what, cost, link in sent:
            links[link][(what, chunk)] = cost * width
    back = done[("run", max(0, len(widths) - 2))] + RETURN
    return max(now, back) + 0.02 * sum(done[("run", chunk)] for chunk in range(len(widths)))


def arrange(steps, rank):
    sender = {what: name for name, step in STEPS.items() for what, _, _ in step[2]}
    placed, order, left = set(), [], sorted(steps, key=lambda step: rank[step])
    while left:
        for step in left:
            needs = [(sender.get(n, n), c) for n, c in needs_of(*step) if n not in ("t1", "t3")]
            if step == ("line", 0):
                needs = [("pair", 0)]
            if all(need in placed for need in needs):
                break
        left.remove(step)
        placed.add(step)
        order.append(step)
    return order


def plan(widths):
    draw = random.Random(0)
    offset = {"pack": 0, "partial": 35, "finish": 65, "join": 95, "run": 115}
    rank = {(name, 0): value for name, value in zip(ONCE, (8, 20, 75))}
    time = 0.0
    for chunk, width in enumerate(widths):
        for name, value in offset.items():
            rank[(name, chunk)] = time + value
        time += 27.0 * width
    steps = list(rank)
    order = arrange(steps, rank)
    best = (play(widths, order), order, rank)
    for _ in range(TRIES):
        trial = dict(best[2])
        for _ in range(draw.randint(1, 3)):
            trial[draw.choice(steps)] += draw.gauss(0.0, 15.0)
        order = arrange(steps, trial)
        end = play(widths, order)
        if end <= best[0]:
            best = (end, order, trial)
    return best[1]


def route_slots(routes, merged_count, tok_dev):
    experts = jnp.arange(merged_count, dtype=jnp.int32)
    hit_table = jnp.sum((routes[:, :, None] == experts).astype(jnp.int32), axis=1)
    hit_table = hit_table.reshape(-1, tok_dev, merged_count)
    position_lookup = jnp.cumsum(hit_table, axis=1) - hit_table
    return (hit_table, position_lookup)


def chunk_widths(blocks):
    if blocks < 6:
        return [1] * blocks
    return [1, 1, blocks - 4, 1, 1]


def shards(tokens, routes, quant_gate, quant_up, gate_scales, up_scales, cluster_ids, frequency):
    expert_count = lax.axis_size("expert")
    own_index = lax.axis_index("expert")
    group_count = lax.axis_size("groups")
    half = lax.axis_index("groups") % 2
    plane = expert_count // PLANES
    place, level = own_index % plane, own_index // plane
    is_inner = (level == 1) | (level == 2)
    depth, full = quant_gate.shape[1:]
    tok_dev = tokens.shape[0]
    top_count = routes.shape[1]
    capacity = min(tok_dev, 2 * tok_dev * top_count // expert_count)

    def wires(pairs, shift):
        return [(a * plane + p, b * plane + (p ^ shift)) for a, b in pairs for p in range(plane)]

    def send(value, pairs, shift=0):
        return lax.ppermute(value, "expert", wires(pairs, shift))

    inward = [(0, 1), (3, 2)]
    outward = [(1, 0), (2, 3)]
    across = [(1, 2), (2, 1)]
    inner = [(1, 1), (2, 2)]
    every = [(z, z) for z in range(PLANES)]
    shifts = range(plane)
    partners = [(g, g ^ 1) for g in range(group_count)]

    info = jnp.stack([place, level, half, is_inner.astype(jnp.int32)]).astype(jnp.int32)
    ids = cluster_ids[:, 0]
    weights = cluster_weights(cluster_ids, frequency)
    scales = jnp.where(half == 0, gate_scales, up_scales)
    scale_blocks = scales.shape[1:]
    scales = scales.reshape(-1)

    hit_table, position_lookup = route_slots(routes, expert_count, tok_dev)
    positions = jnp.arange(capacity, dtype=jnp.int32)

    def in_blocks(table):
        column = lax.dynamic_index_in_dim(table, own_index, 2, keepdims=False)
        column = column.reshape(PLANES, plane, tok_dev)
        column = jnp.take(column, place ^ jnp.arange(plane, dtype=jnp.int32), axis=1)
        return column.transpose(1, 0, 2).reshape(expert_count, 1, tok_dev)

    placing = (
        (in_blocks(hit_table) == 1) & (in_blocks(position_lookup) == positions[None, :, None])
    ).astype(jnp.bfloat16)

    experts = jnp.arange(expert_count, dtype=jnp.int32)
    local_routes = lax.dynamic_slice_in_dim(routes, own_index * tok_dev, tok_dev, 0)
    own_slots = lax.dynamic_index_in_dim(position_lookup, own_index, 0, keepdims=False)
    chosen = local_routes[:, :, None] == experts
    slot_of = jnp.sum(jnp.where(chosen, own_slots[:, None, :], 0), axis=2)
    picking = (chosen[:, :, :, None] & (slot_of[:, :, None, None] == positions)).astype(
        jnp.bfloat16
    )
    picking = picking.reshape(tok_dev * top_count, expert_count * capacity)

    widths = chunk_widths(full // BLOCK)
    starts = [BLOCK * sum(widths[:chunk]) for chunk in range(len(widths))]
    token = jnp.zeros(TOKEN.shape, TOKEN.dtype)
    neighbour = send(tokens, inward + outward)
    near, far, received, inside, outside, own, partner, hiddens = ({} for _ in range(8))
    outputs = ()
    for name, c in plan(widths):
        start, width = starts[c], widths[c] * BLOCK
        if name == "pair":
            both, token = pair(token, tokens, neighbour)
            crossed = send(both, across)
            forwarded = send(crossed, outward)
        elif name == "line":
            whole, token = line(token, info, tokens, neighbour, crossed, forwarded)
            lines = {0: whole}
            bit = plane // 2
            while bit:
                for shift in list(lines):
                    lines[shift ^ bit] = send(lines[shift], every, bit)
                bit //= 2
        elif name == "dispatch":
            grouped, token = dispatch(token, placing, [lines[shift] for shift in shifts])
            grouped = lax.all_gather(grouped, "mp", axis=1, tiled=True)
        elif name == "pack":
            pieces, token = pack(token, info, quant_gate, quant_up, start, width, plane)
            far[c] = [send(pieces[shift], inward, shift) for shift in shifts]
            near[c] = [send(pieces[shift], inner, shift) if shift else pieces[0] for shift in shifts]
        elif name == "partial":
            (partial,), token = merge(
                token, info, ids, weights, scales, near[c], far[c], None, start, scale_blocks
            )
            received[c] = send(partial, across)
        elif name == "finish":
            rows, token = merge(
                token, info, ids, weights, scales, near[c], far[c], received[c], start, scale_blocks
            )
            outside[c] = [send(rows[plane + shift], outward, shift) for shift in shifts]
            inside[c] = [send(rows[shift], inner, shift) if shift else rows[0] for shift in shifts]
        elif name == "join":
            own[c], token = join(token, info, inside[c], outside[c])
            partner[c] = lax.ppermute(own[c], "groups", partners)
        else:
            (*outputs, hiddens[c]), token = run_chunk(
                token, info, grouped, own[c], partner[c], outputs, start, (depth, full), expert_count
            )

    last = len(widths) - 1
    finished = []
    for batch in (range(last), range(last, last + 1)):
        hidden = jnp.concatenate([hiddens[c] for c in batch], axis=2)
        returned = lax.all_to_all(hidden, "expert", split_axis=0, concat_axis=0, tiled=True)
        rows = returned.reshape(expert_count * capacity, returned.shape[2])
        finished.append(
            jnp.dot(picking, rows, preferred_element_type=jnp.float32).astype(jnp.bfloat16)
        )
    output = jnp.concatenate(finished, axis=1)
    merged_gate, merged_up = outputs
    return (merged_gate, merged_up, output.reshape(tok_dev, top_count, full))


def solution(mesh):
    return jax.shard_map(
        shards,
        mesh=mesh,
        in_specs=(
            P(("groups", "expert"), "mp"),
            P("groups", None),
            P("expert", None, "mp"),
            P("expert", None, "mp"),
            P(None, None, "mp"),
            P(None, None, "mp"),
            P(),
            P(),
        ),
        out_specs=(
            P(("groups", "expert"), None, "mp"),
            P(("groups", "expert"), None, "mp"),
            P(("groups", "expert"), None, "mp"),
        ),
        check_vma=False,
    )
```

time: 443 us -> 599 us (1.35)
  starting transfers between devices: 70.4 us -> 221 us
  Pallas kernels: 71.2 us -> 116 us
  waiting for transfers between devices: 246 us -> 223 us
  between operations: 14.9 us -> 2.5 us
  local copies, waits for them, and re-layouts: 28.1 us -> 17.7 us
  other arithmetic: 6.01 us -> 12.5 us
    ppermute x45 -> x81, starting transfers between devices: 54.2 us -> 208 us  [send(): return lax.ppermute(value, 'expert', wires(pairs, shift))]
    pallas_call x40 -> x28, Pallas kernels: 71.2 us -> 116 us  [step_call(): pl.pallas_call(ordered, out_shape=[*out_shape, TOKEN], in_specs=[*in_spec...]
    ppermute x5, waiting for transfers between devices: 34 us -> 20.2 us  [shards(): partner[c] = lax.ppermute(own[c], 'groups', partners)]
    unnamed x75 -> x161, local copies, waits for them, and re-layouts: 19.7 us -> 9.88 us
    ppermute x45 -> x81, waiting for transfers between devices: 188 us -> 179 us  [send(): return lax.ppermute(value, 'expert', wires(pairs, shift))]
  transfers between devices with their start and end apart: 54 -> 88, of which waited for: 34 -> 31; matrix products, arithmetic and copies ran while one was open for 4% -> 3% of each run, Pallas kernels for 14% -> 16%
where the time goes in v4:
time: 599 us; the launch traced here: 594 us
  waiting for transfers between devices  223 us (37%)
  starting transfers between devices  221 us (37%)
  Pallas kernels  116 us (19%)
  local copies, waits for them, and re-layouts  17.7 us (3%)
  other arithmetic  12.5 us (2%)
    ppermute x81, starting transfers between devices, send(): return lax.ppermute(value, 'expert', wires(pairs, shift))  208 us
    ppermute x81, waiting for transfers between devices, send(): return lax.ppermute(value, 'expert', wires(pairs, shift))  179 us
    pallas_call x28, Pallas kernels, step_call(): pl.pallas_call(ordered, out_shape=[*out_shape, TOKEN], in_specs=[*in_spec...  116 us
    all_to_all x2, waiting for transfers between devices, shards(): lax.all_to_all(hidden, 'expert', split_axis=0, concat_axis=0, tiled=True)  23.4 us
    ppermute x5, waiting for transfers between devices, shards(): partner[c] = lax.ppermute(own[c], 'groups', partners)  20.2 us
  transfers between devices with their start and end apart: 88, of which 31 were waited for; matrix products, arithmetic and copies ran while one was open for 3% of the time, Pallas kernels for 16%

profile of v4, /device:TPU:0, one launch (start us, length us, event | category | flops | bytes accessed | tf_op | source)
XLA Modules:
  0.0 593.7 jit_solution(6099610473981552080)
XLA Ops:
  22.6 25.3 %collective-permute-done.2.refs_4_ = bf16[2,64,2560]{2,1,0:T(8,128)(2,1)S(1)} collective-permute-done((bf16[2,64,2560]{2,1,0:T(8,128)(2,1)S(1)}, bf16[2,64,2560]{2,1,0:T(8,128)(2,1)S(1)}, u32[]{:S(2)}, u32[]{:S(2)}) %collective-permute-start.2) | collective-permute-done | bytes 655392 | tf_op jit(solution)/shard_map/ppermute | solution.py:506
  62.9 6.5 %collective-permute-done.11.refs_10_ = bf16[2,640,128]{2,1,0:T(8,128)(2,1)S(1)} collective-permute-done((bf16[2,640,128]{2,1,0:T(8,128)(2,1)}, bf16[2,640,128]{2,1,0:T(8,128)(2,1)S(1)}, u32[]{:S(2)}, u32[]{:S(2)}) %collective-permute-start.11) | collective-permute-done | bytes 327712 | tf_op jit(solution)/shard_map/ppermute | solution.py:506
  70.1 6.0 %collective-permute-done.12.refs_11_ = bf16[2,640,128]{2,1,0:T(8,128)(2,1)S(1)} collective-permute-done((bf16[2,640,128]{2,1,0:T(8,128)(2,1)}, bf16[2,640,128]{2,1,0:T(8,128)(2,1)S(1)}, u32[]{:S(2)}, u32[]{:S(2)}) %collective-permute-start.12) | collective-permute-done | bytes 327712 | tf_op jit(solution)/shard_map/ppermute | solution.py:506
  80.8 17.6 %collective-permute-start.18 = (bf16[2,640,128]{2,1,0:T(8,128)(2,1)}, bf16[2,640,128]{2,1,0:T(8,128)(2,1)S(1)}, u32[]{:S(2)}, u32[]{:S(2)}) collective-permute-start(bf16[2,640,128]{2,1,0:T(8,128)(2,1)} %get-tuple-element.132), channel_id=1, source_target_pairs={{0,5},{1,4},{2,7},{3,6},{12,9},{13,8},{14,11},{15,10},{16,21},{17,... | collective-permute-start | bytes 983048 | tf_op jit(solution)/shard_map/ppermute | solution.py:506
  99.9 14.5 %collective-permute-start.17 = (bf16[2,640,128]{2,1,0:T(8,128)(2,1)S(1)}, bf16[2,640,128]{2,1,0:T(8,128)(2,1)S(1)}, u32[]{:S(2)}, u32[]{:S(2)}) collective-permute-start(bf16[2,640,128]{2,1,0:T(8,128)(2,1)S(1)} %copy-done.12), channel_id=1, source_target_pairs={{0,4},{1,5},{2,6},{3,7},{12,8},{13,9},{14,10},{15,11},{16,20},{17,... | collective-permute-start | bytes 983048 | tf_op jit(solution)/shard_map/ppermute | solution.py:506
  130.4 6.6 %collective-permute-done.19.refs_10_ = bf16[2,640,128]{2,1,0:T(8,128)(2,1)S(1)} collective-permute-done((bf16[2,640,128]{2,1,0:T(8,128)(2,1)}, bf16[2,640,128]{2,1,0:T(8,128)(2,1)S(1)}, u32[]{:S(2)}, u32[]{:S(2)}) %collective-permute-start.19) | collective-permute-done | bytes 327712 | tf_op jit(solution)/shard_map/ppermute | solution.py:506
  144.0 6.3 %fusion.2 = s32[16,64,16]{2,0,1:T(8,128)S(1)} fusion(s32[16,64,16]{2,0,1:T(8,128)S(1)} %copy.34), kind=kOutput, calls=%fused_computation.27 | output fusion | flops 1032192 | bytes 131072 | tf_op jit(solution)/shard_map/jit(cumsum)/reduce_window_sum | solution.py:479
  152.8 6.2 %collective-permute-start.33 = (bf16[2,640,256]{2,1,0:T(8,128)(2,1)}, bf16[2,640,256]{2,1,0:T(8,128)(2,1)S(1)}, u32[]{:S(2)}, u32[]{:S(2)}) collective-permute-start(bf16[2,640,256]{2,1,0:T(8,128)(2,1)} %get-tuple-element.149), channel_id=1, source_target_pairs={{0,5},{1,4},{2,7},{3,6},{12,9},{13,8},{14,11},{15,10},{16,21},{17,... | collective-permute-start | bytes 1966088 | tf_op jit(solution)/shard_map/ppermute | solution.py:506
  159.0 8.1 %collective-permute-start.34 = (bf16[2,640,256]{2,1,0:T(8,128)(2,1)}, bf16[2,640,256]{2,1,0:T(8,128)(2,1)S(1)}, u32[]{:S(2)}, u32[]{:S(2)}) collective-permute-start(bf16[2,640,256]{2,1,0:T(8,128)(2,1)} %get-tuple-element.150), channel_id=1, source_target_pairs={{0,6},{1,7},{2,4},{3,5},{12,10},{13,11},{14,8},{15,9},{16,22},{17,... | collective-permute-start | bytes 1966088 | tf_op jit(solution)/shard_map/ppermute | solution.py:506
  189.5 26.2 %collective-permute-done.32.refs_8_ = bf16[2,640,256]{2,1,0:T(8,128)(2,1)} collective-permute-done((bf16[2,640,256]{2,1,0:T(8,128)(2,1)S(1)}, bf16[2,640,256]{2,1,0:T(8,128)(2,1)}, u32[]{:S(2)}, u32[]{:S(2)}) %collective-permute-start.32) | collective-permute-done | bytes 655392 | tf_op jit(solution)/shard_map/ppermute | solution.py:506
  231.2 15.0 %collective-permute-done.25.refs_5_ = bf16[640,128]{1,0:T(8,128)(2,1)} collective-permute-done((bf16[640,128]{1,0:T(8,128)(2,1)}, bf16[640,128]{1,0:T(8,128)(2,1)}, u32[]{:S(2)}, u32[]{:S(2)}) %collective-permute-start.25) | collective-permute-done | bytes 163872 | tf_op jit(solution)/shard_map/ppermute | solution.py:506
  267.7 51.5 %collective-permute-start.55 = (bf16[2,640,128]{2,1,0:T(8,128)(2,1)}, bf16[2,640,128]{2,1,0:T(8,128)(2,1)}, u32[]{:S(2)}, u32[]{:S(2)}) collective-permute-start(bf16[2,640,128]{2,1,0:T(8,128)(2,1)} %get-tuple-element.173.refs_4_), channel_id=1, source_target_pairs={{0,4},{1,5},{2,6},{3,7},{12,8},{13,9},{14,10},{15,11},{16,20},{17,... | collective-permute-start | bytes 983048 | tf_op jit(solution)/shard_map/ppermute | solution.py:506
  321.4 8.1 %collective-permute-start.57 = (bf16[2,640,128]{2,1,0:T(8,128)(2,1)}, bf16[2,640,128]{2,1,0:T(8,128)(2,1)}, u32[]{:S(2)}, u32[]{:S(2)}) collective-permute-start(bf16[2,640,128]{2,1,0:T(8,128)(2,1)} %get-tuple-element.175), channel_id=1, source_target_pairs={{0,6},{1,7},{2,4},{3,5},{12,10},{13,11},{14,8},{15,9},{16,22},{17,... | collective-permute-start | bytes 983048 | tf_op jit(solution)/shard_map/ppermute | solution.py:506
  354.9 6.1 %merge.15 = (bf16[640,256]{1,0:T(8,128)(2,1)}, bf16[640,256]{1,0:T(8,128)(2,1)}, bf16[640,256]{1,0:T(8,128)(2,1)}, bf16[640,256]{1,0:T(8,128)(2,1)}, bf16[640,25...) custom-call(s32[4]{0:T(128)} %pad_add_fusion.refs_0_, ...), custom_call_target="tpu_custom_call" | custom-call | flops 5242880 | bytes 10485760 | tf_op jit(solution)/shard_map/merge/pallas_call | solution.py:33
  391.8 7.4 %collective-permute-done.50.refs_7_ = bf16[640,256]{1,0:T(8,128)(2,1)} collective-permute-done((bf16[640,256]{1,0:T(8,128)(2,1)}, bf16[640,256]{1,0:T(8,128)(2,1)}, u32[]{:S(2)}, u32[]{:S(2)}) %collective-permute-start.50) | collective-permute-done | bytes 327712 | tf_op jit(solution)/shard_map/ppermute | solution.py:506
  399.1 6.4 %collective-permute-done.51.refs_8_ = bf16[640,256]{1,0:T(8,128)(2,1)} collective-permute-done((bf16[640,256]{1,0:T(8,128)(2,1)}, bf16[640,256]{1,0:T(8,128)(2,1)}, u32[]{:S(2)}, u32[]{:S(2)}) %collective-permute-start.51) | collective-permute-done | bytes 327712 | tf_op jit(solution)/shard_map/ppermute | solution.py:506
  416.3 8.2 %collective-permute-start.42 = (bf16[2,640,128]{2,1,0:T(8,128)(2,1)}, bf16[2,640,128]{2,1,0:T(8,128)(2,1)}, u32[]{:S(2)}, u32[]{:S(2)}) collective-permute-start(bf16[2,640,128]{2,1,0:T(8,128)(2,1)} %get-tuple-element.161), channel_id=1, source_target_pairs={{0,6},{1,7},{2,4},{3,5},{12,10},{13,11},{14,8},{15,9},{16,22},{17,... | collective-permute-start | bytes 983048 | tf_op jit(solution)/shard_map/ppermute | solution.py:506
  429.2 6.5 %collective-permute-done.42.refs_10_ = bf16[2,640,128]{2,1,0:T(8,128)(2,1)} collective-permute-done((bf16[2,640,128]{2,1,0:T(8,128)(2,1)}, bf16[2,640,128]{2,1,0:T(8,128)(2,1)}, u32[]{:S(2)}, u32[]{:S(2)}) %collective-permute-start.42) | collective-permute-done | bytes 327712 | tf_op jit(solution)/shard_map/ppermute | solution.py:506
  435.7 7.0 %collective-permute-done.43.refs_11_ = bf16[2,640,128]{2,1,0:T(8,128)(2,1)S(1)} collective-permute-done((bf16[2,640,128]{2,1,0:T(8,128)(2,1)}, bf16[2,640,128]{2,1,0:T(8,128)(2,1)S(1)}, u32[]{:S(2)}, u32[]{:S(2)}) %collective-permute-start.43) | collective-permute-done | bytes 327712 | tf_op jit(solution)/shard_map/ppermute | solution.py:506
  467.3 6.9 %run_chunk.7 = (bf16[1,2560,768]{2,1,0:T(8,128)(2,1)}, bf16[1,2560,768]{2,1,0:T(8,128)(2,1)}, bf16[16,48,256]{2,1,0:T(8,128)(2,1)}, f32[8,128]{1,0:T(8,128)}) custom-call(s32[4]{0:T(128)} %pad_add_fusion.refs_0_, bf16[768,2560]{1,0:T(8,128)(2,1)} %get-tuple-element.138.refs_1_, ...), custom_call_target="tpu_custom_call", output_to_operand_aliasing={{0}: (4, {}), {1}: (5, {})} | custom-call | flops 2013265920 | bytes 9175040 | tf_op jit(solution)/shard_map/run_chunk/pallas_call | solution.py:33
  474.3 7.9 %collective-permute-done.71.refs_5_ = bf16[640,128]{1,0:T(8,128)(2,1)S(1)} collective-permute-done((bf16[640,128]{1,0:T(8,128)(2,1)}, bf16[640,128]{1,0:T(8,128)(2,1)S(1)}, u32[]{:S(2)}, u32[]{:S(2)}) %collective-permute-start.71) | collective-permute-done | bytes 163872 | tf_op jit(solution)/shard_map/ppermute | solution.py:506
  532.0 15.5 %collective-permute-done.85.refs_3_ = bf16[4,640,128]{2,1,0:T(8,128)(2,1)S(1)} collective-permute-done((bf16[4,640,128]{2,1,0:T(8,128)(2,1)}, bf16[4,640,128]{2,1,0:T(8,128)(2,1)S(1)}, u32[]{:S(2)}, u32[]{:S(2)}) %collective-permute-start.85) | collective-permute-done | bytes 655392 | tf_op jit(solution)/shard_map/ppermute | solution.py:586
  558.5 7.9 %all-to-all-done.1 = bf16[16,48,128]{2,1,0:T(8,128)(2,1)S(1)} async-done(((bf16[16,48,128]{2,1,0:T(8,128)(2,1)}), bf16[16,48,128]{2,1,0:T(8,128)(2,1)S(1)}, u32[]{:S(2)}, u32[]{:S(2)}) %all-to-all-start.1) | async-done | bytes 196640 | tf_op jit(solution)/shard_map/all_to_all | solution.py:596
  576.4 15.5 %all-to-all-done = bf16[16,48,640]{2,1,0:T(8,128)(2,1)S(1)} async-done(((bf16[16,48,640]{2,1,0:T(8,128)(2,1)}), bf16[16,48,640]{2,1,0:T(8,128)(2,1)S(1)}, u32[]{:S(2)}, u32[]{:S(2)}) %all-to-all-start) | async-done | bytes 983072 | tf_op jit(solution)/shard_map/all_to_all | solution.py:596
  (379 shorter events, 298.1 us)
Async XLA Ops:
  15.0 32.9 %collective-permute-start.2 = (bf16[2,64,2560]{2,1,0:T(8,128)(2,1)S(1)}, bf16[2,64,2560]{2,1,0:T(8,128)(2,1)S(1)}, u32[]{:S(2)}, u32[]{:S(2)}) collective-permute-start(bf16[2,64,2560]{2,1,0:T(8,128)(2,1)S(1)} %collective-permute-done.1.refs_3_), channel_id=1, source_target_pairs={{4,0},{5,1},{6,2},{7,3},{8,12},{9,13},{10,14},{11,15},{20,16},{21,... | collective-permute-start | bytes 1966088 | tf_op jit(solution)/shard_map/ppermute | solution.py:506
  51.4 70.9 %collective-permute-start.4 = (bf16[4,64,2560]{2,1,0:T(8,128)(2,1)}, bf16[4,64,2560]{2,1,0:T(8,128)(2,1)}, u32[]{:S(2)}, u32[]{:S(2)}) collective-permute-start(bf16[4,64,2560]{2,1,0:T(8,128)(2,1)} %get-tuple-element.124.refs_1_), channel_id=1, source_target_pairs={{0,2},{1,3},{2,0},{3,1},{4,6},{5,7},{6,4},{7,5},{8,10},{9,11},{10,... | collective-permute-start | bytes 3932168 | tf_op jit(solution)/shard_map/ppermute | solution.py:506
  69.4 29.0 %collective-permute-start.8 = (bf16[2,640,128]{2,1,0:T(8,128)(2,1)}, bf16[2,640,128]{2,1,0:T(8,128)(2,1)S(1)}, u32[]{:S(2)}, u32[]{:S(2)}) collective-permute-start(bf16[2,640,128]{2,1,0:T(8,128)(2,1)} %get-tuple-element.128), channel_id=1, source_target_pairs={{4,7},{5,6},{6,5},{7,4},{8,11},{9,10},{10,9},{11,8},{20,23},{21,22... | collective-permute-start | bytes 983048 | tf_op jit(solution)/shard_map/ppermute | solution.py:506
  80.8 47.8 %collective-permute-start.18 = (bf16[2,640,128]{2,1,0:T(8,128)(2,1)}, bf16[2,640,128]{2,1,0:T(8,128)(2,1)S(1)}, u32[]{:S(2)}, u32[]{:S(2)}) collective-permute-start(bf16[2,640,128]{2,1,0:T(8,128)(2,1)} %get-tuple-element.132), channel_id=1, source_target_pairs={{0,5},{1,4},{2,7},{3,6},{12,9},{13,8},{14,11},{15,10},{16,21},{17,... | collective-permute-start | bytes 983048 | tf_op jit(solution)/shard_map/ppermute | solution.py:506
  120.6 46.5 %collective-permute-start.13 = (bf16[8,640,128]{2,1,0:T(8,128)(2,1)}, bf16[8,640,128]{2,1,0:T(8,128)(2,1)}, u32[]{:S(2)}, u32[]{:S(2)}) collective-permute-start(bf16[8,640,128]{2,1,0:T(8,128)(2,1)} %get-tuple-element.130), channel_id=1, source_target_pairs={{4,8},{5,9},{6,10},{7,11},{8,4},{9,5},{10,6},{11,7},{20,24},{21,25... | collective-permute-start | bytes 3932168 | tf_op jit(solution)/shard_map/ppermute | solution.py:506
  122.3 46.3 %collective-permute-start.3 = (bf16[4,64,2560]{2,1,0:T(8,128)(2,1)}, bf16[4,64,2560]{2,1,0:T(8,128)(2,1)}, u32[]{:S(2)}, u32[]{:S(2)}) collective-permute-start(bf16[4,64,2560]{2,1,0:T(8,128)(2,1)} %get-tuple-element.124.refs_1_), channel_id=1, source_target_pairs={{0,1},{1,0},{2,3},{3,2},{4,5},{5,4},{6,7},{7,6},{8,9},{9,8},{10,11... | collective-permute-start | bytes 3932168 | tf_op jit(solution)/shard_map/ppermute | solution.py:506
  122.3 49.4 %collective-permute-start.5 = (bf16[4,64,2560]{2,1,0:T(8,128)(2,1)}, bf16[4,64,2560]{2,1,0:T(8,128)(2,1)}, u32[]{:S(2)}, u32[]{:S(2)}) collective-permute-start(bf16[4,64,2560]{2,1,0:T(8,128)(2,1)} %collective-permute-done.4.refs_3_), channel_id=1, source_target_pairs={{0,1},{1,0},{2,3},{3,2},{4,5},{5,4},{6,7},{7,6},{8,9},{9,8},{10,11... | collective-permute-start | bytes 3932168 | tf_op jit(solution)/shard_map/ppermute | solution.py:506
  152.8 63.0 %collective-permute-start.33 = (bf16[2,640,256]{2,1,0:T(8,128)(2,1)}, bf16[2,640,256]{2,1,0:T(8,128)(2,1)S(1)}, u32[]{:S(2)}, u32[]{:S(2)}) collective-permute-start(bf16[2,640,256]{2,1,0:T(8,128)(2,1)} %get-tuple-element.149), channel_id=1, source_target_pairs={{0,5},{1,4},{2,7},{3,6},{12,9},{13,8},{14,11},{15,10},{16,21},{17,... | collective-permute-start | bytes 1966088 | tf_op jit(solution)/shard_map/ppermute | solution.py:506
  159.0 56.8 %collective-permute-start.34 = (bf16[2,640,256]{2,1,0:T(8,128)(2,1)}, bf16[2,640,256]{2,1,0:T(8,128)(2,1)S(1)}, u32[]{:S(2)}, u32[]{:S(2)}) collective-permute-start(bf16[2,640,256]{2,1,0:T(8,128)(2,1)} %get-tuple-element.150), channel_id=1, source_target_pairs={{0,6},{1,7},{2,4},{3,5},{12,10},{13,11},{14,8},{15,9},{16,22},{17,... | collective-permute-start | bytes 1966088 | tf_op jit(solution)/shard_map/ppermute | solution.py:506
  168.6 47.2 %collective-permute-start.35 = (bf16[2,640,256]{2,1,0:T(8,128)(2,1)}, bf16[2,640,256]{2,1,0:T(8,128)(2,1)}, u32[]{:S(2)}, u32[]{:S(2)}) collective-permute-start(bf16[2,640,256]{2,1,0:T(8,128)(2,1)} %get-tuple-element.151), channel_id=1, source_target_pairs={{0,7},{1,6},{2,5},{3,4},{12,11},{13,10},{14,9},{15,8},{16,23},{17,... | collective-permute-start | bytes 1966088 | tf_op jit(solution)/shard_map/ppermute | solution.py:506
  171.8 44.0 %collective-permute-start.32 = (bf16[2,640,256]{2,1,0:T(8,128)(2,1)S(1)}, bf16[2,640,256]{2,1,0:T(8,128)(2,1)}, u32[]{:S(2)}, u32[]{:S(2)}) collective-permute-start(bf16[2,640,256]{2,1,0:T(8,128)(2,1)S(1)} %copy-done.1), channel_id=1, source_target_pairs={{0,4},{1,5},{2,6},{3,7},{12,8},{13,9},{14,10},{15,11},{16,20},{17,... | collective-permute-start | bytes 1966088 | tf_op jit(solution)/shard_map/ppermute | solution.py:506
  222.3 131.0 %collective-permute-start.44 = (bf16[8,640,256]{2,1,0:T(8,128)(2,1)}, bf16[8,640,256]{2,1,0:T(8,128)(2,1)S(1)}, u32[]{:S(2)}, u32[]{:S(2)}) collective-permute-start(bf16[8,640,256]{2,1,0:T(8,128)(2,1)} %get-tuple-element.163), channel_id=1, source_target_pairs={{4,8},{5,9},{6,10},{7,11},{8,4},{9,5},{10,6},{11,7},{20,24},{21,25... | collective-permute-start | bytes 7864328 | tf_op jit(solution)/shard_map/ppermute | solution.py:506
  223.2 43.2 %collective-permute-start.21 = (bf16[8,640,128]{2,1,0:T(8,128)(2,1)}, bf16[8,640,128]{2,1,0:T(8,128)(2,1)S(1)}, u32[]{:S(2)}, u32[]{:S(2)}) collective-permute-start(bf16[8,640,128]{2,1,0:T(8,128)(2,1)} %get-tuple-element.139), channel_id=1, source_target_pairs={{4,8},{5,9},{6,10},{7,11},{8,4},{9,5},{10,6},{11,7},{20,24},{21,25... | collective-permute-start | bytes 3932168 | tf_op jit(solution)/shard_map/ppermute | solution.py:506
  259.2 70.3 %collective-permute-start.36 = (bf16[4,640,128]{2,1,0:T(8,128)(2,1)}, bf16[4,640,128]{2,1,0:T(8,128)(2,1)}, u32[]{:S(2)}, u32[]{:S(2)}) collective-permute-start(bf16[4,640,128]{2,1,0:T(8,128)(2,1)} %get-tuple-element.154.refs_2_), channel_id=1, source_target_pairs={{0,16},{16,0},{1,17},{17,1},{2,18},{18,2},{3,19},{19,3},{4,20},{20... | collective-permute-start | bytes 1966088 | tf_op jit(solution)/shard_map/ppermute | solution.py:586
  264.9 54.3 %collective-permute-start.53 = (bf16[2,640,128]{2,1,0:T(8,128)(2,1)}, bf16[2,640,128]{2,1,0:T(8,128)(2,1)}, u32[]{:S(2)}, u32[]{:S(2)}) collective-permute-start(bf16[2,640,128]{2,1,0:T(8,128)(2,1)} %get-tuple-element.175), channel_id=1, source_target_pairs={{4,6},{5,7},{6,4},{7,5},{8,10},{9,11},{10,8},{11,9},{20,22},{21,23... | collective-permute-start | bytes 983048 | tf_op jit(solution)/shard_map/ppermute | solution.py:506
  266.3 55.0 %collective-permute-start.54 = (bf16[2,640,128]{2,1,0:T(8,128)(2,1)}, bf16[2,640,128]{2,1,0:T(8,128)(2,1)}, u32[]{:S(2)}, u32[]{:S(2)}) collective-permute-start(bf16[2,640,128]{2,1,0:T(8,128)(2,1)} %get-tuple-element.176), channel_id=1, source_target_pairs={{4,7},{5,6},{6,5},{7,4},{8,11},{9,10},{10,9},{11,8},{20,23},{21,22... | collective-permute-start | bytes 983048 | tf_op jit(solution)/shard_map/ppermute | solution.py:506
  267.7 74.0 %collective-permute-start.55 = (bf16[2,640,128]{2,1,0:T(8,128)(2,1)}, bf16[2,640,128]{2,1,0:T(8,128)(2,1)}, u32[]{:S(2)}, u32[]{:S(2)}) collective-permute-start(bf16[2,640,128]{2,1,0:T(8,128)(2,1)} %get-tuple-element.173.refs_4_), channel_id=1, source_target_pairs={{0,4},{1,5},{2,6},{3,7},{12,8},{13,9},{14,10},{15,11},{16,20},{17,... | collective-permute-start | bytes 983048 | tf_op jit(solution)/shard_map/ppermute | solution.py:506
  372.0 27.1 %collective-permute-start.50 = (bf16[640,256]{1,0:T(8,128)(2,1)}, bf16[640,256]{1,0:T(8,128)(2,1)}, u32[]{:S(2)}, u32[]{:S(2)}) collective-permute-start(bf16[640,256]{1,0:T(8,128)(2,1)} %get-tuple-element.171), channel_id=1, source_target_pairs={{4,2},{5,3},{6,0},{7,1},{8,14},{9,15},{10,12},{11,13},{20,18},{21,... | collective-permute-start | bytes 983048 | tf_op jit(solution)/shard_map/ppermute | solution.py:506
  373.3 32.2 %collective-permute-start.51 = (bf16[640,256]{1,0:T(8,128)(2,1)}, bf16[640,256]{1,0:T(8,128)(2,1)}, u32[]{:S(2)}, u32[]{:S(2)}) collective-permute-start(bf16[640,256]{1,0:T(8,128)(2,1)} %get-tuple-element.172), channel_id=1, source_target_pairs={{4,3},{5,2},{6,1},{7,0},{8,15},{9,14},{10,13},{11,12},{20,19},{21,... | collective-permute-start | bytes 983048 | tf_op jit(solution)/shard_map/ppermute | solution.py:506
  374.7 36.2 %collective-permute-start.37 = (bf16[2,640,128]{2,1,0:T(8,128)(2,1)}, bf16[2,640,128]{2,1,0:T(8,128)(2,1)S(1)}, u32[]{:S(2)}, u32[]{:S(2)}) collective-permute-start(bf16[2,640,128]{2,1,0:T(8,128)(2,1)} %get-tuple-element.160), channel_id=1, source_target_pairs={{4,5},{5,4},{6,7},{7,6},{8,9},{9,8},{10,11},{11,10},{20,21},{21,20... | collective-permute-start | bytes 983048 | tf_op jit(solution)/shard_map/ppermute | solution.py:506
  384.7 63.9 %collective-permute-start.67 = (bf16[8,640,128]{2,1,0:T(8,128)(2,1)}, bf16[8,640,128]{2,1,0:T(8,128)(2,1)S(1)}, u32[]{:S(2)}, u32[]{:S(2)}) collective-permute-start(bf16[8,640,128]{2,1,0:T(8,128)(2,1)} %get-tuple-element.190), channel_id=1, source_target_pairs={{4,8},{5,9},{6,10},{7,11},{8,4},{9,5},{10,6},{11,7},{20,24},{21,25... | collective-permute-start | bytes 3932168 | tf_op jit(solution)/shard_map/ppermute | solution.py:506
  408.6 57.4 %collective-permute-start.75 = (bf16[4,640,256]{2,1,0:T(8,128)(2,1)}, bf16[4,640,256]{2,1,0:T(8,128)(2,1)S(1)}, u32[]{:S(2)}, u32[]{:S(2)}) collective-permute-start(bf16[4,640,256]{2,1,0:T(8,128)(2,1)} %get-tuple-element.200.refs_2_), channel_id=1, source_target_pairs={{0,16},{16,0},{1,17},{17,1},{2,18},{18,2},{3,19},{19,3},{4,20},{20... | collective-permute-start | bytes 3932168 | tf_op jit(solution)/shard_map/ppermute | solution.py:586
  428.7 27.0 %collective-permute-start.76 = (bf16[4,640,128]{2,1,0:T(8,128)(2,1)}, bf16[4,640,128]{2,1,0:T(8,128)(2,1)}, u32[]{:S(2)}, u32[]{:S(2)}) collective-permute-start(bf16[4,640,128]{2,1,0:T(8,128)(2,1)} %get-tuple-element.201.refs_2_), channel_id=1, source_target_pairs={{0,16},{16,0},{1,17},{17,1},{2,18},{18,2},{3,19},{19,3},{4,20},{20... | collective-permute-start | bytes 1966088 | tf_op jit(solution)/shard_map/ppermute | solution.py:586
  447.8 48.5 %collective-permute-start.66 = (bf16[8,640,128]{2,1,0:T(8,128)(2,1)}, bf16[8,640,128]{2,1,0:T(8,128)(2,1)S(1)}, u32[]{:S(2)}, u32[]{:S(2)}) collective-permute-start(bf16[8,640,128]{2,1,0:T(8,128)(2,1)} %get-tuple-element.189), channel_id=1, source_target_pairs={{4,8},{5,9},{6,10},{7,11},{8,4},{9,5},{10,6},{11,7},{20,24},{21,25... | collective-permute-start | bytes 3932168 | tf_op jit(solution)/shard_map/ppermute | solution.py:506
  (144 other events, 2485.7 us)

commit v5 on v4

--- a/solution.py
+++ b/solution.py
@@ -47,25 +47,24 @@
     rows = depth // plane
 
     def kernel(info_ref, gate_ref, up_ref, *rest):
-        outs, held, in_sems, out_sems = rest[:plane], *rest[plane:]
-        place = info_ref[0]
+        out, held, in_sems, out_sems = rest
 
         def move(source):
             loads = [
                 pltpu.make_async_copy(
                     source.at[
                         :,
-                        pl.ds(pl.multiple_of((place ^ shift) * rows, 16), rows),
+                        pl.ds(part * rows, rows),
                         pl.ds(start, width),
                     ],
-                    held.at[shift],
-                    in_sems.at[shift],
+                    held.at[part],
+                    in_sems.at[part],
                 )
-                for shift in range(plane)
+                for part in range(plane)
             ]
             stores = [
-                pltpu.make_async_copy(held.at[shift], outs[shift], out_sems.at[shift])
-                for shift in range(plane)
+                pltpu.make_async_copy(held.at[part], out.at[part], out_sems.at[part])
+                for part in range(plane)
             ]
             for load in loads:
                 load.start()
@@ -88,8 +87,8 @@
         token,
         (info, gate, up),
         [SMEM, ANY, ANY],
-        [jax.ShapeDtypeStruct((sources, rows, width), gate.dtype)] * plane,
-        [ANY] * plane,
+        [jax.ShapeDtypeStruct((plane, sources, rows, width), gate.dtype)],
+        [ANY],
         (0, 4 * sources * depth * width),
         scratch_shapes=[
             pltpu.VMEM((plane, sources, rows, width), gate.dtype),
@@ -100,15 +99,32 @@
     )
 
 
+def hold(token, value, earlier):
+    def kernel(*refs):
+        pass
+
+    (value,), token = step_call(
+        kernel,
+        token,
+        (value, *earlier),
+        [ANY] * (1 + len(earlier)),
+        [jax.ShapeDtypeStruct(value.shape, value.dtype)],
+        [ANY],
+        (0, 0),
+        input_output_aliases={0: 0},
+        name="hold",
+    )
+    return value, token
+
+
 def merge(token, info, ids, weights, scales, near, far, received, start, scale_blocks):
-    plane = len(near)
-    sources, rows, width = near[0].shape
+    plane, sources, rows, width = near.shape
     step = math.gcd(rows, BLOCK)
     row_blocks, column_blocks = scale_blocks
     first = start // BLOCK
 
-    def kernel(info_ref, ids_ref, weights_ref, scales_ref, *rest):
-        blocks, rest, total = rest[: 2 * plane], rest[2 * plane : -1], rest[-1]
+    def kernel(info_ref, ids_ref, weights_ref, scales_ref, near_ref, far_ref, *rest):
+        total = rest[-1]
         place, inner = info_ref[0], info_ref[1]
         outer = jnp.where(inner == 1, 0, PLANES - 1)
         to_inner = inner if received is not None else PLANES - 1 - inner
@@ -121,94 +137,83 @@
                 total[...] = jnp.zeros_like(total)
             else:
                 total[...] = rest[0][...].astype(jnp.float32)
-            for index, block in enumerate(blocks):
-                held = inner if index < plane else outer
-                for number in range(sources):
-                    source = (held * plane + (place ^ (index % plane))) * sources + number
-                    target = ids_ref[source]
-                    target_plane = target // plane
-                    slot = (target % plane) ^ place
-
-                    @pl.when((target_plane == to_inner) | (target_plane == to_outer))
-                    def _():
-                        into = jnp.where(target_plane == to_outer, plane, 0) + slot
-                        base = (source * row_blocks + row_block) * column_blocks + first
-                        for part in range(width // BLOCK):
-                            lanes = pl.ds(part * BLOCK, BLOCK)
-                            factor = weights_ref[source] * scales_ref[base + part]
-                            total[into, :, lanes] += (
-                                block[number, :, lanes].astype(jnp.float32) * factor
-                            )
+            for block, held in ((near_ref, inner), (far_ref, outer)):
+                for piece in range(plane):
+                    for number in range(sources):
+                        source = (held * plane + piece) * sources + number
+                        target = ids_ref[source]
+                        target_plane = target // plane
+                        slot = target % plane
+
+                        @pl.when((target_plane == to_inner) | (target_plane == to_outer))
+                        def _():
+                            index = jnp.where(target_plane == to_outer, plane, 0) + slot
+                            base = (source * row_blocks + row_block) * column_blocks + first
+                            for part in range(width // BLOCK):
+                                lanes = pl.ds(part * BLOCK, BLOCK)
+                                factor = weights_ref[source] * scales_ref[base + part]
+                                total[index, :, lanes] += (
+                                    block[piece, number, :, lanes].astype(jnp.float32) * factor
+                                )
 
             if received is None:
                 rest[0][...] = total[...].astype(jnp.bfloat16)
             else:
-                for index in range(2 * plane):
-                    rest[1 + index][...] = total[index].astype(jnp.bfloat16)
-
-    pieces = pl.BlockSpec((sources, step, width), lambda i: (0, i, 0))
+                rest[1][...] = total[:plane].astype(jnp.bfloat16)
+                rest[2][...] = total[plane:].astype(jnp.bfloat16)
+
+    pieces = pl.BlockSpec((plane, sources, step, width), lambda i: (0, 0, i, 0))
     both = pl.BlockSpec((2 * plane, step, width), lambda i: (0, i, 0))
-    one = pl.BlockSpec((step, width), lambda i: (i, 0))
+    one = pl.BlockSpec((plane, step, width), lambda i: (0, i, 0))
     if received is None:
         extra, extra_specs = (), []
         out_shape = [jax.ShapeDtypeStruct((2 * plane, rows, width), jnp.bfloat16)]
         out_specs = [both]
     else:
         extra, extra_specs = (received,), [both]
-        out_shape = [jax.ShapeDtypeStruct((rows, width), jnp.bfloat16)] * (2 * plane)
-        out_specs = [one] * (2 * plane)
-    size = plane * near[0].size
+        out_shape = [jax.ShapeDtypeStruct((plane, rows, width), jnp.bfloat16)] * 2
+        out_specs = [one, one]
     return step_call(
         kernel,
         token,
-        (info, ids, weights, scales, *near, *far, *extra),
-        [SMEM] * 4 + [pieces] * (2 * plane) + extra_specs,
+        (info, ids, weights, scales, near, far, *extra),
+        [SMEM] * 4 + [pieces, pieces] + extra_specs,
         out_shape,
         out_specs,
-        (4 * size, 8 * size),
+        (4 * near.size, 8 * near.size),
         grid=(rows // step,),
         scratch_shapes=[pltpu.VMEM((2 * plane, step, width), jnp.float32)],
         name="merge",
     )
 
 
-def join(token, info, inside, outside):
-    plane = len(inside)
-    rows, width = inside[0].shape
-
-    def kernel(info_ref, *rest):
-        out, sems = rest[2 * plane :]
-
-        def move(sources):
-            copies = [
-                pltpu.make_async_copy(sources[shift], out.at[shift], sems.at[shift])
-                for shift in range(plane)
-            ]
-            for copy in copies:
-                copy.start()
-            for copy in copies:
-                copy.wait()
+def choose(token, info, inside, outside):
+    def kernel(info_ref, inside_ref, outside_ref, out_ref, sem):
+        def move(source):
+            copy = pltpu.make_async_copy(source, out_ref, sem)
+            copy.start()
+            copy.wait()
 
         @pl.when(info_ref[3] == 1)
         def _():
-            move(rest[:plane])
+            move(inside_ref)
 
         @pl.when(info_ref[3] != 1)
         def _():
-            move(rest[plane : 2 * plane])
-
-    (own,), token = step_call(
-        kernel,
-        token,
-        (info, *inside, *outside),
-        [SMEM] + [ANY] * (2 * plane),
-        [jax.ShapeDtypeStruct((plane, rows, width), inside[0].dtype)],
+            move(outside_ref)
+
+    (rows,), token = step_call(
+        kernel,
+        token,
+        (info, inside, outside),
+        [SMEM, ANY, ANY],
+        [jax.ShapeDtypeStruct(inside.shape, inside.dtype)],
         [VMEM],
-        (0, 4 * plane * rows * width),
-        scratch_shapes=[pltpu.SemaphoreType.DMA((plane,))],
-        name="join",
-    )
-    return own, token
+        (0, 4 * inside.size),
+        scratch_shapes=[pltpu.SemaphoreType.DMA],
+        name="choose",
+    )
+    return rows, token
 
 
 def pair(token, tokens, other):
@@ -261,104 +266,49 @@
     return whole, token
 
 
-def dispatch(token, placing, lines):
-    count, capacity, tok_dev = placing.shape
-    width = lines[0].shape[2]
-
-    def kernel(placing_ref, *rest):
-        out_ref = rest[len(lines)]
-        for block in range(count):
-            rows = rest[block // PLANES][block % PLANES]
-            out_ref[block * capacity : (block + 1) * capacity] = jnp.dot(
-                placing_ref[block], rows, preferred_element_type=jnp.float32
-            ).astype(jnp.bfloat16)
-
-    (grouped,), token = step_call(
-        kernel,
-        token,
-        (placing, *lines),
-        [VMEM] * (1 + len(lines)),
-        [jax.ShapeDtypeStruct((count * capacity, width), jnp.bfloat16)],
-        [VMEM],
-        (2 * count * capacity * tok_dev * width, 4 * count * tok_dev * width),
-        name="dispatch",
-    )
-    return grouped, token
-
-
-def run_chunk(token, info, grouped, own, partner, outputs, start, shape, devices):
-    plane, rows, width = own.shape
-    depth, full = shape
+def run_chunk(token, info, grouped, own, partner, outputs, start, full, blocks):
+    depth, width = own.shape
     count = grouped.shape[0]
-    each = count // devices
+    each = count // len(blocks)
     factor = 1.0 / math.sqrt(D)
 
     def kernel(info_ref, grouped_ref, own_ref, partner_ref, *rest):
-        gate_out, up_out, hidden_ref, whole, sems, out_sems = rest[len(outputs) :]
-        place = info_ref[0]
-
-        def load(pieces, column, base):
-            return [
-                pltpu.make_async_copy(
-                    pieces.at[shift],
-                    whole.at[
-                        pl.ds(pl.multiple_of((place ^ shift) * rows, 16), rows),
-                        pl.ds(column, width),
-                    ],
-                    sems.at[base + shift],
-                )
-                for shift in range(plane)
+        gate_out, up_out, hidden_ref, sems = rest[len(outputs) :]
+
+        def work(gate_ref, up_ref):
+            stores = [
+                pltpu.make_async_copy(source, out.at[0, :, pl.ds(start, width)], sems.at[index])
+                for index, (source, out) in enumerate(((gate_ref, gate_out), (up_ref, up_out)))
             ]
-
-        def fill(gate, up):
-            copies = load(gate, 0, 0) + load(up, width, plane)
-            for copy in copies:
-                copy.start()
-            for copy in copies:
-                copy.wait()
+            for store in stores:
+                store.start()
+            rows = grouped_ref[...]
+            gate_value = jnp.dot(rows, gate_ref[...], preferred_element_type=jnp.float32) * factor
+            up_value = jnp.dot(rows, up_ref[...], preferred_element_type=jnp.float32) * factor
+            hidden = (gate_value / (1.0 + jnp.exp(-gate_value)) * up_value).astype(jnp.bfloat16)
+            for index, block in enumerate(blocks):
+                hidden_ref[block] = hidden[index * each : (index + 1) * each]
+            for store in stores:
+                store.wait()
 
         @pl.when(info_ref[2] == 0)
         def _():
-            fill(own_ref, partner_ref)
+            work(own_ref, partner_ref)
 
         @pl.when(info_ref[2] != 0)
         def _():
-            fill(partner_ref, own_ref)
-
-        stores = [
-            pltpu.make_async_copy(
-                whole.at[:, pl.ds(index * width, width)],
-                out.at[0, :, pl.ds(start, width)],
-                out_sems.at[index],
-            )
-            for index, out in enumerate((gate_out, up_out))
-        ]
-        for store in stores:
-            store.start()
-        values = jnp.dot(grouped_ref[...], whole[...], preferred_element_type=jnp.float32)
-        gate_value = values[:, :width] * factor
-        up_value = values[:, width:] * factor
-        hidden = (gate_value / (1.0 + jnp.exp(-gate_value)) * up_value).astype(jnp.bfloat16)
-        for index in range(devices):
-            device = (index % PLANES) * plane + (place ^ (index // PLANES))
-            hidden_ref[device] = hidden[index * each : (index + 1) * each]
-        for store in stores:
-            store.wait()
+            work(partner_ref, own_ref)
 
     weights = jax.ShapeDtypeStruct((1, depth, full), jnp.bfloat16)
     return step_call(
         kernel,
         token,
         (info, grouped, own, partner, *outputs),
-        [SMEM, VMEM, ANY, ANY] + [ANY] * len(outputs),
-        [weights, weights, jax.ShapeDtypeStruct((devices, each, width), jnp.bfloat16)],
+        [SMEM, VMEM, VMEM, VMEM] + [ANY] * len(outputs),
+        [weights, weights, jax.ShapeDtypeStruct((len(blocks), each, width), jnp.bfloat16)],
         [ANY, ANY, VMEM],
         (4 * count * depth * width, 2 * (grouped.size + 4 * depth * width)),
-        scratch_shapes=[
-            pltpu.VMEM((depth, 2 * width), jnp.bfloat16),
-            pltpu.SemaphoreType.DMA((2 * plane,)),
-            pltpu.SemaphoreType.DMA((2,)),
-        ],
+        scratch_shapes=[pltpu.SemaphoreType.DMA((2,))],
         input_output_aliases={4 + index: index for index in range(len(outputs))},
         name="run_chunk",
     )
@@ -366,15 +316,16 @@
 
 STEPS = {
     "pair": (("t1",), (3.0, 0.0), (("t2", 13.0, "middle"),)),
-    "line": (("t3",), (4.0, 0.0), (("t4", 40.0, "y"),)),
-    "dispatch": (("t4",), (6.0, 0.0), ()),
-    "pack": (("pack before",), (8.0, 0.6), (("a", 25.0, "in"), ("b", 13.0, "y"))),
-    "partial": (("a", "b"), (5.0, 1.5), (("m", 25.0, "middle"),)),
-    "finish": (("m",), (8.0, 2.0), (("d", 13.0, "out"), ("e", 13.0, "y"))),
-    "join": (("d", "e"), (2.5, 0.5), (("x", 12.0, "x"),)),
-    "run": (("x", "dispatch", "run before"), (2.0, 1.5), ()),
+    "line": (("t3",), (4.0, 0.0), ()),
+    "pack": (("pack before",), (7.0, 0.6), (("b", 13.0, "y"),)),
+    "send": (("b", "send before"), (2.0, 0.0), (("a", 25.0, "in"),)),
+    "partial": (("a",), (5.0, 1.5), (("m", 25.0, "middle"),)),
+    "finish": (("m",), (5.0, 2.0), (("d", 13.0, "out"),)),
+    "choose": (("d",), (6.0, 0.5), (("e", 7.0, "y"),)),
+    "trade": (("e",), (2.5, 0.0), (("x", 12.0, "x"),)),
+    "run": (("x", "line", "run before"), (2.0, 1.5), ()),
 }
-ONCE = ("pair", "line", "dispatch")
+ONCE = ("pair", "line")
 LATENCY = 2.0
 RETURN = 30.0
 TRIES = 2500
@@ -423,6 +374,9 @@
                 clock = advance(clock, clock + 1.0, links, done)
             now = max(now, done[need] + extra)
         _, (fixed, each), sent = STEPS[name]
+        while sent and sent[0][2] == "y" and links["y"]:
+            clock = advance(clock, clock + 1.0, links, done)
+            now = max(now, clock)
         width = 1 if name in ONCE else widths[chunk]
         now += fixed + each * width
         clock = advance(clock, max(clock, now), links, done)
@@ -451,8 +405,8 @@
 
 def plan(widths):
     draw = random.Random(0)
-    offset = {"pack": 0, "partial": 35, "finish": 65, "join": 95, "run": 115}
-    rank = {(name, 0): value for name, value in zip(ONCE, (8, 20, 75))}
+    offset = dict(pack=0, send=20, partial=45, finish=75, choose=95, trade=110, run=125)
+    rank = {(name, 0): value for name, value in zip(ONCE, (8, 25))}
     time = 0.0
     for chunk, width in enumerate(widths):
         for name, value in offset.items():
@@ -499,18 +453,17 @@
     top_count = routes.shape[1]
     capacity = min(tok_dev, 2 * tok_dev * top_count // expert_count)
 
-    def wires(pairs, shift):
-        return [(a * plane + p, b * plane + (p ^ shift)) for a, b in pairs for p in range(plane)]
-
-    def send(value, pairs, shift=0):
-        return lax.ppermute(value, "expert", wires(pairs, shift))
+    def send(value, pairs):
+        wires = [(a * plane + p, b * plane + p) for a, b in pairs for p in range(plane)]
+        return lax.ppermute(value, "expert", wires)
+
+    def exchange(pieces):
+        return lax.all_to_all(pieces, "expert", 0, 0, tiled=True, axis_index_groups=by_plane)
 
     inward = [(0, 1), (3, 2)]
     outward = [(1, 0), (2, 3)]
     across = [(1, 2), (2, 1)]
-    inner = [(1, 1), (2, 2)]
-    every = [(z, z) for z in range(PLANES)]
-    shifts = range(plane)
+    by_plane = [[z * plane + p for p in range(plane)] for z in range(PLANES)]
     partners = [(g, g ^ 1) for g in range(group_count)]
 
     info = jnp.stack([place, level, half, is_inner.astype(jnp.int32)]).astype(jnp.int32)
@@ -523,11 +476,12 @@
     hit_table, position_lookup = route_slots(routes, expert_count, tok_dev)
     positions = jnp.arange(capacity, dtype=jnp.int32)
 
+    blocks = [z * plane + p for p in range(plane) for z in range(PLANES)]
+
     def in_blocks(table):
         column = lax.dynamic_index_in_dim(table, own_index, 2, keepdims=False)
-        column = column.reshape(PLANES, plane, tok_dev)
-        column = jnp.take(column, place ^ jnp.arange(plane, dtype=jnp.int32), axis=1)
-        return column.transpose(1, 0, 2).reshape(expert_count, 1, tok_dev)
+        column = column.reshape(PLANES, plane, tok_dev).transpose(1, 0, 2)
+        return column.reshape(expert_count, 1, tok_dev)
 
     placing = (
         (in_blocks(hit_table) == 1) & (in_blocks(position_lookup) == positions[None, :, None])
@@ -557,36 +511,37 @@
             forwarded = send(crossed, outward)
         elif name == "line":
             whole, token = line(token, info, tokens, neighbour, crossed, forwarded)
-            lines = {0: whole}
-            bit = plane // 2
-            while bit:
-                for shift in list(lines):
-                    lines[shift ^ bit] = send(lines[shift], every, bit)
-                bit //= 2
-        elif name == "dispatch":
-            grouped, token = dispatch(token, placing, [lines[shift] for shift in shifts])
-            grouped = lax.all_gather(grouped, "mp", axis=1, tiled=True)
+            everyone = lax.all_gather(whole, "expert", axis=0, tiled=True, axis_index_groups=by_plane)
+            arrived = jnp.einsum(
+                "jct,jtd->jcd", placing, everyone, preferred_element_type=jnp.float32
+            ).astype(jnp.bfloat16)
+            arrived = lax.all_gather(arrived, "mp", axis=2, tiled=True)
+            grouped = arrived.reshape(expert_count * capacity, depth)
         elif name == "pack":
-            pieces, token = pack(token, info, quant_gate, quant_up, start, width, plane)
-            far[c] = [send(pieces[shift], inward, shift) for shift in shifts]
-            near[c] = [send(pieces[shift], inner, shift) if shift else pieces[0] for shift in shifts]
+            (pieces,), token = pack(token, info, quant_gate, quant_up, start, width, plane)
+            near[c] = exchange(pieces)
+        elif name == "send":
+            near[c], token = hold(token, near[c], [])
+            far[c] = send(near[c], inward)
         elif name == "partial":
             (partial,), token = merge(
                 token, info, ids, weights, scales, near[c], far[c], None, start, scale_blocks
             )
             received[c] = send(partial, across)
         elif name == "finish":
-            rows, token = merge(
+            (inside[c], outward_rows), token = merge(
                 token, info, ids, weights, scales, near[c], far[c], received[c], start, scale_blocks
             )
-            outside[c] = [send(rows[plane + shift], outward, shift) for shift in shifts]
-            inside[c] = [send(rows[shift], inner, shift) if shift else rows[0] for shift in shifts]
-        elif name == "join":
-            own[c], token = join(token, info, inside[c], outside[c])
+            outside[c] = send(outward_rows, outward)
+        elif name == "choose":
+            rows, token = choose(token, info, inside[c], outside[c])
+            own[c] = exchange(rows)
+        elif name == "trade":
+            own[c], token = hold(token, own[c].reshape(depth, width), [])
             partner[c] = lax.ppermute(own[c], "groups", partners)
         else:
             (*outputs, hiddens[c]), token = run_chunk(
-                token, info, grouped, own[c], partner[c], outputs, start, (depth, full), expert_count
+                token, info, grouped, own[c], partner[c], outputs, start, full, blocks
             )
 
     last = len(widths) - 1

time: 599 us -> 505 us (0.84)
  starting transfers between devices: 221 us -> 102 us
  blocking collectives: 0 us -> 14.5 us
  between operations: 2.5 us -> 14.8 us
  Pallas kernels: 116 us -> 108 us
    ppermute x81 -> x18, starting transfers between devices: 208 us -> 55.2 us  [send(): return lax.ppermute(value, 'expert', wires)]
    ppermute x81 -> x18, waiting for transfers between devices: 179 us -> 126 us  [send(): return lax.ppermute(value, 'expert', wires)]
    all_to_all x0 -> x9, waiting for transfers between devices: none -> 46.4 us  [exchange(): lax.all_to_all(pieces, 'expert', 0, 0, tiled=True, axis_index_groups=by_p...]
    all_to_all x0 -> x9, starting transfers between devices: none -> 32.7 us  [exchange(): lax.all_to_all(pieces, 'expert', 0, 0, tiled=True, axis_index_groups=by_p...]
    all_to_all x0 -> x1, blocking collectives: none -> 14.5 us  [exchange(): lax.all_to_all(pieces, 'expert', 0, 0, tiled=True, axis_index_groups=by_p...]
    unnamed x161 -> x71, local copies, waits for them, and re-layouts: 9.88 us -> 18.3 us
    pallas_call x28 -> x37, Pallas kernels: 116 us -> 108 us  [step_call(): pl.pallas_call(ordered, out_shape=[*out_shape, TOKEN], in_specs=[*in_spec...]
  transfers between devices with their start and end apart: 88 -> 35, of which waited for: 31 -> 17; matrix products, arithmetic and copies ran while one was open for 3% -> 4% of each run, Pallas kernels for 16% -> 19%
where the time goes in v5:
time: 505 us; the launch traced here: 501 us
  waiting for transfers between devices  220 us (44%)
  Pallas kernels  108 us (21%)
  starting transfers between devices  102 us (20%)
  local copies, waits for them, and re-layouts  23.6 us (5%)
  between operations  14.8 us (3%)
  blocking collectives  14.5 us (3%)
  other arithmetic  11.6 us (2%)
  matrix products  6.58 us (1%)
    ppermute x18, waiting for transfers between devices, send(): return lax.ppermute(value, 'expert', wires)  126 us
    pallas_call x37, Pallas kernels, step_call(): pl.pallas_call(ordered, out_shape=[*out_shape, TOKEN], in_specs=[*in_spec...  108 us
    ppermute x18, starting transfers between devices, send(): return lax.ppermute(value, 'expert', wires)  55.2 us
    all_to_all x9, waiting for transfers between devices, exchange(): lax.all_to_all(pieces, 'expert', 0, 0, tiled=True, axis_index_groups=by_p...  46.4 us
    all_to_all x9, starting transfers between devices, exchange(): lax.all_to_all(pieces, 'expert', 0, 0, tiled=True, axis_index_groups=by_p...  32.7 us
    all_to_all x2, waiting for transfers between devices, shards(): lax.all_to_all(hidden, 'expert', split_axis=0, concat_axis=0, tiled=True)  23.9 us
    ppermute x5, waiting for transfers between devices, shards(): partner[c] = lax.ppermute(own[c], 'groups', partners)  23.8 us
    unnamed x71, local copies, waits for them, and re-layouts  18.3 us
  transfers between devices with their start and end apart: 35, of which 17 were waited for; matrix products, arithmetic and copies ran while one was open for 4% of the time, Pallas kernels for 19%

profile of v5, /device:TPU:0, one launch (start us, length us, event | category | flops | bytes accessed | tf_op | source)
XLA Modules:
  0.0 501.4 jit_solution(9539046271950323843)
XLA Ops:
  18.3 14.5 %all-to-all-done.refs_0_ = bf16[4,2,640,128]{3,2,1,0:T(8,128)(2,1)S(1)} async-done(((bf16[4,2,640,128]{3,2,1,0:T(8,128)(2,1)}), bf16[4,2,640,128]{3,2,1,0:T(8,128)(2,1)S(1)}, u32[]{:S(2)}, u32[]{:S(2)}) %all-to-all-start) | async-done | bytes 1310752 | tf_op jit(solution)/shard_map/all_to_all | solution.py:461
  40.7 13.9 %all-to-all-done.1.refs_0_ = bf16[4,2,640,128]{3,2,1,0:T(8,128)(2,1)S(1)} async-done(((bf16[4,2,640,128]{3,2,1,0:T(8,128)(2,1)}), bf16[4,2,640,128]{3,2,1,0:T(8,128)(2,1)S(1)}, u32[]{:S(2)}, u32[]{:S(2)}) %all-to-all-start.1) | async-done | bytes 1310752 | tf_op jit(solution)/shard_map/all_to_all | solution.py:461
  82.7 15.3 %collective-permute-done.4.refs_5_ = bf16[4,2,640,128]{3,2,1,0:T(8,128)(2,1)} collective-permute-done((bf16[4,2,640,128]{3,2,1,0:T(8,128)(2,1)}, bf16[4,2,640,128]{3,2,1,0:T(8,128)(2,1)}, u32[]{:S(2)}, u32[]{:S(2)}) %collective-permute-start.4) | collective-permute-done | bytes 1310752 | tf_op jit(solution)/shard_map/ppermute | solution.py:458
  103.8 21.9 %collective-permute-done.3.refs_5_ = bf16[4,2,640,128]{3,2,1,0:T(8,128)(2,1)} collective-permute-done((bf16[4,2,640,128]{3,2,1,0:T(8,128)(2,1)}, bf16[4,2,640,128]{3,2,1,0:T(8,128)(2,1)}, u32[]{:S(2)}, u32[]{:S(2)}) %collective-permute-start.3) | collective-permute-done | bytes 1310752 | tf_op jit(solution)/shard_map/ppermute | solution.py:458
  132.8 7.0 %collective-permute-start.7 = (bf16[4,2,640,256]{3,2,1,0:T(8,128)(2,1)S(1)}, bf16[4,2,640,256]{3,2,1,0:T(8,128)(2,1)}, u32[]{:S(2)}, u32[]{:S(2)}) collective-permute-start(bf16[4,2,640,256]{3,2,1,0:T(8,128)(2,1)S(1)} %copy-done.1), channel_id=1, source_target_pairs={{0,4},{1,5},{2,6},{3,7},{12,8},{13,9},{14,10},{15,11},{16,20},{17,... | collective-permute-start | bytes 7864328 | tf_op jit(solution)/shard_map/ppermute | solution.py:458
  149.3 41.5 %collective-permute-done.6.refs_2_ = bf16[4,640,128]{2,1,0:T(8,128)(2,1)S(1)} collective-permute-done((bf16[4,640,128]{2,1,0:T(8,128)(2,1)}, bf16[4,640,128]{2,1,0:T(8,128)(2,1)S(1)}, u32[]{:S(2)}, u32[]{:S(2)}) %collective-permute-start.6) | collective-permute-done | bytes 655392 | tf_op jit(solution)/shard_map/ppermute | solution.py:458
  198.9 5.4 %merge.14 = (bf16[8,640,256]{2,1,0:T(8,128)(2,1)}, f32[8,128]{1,0:T(8,128)}) custom-call(s32[4]{0:T(128)} %pad_add_fusion.refs_0_, s32[32]{0:T(128)} %bitcast.49, f32[32]{0:T(128)} %div.14.refs_2_, f32[3840]{0:T(1024)} %reshape.95.refs_3_, bf16[4,2,640,256]{3,2,1,0:T(8,128)(2,1)} %get-tuple-element.113.refs_4_, ...), custom_call_target="tpu_custom_call" | custom-call | flops 5242880 | bytes 10485760 | tf_op jit(solution)/shard_map/merge/pallas_call | solution.py:33
  210.6 9.8 %all-to-all-done.3 = bf16[4,640,128]{2,1,0:T(8,128)(2,1)S(1)} async-done(((bf16[4,640,128]{2,1,0:T(8,128)(2,1)}), bf16[4,640,128]{2,1,0:T(8,128)(2,1)S(1)}, u32[]{:S(2)}, u32[]{:S(2)}) %all-to-all-start.3) | async-done | bytes 655392 | tf_op jit(solution)/shard_map/all_to_all | solution.py:461
  227.6 6.3 %fusion.4 = s32[16,64,16]{2,0,1:T(8,128)S(1)} fusion(s32[16,64,16]{2,0,1:T(8,128)S(1)} %copy.63), kind=kOutput, calls=%fused_computation.22 | output fusion | flops 1032192 | bytes 131072 | tf_op jit(solution)/shard_map/jit(cumsum)/reduce_window_sum | solution.py:433
  237.5 5.6 %convolution_convert_fusion = bf16[16,48,2560]{2,1,0:T(8,128)(2,1)} fusion(bf16[16,64,2560]{2,1,0:T(8,128)(2,1)} %all-gather.2.cloned.1.call-done, s32[16,64]{1,0:T(8,128)S(1)} %bitcast.57, pred[16,64]{1,0:T(8,128)(4,1)S(1)} %bitcast.58), kind=kOutput, calls=%fused_computation | convolution fusion | flops 253722624 | bytes 9180160 | tf_op jit(solution)/shard_map/jct,jtd->jcd/dot_general | solution.py:515
  243.2 8.0 %collective-permute-done.9.refs_3_ = bf16[2560,128]{1,0:T(8,128)(2,1)S(1)} collective-permute-done((bf16[2560,128]{1,0:T(8,128)(2,1)S(1)}, bf16[2560,128]{1,0:T(8,128)(2,1)S(1)}, u32[]{:S(2)}, u32[]{:S(2)}) %collective-permute-start.9) | collective-permute-done | bytes 655392 | tf_op jit(solution)/shard_map/ppermute | solution.py:541
  264.0 14.5 %all_to_all.60 = bf16[4,640,128]{2,1,0:T(8,128)(2,1)} all-to-all(bf16[4,640,128]{2,1,0:T(8,128)(2,1)} %get-tuple-element.128), channel_id=1, replica_groups={{0,1,2,3},{4,5,6,7},{8,9,10,11},{12,13,14,15},{16,17,18,19},{20,21,22,2..., dimensions={0} | all-to-all | bytes 1310720 | tf_op jit(solution)/shard_map/all_to_all | solution.py:461
  282.2 10.0 %collective-permute-start.15 = (bf16[4,2,640,128]{3,2,1,0:T(8,128)(2,1)S(1)}, bf16[4,2,640,128]{3,2,1,0:T(8,128)(2,1)}, u32[]{:S(2)}, u32[]{:S(2)}) collective-permute-start(bf16[4,2,640,128]{3,2,1,0:T(8,128)(2,1)S(1)} %copy-done.3), channel_id=1, source_target_pairs={{0,4},{1,5},{2,6},{3,7},{12,8},{13,9},{14,10},{15,11},{16,20},{17,... | collective-permute-start | bytes 3932168 | tf_op jit(solution)/shard_map/ppermute | solution.py:458
  292.2 6.0 %merge.15 = (bf16[4,640,256]{2,1,0:T(8,128)(2,1)}, bf16[4,640,256]{2,1,0:T(8,128)(2,1)}, f32[8,128]{1,0:T(8,128)}) custom-call(s32[4]{0:T(128)} %pad_add_fusion.refs_0_, s32[32]{0:T(128)} %bitcast.50, f32[32]{0:T(128)} %div.14.refs_2_, f32[3840]{0:T(1024)} %reshape.95.refs_3_, bf16[4,2,640,256]{3,2,1,0:T(8,128)(2,1)} %get-tuple-element.113.refs_4_, ...), custom_call_target="tpu_custom_call" | custom-call | flops 5242880 | bytes 10485760 | tf_op jit(solution)/shard_map/merge/pallas_call | solution.py:33
  300.5 8.9 %collective-permute-start.12 = (bf16[4,2,640,128]{3,2,1,0:T(8,128)(2,1)}, bf16[4,2,640,128]{3,2,1,0:T(8,128)(2,1)S(1)}, u32[]{:S(2)}, u32[]{:S(2)}) collective-permute-start(bf16[4,2,640,128]{3,2,1,0:T(8,128)(2,1)} %get-tuple-element.133.refs_4_), channel_id=1, source_target_pairs={{0,4},{1,5},{2,6},{3,7},{12,8},{13,9},{14,10},{15,11},{16,20},{17,... | collective-permute-start | bytes 3932168 | tf_op jit(solution)/shard_map/ppermute | solution.py:458
  311.1 9.1 %collective-permute-done.15.refs_5_ = bf16[4,2,640,128]{3,2,1,0:T(8,128)(2,1)} collective-permute-done((bf16[4,2,640,128]{3,2,1,0:T(8,128)(2,1)S(1)}, bf16[4,2,640,128]{3,2,1,0:T(8,128)(2,1)}, u32[]{:S(2)}, u32[]{:S(2)}) %collective-permute-start.15) | collective-permute-done | bytes 1310752 | tf_op jit(solution)/shard_map/ppermute | solution.py:458
  326.3 5.6 %run_chunk.6 = (bf16[1,2560,768]{2,1,0:T(8,128)(2,1)}, bf16[1,2560,768]{2,1,0:T(8,128)(2,1)}, bf16[16,48,128]{2,1,0:T(8,128)(2,1)}, f32[8,128]{1,0:T(8,128)}) custom-call(s32[4]{0:T(128)} %pad_add_fusion.refs_0_, bf16[768,2560]{1,0:T(8,128)(2,1)} %bitcast.33, ...), custom_call_target="tpu_custom_call", output_to_operand_aliasing={{0}: (4, {}), {1}: (5, {})} | custom-call | flops 1006632960 | bytes 6553600 | tf_op jit(solution)/shard_map/run_chunk/pallas_call | solution.py:33
  338.5 9.4 %collective-permute-done.12.refs_5_ = bf16[4,2,640,128]{3,2,1,0:T(8,128)(2,1)S(1)} collective-permute-done((bf16[4,2,640,128]{3,2,1,0:T(8,128)(2,1)}, bf16[4,2,640,128]{3,2,1,0:T(8,128)(2,1)S(1)}, u32[]{:S(2)}, u32[]{:S(2)}) %collective-permute-start.12) | collective-permute-done | bytes 1310752 | tf_op jit(solution)/shard_map/ppermute | solution.py:458
  363.6 19.1 %collective-permute-done.18.refs_2_ = bf16[4,640,128]{2,1,0:T(8,128)(2,1)S(1)} collective-permute-done((bf16[4,640,128]{2,1,0:T(8,128)(2,1)S(1)}, bf16[4,640,128]{2,1,0:T(8,128)(2,1)S(1)}, u32[]{:S(2)}, u32[]{:S(2)}) %collective-permute-start.18) | collective-permute-done | bytes 655392 | tf_op jit(solution)/shard_map/ppermute | solution.py:458
  402.5 5.9 %run_chunk.7 = (bf16[1,2560,768]{2,1,0:T(8,128)(2,1)}, bf16[1,2560,768]{2,1,0:T(8,128)(2,1)}, bf16[16,48,256]{2,1,0:T(8,128)(2,1)}, f32[8,128]{1,0:T(8,128)}) custom-call(s32[4]{0:T(128)} %pad_add_fusion.refs_0_, bf16[768,2560]{1,0:T(8,128)(2,1)} %bitcast.34, ...), custom_call_target="tpu_custom_call", output_to_operand_aliasing={{0}: (4, {}), {1}: (5, {})} | custom-call | flops 2013265920 | bytes 9175040 | tf_op jit(solution)/shard_map/run_chunk/pallas_call | solution.py:33
  432.2 15.8 %collective-permute-done.22.refs_3_ = bf16[2560,128]{1,0:T(8,128)(2,1)S(1)} collective-permute-done((bf16[2560,128]{1,0:T(8,128)(2,1)}, bf16[2560,128]{1,0:T(8,128)(2,1)S(1)}, u32[]{:S(2)}, u32[]{:S(2)}) %collective-permute-start.22) | collective-permute-done | bytes 655392 | tf_op jit(solution)/shard_map/ppermute | solution.py:541
  448.9 5.5 %run_chunk.9 = (bf16[1,2560,768]{2,1,0:T(8,128)(2,1)}, bf16[1,2560,768]{2,1,0:T(8,128)(2,1)}, bf16[16,48,128]{2,1,0:T(8,128)(2,1)}, f32[8,128]{1,0:T(8,128)}) custom-call(s32[4]{0:T(128)} %pad_add_fusion.refs_0_, bf16[768,2560]{1,0:T(8,128)(2,1)} %bitcast.36, ...), custom_call_target="tpu_custom_call", output_to_operand_aliasing={{0}: (4, {}), {1}: (5, {})} | custom-call | flops 1006632960 | bytes 6553600 | tf_op jit(solution)/shard_map/run_chunk/pallas_call | solution.py:33
  459.4 7.9 %all-to-all-done.11 = bf16[16,48,128]{2,1,0:T(8,128)(2,1)S(1)} async-done(((bf16[16,48,128]{2,1,0:T(8,128)(2,1)}), bf16[16,48,128]{2,1,0:T(8,128)(2,1)S(1)}, u32[]{:S(2)}, u32[]{:S(2)}) %all-to-all-start.11) | async-done | bytes 196640 | tf_op jit(solution)/shard_map/all_to_all | solution.py:551
  476.8 16.0 %all-to-all-done.10 = bf16[16,48,640]{2,1,0:T(8,128)(2,1)S(1)} async-done(((bf16[16,48,640]{2,1,0:T(8,128)(2,1)}), bf16[16,48,640]{2,1,0:T(8,128)(2,1)S(1)}, u32[]{:S(2)}, u32[]{:S(2)}) %all-to-all-start.10) | async-done | bytes 983072 | tf_op jit(solution)/shard_map/all_to_all | solution.py:551
  (187 shorter events, 204.0 us)
Async XLA Ops:
  11.2 21.5 %all-to-all-start = ((bf16[4,2,640,128]{3,2,1,0:T(8,128)(2,1)}), bf16[4,2,640,128]{3,2,1,0:T(8,128)(2,1)S(1)}, u32[]{:S(2)}, u32[]{:S(2)}) async-start(bf16[4,2,640,128]{3,2,1,0:T(8,128)(2,1)} %get-tuple-element.91), calls=%async_computation | async-start | bytes 2621440 | tf_op jit(solution)/shard_map/all_to_all | solution.py:461
  33.8 20.8 %all-to-all-start.1 = ((bf16[4,2,640,128]{3,2,1,0:T(8,128)(2,1)}), bf16[4,2,640,128]{3,2,1,0:T(8,128)(2,1)S(1)}, u32[]{:S(2)}, u32[]{:S(2)}) async-start(bf16[4,2,640,128]{3,2,1,0:T(8,128)(2,1)} %get-tuple-element.97), calls=%async_computation.1 | async-start | bytes 2621440 | tf_op jit(solution)/shard_map/all_to_all | solution.py:461
  55.7 46.6 %all-to-all-start.2 = ((bf16[4,2,640,256]{3,2,1,0:T(8,128)(2,1)}), bf16[4,2,640,256]{3,2,1,0:T(8,128)(2,1)S(1)}, u32[]{:S(2)}, u32[]{:S(2)}) async-start(bf16[4,2,640,256]{3,2,1,0:T(8,128)(2,1)} %get-tuple-element.100), calls=%async_computation.2 | async-start | bytes 5242880 | tf_op jit(solution)/shard_map/all_to_all | solution.py:461
  59.3 178.2 %all-gather.2.cloned.1.call-start = ((), (), s32[]{:S(2)}) async-start(), calls=%async_computation.12 | async-start | bytes 6553600 | tf_op jit(solution)/shard_map/all_gather | solution.py:514
  61.8 36.2 %collective-permute-start.4 = (bf16[4,2,640,128]{3,2,1,0:T(8,128)(2,1)}, bf16[4,2,640,128]{3,2,1,0:T(8,128)(2,1)}, u32[]{:S(2)}, u32[]{:S(2)}) collective-permute-start(bf16[4,2,640,128]{3,2,1,0:T(8,128)(2,1)} %get-tuple-element.101.refs_4_), channel_id=1, source_target_pairs={{0,4},{1,5},{2,6},{3,7},{12,8},{13,9},{14,10},{15,11},{16,20},{17,... | collective-permute-start | bytes 3932168 | tf_op jit(solution)/shard_map/ppermute | solution.py:458
  72.8 52.9 %collective-permute-start.3 = (bf16[4,2,640,128]{3,2,1,0:T(8,128)(2,1)}, bf16[4,2,640,128]{3,2,1,0:T(8,128)(2,1)}, u32[]{:S(2)}, u32[]{:S(2)}) collective-permute-start(bf16[4,2,640,128]{3,2,1,0:T(8,128)(2,1)} %get-tuple-element.99.refs_4_), channel_id=1, source_target_pairs={{0,4},{1,5},{2,6},{3,7},{12,8},{13,9},{14,10},{15,11},{16,20},{17,... | collective-permute-start | bytes 3932168 | tf_op jit(solution)/shard_map/ppermute | solution.py:458
  79.6 50.3 %collective-permute-start.2 = (bf16[2,64,2560]{2,1,0:T(8,128)(2,1)}, bf16[2,64,2560]{2,1,0:T(8,128)(2,1)}, u32[]{:S(2)}, u32[]{:S(2)}) collective-permute-start(bf16[2,64,2560]{2,1,0:T(8,128)(2,1)} %collective-permute-done.1.refs_3_), channel_id=1, source_target_pairs={{4,0},{5,1},{6,2},{7,3},{8,12},{9,13},{10,14},{11,15},{20,16},{21,... | collective-permute-start | bytes 1966088 | tf_op jit(solution)/shard_map/ppermute | solution.py:458
  132.8 66.1 %collective-permute-start.7 = (bf16[4,2,640,256]{3,2,1,0:T(8,128)(2,1)S(1)}, bf16[4,2,640,256]{3,2,1,0:T(8,128)(2,1)}, u32[]{:S(2)}, u32[]{:S(2)}) collective-permute-start(bf16[4,2,640,256]{3,2,1,0:T(8,128)(2,1)S(1)} %copy-done.1), channel_id=1, source_target_pairs={{0,4},{1,5},{2,6},{3,7},{12,8},{13,9},{14,10},{15,11},{16,20},{17,... | collective-permute-start | bytes 7864328 | tf_op jit(solution)/shard_map/ppermute | solution.py:458
  141.5 52.8 %collective-permute-start.8 = (bf16[8,640,128]{2,1,0:T(8,128)(2,1)}, bf16[8,640,128]{2,1,0:T(8,128)(2,1)}, u32[]{:S(2)}, u32[]{:S(2)}) collective-permute-start(bf16[8,640,128]{2,1,0:T(8,128)(2,1)} %get-tuple-element.114), channel_id=1, source_target_pairs={{4,8},{5,9},{6,10},{7,11},{8,4},{9,5},{10,6},{11,7},{20,24},{21,25... | collective-permute-start | bytes 3932168 | tf_op jit(solution)/shard_map/ppermute | solution.py:458
  148.0 42.8 %collective-permute-start.6 = (bf16[4,640,128]{2,1,0:T(8,128)(2,1)}, bf16[4,640,128]{2,1,0:T(8,128)(2,1)S(1)}, u32[]{:S(2)}, u32[]{:S(2)}) collective-permute-start(bf16[4,640,128]{2,1,0:T(8,128)(2,1)} %get-tuple-element.110), channel_id=1, source_target_pairs={{4,0},{5,1},{6,2},{7,3},{8,12},{9,13},{10,14},{11,15},{20,16},{21,... | collective-permute-start | bytes 1966088 | tf_op jit(solution)/shard_map/ppermute | solution.py:458
  204.4 87.8 %collective-permute-start.11 = (bf16[8,640,256]{2,1,0:T(8,128)(2,1)}, bf16[8,640,256]{2,1,0:T(8,128)(2,1)}, u32[]{:S(2)}, u32[]{:S(2)}) collective-permute-start(bf16[8,640,256]{2,1,0:T(8,128)(2,1)} %get-tuple-element.129), channel_id=1, source_target_pairs={{4,8},{5,9},{6,10},{7,11},{8,4},{9,5},{10,6},{11,7},{20,24},{21,25... | collective-permute-start | bytes 7864328 | tf_op jit(solution)/shard_map/ppermute | solution.py:458
  224.1 36.2 %all-to-all-start.5 = ((bf16[4,2,640,128]{3,2,1,0:T(8,128)(2,1)}), bf16[4,2,640,128]{3,2,1,0:T(8,128)(2,1)S(1)}, u32[]{:S(2)}, u32[]{:S(2)}) async-start(bf16[4,2,640,128]{3,2,1,0:T(8,128)(2,1)} %get-tuple-element.125), calls=%async_computation.5 | async-start | bytes 2621440 | tf_op jit(solution)/shard_map/all_to_all | solution.py:461
  236.2 25.2 %collective-permute-start.10 = (bf16[4,640,128]{2,1,0:T(8,128)(2,1)}, bf16[4,640,128]{2,1,0:T(8,128)(2,1)}, u32[]{:S(2)}, u32[]{:S(2)}) collective-permute-start(bf16[4,640,128]{2,1,0:T(8,128)(2,1)} %get-tuple-element.124), channel_id=1, source_target_pairs={{4,0},{5,1},{6,2},{7,3},{8,12},{9,13},{10,14},{11,15},{20,16},{21,... | collective-permute-start | bytes 1966088 | tf_op jit(solution)/shard_map/ppermute | solution.py:458
  278.5 21.0 %all-to-all-start.4 = ((bf16[4,2,640,128]{3,2,1,0:T(8,128)(2,1)}), bf16[4,2,640,128]{3,2,1,0:T(8,128)(2,1)S(1)}, u32[]{:S(2)}, u32[]{:S(2)}) async-start(bf16[4,2,640,128]{3,2,1,0:T(8,128)(2,1)} %get-tuple-element.122), calls=%async_computation.4 | async-start | bytes 2621440 | tf_op jit(solution)/shard_map/all_to_all | solution.py:461
  282.2 38.0 %collective-permute-start.15 = (bf16[4,2,640,128]{3,2,1,0:T(8,128)(2,1)S(1)}, bf16[4,2,640,128]{3,2,1,0:T(8,128)(2,1)}, u32[]{:S(2)}, u32[]{:S(2)}) collective-permute-start(bf16[4,2,640,128]{3,2,1,0:T(8,128)(2,1)S(1)} %copy-done.3), channel_id=1, source_target_pairs={{0,4},{1,5},{2,6},{3,7},{12,8},{13,9},{14,10},{15,11},{16,20},{17,... | collective-permute-start | bytes 3932168 | tf_op jit(solution)/shard_map/ppermute | solution.py:458
  298.2 33.7 %collective-permute-start.13 = (bf16[4,640,256]{2,1,0:T(8,128)(2,1)}, bf16[4,640,256]{2,1,0:T(8,128)(2,1)}, u32[]{:S(2)}, u32[]{:S(2)}) collective-permute-start(bf16[4,640,256]{2,1,0:T(8,128)(2,1)} %get-tuple-element.135), channel_id=1, source_target_pairs={{4,0},{5,1},{6,2},{7,3},{8,12},{9,13},{10,14},{11,15},{20,16},{21,... | collective-permute-start | bytes 3932168 | tf_op jit(solution)/shard_map/ppermute | solution.py:458
  300.5 47.4 %collective-permute-start.12 = (bf16[4,2,640,128]{3,2,1,0:T(8,128)(2,1)}, bf16[4,2,640,128]{3,2,1,0:T(8,128)(2,1)S(1)}, u32[]{:S(2)}, u32[]{:S(2)}) collective-permute-start(bf16[4,2,640,128]{3,2,1,0:T(8,128)(2,1)} %get-tuple-element.133.refs_4_), channel_id=1, source_target_pairs={{0,4},{1,5},{2,6},{3,7},{12,8},{13,9},{14,10},{15,11},{16,20},{17,... | collective-permute-start | bytes 3932168 | tf_op jit(solution)/shard_map/ppermute | solution.py:458
  324.5 30.6 %collective-permute-start.17 = (bf16[8,640,128]{2,1,0:T(8,128)(2,1)}, bf16[8,640,128]{2,1,0:T(8,128)(2,1)}, u32[]{:S(2)}, u32[]{:S(2)}) collective-permute-start(bf16[8,640,128]{2,1,0:T(8,128)(2,1)} %get-tuple-element.145), channel_id=1, source_target_pairs={{4,8},{5,9},{6,10},{7,11},{8,4},{9,5},{10,6},{11,7},{20,24},{21,25... | collective-permute-start | bytes 3932168 | tf_op jit(solution)/shard_map/ppermute | solution.py:458
  335.0 24.7 %all-to-all-start.7 = ((bf16[4,640,256]{2,1,0:T(8,128)(2,1)}), bf16[4,640,256]{2,1,0:T(8,128)(2,1)S(1)}, u32[]{:S(2)}, u32[]{:S(2)}) async-start(bf16[4,640,256]{2,1,0:T(8,128)(2,1)} %get-tuple-element.149), calls=%async_computation.7 | async-start | bytes 2621440 | tf_op jit(solution)/shard_map/all_to_all | solution.py:461
  353.4 36.3 %collective-permute-start.16 = (bf16[8,640,128]{2,1,0:T(8,128)(2,1)}, bf16[8,640,128]{2,1,0:T(8,128)(2,1)}, u32[]{:S(2)}, u32[]{:S(2)}) collective-permute-start(bf16[8,640,128]{2,1,0:T(8,128)(2,1)} %get-tuple-element.144), channel_id=1, source_target_pairs={{4,8},{5,9},{6,10},{7,11},{8,4},{9,5},{10,6},{11,7},{20,24},{21,25... | collective-permute-start | bytes 3932168 | tf_op jit(solution)/shard_map/ppermute | solution.py:458
  360.7 40.7 %collective-permute-start.20 = (bf16[2560,256]{1,0:T(8,128)(2,1)}, bf16[2560,256]{1,0:T(8,128)(2,1)S(1)}, u32[]{:S(2)}, u32[]{:S(2)}) collective-permute-start(bf16[2560,256]{1,0:T(8,128)(2,1)} %get-tuple-element.155.refs_2_), channel_id=1, source_target_pairs={{0,16},{16,0},{1,17},{17,1},{2,18},{18,2},{3,19},{19,3},{4,20},{20... | collective-permute-start | bytes 3932168 | tf_op jit(solution)/shard_map/ppermute | solution.py:541
  362.3 20.4 %collective-permute-start.18 = (bf16[4,640,128]{2,1,0:T(8,128)(2,1)S(1)}, bf16[4,640,128]{2,1,0:T(8,128)(2,1)S(1)}, u32[]{:S(2)}, u32[]{:S(2)}) collective-permute-start(bf16[4,640,128]{2,1,0:T(8,128)(2,1)S(1)} %copy-done.33), channel_id=1, source_target_pairs={{4,0},{5,1},{6,2},{7,3},{8,12},{9,13},{10,14},{11,15},{20,16},{21,... | collective-permute-start | bytes 1966088 | tf_op jit(solution)/shard_map/ppermute | solution.py:458
  400.8 19.7 %collective-permute-start.21 = (bf16[2560,128]{1,0:T(8,128)(2,1)}, bf16[2560,128]{1,0:T(8,128)(2,1)S(1)}, u32[]{:S(2)}, u32[]{:S(2)}) collective-permute-start(bf16[2560,128]{1,0:T(8,128)(2,1)} %get-tuple-element.163.refs_2_), channel_id=1, source_target_pairs={{0,16},{16,0},{1,17},{17,1},{2,18},{18,2},{3,19},{19,3},{4,20},{20... | collective-permute-start | bytes 1966088 | tf_op jit(solution)/shard_map/ppermute | solution.py:541
  467.3 25.5 %all-to-all-start.10 = ((bf16[16,48,640]{2,1,0:T(8,128)(2,1)}), bf16[16,48,640]{2,1,0:T(8,128)(2,1)S(1)}, u32[]{:S(2)}, u32[]{:S(2)}) async-start(bf16[16,48,640]{2,1,0:T(8,128)(2,1)} %pad_maximum_fusion), calls=%async_computation.10 | async-start | bytes 1966080 | tf_op jit(solution)/shard_map/all_to_all | solution.py:551
  (46 other events, 299.4 us)
Sparse Core Ops, SparseCore 0:
  132.9 42.6 all-gather.1

commit v6 on v0

v6 whole, which is shorter than its diff:
```python
import math

import jax
import jax.numpy as jnp
from jax import lax
from jax.experimental import pallas as pl
from jax.experimental.pallas import tpu as pltpu
from jax.sharding import PartitionSpec as P

D = 2560
BLOCK = 128
PLANES = 4
TOKEN = jax.ShapeDtypeStruct((8, 128), jnp.float32)
ANY = pl.BlockSpec(memory_space=pl.ANY)
SMEM = pl.BlockSpec(memory_space=pltpu.SMEM)
VMEM = pl.BlockSpec(memory_space=pltpu.VMEM)
VMEM_LIMIT = 60 * 1024 * 1024


def cluster_weights(cluster_ids, frequency):
    ids = cluster_ids[:, 0]
    same = (ids[:, None] == ids[None, :]).astype(jnp.float32)
    return frequency / jnp.sum(same * frequency[None, :], axis=1)


def step_call(kernel, token, operands, in_specs, out_shape, out_specs, **options):
    count = len(operands)

    def ordered(*refs):
        kernel(*refs[:count], *refs[count + 1 : count + 1 + len(out_shape)], *refs[count + 2 + len(out_shape) :])

    *results, token = pl.pallas_call(
        ordered,
        out_shape=[*out_shape, TOKEN],
        in_specs=[*in_specs, ANY],
        out_specs=[*out_specs, ANY],
        compiler_params=pltpu.CompilerParams(vmem_limit_bytes=VMEM_LIMIT),
        cost_estimate=pl.CostEstimate(flops=0, bytes_accessed=0, transcendentals=0),
        **options,
    )(*operands, token)
    return results, token


def pack(token, info, gate, up, start, width, devices):
    sources, depth, _ = gate.shape
    rows = depth // devices

    def kernel(info_ref, gate_ref, up_ref, *rest):
        out, held, in_sems, out_sems = rest

        def move(source):
            loads = [
                pltpu.make_async_copy(
                    source.at[
                        :,
                        pl.ds(part * rows, rows),
                        pl.ds(start, width),
                    ],
                    held.at[part],
                    in_sems.at[part],
                )
                for part in range(devices)
            ]
            stores = [
                pltpu.make_async_copy(held.at[part], out.at[part], out_sems.at[part])
                for part in range(devices)
            ]
            for load in loads:
                load.start()
            for load, store in zip(loads, stores):
                load.wait()
                store.start()
            for store in stores:
                store.wait()

        @pl.when(info_ref[1] == 0)
        def _():
            move(gate_ref)

        @pl.when(info_ref[1] != 0)
        def _():
            move(up_ref)

    return step_call(
        kernel,
        token,
        (info, gate, up),
        [SMEM, ANY, ANY],
        [jax.ShapeDtypeStruct((devices, sources, rows, width), gate.dtype)],
        [ANY],
        scratch_shapes=[
            pltpu.VMEM((devices, sources, rows, width), gate.dtype),
            pltpu.SemaphoreType.DMA((devices,)),
            pltpu.SemaphoreType.DMA((devices,)),
        ],
        name="pack",
    )


def hold(token, value, earlier):
    def kernel(*refs):
        pass

    (value,), token = step_call(
        kernel,
        token,
        (value, *earlier),
        [ANY] * (1 + len(earlier)),
        [jax.ShapeDtypeStruct(value.shape, value.dtype)],
        [ANY],
        input_output_aliases={0: 0},
        name="hold",
    )
    return value, token


def merge(token, slots, factors, rows_of, received, start, blocks):
    devices, sources, rows, width = rows_of.shape
    steps, column_blocks = blocks
    step = rows // steps
    first = start // BLOCK
    base_slot = 0 if received is None else devices * sources

    def kernel(slots_ref, factors_ref, rows_ref, *rest):
        out_ref, total = rest[-2:]
        piece = pl.program_id(0)

        @pl.when(piece == 0)
        def _():
            if received is None:
                total[...] = jnp.zeros_like(total)
            else:
                total[...] = rest[0][...].astype(jnp.float32)

        for number in range(sources):
            source = piece * sources + number
            slot = slots_ref[base_slot + source]

            @pl.when(slot >= 0)
            def _():
                for index in range(steps):
                    for part in range(width // BLOCK):
                        base = (source * steps + index) * column_blocks + first
                        lanes = slice(part * BLOCK, (part + 1) * BLOCK)
                        place = slice(index * step, (index + 1) * step)
                        total[slot, place, lanes] += (
                            rows_ref[0, number, place, lanes].astype(jnp.float32)
                            * factors_ref[base + part]
                        )

        @pl.when(piece == devices - 1)
        def _():
            out_ref[...] = total[...].astype(jnp.bfloat16)

    whole = pl.BlockSpec((devices, rows, width), lambda i: (0, 0, 0))
    extra = () if received is None else (received,)
    (merged,), token = step_call(
        kernel,
        token,
        (slots, factors, rows_of, *extra),
        [SMEM, SMEM, pl.BlockSpec((1, sources, rows, width), lambda i: (i, 0, 0, 0))]
        + [whole] * len(extra),
        [jax.ShapeDtypeStruct((devices, rows, width), jnp.bfloat16)],
        [whole],
        grid=(devices,),
        scratch_shapes=[pltpu.VMEM((devices, rows, width), jnp.float32)],
        name="merge",
    )
    return merged, token


def pair(token, tokens, other):
    def kernel(tokens_ref, other_ref, out_ref):
        out_ref[0] = tokens_ref[...]
        out_ref[1] = other_ref[...]

    (both,), token = step_call(
        kernel,
        token,
        (tokens, other),
        [VMEM, VMEM],
        [jax.ShapeDtypeStruct((2,) + tokens.shape, tokens.dtype)],
        [VMEM],
        name="pair",
    )
    return both, token


def line(token, info, both, nearby, tables):
    _, tok_dev, width = both.shape

    def kernel(info_ref, both_ref, nearby_ref, *rest):
        out_ref = rest[len(tables)]
        level = info_ref[0]
        for index, other in enumerate((both_ref, nearby_ref)):
            out_ref[level ^ index] = other[0]
            out_ref[level ^ index ^ (PLANES // 2)] = other[1]

    (whole,), _ = step_call(
        kernel,
        token,
        (info, both, nearby, *tables),
        [SMEM] + [VMEM] * 2 + [ANY] * len(tables),
        [jax.ShapeDtypeStruct((PLANES, tok_dev, width), both.dtype)],
        [VMEM],
        name="line",
    )
    return whole


def run_chunk(token, info, grouped, own, partner, outputs, start, full, blocks):
    depth, width = own.shape
    count = grouped.shape[0]
    each = count // len(blocks)
    factor = 1.0 / math.sqrt(D)

    def kernel(info_ref, grouped_ref, own_ref, partner_ref, *rest):
        gate_out, up_out, hidden_ref, whole, in_sems, out_sems = rest[len(outputs) :]
        halves = [whole.at[:, pl.ds(index * width, width)] for index in range(2)]

        def fill(*sources):
            loads = [
                pltpu.make_async_copy(source, half, in_sems.at[index])
                for index, (source, half) in enumerate(zip(sources, halves))
            ]
            for load in loads:
                load.start()
            for load in loads:
                load.wait()

        @pl.when(info_ref[1] == 0)
        def _():
            fill(own_ref, partner_ref)

        @pl.when(info_ref[1] != 0)
        def _():
            fill(partner_ref, own_ref)

        stores = [
            pltpu.make_async_copy(half, out.at[0, :, pl.ds(start, width)], out_sems.at[index])
            for index, (half, out) in enumerate(zip(halves, (gate_out, up_out)))
        ]
        for store in stores:
            store.start()
        values = jnp.dot(grouped_ref[...], whole[...], preferred_element_type=jnp.float32)
        gate_value = values[:, :width] * factor
        up_value = values[:, width:] * factor
        hidden = (gate_value / (1.0 + jnp.exp(-gate_value)) * up_value).astype(jnp.bfloat16)
        for index, block in enumerate(blocks):
            hidden_ref[block] = hidden[index * each : (index + 1) * each]
        for store in stores:
            store.wait()

    weights = jax.ShapeDtypeStruct((1, depth, full), jnp.bfloat16)
    return step_call(
        kernel,
        token,
        (info, grouped, own, partner, *outputs),
        [SMEM, VMEM, ANY, ANY] + [ANY] * len(outputs),
        [weights, weights, jax.ShapeDtypeStruct((len(blocks), each, width), jnp.bfloat16)],
        [ANY, ANY, VMEM],
        scratch_shapes=[
            pltpu.VMEM((depth, 2 * width), jnp.bfloat16),
            pltpu.SemaphoreType.DMA((2,)),
            pltpu.SemaphoreType.DMA((2,)),
        ],
        input_output_aliases={4 + index: index for index in range(len(outputs))},
        name="run_chunk",
    )


def plan(count):
    order = [("pack", 0), ("pair", 0)]
    for chunk in range(count):
        if chunk + 1 < count:
            order.append(("pack", chunk + 1))
        order.append(("partial", chunk))
        if chunk == 0:
            order.append(("line", 0))
        if chunk >= 2:
            order.extend([("finish", chunk - 2), ("trade", chunk - 2)])
    for chunk in range(max(0, count - 2), count):
        order.extend([("finish", chunk), ("trade", chunk)])
    for chunk in range(count):
        place = order.index(("trade", chunk))
        later = [i for i, (name, _) in enumerate(order) if i > place and name in ("partial", "trade")]
        order.insert(later[0] + 1 if later else len(order), ("run", chunk))
    return order


def route_slots(routes, merged_count, tok_dev):
    experts = jnp.arange(merged_count, dtype=jnp.int32)
    hit_table = jnp.sum((routes[:, :, None] == experts).astype(jnp.int32), axis=1)
    hit_table = hit_table.reshape(-1, tok_dev, merged_count)
    position_lookup = jnp.cumsum(hit_table, axis=1) - hit_table
    return (hit_table, position_lookup)


def chunk_widths(blocks):
    if blocks < 4:
        return [1] * blocks
    middle, odd = divmod(blocks - 2, 2)
    return [1] + [2] * middle + [1] * odd + [1]


def shards(tokens, routes, quant_gate, quant_up, gate_scales, up_scales, cluster_ids, frequency):
    expert_count = lax.axis_size("expert")
    own_index = lax.axis_index("expert")
    group_count = lax.axis_size("groups")
    half = lax.axis_index("groups") % 2
    plane = expert_count // PLANES
    level = own_index // plane
    halfway = expert_count // 2
    side, place = own_index // halfway, own_index % halfway
    depth, full = quant_gate.shape[1:]
    tok_dev = tokens.shape[0]
    top_count = routes.shape[1]
    capacity = min(tok_dev, 2 * tok_dev * top_count // expert_count)

    by_plane = [[z * plane + p for p in range(plane)] for z in range(PLANES)]
    by_half = [[part * halfway + i for i in range(halfway)] for part in range(2)]
    across = [(i, (i + halfway) % expert_count) for i in range(expert_count)]
    beside = [(i, (i // plane ^ 1) * plane + i % plane) for i in range(expert_count)]
    partners = [(g, g ^ 1) for g in range(group_count)]

    def exchange(pieces):
        return lax.all_to_all(pieces, "expert", 0, 0, tiled=True, axis_index_groups=by_half)

    info = jnp.stack([level, half]).astype(jnp.int32)
    sources = quant_gate.shape[0]
    rows = depth // halfway
    step = math.gcd(rows, BLOCK)
    held = side * halfway * sources + jnp.arange(halfway * sources, dtype=jnp.int32)
    target = jnp.take(cluster_ids[:, 0], held)
    slots = jnp.concatenate(
        [
            jnp.where(target // halfway != side, target % halfway, -1),
            jnp.where(target // halfway == side, target % halfway, -1),
        ]
    )
    weights = jnp.take(cluster_weights(cluster_ids, frequency), held)
    scales = jnp.take(jnp.where(half == 0, gate_scales, up_scales), held, axis=0)
    row_blocks = (place * rows + step * jnp.arange(rows // step, dtype=jnp.int32)) // BLOCK
    factors = jnp.take(scales, row_blocks, axis=1) * weights[:, None, None]
    blocks_of_rows = factors.shape[1:]
    factors = factors.reshape(-1)

    hit_table, position_lookup = route_slots(routes, expert_count, tok_dev)
    positions = jnp.arange(capacity, dtype=jnp.int32)

    blocks = [z * plane + p for p in range(plane) for z in range(PLANES)]

    def in_blocks(table):
        column = lax.dynamic_index_in_dim(table, own_index, 2, keepdims=False)
        column = column.reshape(PLANES, plane, tok_dev).transpose(1, 0, 2)
        return column.reshape(expert_count, 1, tok_dev)

    placing = (
        (in_blocks(hit_table) == 1) & (in_blocks(position_lookup) == positions[None, :, None])
    ).astype(jnp.bfloat16)

    experts = jnp.arange(expert_count, dtype=jnp.int32)
    local_routes = lax.dynamic_slice_in_dim(routes, own_index * tok_dev, tok_dev, 0)
    own_slots = lax.dynamic_index_in_dim(position_lookup, own_index, 0, keepdims=False)
    chosen = local_routes[:, :, None] == experts
    slot_of = jnp.sum(jnp.where(chosen, own_slots[:, None, :], 0), axis=2)
    picking = (chosen[:, :, :, None] & (slot_of[:, :, None, None] == positions)).astype(
        jnp.bfloat16
    )
    picking = picking.reshape(tok_dev * top_count, expert_count * capacity)

    widths = chunk_widths(full // BLOCK)
    starts = [BLOCK * sum(widths[:chunk]) for chunk in range(len(widths))]
    token = jnp.zeros(TOKEN.shape, TOKEN.dtype)
    opposite = lax.ppermute(tokens, "expert", across)
    gathered, received, own, partner, hiddens = ({} for _ in range(5))
    outputs = ()
    for name, c in plan(len(widths)):
        start, width = starts[c], widths[c] * BLOCK
        if name == "pair":
            both, token = pair(token, tokens, opposite)
            nearby = lax.ppermute(both, "expert", beside)
        elif name == "line":
            whole = line(token, info, both, nearby, (placing, picking))
            everyone = lax.all_gather(whole, "expert", axis=0, tiled=True, axis_index_groups=by_plane)
            arrived = jnp.einsum(
                "jct,jtd->jcd", placing, everyone, preferred_element_type=jnp.float32
            ).astype(jnp.bfloat16)
            arrived = lax.all_gather(arrived, "mp", axis=2, tiled=True)
            grouped = arrived.reshape(expert_count * capacity, depth)
        elif name == "pack":
            (pieces,), token = pack(token, info, quant_gate, quant_up, start, width, halfway)
            gathered[c] = exchange(pieces)
        elif name == "partial":
            partial, token = merge(token, slots, factors, gathered[c], None, start, blocks_of_rows)
            received[c] = lax.ppermute(partial, "expert", across)
        elif name == "finish":
            merged, token = merge(
                token, slots, factors, gathered[c], received[c], start, blocks_of_rows
            )
            own[c] = exchange(merged)
        elif name == "trade":
            own[c], token = hold(token, own[c].reshape(depth, width), [])
            partner[c] = lax.ppermute(own[c], "groups", partners)
        else:
            (*outputs, hiddens[c]), token = run_chunk(
                token, info, grouped, own[c], partner[c], outputs, start, full, blocks
            )

    last = len(widths) - 1
    finished = []
    before = []
    for batch in (range(last), range(last, last + 1)):
        hidden = jnp.concatenate([hiddens[c] for c in batch], axis=2)
        hidden, token = hold(token, hidden, before)
        returned = lax.all_to_all(hidden, "expert", split_axis=0, concat_axis=0, tiled=True)
        before = [returned]
        rows = returned.reshape(expert_count * capacity, returned.shape[2])
        finished.append(
            jnp.dot(picking, rows, preferred_element_type=jnp.float32).astype(jnp.bfloat16)
        )
    output = jnp.concatenate(finished, axis=1)
    merged_gate, merged_up = outputs
    return (merged_gate, merged_up, output.reshape(tok_dev, top_count, full))


def solution(mesh):
    return jax.shard_map(
        shards,
        mesh=mesh,
        in_specs=(
            P(("groups", "expert"), "mp"),
            P("groups", None),
            P("expert", None, "mp"),
            P("expert", None, "mp"),
            P(None, None, "mp"),
            P(None, None, "mp"),
            P(),
            P(),
        ),
        out_specs=(
            P(("groups", "expert"), None, "mp"),
            P(("groups", "expert"), None, "mp"),
            P(("groups", "expert"), None, "mp"),
        ),
        check_vma=False,
    )
```

time: 652 us -> 466 us (0.71)
  waiting for transfers between devices: 349 us -> 220 us
  local copies, waits for them, and re-layouts: 121 us -> 24.6 us
  Pallas kernels: 0 us -> 86.2 us
  starting transfers between devices: 114 us -> 49.1 us
  blocking collectives: 0 us -> 43.3 us
  matrix products: 40.6 us -> 7.74 us
  other arithmetic: 9.32 us -> 17.5 us
    all_to_all x4 -> x7, waiting for transfers between devices: 328 us -> 122 us  [exchange(): lax.all_to_all(pieces, 'expert', 0, 0, tiled=True, axis_index_groups=by_h...]
    ppermute x0 -> x10, waiting for transfers between devices: none -> 91.2 us  [the longest x4 42.8 us: shards(): received[c] = lax.ppermute(partial, 'expert', across)]
    pallas_call x0 -> x24, Pallas kernels: none -> 86.2 us  [step_call(): pl.pallas_call(ordered, out_shape=[*out_shape, TOKEN], in_specs=[*in_spec...]
    all_to_all x4 -> x7, starting transfers between devices: 94.9 us -> 31.5 us  [exchange(): lax.all_to_all(pieces, 'expert', 0, 0, tiled=True, axis_index_groups=by_h...]
    all_to_all x0 -> x2, blocking collectives: none -> 43.3 us  [the longest x1 28.2 us: shards(): lax.all_to_all(hidden, 'expert', split_axis=0, concat_axis=0, tiled=True)]
    reshape x3 -> x1, local copies, waits for them, and re-layouts: 33.8 us -> 0.2 us  [shards(): return (merged_gate, merged_up, output.reshape(tok_dev, top_count, full))]
    dot_general x8 -> x3, matrix products: 40.6 us -> 7.74 us  [the longest x1 5.58 us: shards(): jnp.einsum('jct,jtd->jcd', placing, everyone, preferred_element_type=jnp....]
    unnamed x19 -> x59, local copies, waits for them, and re-layouts: 42.7 us -> 15.2 us
  transfers between devices with their start and end apart: 6 -> 19, of which waited for: 5 -> 13; matrix products, arithmetic and copies ran while one was open for 21% -> 7% of each run, Pallas kernels for 0% -> 13%
where the time goes in v6:
time: 466 us; the launch traced here: 463 us
  waiting for transfers between devices  220 us (47%)
  Pallas kernels  86.2 us (18%)
  starting transfers between devices  49.1 us (11%)
  blocking collectives  43.3 us (9%)
  local copies, waits for them, and re-layouts  24.6 us (5%)
  other arithmetic  17.5 us (4%)
  between operations  14.6 us (3%)
  matrix products  7.74 us (2%)
    all_to_all x7, waiting for transfers between devices, exchange(): lax.all_to_all(pieces, 'expert', 0, 0, tiled=True, axis_index_groups=by_h...  122 us
    pallas_call x24, Pallas kernels, step_call(): pl.pallas_call(ordered, out_shape=[*out_shape, TOKEN], in_specs=[*in_spec...  86.2 us
    ppermute x4, waiting for transfers between devices, shards(): received[c] = lax.ppermute(partial, 'expert', across)  42.8 us
    all_to_all x7, starting transfers between devices, exchange(): lax.all_to_all(pieces, 'expert', 0, 0, tiled=True, axis_index_groups=by_h...  31.5 us
    all_to_all x1, blocking collectives, shards(): lax.all_to_all(hidden, 'expert', split_axis=0, concat_axis=0, tiled=True)  28.2 us
    ppermute x4, waiting for transfers between devices, shards(): partner[c] = lax.ppermute(own[c], 'groups', partners)  23.1 us
    ppermute x1, waiting for transfers between devices, shards(): opposite = lax.ppermute(tokens, 'expert', across)  19.6 us
    unnamed x59, local copies, waits for them, and re-layouts  15.2 us
  transfers between devices with their start and end apart: 19, of which 13 were waited for; matrix products, arithmetic and copies ran while one was open for 7% of the time, Pallas kernels for 13%

profile of v6, /device:TPU:0, one launch (start us, length us, event | category | flops | bytes accessed | tf_op | source)
XLA Modules:
  0.0 463.5 jit_solution(11543593060103389790)
XLA Ops:
  11.3 5.4 %all-to-all-start = ((bf16[8,2,320,128]{3,2,1,0:T(8,128)(2,1)}), bf16[8,2,320,128]{3,2,1,0:T(8,128)(2,1)S(1)}, u32[]{:S(2)}, u32[]{:S(2)}) async-start(bf16[8,2,320,128]{3,2,1,0:T(8,128)(2,1)} %get-tuple-element.59), calls=%async_computation | async-start | bytes 2621440 | tf_op jit(solution)/shard_map/all_to_all | solution.py:327
  19.3 19.6 %collective-permute-done.refs_1_ = bf16[64,2560]{1,0:T(8,128)(2,1)S(1)} collective-permute-done((bf16[64,2560]{1,0:T(8,128)(2,1)S(1)}, bf16[64,2560]{1,0:T(8,128)(2,1)S(1)}, u32[]{:S(2)}, u32[]{:S(2)}) %collective-permute-start) | collective-permute-done | bytes 327712 | tf_op jit(solution)/shard_map/ppermute | solution.py:375
  46.0 6.8 %all-to-all-start.1 = ((bf16[8,2,320,256]{3,2,1,0:T(8,128)(2,1)}), bf16[8,2,320,256]{3,2,1,0:T(8,128)(2,1)S(1)}, u32[]{:S(2)}, u32[]{:S(2)}) async-start(bf16[8,2,320,256]{3,2,1,0:T(8,128)(2,1)} %get-tuple-element.64), calls=%async_computation.1 | async-start | bytes 5242880 | tf_op jit(solution)/shard_map/all_to_all | solution.py:327
  53.3 6.3 %fusion.7 = s32[16,64,16]{2,0,1:T(8,128)S(1)} fusion(s32[16,64,16]{2,0,1:T(8,128)S(1)} %copy.66), kind=kOutput, calls=%fused_computation.57 | output fusion | flops 1032192 | bytes 131072 | tf_op jit(solution)/shard_map/jit(cumsum)/reduce_window_sum | solution.py:295
  93.1 5.7 %collective-permute-done.1.refs_2_ = bf16[2,64,2560]{2,1,0:T(8,128)(2,1)} collective-permute-done((bf16[2,64,2560]{2,1,0:T(8,128)(2,1)}, bf16[2,64,2560]{2,1,0:T(8,128)(2,1)}, u32[]{:S(2)}, u32[]{:S(2)}) %collective-permute-start.1) | collective-permute-done | bytes 655392 | tf_op jit(solution)/shard_map/ppermute | solution.py:382
  101.4 5.8 %merge.9 = (bf16[8,320,256]{2,1,0:T(8,128)(2,1)}, f32[8,128]{1,0:T(8,128)}) custom-call(s32[32]{0:T(128)} %pad_add_fusion.1.refs_0_, f32[480]{0:T(512)} %mul.53.refs_1_, bf16[8,2,320,256]{3,2,1,0:T(8,128)(2,1)} %copy-done.1, f32[8,128]{1,0:T(8,128)} %get-tuple-element.65.refs_3_), custom_call_target="tpu_custom_call" | custom-call | tf_op jit(solution)/shard_map/merge/pallas_call | solution.py:32
  110.3 30.2 %all-to-all-done.3.refs_2_ = bf16[8,2,320,256]{3,2,1,0:T(8,128)(2,1)} async-done(((bf16[8,2,320,256]{3,2,1,0:T(8,128)(2,1)}), bf16[8,2,320,256]{3,2,1,0:T(8,128)(2,1)}, u32[]{:S(2)}, u32[]{:S(2)}) %all-to-all-start.3) | async-done | bytes 2621472 | tf_op jit(solution)/shard_map/all_to_all | solution.py:327
  140.5 5.8 %merge.10 = (bf16[8,320,256]{2,1,0:T(8,128)(2,1)}, f32[8,128]{1,0:T(8,128)}) custom-call(s32[32]{0:T(128)} %pad_add_fusion.1.refs_0_, f32[480]{0:T(512)} %mul.53.refs_1_, bf16[8,2,320,256]{3,2,1,0:T(8,128)(2,1)} %all-to-all-done.3.refs_2_, f32[8,128]{1,0:T(8,128)} %get-tuple-element.70.refs_3_), custom_call_target="tpu_custom_call" | custom-call | tf_op jit(solution)/shard_map/merge/pallas_call | solution.py:32
  147.1 5.4 %merge.11 = (bf16[8,320,128]{2,1,0:T(8,128)(2,1)}, f32[8,128]{1,0:T(8,128)}) custom-call(s32[32]{0:T(128)} %pad_add_fusion.1.refs_0_, f32[480]{0:T(512)} %mul.53.refs_1_, bf16[8,2,320,128]{3,2,1,0:T(8,128)(2,1)} %copy-done.2, bf16[8,320,128]{2,1,0:T(8,128)(2,1)} %copy-done.16, f32[8,128]{1,0:T(8,128)} %get-tuple-element.71.refs_4_), custom_call_target="tpu_custom_call" | custom-call | tf_op jit(solution)/shard_map/merge/pallas_call | solution.py:32
  152.4 15.1 %all_to_all.50 = bf16[8,320,128]{2,1,0:T(8,128)(2,1)} all-to-all(bf16[8,320,128]{2,1,0:T(8,128)(2,1)} %get-tuple-element.72), channel_id=1, replica_groups={{0,1,2,3,4,5,6,7},{8,9,10,11,12,13,14,15},{16,17,18,19,20,21,22,23},{24..., dimensions={0} | all-to-all | bytes 1310720 | tf_op jit(solution)/shard_map/all_to_all | solution.py:327
  172.8 26.8 %all-to-all-done.2.refs_2_ = bf16[8,2,320,128]{3,2,1,0:T(8,128)(2,1)S(1)} async-done(((bf16[8,2,320,128]{3,2,1,0:T(8,128)(2,1)}), bf16[8,2,320,128]{3,2,1,0:T(8,128)(2,1)S(1)}, u32[]{:S(2)}, u32[]{:S(2)}) %all-to-all-start.2) | async-done | bytes 1310752 | tf_op jit(solution)/shard_map/all_to_all | solution.py:327
  205.7 5.6 %convolution_convert_fusion = bf16[16,48,2560]{2,1,0:T(8,128)(2,1)} fusion(bf16[16,64,2560]{2,1,0:T(8,128)(2,1)} %all-gather.2.cloned.1.call-done, s32[16,64]{1,0:T(8,128)S(1)} %bitcast.49, pred[16,64]{1,0:T(8,128)(4,1)S(1)} %bitcast.52), kind=kOutput, calls=%fused_computation.4 | convolution fusion | flops 253722624 | bytes 9180160 | tf_op jit(solution)/shard_map/jct,jtd->jcd/dot_general | solution.py:386
  217.5 13.9 %collective-permute-done.4.refs_3_ = bf16[8,320,256]{2,1,0:T(8,128)(2,1)S(1)} collective-permute-done((bf16[8,320,256]{2,1,0:T(8,128)(2,1)}, bf16[8,320,256]{2,1,0:T(8,128)(2,1)S(1)}, u32[]{:S(2)}, u32[]{:S(2)}) %collective-permute-start.4) | collective-permute-done | bytes 1310752 | tf_op jit(solution)/shard_map/ppermute | solution.py:396
  232.5 6.2 %merge.13 = (bf16[8,320,256]{2,1,0:T(8,128)(2,1)}, f32[8,128]{1,0:T(8,128)}) custom-call(s32[32]{0:T(128)} %pad_add_fusion.1.refs_0_, f32[480]{0:T(512)} %mul.53.refs_1_, bf16[8,2,320,256]{3,2,1,0:T(8,128)(2,1)} %copy-done.1, bf16[8,320,256]{2,1,0:T(8,128)(2,1)} %copy-done.11, f32[8,128]{1,0:T(8,128)} %get-tuple-element.79.refs_4_), custom_call_target="tpu_custom_call" | custom-call | tf_op jit(solution)/shard_map/merge/pallas_call | solution.py:32
  242.8 29.8 %all-to-all-done.5 = bf16[8,320,256]{2,1,0:T(8,128)(2,1)S(1)} async-done(((bf16[8,320,256]{2,1,0:T(8,128)(2,1)}), bf16[8,320,256]{2,1,0:T(8,128)(2,1)S(1)}, u32[]{:S(2)}, u32[]{:S(2)}) %all-to-all-start.5) | async-done | bytes 1310752 | tf_op jit(solution)/shard_map/all_to_all | solution.py:327
  273.7 28.9 %collective-permute-done.7.refs_3_ = bf16[8,320,256]{2,1,0:T(8,128)(2,1)S(1)} collective-permute-done((bf16[8,320,256]{2,1,0:T(8,128)(2,1)}, bf16[8,320,256]{2,1,0:T(8,128)(2,1)S(1)}, u32[]{:S(2)}, u32[]{:S(2)}) %collective-permute-start.7) | collective-permute-done | bytes 1310752 | tf_op jit(solution)/shard_map/ppermute | solution.py:396
  303.7 6.2 %merge.14 = (bf16[8,320,256]{2,1,0:T(8,128)(2,1)}, f32[8,128]{1,0:T(8,128)}) custom-call(s32[32]{0:T(128)} %pad_add_fusion.1.refs_0_, f32[480]{0:T(512)} %mul.53.refs_1_, bf16[8,2,320,256]{3,2,1,0:T(8,128)(2,1)} %all-to-all-done.3.refs_2_, bf16[8,320,256]{2,1,0:T(8,128)(2,1)} %copy-done.12, f32[8,128]{1,0:T(8,128)} %get-tuple-element.86.refs_4_), custom_call_target="tpu_custom_call" | custom-call | tf_op jit(solution)/shard_map/merge/pallas_call | solution.py:32
  316.1 26.9 %all-to-all-done.6 = bf16[8,320,256]{2,1,0:T(8,128)(2,1)S(1)} async-done(((bf16[8,320,256]{2,1,0:T(8,128)(2,1)}), bf16[8,320,256]{2,1,0:T(8,128)(2,1)S(1)}, u32[]{:S(2)}, u32[]{:S(2)}) %all-to-all-start.6) | async-done | bytes 1310752 | tf_op jit(solution)/shard_map/all_to_all | solution.py:327
  344.8 6.9 %run_chunk.5 = (bf16[1,2560,768]{2,1,0:T(8,128)(2,1)}, bf16[1,2560,768]{2,1,0:T(8,128)(2,1)}, bf16[16,48,256]{2,1,0:T(8,128)(2,1)}, f32[8,128]{1,0:T(8,128)}) custom-call(s32[2]{0:T(128)} %pad_add_fusion.refs_0_, bf16[768,2560]{1,0:T(8,128)(2,1)} %bitcast.38, ...), custom_call_target="tpu_custom_call", output_to_operand_aliasing={{0}: (4, {}), {1}: (5, {})} | custom-call | tf_op jit(solution)/shard_map/run_chunk/pallas_call | solution.py:32
  363.5 8.5 %all-to-all-done.7 = bf16[8,320,128]{2,1,0:T(8,128)(2,1)S(1)} async-done(((bf16[8,320,128]{2,1,0:T(8,128)(2,1)}), bf16[8,320,128]{2,1,0:T(8,128)(2,1)S(1)}, u32[]{:S(2)}, u32[]{:S(2)}) %all-to-all-start.7) | async-done | bytes 655392 | tf_op jit(solution)/shard_map/all_to_all | solution.py:327
  374.5 19.0 %collective-permute-done.9.refs_3_ = bf16[2560,256]{1,0:T(8,128)(2,1)S(1)} collective-permute-done((bf16[2560,256]{1,0:T(8,128)(2,1)S(1)}, bf16[2560,256]{1,0:T(8,128)(2,1)S(1)}, u32[]{:S(2)}, u32[]{:S(2)}) %collective-permute-start.9) | collective-permute-done | bytes 1310752 | tf_op jit(solution)/shard_map/ppermute | solution.py:404
  394.5 7.0 %run_chunk.6 = (bf16[1,2560,768]{2,1,0:T(8,128)(2,1)}, bf16[1,2560,768]{2,1,0:T(8,128)(2,1)}, bf16[16,48,256]{2,1,0:T(8,128)(2,1)}, f32[8,128]{1,0:T(8,128)}) custom-call(s32[2]{0:T(128)} %pad_add_fusion.refs_0_, bf16[768,2560]{1,0:T(8,128)(2,1)} %bitcast.39, ...), custom_call_target="tpu_custom_call", output_to_operand_aliasing={{0}: (4, {}), {1}: (5, {})} | custom-call | tf_op jit(solution)/shard_map/run_chunk/pallas_call | solution.py:32
  413.2 28.2 %all_to_all.51.refs_1_ = bf16[16,48,640]{2,1,0:T(8,128)(2,1)} all-to-all(bf16[16,48,640]{2,1,0:T(8,128)(2,1)} %get-tuple-element.107), channel_id=1, replica_groups=mesh['groups'=2,'expert'=16,'mp'=1] {'expert'}, dimensions={0} | all-to-all | bytes 1966080 | tf_op jit(solution)/shard_map/all_to_all | solution.py:416
  448.0 7.1 %all-to-all-done.9 = bf16[16,48,128]{2,1,0:T(8,128)(2,1)S(1)} async-done(((bf16[16,48,128]{2,1,0:T(8,128)(2,1)}), bf16[16,48,128]{2,1,0:T(8,128)(2,1)S(1)}, u32[]{:S(2)}, u32[]{:S(2)}) %all-to-all-start.9) | async-done | bytes 196640 | tf_op jit(solution)/shard_map/all_to_all | solution.py:416
  (150 shorter events, 122.0 us)
Async XLA Ops:
  11.3 33.6 %all-to-all-start = ((bf16[8,2,320,128]{3,2,1,0:T(8,128)(2,1)}), bf16[8,2,320,128]{3,2,1,0:T(8,128)(2,1)S(1)}, u32[]{:S(2)}, u32[]{:S(2)}) async-start(bf16[8,2,320,128]{3,2,1,0:T(8,128)(2,1)} %get-tuple-element.59), calls=%async_computation | async-start | bytes 2621440 | tf_op jit(solution)/shard_map/all_to_all | solution.py:327
  16.7 22.2 %collective-permute-start = (bf16[64,2560]{1,0:T(8,128)(2,1)S(1)}, bf16[64,2560]{1,0:T(8,128)(2,1)S(1)}, u32[]{:S(2)}, u32[]{:S(2)}) collective-permute-start(bf16[64,2560]{1,0:T(8,128)(2,1)S(1)} %copy-done.18), channel_id=1, source_target_pairs={{0,8},{1,9},{2,10},{3,11},{4,12},{5,13},{6,14},{7,15},{8,0},{9,1},... | collective-permute-start | bytes 983048 | tf_op jit(solution)/shard_map/ppermute | solution.py:375
  44.9 7.9 %copy-start.24 = (s32[1024,6]{0,1:T(8,128)S(1)}, s32[1024,6]{0,1:T(8,128)}, u32[]{:S(2)}) copy-start(s32[1024,6]{0,1:T(8,128)} %param.9) | copy-start | bytes 73732
  46.0 40.4 %all-to-all-start.1 = ((bf16[8,2,320,256]{3,2,1,0:T(8,128)(2,1)}), bf16[8,2,320,256]{3,2,1,0:T(8,128)(2,1)S(1)}, u32[]{:S(2)}, u32[]{:S(2)}) async-start(bf16[8,2,320,256]{3,2,1,0:T(8,128)(2,1)} %get-tuple-element.64), calls=%async_computation.1 | async-start | bytes 5242880 | tf_op jit(solution)/shard_map/all_to_all | solution.py:327
  53.3 9.0 %copy-start.22 = (f32[32,20,6]{0,1,2:T(8,128)S(1)}, f32[32,20,6]{0,1,2:T(8,128)}, u32[]{:S(2)}) copy-start(f32[32,20,6]{0,1,2:T(8,128)} %param.12) | copy-start | bytes 46084
  70.5 28.3 %collective-permute-start.1 = (bf16[2,64,2560]{2,1,0:T(8,128)(2,1)}, bf16[2,64,2560]{2,1,0:T(8,128)(2,1)}, u32[]{:S(2)}, u32[]{:S(2)}) collective-permute-start(bf16[2,64,2560]{2,1,0:T(8,128)(2,1)} %get-tuple-element.58.refs_1_), channel_id=1, source_target_pairs={{0,4},{1,5},{2,6},{3,7},{4,0},{5,1},{6,2},{7,3},{8,12},{9,13},{10,... | collective-permute-start | bytes 1966088 | tf_op jit(solution)/shard_map/ppermute | solution.py:382
  87.9 52.6 %all-to-all-start.3 = ((bf16[8,2,320,256]{3,2,1,0:T(8,128)(2,1)}), bf16[8,2,320,256]{3,2,1,0:T(8,128)(2,1)}, u32[]{:S(2)}, u32[]{:S(2)}) async-start(bf16[8,2,320,256]{3,2,1,0:T(8,128)(2,1)} %get-tuple-element.69), calls=%async_computation.3 | async-start | bytes 5242880 | tf_op jit(solution)/shard_map/all_to_all | solution.py:327
  92.3 8.9 %copy-start.27 = (bf16[8,320,128]{2,1,0:T(8,128)(2,1)S(1)}, bf16[8,320,128]{2,1,0:T(8,128)(2,1)}, u32[]{:S(2)}) copy-start(bf16[8,320,128]{2,1,0:T(8,128)(2,1)} %get-tuple-element.68) | copy-start | bytes 1966084
  92.3 113.4 %all-gather.2.cloned.1.call-start = ((), (), s32[]{:S(2)}) async-start(), calls=%async_computation.10 | async-start | bytes 6553600 | tf_op jit(solution)/shard_map/all_gather | solution.py:385
  101.2 45.0 %collective-permute-start.2 = (bf16[8,320,128]{2,1,0:T(8,128)(2,1)S(1)}, bf16[8,320,128]{2,1,0:T(8,128)(2,1)S(1)}, u32[]{:S(2)}, u32[]{:S(2)}) collective-permute-start(bf16[8,320,128]{2,1,0:T(8,128)(2,1)S(1)} %copy-done.27), channel_id=1, source_target_pairs={{0,8},{1,9},{2,10},{3,11},{4,12},{5,13},{6,14},{7,15},{8,0},{9,1},... | collective-permute-start | bytes 1966088 | tf_op jit(solution)/shard_map/ppermute | solution.py:396
  167.5 32.1 %all-to-all-start.2 = ((bf16[8,2,320,128]{3,2,1,0:T(8,128)(2,1)}), bf16[8,2,320,128]{3,2,1,0:T(8,128)(2,1)S(1)}, u32[]{:S(2)}, u32[]{:S(2)}) async-start(bf16[8,2,320,128]{3,2,1,0:T(8,128)(2,1)} %get-tuple-element.67), calls=%async_computation.2 | async-start | bytes 2621440 | tf_op jit(solution)/shard_map/all_to_all | solution.py:327
  171.1 60.3 %collective-permute-start.4 = (bf16[8,320,256]{2,1,0:T(8,128)(2,1)}, bf16[8,320,256]{2,1,0:T(8,128)(2,1)S(1)}, u32[]{:S(2)}, u32[]{:S(2)}) collective-permute-start(bf16[8,320,256]{2,1,0:T(8,128)(2,1)} %get-tuple-element.76), channel_id=1, source_target_pairs={{0,8},{1,9},{2,10},{3,11},{4,12},{5,13},{6,14},{7,15},{8,0},{9,1},... | collective-permute-start | bytes 3932168 | tf_op jit(solution)/shard_map/ppermute | solution.py:396
  171.2 40.1 %collective-permute-start.5 = (bf16[2560,128]{1,0:T(8,128)(2,1)}, bf16[2560,128]{1,0:T(8,128)(2,1)S(1)}, u32[]{:S(2)}, u32[]{:S(2)}) collective-permute-start(bf16[2560,128]{1,0:T(8,128)(2,1)} %get-tuple-element.77.refs_2_), channel_id=1, source_target_pairs={{0,16},{16,0},{1,17},{17,1},{2,18},{18,2},{3,19},{19,3},{4,20},{20... | collective-permute-start | bytes 1966088 | tf_op jit(solution)/shard_map/ppermute | solution.py:404
  238.7 33.9 %all-to-all-start.5 = ((bf16[8,320,256]{2,1,0:T(8,128)(2,1)}), bf16[8,320,256]{2,1,0:T(8,128)(2,1)S(1)}, u32[]{:S(2)}, u32[]{:S(2)}) async-start(bf16[8,320,256]{2,1,0:T(8,128)(2,1)} %get-tuple-element.80), calls=%async_computation.5 | async-start | bytes 2621440 | tf_op jit(solution)/shard_map/all_to_all | solution.py:327
  242.3 60.3 %collective-permute-start.7 = (bf16[8,320,256]{2,1,0:T(8,128)(2,1)}, bf16[8,320,256]{2,1,0:T(8,128)(2,1)S(1)}, u32[]{:S(2)}, u32[]{:S(2)}) collective-permute-start(bf16[8,320,256]{2,1,0:T(8,128)(2,1)} %get-tuple-element.85), channel_id=1, source_target_pairs={{0,8},{1,9},{2,10},{3,11},{4,12},{5,13},{6,14},{7,15},{8,0},{9,1},... | collective-permute-start | bytes 3932168 | tf_op jit(solution)/shard_map/ppermute | solution.py:396
  309.9 33.1 %all-to-all-start.6 = ((bf16[8,320,256]{2,1,0:T(8,128)(2,1)}), bf16[8,320,256]{2,1,0:T(8,128)(2,1)S(1)}, u32[]{:S(2)}, u32[]{:S(2)}) async-start(bf16[8,320,256]{2,1,0:T(8,128)(2,1)} %get-tuple-element.87), calls=%async_computation.6 | async-start | bytes 2621440 | tf_op jit(solution)/shard_map/all_to_all | solution.py:327
  313.8 31.0 %collective-permute-start.6 = (bf16[2560,256]{1,0:T(8,128)(2,1)S(1)}, bf16[2560,256]{1,0:T(8,128)(2,1)}, u32[]{:S(2)}, u32[]{:S(2)}) collective-permute-start(bf16[2560,256]{1,0:T(8,128)(2,1)S(1)} %copy-done.7), channel_id=1, source_target_pairs={{0,16},{16,0},{1,17},{17,1},{2,18},{18,2},{3,19},{19,3},{4,20},{20... | collective-permute-start | bytes 3932168 | tf_op jit(solution)/shard_map/ppermute | solution.py:404
  315.4 36.3 %collective-permute-start.3 = (bf16[8,320,128]{2,1,0:T(8,128)(2,1)}, bf16[8,320,128]{2,1,0:T(8,128)(2,1)S(1)}, u32[]{:S(2)}, u32[]{:S(2)}) collective-permute-start(bf16[8,320,128]{2,1,0:T(8,128)(2,1)} %get-tuple-element.75), channel_id=1, source_target_pairs={{0,8},{1,9},{2,10},{3,11},{4,12},{5,13},{6,14},{7,15},{8,0},{9,1},... | collective-permute-start | bytes 1966088 | tf_op jit(solution)/shard_map/ppermute | solution.py:396
  351.7 10.1 %copy-start.5 = (bf16[2560,256]{1,0:T(8,128)(2,1)S(1)}, bf16[2560,256]{1,0:T(8,128)(2,1)}, u32[]{:S(2)}) copy-start(bf16[2560,256]{1,0:T(8,128)(2,1)} %get-tuple-element.94.refs_2_) | copy-start | bytes 3932164
  357.9 14.1 %all-to-all-start.7 = ((bf16[8,320,128]{2,1,0:T(8,128)(2,1)}), bf16[8,320,128]{2,1,0:T(8,128)(2,1)S(1)}, u32[]{:S(2)}, u32[]{:S(2)}) async-start(bf16[8,320,128]{2,1,0:T(8,128)(2,1)} %get-tuple-element.91), calls=%async_computation.7 | async-start | bytes 1310720 | tf_op jit(solution)/shard_map/all_to_all | solution.py:327
  361.8 31.7 %collective-permute-start.9 = (bf16[2560,256]{1,0:T(8,128)(2,1)S(1)}, bf16[2560,256]{1,0:T(8,128)(2,1)S(1)}, u32[]{:S(2)}, u32[]{:S(2)}) collective-permute-start(bf16[2560,256]{1,0:T(8,128)(2,1)S(1)} %copy-done.5), channel_id=1, source_target_pairs={{0,16},{16,0},{1,17},{17,1},{2,18},{18,2},{3,19},{19,3},{4,20},{20... | collective-permute-start | bytes 3932168 | tf_op jit(solution)/shard_map/ppermute | solution.py:404
  372.9 34.1 %collective-permute-start.8 = (bf16[2560,128]{1,0:T(8,128)(2,1)}, bf16[2560,128]{1,0:T(8,128)(2,1)S(1)}, u32[]{:S(2)}, u32[]{:S(2)}) collective-permute-start(bf16[2560,128]{1,0:T(8,128)(2,1)} %get-tuple-element.93.refs_2_), channel_id=1, source_target_pairs={{0,16},{16,0},{1,17},{17,1},{2,18},{18,2},{3,19},{19,3},{4,20},{20... | collective-permute-start | bytes 1966088 | tf_op jit(solution)/shard_map/ppermute | solution.py:404
  413.2 32.9 %copy-start.9 = (pred[384,768]{1,0:T(32,128)(4,1)S(1)}, pred[384,768]{1,0:T(32,128)(4,1)}, u32[]{:S(2)}) copy-start(pred[384,768]{1,0:T(32,128)(4,1)} %convert_element_type.25) | copy-start | bytes 884740
  441.4 13.7 %all-to-all-start.9 = ((bf16[16,48,128]{2,1,0:T(8,128)(2,1)}), bf16[16,48,128]{2,1,0:T(8,128)(2,1)S(1)}, u32[]{:S(2)}, u32[]{:S(2)}) async-start(bf16[16,48,128]{2,1,0:T(8,128)(2,1)} %get-tuple-element.110), calls=%async_computation.9 | async-start | bytes 393216 | tf_op jit(solution)/shard_map/all_to_all | solution.py:416
  (23 other events, 55.3 us)
Sparse Core Ops, SparseCore 0:
  101.3 51.8 all-gather.1

commit v7 on v6

--- a/solution.py
+++ b/solution.py
@@ -121,8 +121,11 @@
     first = start // BLOCK
     base_slot = 0 if received is None else devices * sources
 
+    middle = devices // 2
+    halves = (slice(0, middle), slice(middle, devices))
+
     def kernel(slots_ref, factors_ref, rows_ref, *rest):
-        out_ref, total = rest[-2:]
+        total = rest[-1]
         piece = pl.program_id(0)
 
         @pl.when(piece == 0)
@@ -130,7 +133,8 @@
             if received is None:
                 total[...] = jnp.zeros_like(total)
             else:
-                total[...] = rest[0][...].astype(jnp.float32)
+                for part, share in enumerate(halves):
+                    total[share] = rest[part][...].astype(jnp.float32)
 
         for number in range(sources):
             source = piece * sources + number
@@ -150,23 +154,28 @@
 
         @pl.when(piece == devices - 1)
         def _():
-            out_ref[...] = total[...].astype(jnp.bfloat16)
+            if received is None:
+                for part, share in enumerate(halves):
+                    rest[part][...] = total[share].astype(jnp.bfloat16)
+            else:
+                rest[2][...] = total[...].astype(jnp.bfloat16)
 
     whole = pl.BlockSpec((devices, rows, width), lambda i: (0, 0, 0))
-    extra = () if received is None else (received,)
-    (merged,), token = step_call(
+    half = pl.BlockSpec((middle, rows, width), lambda i: (0, 0, 0))
+    extra = () if received is None else tuple(received)
+    out_count = 2 if received is None else 1
+    return step_call(
         kernel,
         token,
         (slots, factors, rows_of, *extra),
         [SMEM, SMEM, pl.BlockSpec((1, sources, rows, width), lambda i: (i, 0, 0, 0))]
-        + [whole] * len(extra),
-        [jax.ShapeDtypeStruct((devices, rows, width), jnp.bfloat16)],
-        [whole],
+        + [half] * len(extra),
+        [jax.ShapeDtypeStruct((devices // out_count, rows, width), jnp.bfloat16)] * out_count,
+        [whole] if received is not None else [half, half],
         grid=(devices,),
         scratch_shapes=[pltpu.VMEM((devices, rows, width), jnp.float32)],
         name="merge",
     )
-    return merged, token
 
 
 def pair(token, tokens, other):
@@ -270,21 +279,29 @@
 
 
 def plan(count):
-    order = [("pack", 0), ("pair", 0)]
-    for chunk in range(count):
+    order = [("pack", 0)]
+    for chunk in range(count + 1):
         if chunk + 1 < count:
             order.append(("pack", chunk + 1))
-        order.append(("partial", chunk))
+        if chunk >= 2:
+            order.append(("trade", chunk - 2))
+        if chunk < count:
+            order.append(("partial", chunk))
         if chunk == 0:
+            order.append(("pair", 0))
+        if chunk == 1:
             order.append(("line", 0))
-        if chunk >= 2:
-            order.extend([("finish", chunk - 2), ("trade", chunk - 2)])
-    for chunk in range(max(0, count - 2), count):
-        order.extend([("finish", chunk), ("trade", chunk)])
-    for chunk in range(count):
-        place = order.index(("trade", chunk))
-        later = [i for i, (name, _) in enumerate(order) if i > place and name in ("partial", "trade")]
-        order.insert(later[0] + 1 if later else len(order), ("run", chunk))
+        if chunk >= 1:
+            order.append(("finish", chunk - 1))
+        if chunk >= 3:
+            order.append(("run", chunk - 3))
+        if chunk >= 1:
+            order.append(("back", chunk - 1))
+    order.append(("run", count - 2))
+    order.append(("trade", count - 1))
+    order.append(("give", 0))
+    order.append(("run", count - 1))
+    order.append(("give", 1))
     return order
 
 
@@ -373,8 +390,8 @@
     starts = [BLOCK * sum(widths[:chunk]) for chunk in range(len(widths))]
     token = jnp.zeros(TOKEN.shape, TOKEN.dtype)
     opposite = lax.ppermute(tokens, "expert", across)
-    gathered, received, own, partner, hiddens = ({} for _ in range(5))
-    outputs = ()
+    gathered, received, merged, own, partner, hiddens = ({} for _ in range(6))
+    outputs, returned, last = (), [], len(widths) - 1
     for name, c in plan(len(widths)):
         start, width = starts[c], widths[c] * BLOCK
         if name == "pair":
@@ -393,32 +410,38 @@
             gathered[c] = exchange(pieces)
         elif name == "partial":
             partial, token = merge(token, slots, factors, gathered[c], None, start, blocks_of_rows)
-            received[c] = lax.ppermute(partial, "expert", across)
+            received[c] = [lax.ppermute(part, "expert", across) for part in partial]
         elif name == "finish":
-            merged, token = merge(
+            (merged[c],), token = merge(
                 token, slots, factors, gathered[c], received[c], start, blocks_of_rows
             )
-            own[c] = exchange(merged)
+        elif name == "back":
+            earlier = [gathered[c + 2]] if c + 2 in gathered else []
+            earlier += [received[c + 1][0]] if c + 1 in received else []
+            merged[c], token = hold(token, merged[c], earlier)
+            own[c] = exchange(merged[c])
         elif name == "trade":
             own[c], token = hold(token, own[c].reshape(depth, width), [])
             partner[c] = lax.ppermute(own[c], "groups", partners)
-        else:
+        elif name == "run":
             (*outputs, hiddens[c]), token = run_chunk(
                 token, info, grouped, own[c], partner[c], outputs, start, full, blocks
             )
-
-    last = len(widths) - 1
-    finished = []
-    before = []
-    for batch in (range(last), range(last, last + 1)):
-        hidden = jnp.concatenate([hiddens[c] for c in batch], axis=2)
-        hidden, token = hold(token, hidden, before)
-        returned = lax.all_to_all(hidden, "expert", split_axis=0, concat_axis=0, tiled=True)
-        before = [returned]
-        rows = returned.reshape(expert_count * capacity, returned.shape[2])
-        finished.append(
-            jnp.dot(picking, rows, preferred_element_type=jnp.float32).astype(jnp.bfloat16)
-        )
+        else:
+            batch = [hiddens[i] for i in (range(last) if c == 0 else range(last, last + 1))]
+            hidden, token = hold(token, jnp.concatenate(batch, axis=2), returned[:c])
+            returned.append(
+                lax.all_to_all(hidden, "expert", split_axis=0, concat_axis=0, tiled=True)
+            )
+
+    finished = [
+        jnp.dot(
+            picking,
+            part.reshape(expert_count * capacity, part.shape[2]),
+            preferred_element_type=jnp.float32,
+        ).astype(jnp.bfloat16)
+        for part in returned
+    ]
     output = jnp.concatenate(finished, axis=1)
     merged_gate, merged_up = outputs
     return (merged_gate, merged_up, output.reshape(tok_dev, top_count, full))

time: 466 us -> 471 us (1.011)
  blocking collectives: 43.3 us -> 0 us
  waiting for transfers between devices: 220 us -> 253 us
  starting transfers between devices: 49.1 us -> 66.7 us
    ppermute x4 -> x8, waiting for transfers between devices: 42.8 us -> 101 us  [shards(): received[c] = [lax.ppermute(part, 'expert', across) for part in partial]]
    all_to_all x7 -> x8, waiting for transfers between devices: 122 us -> 69.4 us  [exchange(): lax.all_to_all(pieces, 'expert', 0, 0, tiled=True, axis_index_groups=by_h...]
    all_to_all x2 -> x0, blocking collectives: 43.3 us -> none  [the longest x1 28.2 us: shards(): lax.all_to_all(hidden, 'expert', split_axis=0, concat_axis=0, tiled=True)]
    ppermute x1, waiting for transfers between devices: 5.67 us -> 21 us  [shards(): nearby = lax.ppermute(both, 'expert', beside)]
    ppermute x4, waiting for transfers between devices: 23.1 us -> 31.2 us  [shards(): partner[c] = lax.ppermute(own[c], 'groups', partners)]
    ppermute x4 -> x8, starting transfers between devices: 1.37 us -> 9.37 us  [shards(): received[c] = [lax.ppermute(part, 'expert', across) for part in partial]]
    all_to_all x1 -> x2, starting transfers between devices: 4.73 us -> 11.6 us  [shards(): lax.all_to_all(hidden, 'expert', split_axis=0, concat_axis=0, tiled=True)]
    all_to_all x7 -> x8, starting transfers between devices: 31.5 us -> 34.4 us  [exchange(): lax.all_to_all(pieces, 'expert', 0, 0, tiled=True, axis_index_groups=by_h...]
  transfers between devices with their start and end apart: 19 -> 25, of which waited for: 13 -> 13; matrix products, arithmetic and copies ran while one was open for 7% -> 6% of each run, Pallas kernels for 13% -> 18%
where the time goes in v7:
time: 471 us; the launch traced here: 469 us
  waiting for transfers between devices  253 us (54%)
  Pallas kernels  85.9 us (18%)
  starting transfers between devices  66.7 us (14%)
  local copies, waits for them, and re-layouts  24.9 us (5%)
  other arithmetic  15.6 us (3%)
  between operations  14.6 us (3%)
  matrix products  7.74 us (2%)
    ppermute x8, waiting for transfers between devices, shards(): received[c] = [lax.ppermute(part, 'expert', across) for part in partial]  101 us
    pallas_call x28, Pallas kernels, step_call(): pl.pallas_call(ordered, out_shape=[*out_shape, TOKEN], in_specs=[*in_spec...  85.9 us
    all_to_all x8, waiting for transfers between devices, exchange(): lax.all_to_all(pieces, 'expert', 0, 0, tiled=True, axis_index_groups=by_h...  69.4 us
    all_to_all x8, starting transfers between devices, exchange(): lax.all_to_all(pieces, 'expert', 0, 0, tiled=True, axis_index_groups=by_h...  34.4 us
    ppermute x4, waiting for transfers between devices, shards(): partner[c] = lax.ppermute(own[c], 'groups', partners)  31.2 us
    ppermute x1, waiting for transfers between devices, shards(): opposite = lax.ppermute(tokens, 'expert', across)  23.6 us
    ppermute x1, waiting for transfers between devices, shards(): nearby = lax.ppermute(both, 'expert', beside)  21 us
    unnamed x67, local copies, waits for them, and re-layouts  16.6 us
  transfers between devices with their start and end apart: 25, of which 13 were waited for; matrix products, arithmetic and copies ran while one was open for 6% of the time, Pallas kernels for 18%

profile of v7, /device:TPU:0, one launch (start us, length us, event | category | flops | bytes accessed | tf_op | source)
XLA Modules:
  0.0 469.0 jit_solution(10523571643185280351)
XLA Ops:
  19.9 14.0 %all-to-all-done.refs_2_ = bf16[8,2,320,128]{3,2,1,0:T(8,128)(2,1)S(1)} async-done(((bf16[8,2,320,128]{3,2,1,0:T(8,128)(2,1)}), bf16[8,2,320,128]{3,2,1,0:T(8,128)(2,1)S(1)}, u32[]{:S(2)}, u32[]{:S(2)}) %all-to-all-start) | async-done | bytes 1310752 | tf_op jit(solution)/shard_map/all_to_all | solution.py:344
  51.4 23.6 %collective-permute-done.refs_1_ = bf16[64,2560]{1,0:T(8,128)(2,1)} collective-permute-done((bf16[64,2560]{1,0:T(8,128)(2,1)S(1)}, bf16[64,2560]{1,0:T(8,128)(2,1)}, u32[]{:S(2)}, u32[]{:S(2)}) %collective-permute-start) | collective-permute-done | bytes 327712 | tf_op jit(solution)/shard_map/ppermute | solution.py:392
  81.8 7.0 %all-to-all-start.2 = ((bf16[8,2,320,256]{3,2,1,0:T(8,128)(2,1)}), bf16[8,2,320,256]{3,2,1,0:T(8,128)(2,1)S(1)}, u32[]{:S(2)}, u32[]{:S(2)}) async-start(bf16[8,2,320,256]{3,2,1,0:T(8,128)(2,1)} %get-tuple-element.82), calls=%async_computation.2 | async-start | bytes 5242880 | tf_op jit(solution)/shard_map/all_to_all | solution.py:344
  89.5 6.3 %fusion.7 = s32[16,64,16]{2,0,1:T(8,128)S(1)} fusion(s32[16,64,16]{2,0,1:T(8,128)S(1)} %copy.70), kind=kOutput, calls=%fused_computation.57 | output fusion | flops 1032192 | bytes 131072 | tf_op jit(solution)/shard_map/jit(cumsum)/reduce_window_sum | solution.py:312
  107.5 5.6 %merge.9 = (bf16[4,320,256]{2,1,0:T(8,128)(2,1)}, bf16[4,320,256]{2,1,0:T(8,128)(2,1)}, f32[8,128]{1,0:T(8,128)}) custom-call(s32[32]{0:T(128)} %pad_add_fusion.1.refs_0_, f32[480]{0:T(512)} %mul.52.refs_1_, bf16[8,2,320,256]{3,2,1,0:T(8,128)(2,1)} %copy-done.2, f32[8,128]{1,0:T(8,128)} %get-tuple-element.76.refs_3_), custom_call_target="tpu_custom_call" | custom-call | tf_op jit(solution)/shard_map/merge/pallas_call | solution.py:32
  113.2 21.0 %collective-permute-done.1.refs_2_ = bf16[2,64,2560]{2,1,0:T(8,128)(2,1)} collective-permute-done((bf16[2,64,2560]{2,1,0:T(8,128)(2,1)}, bf16[2,64,2560]{2,1,0:T(8,128)(2,1)}, u32[]{:S(2)}, u32[]{:S(2)}) %collective-permute-start.1) | collective-permute-done | bytes 655392 | tf_op jit(solution)/shard_map/ppermute | solution.py:399
  139.8 49.7 %collective-permute-done.2.refs_3_ = bf16[4,320,128]{2,1,0:T(8,128)(2,1)S(1)} collective-permute-done((bf16[4,320,128]{2,1,0:T(8,128)(2,1)}, bf16[4,320,128]{2,1,0:T(8,128)(2,1)S(1)}, u32[]{:S(2)}, u32[]{:S(2)}) %collective-permute-start.2) | collective-permute-done | bytes 327712 | tf_op jit(solution)/shard_map/ppermute | solution.py:413
  189.5 6.9 %collective-permute-done.3.refs_4_ = bf16[4,320,128]{2,1,0:T(8,128)(2,1)} collective-permute-done((bf16[4,320,128]{2,1,0:T(8,128)(2,1)}, bf16[4,320,128]{2,1,0:T(8,128)(2,1)}, u32[]{:S(2)}, u32[]{:S(2)}) %collective-permute-start.3) | collective-permute-done | bytes 327712 | tf_op jit(solution)/shard_map/ppermute | solution.py:413
  210.0 7.2 %all-to-all-done.4 = bf16[8,320,128]{2,1,0:T(8,128)(2,1)S(1)} async-done(((bf16[8,320,128]{2,1,0:T(8,128)(2,1)}), bf16[8,320,128]{2,1,0:T(8,128)(2,1)S(1)}, u32[]{:S(2)}, u32[]{:S(2)}) %all-to-all-start.4) | async-done | bytes 655392 | tf_op jit(solution)/shard_map/all_to_all | solution.py:344
  220.8 5.6 %merge.11 = (bf16[4,320,256]{2,1,0:T(8,128)(2,1)}, bf16[4,320,256]{2,1,0:T(8,128)(2,1)}, f32[8,128]{1,0:T(8,128)}) custom-call(s32[32]{0:T(128)} %pad_add_fusion.1.refs_0_, f32[480]{0:T(512)} %mul.52.refs_1_, bf16[8,2,320,256]{3,2,1,0:T(8,128)(2,1)} %copy-done.1, f32[8,128]{1,0:T(8,128)} %get-tuple-element.90.refs_3_), custom_call_target="tpu_custom_call" | custom-call | tf_op jit(solution)/shard_map/merge/pallas_call | solution.py:32
  229.5 38.1 %collective-permute-done.5.refs_4_ = bf16[4,320,256]{2,1,0:T(8,128)(2,1)S(1)} collective-permute-done((bf16[4,320,256]{2,1,0:T(8,128)(2,1)}, bf16[4,320,256]{2,1,0:T(8,128)(2,1)S(1)}, u32[]{:S(2)}, u32[]{:S(2)}) %collective-permute-start.5) | collective-permute-done | bytes 655392 | tf_op jit(solution)/shard_map/ppermute | solution.py:413
  268.5 6.2 %merge.12 = (bf16[8,320,256]{2,1,0:T(8,128)(2,1)}, f32[8,128]{1,0:T(8,128)}) custom-call(s32[32]{0:T(128)} %pad_add_fusion.1.refs_0_, f32[480]{0:T(512)} %mul.52.refs_1_, bf16[8,2,320,256]{3,2,1,0:T(8,128)(2,1)} %copy-done.2, bf16[4,320,256]{2,1,0:T(8,128)(2,1)} %copy-done.14, bf16[4,320,256]{2,1,0:T(8,128)(2,1)} %copy-done.21, ...), custom_call_target="tpu_custom_call" | custom-call | tf_op jit(solution)/shard_map/merge/pallas_call | solution.py:32
  274.7 6.4 %collective-permute-done.6.refs_2_.refs_3_ = bf16[4,320,256]{2,1,0:T(8,128)(2,1)S(1)} collective-permute-done((bf16[4,320,256]{2,1,0:T(8,128)(2,1)}, bf16[4,320,256]{2,1,0:T(8,128)(2,1)S(1)}, u32[]{:S(2)}, u32[]{:S(2)}) %collective-permute-start.6) | collective-permute-done | bytes 655392 | tf_op jit(solution)/shard_map/ppermute | solution.py:413
  288.2 28.2 %all-to-all-done.5 = bf16[8,320,256]{2,1,0:T(8,128)(2,1)S(1)} async-done(((bf16[8,320,256]{2,1,0:T(8,128)(2,1)}), bf16[8,320,256]{2,1,0:T(8,128)(2,1)S(1)}, u32[]{:S(2)}, u32[]{:S(2)}) %all-to-all-start.5) | async-done | bytes 1310752 | tf_op jit(solution)/shard_map/all_to_all | solution.py:344
  322.5 6.3 %merge.14 = (bf16[8,320,256]{2,1,0:T(8,128)(2,1)}, f32[8,128]{1,0:T(8,128)}) custom-call(s32[32]{0:T(128)} %pad_add_fusion.1.refs_0_, f32[480]{0:T(512)} %mul.52.refs_1_, bf16[8,2,320,256]{3,2,1,0:T(8,128)(2,1)} %copy-done.1, bf16[4,320,256]{2,1,0:T(8,128)(2,1)} %copy-done.15, bf16[4,320,256]{2,1,0:T(8,128)(2,1)} %collective-permute-done.9.refs_4_, ...), custom_call_target="tpu_custom_call" | custom-call | tf_op jit(solution)/shard_map/merge/pallas_call | solution.py:32
  328.9 5.6 %convolution_convert_fusion = bf16[16,48,2560]{2,1,0:T(8,128)(2,1)} fusion(bf16[16,64,2560]{2,1,0:T(8,128)(2,1)} %all-gather.2.cloned.1.call-done, s32[16,64]{1,0:T(8,128)S(1)} %bitcast.49, pred[16,64]{1,0:T(8,128)(4,1)S(1)} %bitcast.52), kind=kOutput, calls=%fused_computation.4 | convolution fusion | flops 253722624 | bytes 9180160 | tf_op jit(solution)/shard_map/jct,jtd->jcd/dot_general | solution.py:403
  349.7 20.0 %all-to-all-done.6 = bf16[8,320,256]{2,1,0:T(8,128)(2,1)S(1)} async-done(((bf16[8,320,256]{2,1,0:T(8,128)(2,1)}), bf16[8,320,256]{2,1,0:T(8,128)(2,1)S(1)}, u32[]{:S(2)}, u32[]{:S(2)}) %all-to-all-start.6) | async-done | bytes 1310752 | tf_op jit(solution)/shard_map/all_to_all | solution.py:344
  378.5 6.9 %run_chunk.5 = (bf16[1,2560,768]{2,1,0:T(8,128)(2,1)}, bf16[1,2560,768]{2,1,0:T(8,128)(2,1)}, bf16[16,48,256]{2,1,0:T(8,128)(2,1)}, f32[8,128]{1,0:T(8,128)}) custom-call(s32[2]{0:T(128)} %pad_add_fusion.refs_0_, bf16[768,2560]{1,0:T(8,128)(2,1)} %bitcast.38, ...), custom_call_target="tpu_custom_call", output_to_operand_aliasing={{0}: (4, {}), {1}: (5, {})} | custom-call | tf_op jit(solution)/shard_map/run_chunk/pallas_call | solution.py:32
  389.0 15.7 %collective-permute-done.12.refs_3_ = bf16[2560,256]{1,0:T(8,128)(2,1)S(1)} collective-permute-done((bf16[2560,256]{1,0:T(8,128)(2,1)}, bf16[2560,256]{1,0:T(8,128)(2,1)S(1)}, u32[]{:S(2)}, u32[]{:S(2)}) %collective-permute-start.12) | collective-permute-done | bytes 1310752 | tf_op jit(solution)/shard_map/ppermute | solution.py:425
  405.8 7.0 %run_chunk.6 = (bf16[1,2560,768]{2,1,0:T(8,128)(2,1)}, bf16[1,2560,768]{2,1,0:T(8,128)(2,1)}, bf16[16,48,256]{2,1,0:T(8,128)(2,1)}, f32[8,128]{1,0:T(8,128)}) custom-call(s32[2]{0:T(128)} %pad_add_fusion.refs_0_, bf16[768,2560]{1,0:T(8,128)(2,1)} %bitcast.39, ...), custom_call_target="tpu_custom_call", output_to_operand_aliasing={{0}: (4, {}), {1}: (5, {})} | custom-call | tf_op jit(solution)/shard_map/run_chunk/pallas_call | solution.py:32
  415.7 5.9 %all-to-all-start.8 = ((bf16[16,48,640]{2,1,0:T(8,128)(2,1)}), bf16[16,48,640]{2,1,0:T(8,128)(2,1)S(1)}, u32[]{:S(2)}, u32[]{:S(2)}) async-start(bf16[16,48,640]{2,1,0:T(8,128)(2,1)} %get-tuple-element.131), calls=%async_computation.8 | async-start | bytes 1966080 | tf_op jit(solution)/shard_map/all_to_all | solution.py:434
  423.3 15.5 %collective-permute-done.13.refs_3_ = bf16[2560,128]{1,0:T(8,128)(2,1)S(1)} collective-permute-done((bf16[2560,128]{1,0:T(8,128)(2,1)S(1)}, bf16[2560,128]{1,0:T(8,128)(2,1)S(1)}, u32[]{:S(2)}, u32[]{:S(2)}) %collective-permute-start.13) | collective-permute-done | bytes 655392 | tf_op jit(solution)/shard_map/ppermute | solution.py:425
  445.9 5.7 %all-to-all-start.9 = ((bf16[16,48,128]{2,1,0:T(8,128)(2,1)}), bf16[16,48,128]{2,1,0:T(8,128)(2,1)S(1)}, u32[]{:S(2)}, u32[]{:S(2)}) async-start(bf16[16,48,128]{2,1,0:T(8,128)(2,1)} %get-tuple-element.134), calls=%async_computation.9 | async-start | bytes 393216 | tf_op jit(solution)/shard_map/all_to_all | solution.py:434
  453.5 7.1 %all-to-all-done.9 = bf16[16,48,128]{2,1,0:T(8,128)(2,1)S(1)} async-done(((bf16[16,48,128]{2,1,0:T(8,128)(2,1)}), bf16[16,48,128]{2,1,0:T(8,128)(2,1)S(1)}, u32[]{:S(2)}, u32[]{:S(2)}) %all-to-all-start.9) | async-done | bytes 196640 | tf_op jit(solution)/shard_map/all_to_all | solution.py:434
  (172 shorter events, 132.7 us)
Async XLA Ops:
  11.4 22.5 %all-to-all-start = ((bf16[8,2,320,128]{3,2,1,0:T(8,128)(2,1)}), bf16[8,2,320,128]{3,2,1,0:T(8,128)(2,1)S(1)}, u32[]{:S(2)}, u32[]{:S(2)}) async-start(bf16[8,2,320,128]{3,2,1,0:T(8,128)(2,1)} %get-tuple-element.69), calls=%async_computation | async-start | bytes 2621440 | tf_op jit(solution)/shard_map/all_to_all | solution.py:344
  35.1 45.2 %all-to-all-start.1 = ((bf16[8,2,320,256]{3,2,1,0:T(8,128)(2,1)}), bf16[8,2,320,256]{3,2,1,0:T(8,128)(2,1)S(1)}, u32[]{:S(2)}, u32[]{:S(2)}) async-start(bf16[8,2,320,256]{3,2,1,0:T(8,128)(2,1)} %get-tuple-element.74), calls=%async_computation.1 | async-start | bytes 5242880 | tf_op jit(solution)/shard_map/all_to_all | solution.py:344
  38.9 36.2 %collective-permute-start = (bf16[64,2560]{1,0:T(8,128)(2,1)S(1)}, bf16[64,2560]{1,0:T(8,128)(2,1)}, u32[]{:S(2)}, u32[]{:S(2)}) collective-permute-start(bf16[64,2560]{1,0:T(8,128)(2,1)S(1)} %copy-done.25), channel_id=1, source_target_pairs={{0,8},{1,9},{2,10},{3,11},{4,12},{5,13},{6,14},{7,15},{8,0},{9,1},... | collective-permute-start | bytes 983048 | tf_op jit(solution)/shard_map/ppermute | solution.py:392
  81.8 119.9 %all-to-all-start.2 = ((bf16[8,2,320,256]{3,2,1,0:T(8,128)(2,1)}), bf16[8,2,320,256]{3,2,1,0:T(8,128)(2,1)S(1)}, u32[]{:S(2)}, u32[]{:S(2)}) async-start(bf16[8,2,320,256]{3,2,1,0:T(8,128)(2,1)} %get-tuple-element.82), calls=%async_computation.2 | async-start | bytes 5242880 | tf_op jit(solution)/shard_map/all_to_all | solution.py:344
  88.8 240.1 %all-gather.2.cloned.1.call-start = ((), (), s32[]{:S(2)}) async-start(), calls=%async_computation.10 | async-start | bytes 6553600 | tf_op jit(solution)/shard_map/all_gather | solution.py:402
  99.5 34.7 %collective-permute-start.1 = (bf16[2,64,2560]{2,1,0:T(8,128)(2,1)}, bf16[2,64,2560]{2,1,0:T(8,128)(2,1)}, u32[]{:S(2)}, u32[]{:S(2)}) collective-permute-start(bf16[2,64,2560]{2,1,0:T(8,128)(2,1)} %get-tuple-element.73.refs_1_), channel_id=1, source_target_pairs={{0,4},{1,5},{2,6},{3,7},{4,0},{5,1},{6,2},{7,3},{8,12},{9,13},{10,... | collective-permute-start | bytes 1966088 | tf_op jit(solution)/shard_map/ppermute | solution.py:399
  136.7 65.0 %collective-permute-start.4 = (bf16[4,320,256]{2,1,0:T(8,128)(2,1)}, bf16[4,320,256]{2,1,0:T(8,128)(2,1)S(1)}, u32[]{:S(2)}, u32[]{:S(2)}) collective-permute-start(bf16[4,320,256]{2,1,0:T(8,128)(2,1)} %get-tuple-element.83), channel_id=1, source_target_pairs={{0,8},{1,9},{2,10},{3,11},{4,12},{5,13},{6,14},{7,15},{8,0},{9,1},... | collective-permute-start | bytes 1966088 | tf_op jit(solution)/shard_map/ppermute | solution.py:413
  136.8 52.7 %collective-permute-start.2 = (bf16[4,320,128]{2,1,0:T(8,128)(2,1)}, bf16[4,320,128]{2,1,0:T(8,128)(2,1)S(1)}, u32[]{:S(2)}, u32[]{:S(2)}) collective-permute-start(bf16[4,320,128]{2,1,0:T(8,128)(2,1)} %get-tuple-element.79), channel_id=1, source_target_pairs={{0,8},{1,9},{2,10},{3,11},{4,12},{5,13},{6,14},{7,15},{8,0},{9,1},... | collective-permute-start | bytes 983048 | tf_op jit(solution)/shard_map/ppermute | solution.py:413
  139.7 56.7 %collective-permute-start.3 = (bf16[4,320,128]{2,1,0:T(8,128)(2,1)}, bf16[4,320,128]{2,1,0:T(8,128)(2,1)}, u32[]{:S(2)}, u32[]{:S(2)}) collective-permute-start(bf16[4,320,128]{2,1,0:T(8,128)(2,1)} %get-tuple-element.80), channel_id=1, source_target_pairs={{0,8},{1,9},{2,10},{3,11},{4,12},{5,13},{6,14},{7,15},{8,0},{9,1},... | collective-permute-start | bytes 983048 | tf_op jit(solution)/shard_map/ppermute | solution.py:413
  217.1 63.9 %all-to-all-start.3 = ((bf16[8,2,320,128]{3,2,1,0:T(8,128)(2,1)}), bf16[8,2,320,128]{3,2,1,0:T(8,128)(2,1)S(1)}, u32[]{:S(2)}, u32[]{:S(2)}) async-start(bf16[8,2,320,128]{3,2,1,0:T(8,128)(2,1)} %get-tuple-element.86), calls=%async_computation.3 | async-start | bytes 2621440 | tf_op jit(solution)/shard_map/all_to_all | solution.py:344
  220.7 46.9 %collective-permute-start.5 = (bf16[4,320,256]{2,1,0:T(8,128)(2,1)}, bf16[4,320,256]{2,1,0:T(8,128)(2,1)S(1)}, u32[]{:S(2)}, u32[]{:S(2)}) collective-permute-start(bf16[4,320,256]{2,1,0:T(8,128)(2,1)} %get-tuple-element.87), channel_id=1, source_target_pairs={{0,8},{1,9},{2,10},{3,11},{4,12},{5,13},{6,14},{7,15},{8,0},{9,1},... | collective-permute-start | bytes 1966088 | tf_op jit(solution)/shard_map/ppermute | solution.py:413
  226.5 54.6 %collective-permute-start.6 = (bf16[4,320,256]{2,1,0:T(8,128)(2,1)}, bf16[4,320,256]{2,1,0:T(8,128)(2,1)S(1)}, u32[]{:S(2)}, u32[]{:S(2)}) collective-permute-start(bf16[4,320,256]{2,1,0:T(8,128)(2,1)} %get-tuple-element.93), channel_id=1, source_target_pairs={{0,8},{1,9},{2,10},{3,11},{4,12},{5,13},{6,14},{7,15},{8,0},{9,1},... | collective-permute-start | bytes 1966088 | tf_op jit(solution)/shard_map/ppermute | solution.py:413
  282.3 34.1 %all-to-all-start.5 = ((bf16[8,320,256]{2,1,0:T(8,128)(2,1)}), bf16[8,320,256]{2,1,0:T(8,128)(2,1)S(1)}, u32[]{:S(2)}, u32[]{:S(2)}) async-start(bf16[8,320,256]{2,1,0:T(8,128)(2,1)} %get-tuple-element.95), calls=%async_computation.5 | async-start | bytes 2621440 | tf_op jit(solution)/shard_map/all_to_all | solution.py:344
  286.0 36.5 %collective-permute-start.9 = (bf16[4,320,256]{2,1,0:T(8,128)(2,1)}, bf16[4,320,256]{2,1,0:T(8,128)(2,1)}, u32[]{:S(2)}, u32[]{:S(2)}) collective-permute-start(bf16[4,320,256]{2,1,0:T(8,128)(2,1)} %get-tuple-element.100), channel_id=1, source_target_pairs={{0,8},{1,9},{2,10},{3,11},{4,12},{5,13},{6,14},{7,15},{8,0},{9,1},... | collective-permute-start | bytes 1966088 | tf_op jit(solution)/shard_map/ppermute | solution.py:413
  286.6 47.8 %collective-permute-start.10 = (bf16[2560,128]{1,0:T(8,128)(2,1)S(1)}, bf16[2560,128]{1,0:T(8,128)(2,1)S(1)}, u32[]{:S(2)}, u32[]{:S(2)}) collective-permute-start(bf16[2560,128]{1,0:T(8,128)(2,1)S(1)} %copy-done.11), channel_id=1, source_target_pairs={{0,16},{16,0},{1,17},{17,1},{2,18},{18,2},{3,19},{19,3},{4,20},{20... | collective-permute-start | bytes 1966088 | tf_op jit(solution)/shard_map/ppermute | solution.py:425
  322.5 18.1 %collective-permute-start.7 = (bf16[4,320,128]{2,1,0:T(8,128)(2,1)}, bf16[4,320,128]{2,1,0:T(8,128)(2,1)S(1)}, u32[]{:S(2)}, u32[]{:S(2)}) collective-permute-start(bf16[4,320,128]{2,1,0:T(8,128)(2,1)} %get-tuple-element.98), channel_id=1, source_target_pairs={{0,8},{1,9},{2,10},{3,11},{4,12},{5,13},{6,14},{7,15},{8,0},{9,1},... | collective-permute-start | bytes 983048 | tf_op jit(solution)/shard_map/ppermute | solution.py:413
  341.4 28.3 %all-to-all-start.6 = ((bf16[8,320,256]{2,1,0:T(8,128)(2,1)}), bf16[8,320,256]{2,1,0:T(8,128)(2,1)S(1)}, u32[]{:S(2)}, u32[]{:S(2)}) async-start(bf16[8,320,256]{2,1,0:T(8,128)(2,1)} %get-tuple-element.106), calls=%async_computation.6 | async-start | bytes 2621440 | tf_op jit(solution)/shard_map/all_to_all | solution.py:344
  345.4 33.1 %collective-permute-start.11 = (bf16[2560,256]{1,0:T(8,128)(2,1)S(1)}, bf16[2560,256]{1,0:T(8,128)(2,1)}, u32[]{:S(2)}, u32[]{:S(2)}) collective-permute-start(bf16[2560,256]{1,0:T(8,128)(2,1)S(1)} %copy-done.6), channel_id=1, source_target_pairs={{0,16},{16,0},{1,17},{17,1},{2,18},{18,2},{3,19},{19,3},{4,20},{20... | collective-permute-start | bytes 3932168 | tf_op jit(solution)/shard_map/ppermute | solution.py:425
  347.1 25.3 %collective-permute-start.8 = (bf16[4,320,128]{2,1,0:T(8,128)(2,1)S(1)}, bf16[4,320,128]{2,1,0:T(8,128)(2,1)S(1)}, u32[]{:S(2)}, u32[]{:S(2)}) collective-permute-start(bf16[4,320,128]{2,1,0:T(8,128)(2,1)S(1)} %copy-done.31), channel_id=1, source_target_pairs={{0,8},{1,9},{2,10},{3,11},{4,12},{5,13},{6,14},{7,15},{8,0},{9,1},... | collective-permute-start | bytes 983048 | tf_op jit(solution)/shard_map/ppermute | solution.py:413
  370.8 33.9 %collective-permute-start.12 = (bf16[2560,256]{1,0:T(8,128)(2,1)}, bf16[2560,256]{1,0:T(8,128)(2,1)S(1)}, u32[]{:S(2)}, u32[]{:S(2)}) collective-permute-start(bf16[2560,256]{1,0:T(8,128)(2,1)} %get-tuple-element.116.refs_2_), channel_id=1, source_target_pairs={{0,16},{16,0},{1,17},{17,1},{2,18},{18,2},{3,19},{19,3},{4,20},{20... | collective-permute-start | bytes 3932168 | tf_op jit(solution)/shard_map/ppermute | solution.py:425
  385.4 27.3 %all-to-all-start.7 = ((bf16[8,320,128]{2,1,0:T(8,128)(2,1)}), bf16[8,320,128]{2,1,0:T(8,128)(2,1)S(1)}, u32[]{:S(2)}, u32[]{:S(2)}) async-start(bf16[8,320,128]{2,1,0:T(8,128)(2,1)} %get-tuple-element.115), calls=%async_computation.7 | async-start | bytes 1310720 | tf_op jit(solution)/shard_map/all_to_all | solution.py:344
  415.7 29.3 %all-to-all-start.8 = ((bf16[16,48,640]{2,1,0:T(8,128)(2,1)}), bf16[16,48,640]{2,1,0:T(8,128)(2,1)S(1)}, u32[]{:S(2)}, u32[]{:S(2)}) async-start(bf16[16,48,640]{2,1,0:T(8,128)(2,1)} %get-tuple-element.131), calls=%async_computation.8 | async-start | bytes 1966080 | tf_op jit(solution)/shard_map/all_to_all | solution.py:434
  421.6 17.1 %collective-permute-start.13 = (bf16[2560,128]{1,0:T(8,128)(2,1)S(1)}, bf16[2560,128]{1,0:T(8,128)(2,1)S(1)}, u32[]{:S(2)}, u32[]{:S(2)}) collective-permute-start(bf16[2560,128]{1,0:T(8,128)(2,1)S(1)} %copy-done.9), channel_id=1, source_target_pairs={{0,16},{16,0},{1,17},{17,1},{2,18},{18,2},{3,19},{19,3},{4,20},{20... | collective-permute-start | bytes 1966088 | tf_op jit(solution)/shard_map/ppermute | solution.py:425
  445.9 14.7 %all-to-all-start.9 = ((bf16[16,48,128]{2,1,0:T(8,128)(2,1)}), bf16[16,48,128]{2,1,0:T(8,128)(2,1)S(1)}, u32[]{:S(2)}, u32[]{:S(2)}) async-start(bf16[16,48,128]{2,1,0:T(8,128)(2,1)} %get-tuple-element.134), calls=%async_computation.9 | async-start | bytes 393216 | tf_op jit(solution)/shard_map/all_to_all | solution.py:434
  (33 other events, 130.6 us)
Sparse Core Ops, SparseCore 0:
  136.8 38.6 all-gather.1

commit v8 on v7

--- a/solution.py
+++ b/solution.py
@@ -9,7 +9,6 @@
 
 D = 2560
 BLOCK = 128
-PLANES = 4
 TOKEN = jax.ShapeDtypeStruct((8, 128), jnp.float32)
 ANY = pl.BlockSpec(memory_space=pl.ANY)
 SMEM = pl.BlockSpec(memory_space=pltpu.SMEM)
@@ -73,11 +72,11 @@
             for store in stores:
                 store.wait()
 
-        @pl.when(info_ref[1] == 0)
+        @pl.when(info_ref[0] == 0)
         def _():
             move(gate_ref)
 
-        @pl.when(info_ref[1] != 0)
+        @pl.when(info_ref[0] != 0)
         def _():
             move(up_ref)
 
@@ -114,6 +113,10 @@
     return value, token
 
 
+def first_share(devices):
+    return (5 * devices) // 8
+
+
 def merge(token, slots, factors, rows_of, received, start, blocks):
     devices, sources, rows, width = rows_of.shape
     steps, column_blocks = blocks
@@ -121,8 +124,8 @@
     first = start // BLOCK
     base_slot = 0 if received is None else devices * sources
 
-    middle = devices // 2
-    halves = (slice(0, middle), slice(middle, devices))
+    cut = first_share(devices)
+    halves = (slice(0, cut), slice(cut, devices))
 
     def kernel(slots_ref, factors_ref, rows_ref, *rest):
         total = rest[-1]
@@ -161,66 +164,27 @@
                 rest[2][...] = total[...].astype(jnp.bfloat16)
 
     whole = pl.BlockSpec((devices, rows, width), lambda i: (0, 0, 0))
-    half = pl.BlockSpec((middle, rows, width), lambda i: (0, 0, 0))
+    parts = [pl.BlockSpec((count, rows, width), lambda i: (0, 0, 0)) for count in (cut, devices - cut)]
     extra = () if received is None else tuple(received)
-    out_count = 2 if received is None else 1
+    out_counts = (cut, devices - cut) if received is None else (devices,)
     return step_call(
         kernel,
         token,
         (slots, factors, rows_of, *extra),
         [SMEM, SMEM, pl.BlockSpec((1, sources, rows, width), lambda i: (i, 0, 0, 0))]
-        + [half] * len(extra),
-        [jax.ShapeDtypeStruct((devices // out_count, rows, width), jnp.bfloat16)] * out_count,
-        [whole] if received is not None else [half, half],
+        + parts[: len(extra)],
+        [jax.ShapeDtypeStruct((count, rows, width), jnp.bfloat16) for count in out_counts],
+        [whole] if received is not None else parts,
         grid=(devices,),
         scratch_shapes=[pltpu.VMEM((devices, rows, width), jnp.float32)],
         name="merge",
     )
 
 
-def pair(token, tokens, other):
-    def kernel(tokens_ref, other_ref, out_ref):
-        out_ref[0] = tokens_ref[...]
-        out_ref[1] = other_ref[...]
-
-    (both,), token = step_call(
-        kernel,
-        token,
-        (tokens, other),
-        [VMEM, VMEM],
-        [jax.ShapeDtypeStruct((2,) + tokens.shape, tokens.dtype)],
-        [VMEM],
-        name="pair",
-    )
-    return both, token
-
-
-def line(token, info, both, nearby, tables):
-    _, tok_dev, width = both.shape
-
-    def kernel(info_ref, both_ref, nearby_ref, *rest):
-        out_ref = rest[len(tables)]
-        level = info_ref[0]
-        for index, other in enumerate((both_ref, nearby_ref)):
-            out_ref[level ^ index] = other[0]
-            out_ref[level ^ index ^ (PLANES // 2)] = other[1]
-
-    (whole,), _ = step_call(
-        kernel,
-        token,
-        (info, both, nearby, *tables),
-        [SMEM] + [VMEM] * 2 + [ANY] * len(tables),
-        [jax.ShapeDtypeStruct((PLANES, tok_dev, width), both.dtype)],
-        [VMEM],
-        name="line",
-    )
-    return whole
-
-
-def run_chunk(token, info, grouped, own, partner, outputs, start, full, blocks):
+def run_chunk(token, info, grouped, own, partner, outputs, start, full, devices):
     depth, width = own.shape
     count = grouped.shape[0]
-    each = count // len(blocks)
+    each = count // devices
     factor = 1.0 / math.sqrt(D)
 
     def kernel(info_ref, grouped_ref, own_ref, partner_ref, *rest):
@@ -237,11 +201,11 @@
             for load in loads:
                 load.wait()
 
-        @pl.when(info_ref[1] == 0)
+        @pl.when(info_ref[0] == 0)
         def _():
             fill(own_ref, partner_ref)
 
-        @pl.when(info_ref[1] != 0)
+        @pl.when(info_ref[0] != 0)
         def _():
             fill(partner_ref, own_ref)
 
@@ -255,8 +219,7 @@
         gate_value = values[:, :width] * factor
         up_value = values[:, width:] * factor
         hidden = (gate_value / (1.0 + jnp.exp(-gate_value)) * up_value).astype(jnp.bfloat16)
-        for index, block in enumerate(blocks):
-            hidden_ref[block] = hidden[index * each : (index + 1) * each]
+        hidden_ref[...] = hidden.reshape(devices, each, width)
         for store in stores:
             store.wait()
 
@@ -266,7 +229,7 @@
         token,
         (info, grouped, own, partner, *outputs),
         [SMEM, VMEM, ANY, ANY] + [ANY] * len(outputs),
-        [weights, weights, jax.ShapeDtypeStruct((len(blocks), each, width), jnp.bfloat16)],
+        [weights, weights, jax.ShapeDtypeStruct((devices, each, width), jnp.bfloat16)],
         [ANY, ANY, VMEM],
         scratch_shapes=[
             pltpu.VMEM((depth, 2 * width), jnp.bfloat16),
@@ -287,10 +250,6 @@
             order.append(("trade", chunk - 2))
         if chunk < count:
             order.append(("partial", chunk))
-        if chunk == 0:
-            order.append(("pair", 0))
-        if chunk == 1:
-            order.append(("line", 0))
         if chunk >= 1:
             order.append(("finish", chunk - 1))
         if chunk >= 3:
@@ -325,8 +284,6 @@
     own_index = lax.axis_index("expert")
     group_count = lax.axis_size("groups")
     half = lax.axis_index("groups") % 2
-    plane = expert_count // PLANES
-    level = own_index // plane
     halfway = expert_count // 2
     side, place = own_index // halfway, own_index % halfway
     depth, full = quant_gate.shape[1:]
@@ -334,16 +291,14 @@
     top_count = routes.shape[1]
     capacity = min(tok_dev, 2 * tok_dev * top_count // expert_count)
 
-    by_plane = [[z * plane + p for p in range(plane)] for z in range(PLANES)]
     by_half = [[part * halfway + i for i in range(halfway)] for part in range(2)]
     across = [(i, (i + halfway) % expert_count) for i in range(expert_count)]
-    beside = [(i, (i // plane ^ 1) * plane + i % plane) for i in range(expert_count)]
     partners = [(g, g ^ 1) for g in range(group_count)]
 
     def exchange(pieces):
         return lax.all_to_all(pieces, "expert", 0, 0, tiled=True, axis_index_groups=by_half)
 
-    info = jnp.stack([level, half]).astype(jnp.int32)
+    info = jnp.stack([half]).astype(jnp.int32)
     sources = quant_gate.shape[0]
     rows = depth // halfway
     step = math.gcd(rows, BLOCK)
@@ -365,11 +320,8 @@
     hit_table, position_lookup = route_slots(routes, expert_count, tok_dev)
     positions = jnp.arange(capacity, dtype=jnp.int32)
 
-    blocks = [z * plane + p for p in range(plane) for z in range(PLANES)]
-
     def in_blocks(table):
         column = lax.dynamic_index_in_dim(table, own_index, 2, keepdims=False)
-        column = column.reshape(PLANES, plane, tok_dev).transpose(1, 0, 2)
         return column.reshape(expert_count, 1, tok_dev)
 
     placing = (
@@ -389,26 +341,27 @@
     widths = chunk_widths(full // BLOCK)
     starts = [BLOCK * sum(widths[:chunk]) for chunk in range(len(widths))]
     token = jnp.zeros(TOKEN.shape, TOKEN.dtype)
-    opposite = lax.ppermute(tokens, "expert", across)
+    everyone = lax.all_gather(tokens, "expert", axis=0, tiled=True)
+    arrived = jnp.einsum(
+        "jct,jtd->jcd",
+        placing,
+        everyone.reshape(expert_count, tok_dev, everyone.shape[1]),
+        preferred_element_type=jnp.float32,
+    ).astype(jnp.bfloat16)
+    arrived = lax.all_gather(arrived, "mp", axis=2, tiled=True)
+    grouped = arrived.reshape(expert_count * capacity, depth)
     gathered, received, merged, own, partner, hiddens = ({} for _ in range(6))
     outputs, returned, last = (), [], len(widths) - 1
     for name, c in plan(len(widths)):
         start, width = starts[c], widths[c] * BLOCK
-        if name == "pair":
-            both, token = pair(token, tokens, opposite)
-            nearby = lax.ppermute(both, "expert", beside)
-        elif name == "line":
-            whole = line(token, info, both, nearby, (placing, picking))
-            everyone = lax.all_gather(whole, "expert", axis=0, tiled=True, axis_index_groups=by_plane)
-            arrived = jnp.einsum(
-                "jct,jtd->jcd", placing, everyone, preferred_element_type=jnp.float32
-            ).astype(jnp.bfloat16)
-            arrived = lax.all_gather(arrived, "mp", axis=2, tiled=True)
-            grouped = arrived.reshape(expert_count * capacity, depth)
-        elif name == "pack":
+        if name == "pack":
             (pieces,), token = pack(token, info, quant_gate, quant_up, start, width, halfway)
             gathered[c] = exchange(pieces)
         elif name == "partial":
+            if c == 1:
+                gathered[c], token = hold(
+                    token, gathered[c], [*received[0], placing, picking]
+                )
             partial, token = merge(token, slots, factors, gathered[c], None, start, blocks_of_rows)
             received[c] = [lax.ppermute(part, "expert", across) for part in partial]
         elif name == "finish":
@@ -418,14 +371,16 @@
         elif name == "back":
             earlier = [gathered[c + 2]] if c + 2 in gathered else []
             earlier += [received[c + 1][0]] if c + 1 in received else []
+            earlier += [grouped] if c == 0 else []
             merged[c], token = hold(token, merged[c], earlier)
             own[c] = exchange(merged[c])
         elif name == "trade":
-            own[c], token = hold(token, own[c].reshape(depth, width), [])
+            earlier = [received[c + 1][1]] if c + 1 in received else []
+            own[c], token = hold(token, own[c].reshape(depth, width), earlier)
             partner[c] = lax.ppermute(own[c], "groups", partners)
         elif name == "run":
             (*outputs, hiddens[c]), token = run_chunk(
-                token, info, grouped, own[c], partner[c], outputs, start, full, blocks
+                token, info, grouped, own[c], partner[c], outputs, start, full, expert_count
             )
         else:
             batch = [hiddens[i] for i in (range(last) if c == 0 else range(last, last + 1))]

time: 471 us -> 461 us (0.979)
  Pallas kernels: 85.9 us -> 78.8 us
    ppermute x8, waiting for transfers between devices: 101 us -> 154 us  [shards(): received[c] = [lax.ppermute(part, 'expert', across) for part in partial]]
    ppermute x2 -> x0, waiting for transfers between devices: 44.7 us -> none  [the longest x1 23.6 us: shards(): opposite = lax.ppermute(tokens, 'expert', across)]
    all_to_all x8, waiting for transfers between devices: 69.4 us -> 61 us  [exchange(): lax.all_to_all(pieces, 'expert', 0, 0, tiled=True, axis_index_groups=by_h...]
    pallas_call x28 -> x27, Pallas kernels: 85.9 us -> 78.8 us  [step_call(): pl.pallas_call(ordered, out_shape=[*out_shape, TOKEN], in_specs=[*in_spec...]
    ppermute x8, starting transfers between devices: 9.37 us -> 15.5 us  [shards(): received[c] = [lax.ppermute(part, 'expert', across) for part in partial]]
    unnamed x67 -> x65, local copies, waits for them, and re-layouts: 16.6 us -> 14.3 us
  transfers between devices with their start and end apart: 25 -> 23, of which waited for: 13 -> 16; matrix products, arithmetic and copies ran while one was open for 6% -> 6% of each run, Pallas kernels for 18% -> 17%
where the time goes in v8:
time: 461 us; the launch traced here: 459 us
  waiting for transfers between devices  256 us (56%)
  Pallas kernels  78.8 us (17%)
  starting transfers between devices  63 us (14%)
  local copies, waits for them, and re-layouts  23.5 us (5%)
  other arithmetic  15 us (3%)
  between operations  14.6 us (3%)
  matrix products  7.74 us (2%)
    ppermute x8, waiting for transfers between devices, shards(): received[c] = [lax.ppermute(part, 'expert', across) for part in partial]  154 us
    pallas_call x27, Pallas kernels, step_call(): pl.pallas_call(ordered, out_shape=[*out_shape, TOKEN], in_specs=[*in_spec...  78.8 us
    all_to_all x8, waiting for transfers between devices, exchange(): lax.all_to_all(pieces, 'expert', 0, 0, tiled=True, axis_index_groups=by_h...  61 us
    ppermute x4, waiting for transfers between devices, shards(): partner[c] = lax.ppermute(own[c], 'groups', partners)  33.6 us
    all_to_all x8, starting transfers between devices, exchange(): lax.all_to_all(pieces, 'expert', 0, 0, tiled=True, axis_index_groups=by_h...  31.1 us
    ppermute x8, starting transfers between devices, shards(): received[c] = [lax.ppermute(part, 'expert', across) for part in partial]  15.5 us
    unnamed x65, local copies, waits for them, and re-layouts  14.3 us
    all_to_all x2, starting transfers between devices, shards(): lax.all_to_all(hidden, 'expert', split_axis=0, concat_axis=0, tiled=True)  10.2 us
  transfers between devices with their start and end apart: 23, of which 16 were waited for; matrix products, arithmetic and copies ran while one was open for 6% of the time, Pallas kernels for 17%

profile of v8, /device:TPU:0, one launch (start us, length us, event | category | flops | bytes accessed | tf_op | source)
XLA Modules:
  0.0 458.7 jit_solution(3964788235099881633)
XLA Ops:
  18.6 17.5 %all-to-all-done.refs_2_ = bf16[8,2,320,128]{3,2,1,0:T(8,128)(2,1)S(1)} async-done(((bf16[8,2,320,128]{3,2,1,0:T(8,128)(2,1)}), bf16[8,2,320,128]{3,2,1,0:T(8,128)(2,1)S(1)}, u32[]{:S(2)}, u32[]{:S(2)}) %all-to-all-start) | async-done | bytes 1310752 | tf_op jit(solution)/shard_map/all_to_all | solution.py:299
  53.7 31.4 %all-to-all-done.1.refs_0_ = bf16[8,2,320,256]{3,2,1,0:T(8,128)(2,1)S(1)} async-done(((bf16[8,2,320,256]{3,2,1,0:T(8,128)(2,1)}), bf16[8,2,320,256]{3,2,1,0:T(8,128)(2,1)S(1)}, u32[]{:S(2)}, u32[]{:S(2)}) %all-to-all-start.1) | async-done | bytes 2621472 | tf_op jit(solution)/shard_map/all_to_all | solution.py:299
  90.8 6.3 %fusion.8 = s32[16,64,16]{2,0,1:T(8,128)S(1)} fusion(s32[16,64,16]{2,0,1:T(8,128)S(1)} %copy.44), kind=kOutput, calls=%fused_computation.57 | output fusion | flops 1032192 | bytes 131072 | tf_op jit(solution)/shard_map/jit(cumsum)/reduce_window_sum | solution.py:271
  109.9 26.5 %collective-permute-done.1.refs_2_.refs_4_ = bf16[3,320,128]{2,1,0:T(8,128)(2,1)} collective-permute-done((bf16[3,320,128]{2,1,0:T(8,128)(2,1)}, bf16[3,320,128]{2,1,0:T(8,128)(2,1)}, u32[]{:S(2)}, u32[]{:S(2)}) %collective-permute-start.1) | collective-permute-done | bytes 245792 | tf_op jit(solution)/shard_map/ppermute | solution.py:366
  136.5 5.7 %merge.9 = (bf16[5,320,256]{2,1,0:T(8,128)(2,1)}, bf16[3,320,256]{2,1,0:T(8,128)(2,1)}, f32[8,128]{1,0:T(8,128)}) custom-call(s32[32]{0:T(128)} %pad_add_fusion.refs_0_, f32[480]{0:T(512)} %mul.52.refs_1_, bf16[8,2,320,256]{3,2,1,0:T(8,128)(2,1)} %get-tuple-element.76.refs_2_, f32[8,128]{1,0:T(8,128)} %get-tuple-element.77.refs_3_), custom_call_target="tpu_custom_call" | custom-call | tf_op jit(solution)/shard_map/merge/pallas_call | solution.py:31
  150.8 5.6 %convolution_convert_fusion = bf16[16,48,2560]{2,1,0:T(8,128)(2,1)} fusion(bf16[16,64,2560]{2,1,0:T(8,128)(2,1)} %bitcast.41, s32[16,64]{1,0:T(8,128)S(1)} %bitcast.46, pred[16,64]{1,0:T(8,128)(4,1)S(1)} %fusion.5), kind=kOutput, calls=%fused_computation.4 | convolution fusion | flops 253722624 | bytes 9180160 | tf_op jit(solution)/shard_map/jct,jtd->jcd/dot_general | solution.py:345
  156.4 25.3 %collective-permute-done.2.refs_2_.refs_3_ = bf16[5,320,256]{2,1,0:T(8,128)(2,1)S(1)} collective-permute-done((bf16[5,320,256]{2,1,0:T(8,128)(2,1)}, bf16[5,320,256]{2,1,0:T(8,128)(2,1)S(1)}, u32[]{:S(2)}, u32[]{:S(2)}) %collective-permute-start.2) | collective-permute-done | bytes 819232 | tf_op jit(solution)/shard_map/ppermute | solution.py:366
  189.3 7.9 %all-to-all-done.4 = bf16[8,320,128]{2,1,0:T(8,128)(2,1)S(1)} async-done(((bf16[8,320,128]{2,1,0:T(8,128)(2,1)}), bf16[8,320,128]{2,1,0:T(8,128)(2,1)S(1)}, u32[]{:S(2)}, u32[]{:S(2)}) %all-to-all-start.4) | async-done | bytes 655392 | tf_op jit(solution)/shard_map/all_to_all | solution.py:299
  202.6 23.9 %collective-permute-done.3.refs_1_.refs_4_ = bf16[3,320,256]{2,1,0:T(8,128)(2,1)S(1)} collective-permute-done((bf16[3,320,256]{2,1,0:T(8,128)(2,1)S(1)}, bf16[3,320,256]{2,1,0:T(8,128)(2,1)S(1)}, u32[]{:S(2)}, u32[]{:S(2)}) %collective-permute-start.3) | collective-permute-done | bytes 491552 | tf_op jit(solution)/shard_map/ppermute | solution.py:366
  227.2 5.8 %merge.11 = (bf16[5,320,256]{2,1,0:T(8,128)(2,1)}, bf16[3,320,256]{2,1,0:T(8,128)(2,1)}, f32[8,128]{1,0:T(8,128)}) custom-call(s32[32]{0:T(128)} %pad_add_fusion.refs_0_, f32[480]{0:T(512)} %mul.52.refs_1_, bf16[8,2,320,256]{3,2,1,0:T(8,128)(2,1)} %copy-done.1, f32[8,128]{1,0:T(8,128)} %get-tuple-element.88.refs_3_), custom_call_target="tpu_custom_call" | custom-call | tf_op jit(solution)/shard_map/merge/pallas_call | solution.py:31
  236.3 6.2 %merge.12 = (bf16[8,320,256]{2,1,0:T(8,128)(2,1)}, f32[8,128]{1,0:T(8,128)}) custom-call(s32[32]{0:T(128)} %pad_add_fusion.refs_0_, f32[480]{0:T(512)} %mul.52.refs_1_, bf16[8,2,320,256]{3,2,1,0:T(8,128)(2,1)} %get-tuple-element.76.refs_2_, bf16[5,320,256]{2,1,0:T(8,128)(2,1)} %copy-done.13, bf16[3,320,256]{2,1,0:T(8,128)(2,1)} %copy-done.17, ...), custom_call_target="tpu_custom_call" | custom-call | tf_op jit(solution)/shard_map/merge/pallas_call | solution.py:31
  242.5 29.9 %collective-permute-done.4.refs_2_.refs_3_ = bf16[5,320,256]{2,1,0:T(8,128)(2,1)S(1)} collective-permute-done((bf16[5,320,256]{2,1,0:T(8,128)(2,1)}, bf16[5,320,256]{2,1,0:T(8,128)(2,1)S(1)}, u32[]{:S(2)}, u32[]{:S(2)}) %collective-permute-start.4) | collective-permute-done | bytes 819232 | tf_op jit(solution)/shard_map/ppermute | solution.py:366
  280.8 22.3 %collective-permute-done.5.refs_1_.refs_4_ = bf16[3,320,256]{2,1,0:T(8,128)(2,1)S(1)} collective-permute-done((bf16[3,320,256]{2,1,0:T(8,128)(2,1)S(1)}, bf16[3,320,256]{2,1,0:T(8,128)(2,1)S(1)}, u32[]{:S(2)}, u32[]{:S(2)}) %collective-permute-start.5) | collective-permute-done | bytes 491552 | tf_op jit(solution)/shard_map/ppermute | solution.py:366
  312.8 6.2 %merge.14 = (bf16[8,320,256]{2,1,0:T(8,128)(2,1)}, f32[8,128]{1,0:T(8,128)}) custom-call(s32[32]{0:T(128)} %pad_add_fusion.refs_0_, f32[480]{0:T(512)} %mul.52.refs_1_, bf16[8,2,320,256]{3,2,1,0:T(8,128)(2,1)} %copy-done.1, bf16[5,320,256]{2,1,0:T(8,128)(2,1)} %copy-done.14, bf16[3,320,256]{2,1,0:T(8,128)(2,1)} %copy-done.16, f32[8,128]{1,0:T(8,128)} %get-tuple-element.99.refs_5_), custom_call_target="tpu_custom_call" | custom-call | tf_op jit(solution)/shard_map/merge/pallas_call | solution.py:31
  319.0 5.3 %run_chunk.4 = (bf16[1,2560,768]{2,1,0:T(8,128)(2,1)}, bf16[1,2560,768]{2,1,0:T(8,128)(2,1)}, bf16[16,48,128]{2,1,0:T(8,128)(2,1)}, f32[8,128]{1,0:T(8,128)}) custom-call(s32[1]{0:T(128)} %bitcast.refs_0_, bf16[768,2560]{1,0:T(8,128)(2,1)} %bitcast.33, bf16[2560,128]{1,0:T(8,128)(2,1)} %get-tuple-element.101.refs_2_, ...), custom_call_target="tpu_custom_call" | custom-call | tf_op jit(solution)/shard_map/run_chunk/pallas_call | solution.py:31
  324.3 8.0 %collective-permute-done.6.refs_1_.refs_3_ = bf16[5,320,128]{2,1,0:T(8,128)(2,1)S(1)} collective-permute-done((bf16[5,320,128]{2,1,0:T(8,128)(2,1)}, bf16[5,320,128]{2,1,0:T(8,128)(2,1)S(1)}, u32[]{:S(2)}, u32[]{:S(2)}) %collective-permute-start.6) | collective-permute-done | bytes 409632 | tf_op jit(solution)/shard_map/ppermute | solution.py:366
  339.2 17.8 %collective-permute-done.7.refs_1_.refs_4_ = bf16[3,320,128]{2,1,0:T(8,128)(2,1)S(1)} collective-permute-done((bf16[3,320,128]{2,1,0:T(8,128)(2,1)S(1)}, bf16[3,320,128]{2,1,0:T(8,128)(2,1)S(1)}, u32[]{:S(2)}, u32[]{:S(2)}) %collective-permute-start.7) | collective-permute-done | bytes 245792 | tf_op jit(solution)/shard_map/ppermute | solution.py:366
  368.6 6.9 %run_chunk.5 = (bf16[1,2560,768]{2,1,0:T(8,128)(2,1)}, bf16[1,2560,768]{2,1,0:T(8,128)(2,1)}, bf16[16,48,256]{2,1,0:T(8,128)(2,1)}, f32[8,128]{1,0:T(8,128)}) custom-call(s32[1]{0:T(128)} %bitcast.refs_0_, bf16[768,2560]{1,0:T(8,128)(2,1)} %bitcast.34, bf16[2560,256]{1,0:T(8,128)(2,1)} %get-tuple-element.108.refs_2_, ...), custom_call_target="tpu_custom_call", output_to_operand_aliasing={{0}: (4, {}), {1}: (5, {})} | custom-call | tf_op jit(solution)/shard_map/run_chunk/pallas_call | solution.py:31
  379.4 16.4 %collective-permute-done.10.refs_3_ = bf16[2560,256]{1,0:T(8,128)(2,1)S(1)} collective-permute-done((bf16[2560,256]{1,0:T(8,128)(2,1)}, bf16[2560,256]{1,0:T(8,128)(2,1)S(1)}, u32[]{:S(2)}, u32[]{:S(2)}) %collective-permute-start.10) | collective-permute-done | bytes 1310752 | tf_op jit(solution)/shard_map/ppermute | solution.py:380
  396.9 6.9 %run_chunk.6 = (bf16[1,2560,768]{2,1,0:T(8,128)(2,1)}, bf16[1,2560,768]{2,1,0:T(8,128)(2,1)}, bf16[16,48,256]{2,1,0:T(8,128)(2,1)}, f32[8,128]{1,0:T(8,128)}) custom-call(s32[1]{0:T(128)} %bitcast.refs_0_, bf16[768,2560]{1,0:T(8,128)(2,1)} %bitcast.35, bf16[2560,256]{1,0:T(8,128)(2,1)} %get-tuple-element.114.refs_2_, ...), custom_call_target="tpu_custom_call", output_to_operand_aliasing={{0}: (4, {}), {1}: (5, {})} | custom-call | tf_op jit(solution)/shard_map/run_chunk/pallas_call | solution.py:31
  412.9 15.6 %collective-permute-done.11.refs_3_ = bf16[2560,128]{1,0:T(8,128)(2,1)S(1)} collective-permute-done((bf16[2560,128]{1,0:T(8,128)(2,1)S(1)}, bf16[2560,128]{1,0:T(8,128)(2,1)S(1)}, u32[]{:S(2)}, u32[]{:S(2)}) %collective-permute-start.11) | collective-permute-done | bytes 655392 | tf_op jit(solution)/shard_map/ppermute | solution.py:380
  429.3 5.4 %run_chunk.7 = (bf16[1,2560,768]{2,1,0:T(8,128)(2,1)}, bf16[1,2560,768]{2,1,0:T(8,128)(2,1)}, bf16[16,48,128]{2,1,0:T(8,128)(2,1)}, f32[8,128]{1,0:T(8,128)}) custom-call(s32[1]{0:T(128)} %bitcast.refs_0_, bf16[768,2560]{1,0:T(8,128)(2,1)} %bitcast.36, bf16[2560,128]{1,0:T(8,128)(2,1)} %get-tuple-element.119.refs_2_, ...), custom_call_target="tpu_custom_call", output_to_operand_aliasing={{0}: (4, {}), {1}: (5, {})} | custom-call | tf_op jit(solution)/shard_map/run_chunk/pallas_call | solution.py:31
  435.7 5.7 %all-to-all-start.9 = ((bf16[16,48,128]{2,1,0:T(8,128)(2,1)}), bf16[16,48,128]{2,1,0:T(8,128)(2,1)S(1)}, u32[]{:S(2)}, u32[]{:S(2)}) async-start(bf16[16,48,128]{2,1,0:T(8,128)(2,1)} %get-tuple-element.132), calls=%async_computation.9 | async-start | bytes 393216 | tf_op jit(solution)/shard_map/all_to_all | solution.py:389
  443.2 7.1 %all-to-all-done.9 = bf16[16,48,128]{2,1,0:T(8,128)(2,1)S(1)} async-done(((bf16[16,48,128]{2,1,0:T(8,128)(2,1)}), bf16[16,48,128]{2,1,0:T(8,128)(2,1)S(1)}, u32[]{:S(2)}, u32[]{:S(2)}) %all-to-all-start.9) | async-done | bytes 196640 | tf_op jit(solution)/shard_map/all_to_all | solution.py:389
  (162 shorter events, 128.7 us)
Async XLA Ops:
  10.0 26.1 %all-to-all-start = ((bf16[8,2,320,128]{3,2,1,0:T(8,128)(2,1)}), bf16[8,2,320,128]{3,2,1,0:T(8,128)(2,1)S(1)}, u32[]{:S(2)}, u32[]{:S(2)}) async-start(bf16[8,2,320,128]{3,2,1,0:T(8,128)(2,1)} %get-tuple-element.68), calls=%async_computation | async-start | bytes 2621440 | tf_op jit(solution)/shard_map/all_to_all | solution.py:299
  15.3 135.5 %all-gather.2.cloned.1.call-start = ((), (), s32[]{:S(2)}) async-start(), calls=%async_computation.10 | async-start | bytes 5570560 | tf_op jit(solution)/shard_map/all_gather | solution.py:344
  37.2 47.8 %all-to-all-start.1 = ((bf16[8,2,320,256]{3,2,1,0:T(8,128)(2,1)}), bf16[8,2,320,256]{3,2,1,0:T(8,128)(2,1)S(1)}, u32[]{:S(2)}, u32[]{:S(2)}) async-start(bf16[8,2,320,256]{3,2,1,0:T(8,128)(2,1)} %get-tuple-element.73), calls=%async_computation.1 | async-start | bytes 5242880 | tf_op jit(solution)/shard_map/all_to_all | solution.py:299
  86.5 95.3 %all-to-all-start.2 = ((bf16[8,2,320,256]{3,2,1,0:T(8,128)(2,1)}), bf16[8,2,320,256]{3,2,1,0:T(8,128)(2,1)S(1)}, u32[]{:S(2)}, u32[]{:S(2)}) async-start(bf16[8,2,320,256]{3,2,1,0:T(8,128)(2,1)} %get-tuple-element.80), calls=%async_computation.2 | async-start | bytes 5242880 | tf_op jit(solution)/shard_map/all_to_all | solution.py:299
  99.9 36.5 %collective-permute-start = (bf16[5,320,128]{2,1,0:T(8,128)(2,1)}, bf16[5,320,128]{2,1,0:T(8,128)(2,1)}, u32[]{:S(2)}, u32[]{:S(2)}) collective-permute-start(bf16[5,320,128]{2,1,0:T(8,128)(2,1)} %get-tuple-element.71), channel_id=1, source_target_pairs={{0,8},{1,9},{2,10},{3,11},{4,12},{5,13},{6,14},{7,15},{8,0},{9,1},... | collective-permute-start | bytes 1228808 | tf_op jit(solution)/shard_map/ppermute | solution.py:366
  103.0 33.4 %collective-permute-start.1 = (bf16[3,320,128]{2,1,0:T(8,128)(2,1)}, bf16[3,320,128]{2,1,0:T(8,128)(2,1)}, u32[]{:S(2)}, u32[]{:S(2)}) collective-permute-start(bf16[3,320,128]{2,1,0:T(8,128)(2,1)} %get-tuple-element.72), channel_id=1, source_target_pairs={{0,8},{1,9},{2,10},{3,11},{4,12},{5,13},{6,14},{7,15},{8,0},{9,1},... | collective-permute-start | bytes 737288 | tf_op jit(solution)/shard_map/ppermute | solution.py:366
  142.2 39.6 %collective-permute-start.2 = (bf16[5,320,256]{2,1,0:T(8,128)(2,1)}, bf16[5,320,256]{2,1,0:T(8,128)(2,1)S(1)}, u32[]{:S(2)}, u32[]{:S(2)}) collective-permute-start(bf16[5,320,256]{2,1,0:T(8,128)(2,1)} %get-tuple-element.81), channel_id=1, source_target_pairs={{0,8},{1,9},{2,10},{3,11},{4,12},{5,13},{6,14},{7,15},{8,0},{9,1},... | collective-permute-start | bytes 2457608 | tf_op jit(solution)/shard_map/ppermute | solution.py:366
  183.5 13.7 %all-to-all-start.4 = ((bf16[8,320,128]{2,1,0:T(8,128)(2,1)}), bf16[8,320,128]{2,1,0:T(8,128)(2,1)S(1)}, u32[]{:S(2)}, u32[]{:S(2)}) async-start(bf16[8,320,128]{2,1,0:T(8,128)(2,1)} %get-tuple-element.86), calls=%async_computation.4 | async-start | bytes 1310720 | tf_op jit(solution)/shard_map/all_to_all | solution.py:299
  197.2 29.2 %copy-start.10 = (bf16[8,320,128]{2,1,0:T(8,128)(2,1)}, bf16[8,320,128]{2,1,0:T(8,128)(2,1)S(1)}, u32[]{:S(2)}) copy-start(bf16[8,320,128]{2,1,0:T(8,128)(2,1)S(1)} %all-to-all-done.4) | copy-start | bytes 1966084
  197.2 75.2 %all-to-all-start.3 = ((bf16[8,2,320,128]{3,2,1,0:T(8,128)(2,1)}), bf16[8,2,320,128]{3,2,1,0:T(8,128)(2,1)S(1)}, u32[]{:S(2)}, u32[]{:S(2)}) async-start(bf16[8,2,320,128]{3,2,1,0:T(8,128)(2,1)} %get-tuple-element.84), calls=%async_computation.3 | async-start | bytes 2621440 | tf_op jit(solution)/shard_map/all_to_all | solution.py:299
  200.8 25.6 %collective-permute-start.3 = (bf16[3,320,256]{2,1,0:T(8,128)(2,1)S(1)}, bf16[3,320,256]{2,1,0:T(8,128)(2,1)S(1)}, u32[]{:S(2)}, u32[]{:S(2)}) collective-permute-start(bf16[3,320,256]{2,1,0:T(8,128)(2,1)S(1)} %copy-done.28), channel_id=1, source_target_pairs={{0,8},{1,9},{2,10},{3,11},{4,12},{5,13},{6,14},{7,15},{8,0},{9,1},... | collective-permute-start | bytes 1474568 | tf_op jit(solution)/shard_map/ppermute | solution.py:366
  233.0 39.4 %collective-permute-start.4 = (bf16[5,320,256]{2,1,0:T(8,128)(2,1)}, bf16[5,320,256]{2,1,0:T(8,128)(2,1)S(1)}, u32[]{:S(2)}, u32[]{:S(2)}) collective-permute-start(bf16[5,320,256]{2,1,0:T(8,128)(2,1)} %get-tuple-element.91), channel_id=1, source_target_pairs={{0,8},{1,9},{2,10},{3,11},{4,12},{5,13},{6,14},{7,15},{8,0},{9,1},... | collective-permute-start | bytes 2457608 | tf_op jit(solution)/shard_map/ppermute | solution.py:366
  273.8 31.4 %all-to-all-start.5 = ((bf16[8,320,256]{2,1,0:T(8,128)(2,1)}), bf16[8,320,256]{2,1,0:T(8,128)(2,1)S(1)}, u32[]{:S(2)}, u32[]{:S(2)}) async-start(bf16[8,320,256]{2,1,0:T(8,128)(2,1)} %get-tuple-element.93), calls=%async_computation.5 | async-start | bytes 2621440 | tf_op jit(solution)/shard_map/all_to_all | solution.py:299
  277.5 25.6 %collective-permute-start.5 = (bf16[3,320,256]{2,1,0:T(8,128)(2,1)S(1)}, bf16[3,320,256]{2,1,0:T(8,128)(2,1)S(1)}, u32[]{:S(2)}, u32[]{:S(2)}) collective-permute-start(bf16[3,320,256]{2,1,0:T(8,128)(2,1)S(1)} %copy-done.29), channel_id=1, source_target_pairs={{0,8},{1,9},{2,10},{3,11},{4,12},{5,13},{6,14},{7,15},{8,0},{9,1},... | collective-permute-start | bytes 1474568 | tf_op jit(solution)/shard_map/ppermute | solution.py:366
  279.3 39.7 %collective-permute-start.8 = (bf16[2560,128]{1,0:T(8,128)(2,1)S(1)}, bf16[2560,128]{1,0:T(8,128)(2,1)}, u32[]{:S(2)}, u32[]{:S(2)}) collective-permute-start(bf16[2560,128]{1,0:T(8,128)(2,1)S(1)} %copy-done.11), channel_id=1, source_target_pairs={{0,16},{16,0},{1,17},{17,1},{2,18},{18,2},{3,19},{19,3},{4,20},{20... | collective-permute-start | bytes 1966088 | tf_op jit(solution)/shard_map/ppermute | solution.py:380
  311.4 20.9 %collective-permute-start.6 = (bf16[5,320,128]{2,1,0:T(8,128)(2,1)}, bf16[5,320,128]{2,1,0:T(8,128)(2,1)S(1)}, u32[]{:S(2)}, u32[]{:S(2)}) collective-permute-start(bf16[5,320,128]{2,1,0:T(8,128)(2,1)} %get-tuple-element.97), channel_id=1, source_target_pairs={{0,8},{1,9},{2,10},{3,11},{4,12},{5,13},{6,14},{7,15},{8,0},{9,1},... | collective-permute-start | bytes 1228808 | tf_op jit(solution)/shard_map/ppermute | solution.py:366
  333.1 26.0 %all-to-all-start.6 = ((bf16[8,320,256]{2,1,0:T(8,128)(2,1)}), bf16[8,320,256]{2,1,0:T(8,128)(2,1)S(1)}, u32[]{:S(2)}, u32[]{:S(2)}) async-start(bf16[8,320,256]{2,1,0:T(8,128)(2,1)} %get-tuple-element.104), calls=%async_computation.6 | async-start | bytes 2621440 | tf_op jit(solution)/shard_map/all_to_all | solution.py:299
  336.8 31.8 %collective-permute-start.9 = (bf16[2560,256]{1,0:T(8,128)(2,1)S(1)}, bf16[2560,256]{1,0:T(8,128)(2,1)}, u32[]{:S(2)}, u32[]{:S(2)}) collective-permute-start(bf16[2560,256]{1,0:T(8,128)(2,1)S(1)} %copy-done.6), channel_id=1, source_target_pairs={{0,16},{16,0},{1,17},{17,1},{2,18},{18,2},{3,19},{19,3},{4,20},{20... | collective-permute-start | bytes 3932168 | tf_op jit(solution)/shard_map/ppermute | solution.py:380
  338.4 18.6 %collective-permute-start.7 = (bf16[3,320,128]{2,1,0:T(8,128)(2,1)S(1)}, bf16[3,320,128]{2,1,0:T(8,128)(2,1)S(1)}, u32[]{:S(2)}, u32[]{:S(2)}) collective-permute-start(bf16[3,320,128]{2,1,0:T(8,128)(2,1)S(1)} %copy-done.30), channel_id=1, source_target_pairs={{0,8},{1,9},{2,10},{3,11},{4,12},{5,13},{6,14},{7,15},{8,0},{9,1},... | collective-permute-start | bytes 737288 | tf_op jit(solution)/shard_map/ppermute | solution.py:366
  360.2 35.6 %collective-permute-start.10 = (bf16[2560,256]{1,0:T(8,128)(2,1)}, bf16[2560,256]{1,0:T(8,128)(2,1)S(1)}, u32[]{:S(2)}, u32[]{:S(2)}) collective-permute-start(bf16[2560,256]{1,0:T(8,128)(2,1)} %get-tuple-element.114.refs_2_), channel_id=1, source_target_pairs={{0,16},{16,0},{1,17},{17,1},{2,18},{18,2},{3,19},{19,3},{4,20},{20... | collective-permute-start | bytes 3932168 | tf_op jit(solution)/shard_map/ppermute | solution.py:380
  375.5 28.4 %all-to-all-start.7 = ((bf16[8,320,128]{2,1,0:T(8,128)(2,1)}), bf16[8,320,128]{2,1,0:T(8,128)(2,1)S(1)}, u32[]{:S(2)}, u32[]{:S(2)}) async-start(bf16[8,320,128]{2,1,0:T(8,128)(2,1)} %get-tuple-element.113), calls=%async_computation.7 | async-start | bytes 1310720 | tf_op jit(solution)/shard_map/all_to_all | solution.py:299
  406.9 27.8 %all-to-all-start.8 = ((bf16[16,48,640]{2,1,0:T(8,128)(2,1)}), bf16[16,48,640]{2,1,0:T(8,128)(2,1)S(1)}, u32[]{:S(2)}, u32[]{:S(2)}) async-start(bf16[16,48,640]{2,1,0:T(8,128)(2,1)} %get-tuple-element.129), calls=%async_computation.8 | async-start | bytes 1966080 | tf_op jit(solution)/shard_map/all_to_all | solution.py:389
  411.3 17.1 %collective-permute-start.11 = (bf16[2560,128]{1,0:T(8,128)(2,1)S(1)}, bf16[2560,128]{1,0:T(8,128)(2,1)S(1)}, u32[]{:S(2)}, u32[]{:S(2)}) collective-permute-start(bf16[2560,128]{1,0:T(8,128)(2,1)S(1)} %copy-done.9), channel_id=1, source_target_pairs={{0,16},{16,0},{1,17},{17,1},{2,18},{18,2},{3,19},{19,3},{4,20},{20... | collective-permute-start | bytes 1966088 | tf_op jit(solution)/shard_map/ppermute | solution.py:380
  435.7 14.7 %all-to-all-start.9 = ((bf16[16,48,128]{2,1,0:T(8,128)(2,1)}), bf16[16,48,128]{2,1,0:T(8,128)(2,1)S(1)}, u32[]{:S(2)}, u32[]{:S(2)}) async-start(bf16[16,48,128]{2,1,0:T(8,128)(2,1)} %get-tuple-element.132), calls=%async_computation.9 | async-start | bytes 393216 | tf_op jit(solution)/shard_map/all_to_all | solution.py:389
  (30 other events, 124.4 us)
Sparse Core Ops, SparseCore 0:
  18.4 80.9 all-gather.1

commit v9 on v8

--- a/solution.py
+++ b/solution.py
@@ -113,31 +113,29 @@
     return value, token
 
 
-def first_share(devices):
-    return (5 * devices) // 8
-
-
-def merge(token, slots, factors, rows_of, received, start, blocks):
+def merge(token, info, slots, factors, rows_of, gathered, start, blocks):
     devices, sources, rows, width = rows_of.shape
     steps, column_blocks = blocks
     step = rows // steps
     first = start // BLOCK
-    base_slot = 0 if received is None else devices * sources
-
-    cut = first_share(devices)
-    halves = (slice(0, cut), slice(cut, devices))
-
-    def kernel(slots_ref, factors_ref, rows_ref, *rest):
-        total = rest[-1]
+    base_slot = 0 if gathered is None else devices * sources
+
+    def kernel(info_ref, slots_ref, factors_ref, rows_ref, *rest):
         piece = pl.program_id(0)
+        if gathered is None:
+            out_ref, total = rest
+        else:
+            gathered_ref, out_ref, total, received, sem = rest
 
         @pl.when(piece == 0)
         def _():
-            if received is None:
+            if gathered is None:
                 total[...] = jnp.zeros_like(total)
             else:
-                for part, share in enumerate(halves):
-                    total[share] = rest[part][...].astype(jnp.float32)
+                copy = pltpu.make_async_copy(gathered_ref.at[1 - info_ref[1]], received, sem)
+                copy.start()
+                copy.wait()
+                total[...] = received[...].astype(jnp.float32)
 
         for number in range(sources):
             source = piece * sources + number
@@ -157,28 +155,26 @@
 
         @pl.when(piece == devices - 1)
         def _():
-            if received is None:
-                for part, share in enumerate(halves):
-                    rest[part][...] = total[share].astype(jnp.bfloat16)
-            else:
-                rest[2][...] = total[...].astype(jnp.bfloat16)
-
-    whole = pl.BlockSpec((devices, rows, width), lambda i: (0, 0, 0))
-    parts = [pl.BlockSpec((count, rows, width), lambda i: (0, 0, 0)) for count in (cut, devices - cut)]
-    extra = () if received is None else tuple(received)
-    out_counts = (cut, devices - cut) if received is None else (devices,)
-    return step_call(
+            out_ref[...] = total[...].astype(jnp.bfloat16)
+
+    scratch = [pltpu.VMEM((devices, rows, width), jnp.float32)]
+    extra = ()
+    if gathered is not None:
+        scratch += [pltpu.VMEM((devices, rows, width), jnp.bfloat16), pltpu.SemaphoreType.DMA]
+        extra = (gathered,)
+    (merged,), token = step_call(
         kernel,
         token,
-        (slots, factors, rows_of, *extra),
-        [SMEM, SMEM, pl.BlockSpec((1, sources, rows, width), lambda i: (i, 0, 0, 0))]
-        + parts[: len(extra)],
-        [jax.ShapeDtypeStruct((count, rows, width), jnp.bfloat16) for count in out_counts],
-        [whole] if received is not None else parts,
+        (info, slots, factors, rows_of, *extra),
+        [SMEM, SMEM, SMEM, pl.BlockSpec((1, sources, rows, width), lambda i: (i, 0, 0, 0))]
+        + [ANY] * len(extra),
+        [jax.ShapeDtypeStruct((devices, rows, width), jnp.bfloat16)],
+        [pl.BlockSpec((devices, rows, width), lambda i: (0, 0, 0))],
         grid=(devices,),
-        scratch_shapes=[pltpu.VMEM((devices, rows, width), jnp.float32)],
+        scratch_shapes=scratch,
         name="merge",
     )
+    return merged, token
 
 
 def run_chunk(token, info, grouped, own, partner, outputs, start, full, devices):
@@ -292,13 +288,13 @@
     capacity = min(tok_dev, 2 * tok_dev * top_count // expert_count)
 
     by_half = [[part * halfway + i for i in range(halfway)] for part in range(2)]
-    across = [(i, (i + halfway) % expert_count) for i in range(expert_count)]
+    pairs = [[i, i + halfway] for i in range(halfway)]
     partners = [(g, g ^ 1) for g in range(group_count)]
 
     def exchange(pieces):
         return lax.all_to_all(pieces, "expert", 0, 0, tiled=True, axis_index_groups=by_half)
 
-    info = jnp.stack([half]).astype(jnp.int32)
+    info = jnp.stack([half, side]).astype(jnp.int32)
     sources = quant_gate.shape[0]
     rows = depth // halfway
     step = math.gcd(rows, BLOCK)
@@ -359,24 +355,22 @@
             gathered[c] = exchange(pieces)
         elif name == "partial":
             if c == 1:
-                gathered[c], token = hold(
-                    token, gathered[c], [*received[0], placing, picking]
-                )
-            partial, token = merge(token, slots, factors, gathered[c], None, start, blocks_of_rows)
-            received[c] = [lax.ppermute(part, "expert", across) for part in partial]
+                gathered[c], token = hold(token, gathered[c], [placing, picking])
+            partial, token = merge(
+                token, info, slots, factors, gathered[c], None, start, blocks_of_rows
+            )
+            received[c] = lax.all_gather(partial, "expert", axis_index_groups=pairs)
         elif name == "finish":
-            (merged[c],), token = merge(
-                token, slots, factors, gathered[c], received[c], start, blocks_of_rows
+            merged[c], token = merge(
+                token, info, slots, factors, gathered[c], received[c], start, blocks_of_rows
             )
         elif name == "back":
             earlier = [gathered[c + 2]] if c + 2 in gathered else []
-            earlier += [received[c + 1][0]] if c + 1 in received else []
             earlier += [grouped] if c == 0 else []
             merged[c], token = hold(token, merged[c], earlier)
             own[c] = exchange(merged[c])
         elif name == "trade":
-            earlier = [received[c + 1][1]] if c + 1 in received else []
-            own[c], token = hold(token, own[c].reshape(depth, width), earlier)
+            own[c], token = hold(token, own[c].reshape(depth, width), [])
             partner[c] = lax.ppermute(own[c], "groups", partners)
         elif name == "run":
             (*outputs, hiddens[c]), token = run_chunk(

time: 461 us -> 446 us (0.967)
  starting transfers between devices: 63 us -> 47.1 us
  Pallas kernels: 78.8 us -> 85.3 us
    ppermute x8 -> x0, waiting for transfers between devices: 154 us -> none  [shards(): received[c] = [lax.ppermute(part, 'expert', across) for part in partial]]
    all_gather x0 -> x4, waiting for transfers between devices: none -> 87.3 us  [shards(): received[c] = lax.all_gather(partial, 'expert', axis_index_groups=pairs)]
    all_to_all x8, waiting for transfers between devices: 61 us -> 106 us  [exchange(): lax.all_to_all(pieces, 'expert', 0, 0, tiled=True, axis_index_groups=by_h...]
    all_gather x1, waiting for transfers between devices: 0.01 us -> 31.2 us  [shards(): everyone = lax.all_gather(tokens, 'expert', axis=0, tiled=True)]
    ppermute x4, waiting for transfers between devices: 33.6 us -> 17.8 us  [shards(): partner[c] = lax.ppermute(own[c], 'groups', partners)]
    ppermute x8 -> x0, starting transfers between devices: 15.5 us -> none  [shards(): received[c] = [lax.ppermute(part, 'expert', across) for part in partial]]
    pallas_call x27, Pallas kernels: 78.8 us -> 85.3 us  [step_call(): pl.pallas_call(ordered, out_shape=[*out_shape, TOKEN], in_specs=[*in_spec...]
    unnamed x65 -> x51, local copies, waits for them, and re-layouts: 14.3 us -> 13.9 us
  transfers between devices with their start and end apart: 23 -> 19, of which waited for: 16 -> 12; matrix products, arithmetic and copies ran while one was open for 6% -> 6% of each run, Pallas kernels for 17% -> 16%
where the time goes in v9:
time: 446 us; the launch traced here: 444 us
  waiting for transfers between devices  252 us (57%)
  Pallas kernels  85.3 us (19%)
  starting transfers between devices  47.1 us (11%)
  local copies, waits for them, and re-layouts  22.2 us (5%)
  other arithmetic  15.6 us (3%)
  between operations  14.4 us (3%)
  matrix products  7.76 us (2%)
    all_to_all x8, waiting for transfers between devices, exchange(): lax.all_to_all(pieces, 'expert', 0, 0, tiled=True, axis_index_groups=by_h...  106 us
    all_gather x4, waiting for transfers between devices, shards(): received[c] = lax.all_gather(partial, 'expert', axis_index_groups=pairs)  87.3 us
    pallas_call x27, Pallas kernels, step_call(): pl.pallas_call(ordered, out_shape=[*out_shape, TOKEN], in_specs=[*in_spec...  85.3 us
    all_gather x1, waiting for transfers between devices, shards(): everyone = lax.all_gather(tokens, 'expert', axis=0, tiled=True)  31.2 us
    all_to_all x8, starting transfers between devices, exchange(): lax.all_to_all(pieces, 'expert', 0, 0, tiled=True, axis_index_groups=by_h...  30.8 us
    ppermute x4, waiting for transfers between devices, shards(): partner[c] = lax.ppermute(own[c], 'groups', partners)  17.8 us
    unnamed x51, local copies, waits for them, and re-layouts  13.9 us
    all_to_all x2, starting transfers between devices, shards(): lax.all_to_all(hidden, 'expert', split_axis=0, concat_axis=0, tiled=True)  9.84 us
  transfers between devices with their start and end apart: 19, of which 12 were waited for; matrix products, arithmetic and copies ran while one was open for 6% of the time, Pallas kernels for 16%

profile of v9, /device:TPU:0, one launch (start us, length us, event | category | flops | bytes accessed | tf_op | source)
XLA Modules:
  0.0 444.1 jit_solution(12115462239899881235)
XLA Ops:
  11.4 5.4 %all-to-all-start = ((bf16[8,2,320,128]{3,2,1,0:T(8,128)(2,1)}), bf16[8,2,320,128]{3,2,1,0:T(8,128)(2,1)S(1)}, u32[]{:S(2)}, u32[]{:S(2)}) async-start(bf16[8,2,320,128]{3,2,1,0:T(8,128)(2,1)} %get-tuple-element.64), calls=%async_computation | async-start | bytes 2621440 | tf_op jit(solution)/shard_map/all_to_all | solution.py:295
  25.1 9.0 %all-to-all-done.refs_3_ = bf16[8,2,320,128]{3,2,1,0:T(8,128)(2,1)S(1)} async-done(((bf16[8,2,320,128]{3,2,1,0:T(8,128)(2,1)}), bf16[8,2,320,128]{3,2,1,0:T(8,128)(2,1)S(1)}, u32[]{:S(2)}, u32[]{:S(2)}) %all-to-all-start) | async-done | bytes 1310752 | tf_op jit(solution)/shard_map/all_to_all | solution.py:295
  48.0 41.9 %all-to-all-done.1.refs_0_ = bf16[8,2,320,256]{3,2,1,0:T(8,128)(2,1)S(1)} async-done(((bf16[8,2,320,256]{3,2,1,0:T(8,128)(2,1)}), bf16[8,2,320,256]{3,2,1,0:T(8,128)(2,1)S(1)}, u32[]{:S(2)}, u32[]{:S(2)}) %all-to-all-start.1) | async-done | bytes 2621472 | tf_op jit(solution)/shard_map/all_to_all | solution.py:295
  95.6 6.3 %fusion.8 = s32[16,64,16]{2,0,1:T(8,128)S(1)} fusion(s32[16,64,16]{2,0,1:T(8,128)S(1)} %copy.55), kind=kOutput, calls=%fused_computation.58 | output fusion | flops 1032192 | bytes 131072 | tf_op jit(solution)/shard_map/jit(cumsum)/reduce_window_sum | solution.py:267
  111.7 5.8 %merge.9 = (bf16[8,320,256]{2,1,0:T(8,128)(2,1)}, f32[8,128]{1,0:T(8,128)}) custom-call(s32[2]{0:T(128)} %pad_add_fusion.refs_0_, s32[32]{0:T(128)} %pad_add_fusion.1.refs_1_, f32[480]{0:T(512)} %mul.52.refs_2_, bf16[8,2,320,256]{3,2,1,0:T(8,128)(2,1)} %get-tuple-element.71.refs_3_, f32[8,128]{1,0:T(8,128)} %get-tuple-element.72.refs_4_), custom_call_target="tpu_custom_call" | custom-call | tf_op jit(solution)/shard_map/merge/pallas_call | solution.py:31
  117.5 6.2 %merge.10 = (bf16[8,320,128]{2,1,0:T(8,128)(2,1)}, f32[8,128]{1,0:T(8,128)}) custom-call(s32[2]{0:T(128)} %pad_add_fusion.refs_0_, s32[32]{0:T(128)} %pad_add_fusion.1.refs_1_, f32[480]{0:T(512)} %mul.52.refs_2_, bf16[8,2,320,128]{3,2,1,0:T(8,128)(2,1)} %copy-done.7, bf16[2,8,320,128]{3,2,1,0:T(8,128)(2,1)} %bitcast.50, f32[8,128]{1,0:T(8,128)} %get-tuple-element.73.refs_5_), custom_call_target="tpu_custom_call" | custom-call | tf_op jit(solution)/shard_map/merge/pallas_call | solution.py:31
  123.6 31.2 %all-gather.10.cloned.1.call-done = bf16[1024,2560]{1,0:T(8,128)(2,1)} async-done(((bf16[64,2560]{1,0:T(8,128)(2,1)}), bf16[1024,2560]{1,0:T(8,128)(2,1)}) %all-gather.10.cloned.1.call-update) | async-done | bytes 5242896 | tf_op jit(solution)/shard_map/all_gather | solution.py:340
  154.8 5.6 %convolution_convert_fusion = bf16[16,48,2560]{2,1,0:T(8,128)(2,1)} fusion(bf16[16,64,2560]{2,1,0:T(8,128)(2,1)} %bitcast.46, s32[16,64]{1,0:T(8,128)S(1)} %bitcast.55, pred[16,64]{1,0:T(8,128)(4,1)S(1)} %fusion.5), kind=kOutput, calls=%fused_computation.4 | convolution fusion | flops 253722624 | bytes 9180160 | tf_op jit(solution)/shard_map/jct,jtd->jcd/dot_general | solution.py:341
  169.1 6.5 %all-to-all-done.4 = bf16[8,320,128]{2,1,0:T(8,128)(2,1)S(1)} async-done(((bf16[8,320,128]{2,1,0:T(8,128)(2,1)}), bf16[8,320,128]{2,1,0:T(8,128)(2,1)S(1)}, u32[]{:S(2)}, u32[]{:S(2)}) %all-to-all-start.4) | async-done | bytes 655392 | tf_op jit(solution)/shard_map/all_to_all | solution.py:295
  179.3 5.8 %merge.11 = (bf16[8,320,256]{2,1,0:T(8,128)(2,1)}, f32[8,128]{1,0:T(8,128)}) custom-call(s32[2]{0:T(128)} %pad_add_fusion.refs_0_, s32[32]{0:T(128)} %pad_add_fusion.1.refs_1_, f32[480]{0:T(512)} %mul.52.refs_2_, bf16[8,2,320,256]{3,2,1,0:T(8,128)(2,1)} %copy-done.1, f32[8,128]{1,0:T(8,128)} %get-tuple-element.82.refs_4_), custom_call_target="tpu_custom_call" | custom-call | tf_op jit(solution)/shard_map/merge/pallas_call | solution.py:31
  185.1 51.4 %all-gather.14.cloned.1.call-done = bf16[16,320,256]{2,1,0:T(8,128)(2,1)} async-done(((bf16[8,320,256]{2,1,0:T(8,128)(2,1)}), bf16[16,320,256]{2,1,0:T(8,128)(2,1)}) %all-gather.14.cloned.1.call-update) | async-done | bytes 2621456 | tf_op jit(solution)/shard_map/all_gather | solution.py:362
  236.5 7.1 %merge.12 = (bf16[8,320,256]{2,1,0:T(8,128)(2,1)}, f32[8,128]{1,0:T(8,128)}) custom-call(s32[2]{0:T(128)} %pad_add_fusion.refs_0_, s32[32]{0:T(128)} %pad_add_fusion.1.refs_1_, f32[480]{0:T(512)} %mul.52.refs_2_, bf16[8,2,320,256]{3,2,1,0:T(8,128)(2,1)} %get-tuple-element.71.refs_3_, bf16[2,8,320,256]{3,2,1,0:T(8,128)(2,1)} %bitcast.49, ...), custom_call_target="tpu_custom_call" | custom-call | tf_op jit(solution)/shard_map/merge/pallas_call | solution.py:31
  250.0 29.5 %all-to-all-done.5 = bf16[8,320,256]{2,1,0:T(8,128)(2,1)S(1)} async-done(((bf16[8,320,256]{2,1,0:T(8,128)(2,1)}), bf16[8,320,256]{2,1,0:T(8,128)(2,1)S(1)}, u32[]{:S(2)}, u32[]{:S(2)}) %all-to-all-start.5) | async-done | bytes 1310752 | tf_op jit(solution)/shard_map/all_to_all | solution.py:295
  285.6 19.4 %all-gather.18.cloned.1.call-done = bf16[16,320,256]{2,1,0:T(8,128)(2,1)} async-done(((bf16[8,320,256]{2,1,0:T(8,128)(2,1)}), bf16[16,320,256]{2,1,0:T(8,128)(2,1)}) %all-gather.18.cloned.1.call-update) | async-done | bytes 2621456 | tf_op jit(solution)/shard_map/all_gather | solution.py:362
  304.9 7.1 %merge.14 = (bf16[8,320,256]{2,1,0:T(8,128)(2,1)}, f32[8,128]{1,0:T(8,128)}) custom-call(s32[2]{0:T(128)} %pad_add_fusion.refs_0_, s32[32]{0:T(128)} %pad_add_fusion.1.refs_1_, f32[480]{0:T(512)} %mul.52.refs_2_, bf16[8,2,320,256]{3,2,1,0:T(8,128)(2,1)} %copy-done.1, bf16[2,8,320,256]{3,2,1,0:T(8,128)(2,1)} %bitcast.48, f32[8,128]{1,0:T(8,128)} %get-tuple-element.91.refs_5_), custom_call_target="tpu_custom_call" | custom-call | tf_op jit(solution)/shard_map/merge/pallas_call | solution.py:31
  324.2 19.6 %all-to-all-done.6 = bf16[8,320,256]{2,1,0:T(8,128)(2,1)S(1)} async-done(((bf16[8,320,256]{2,1,0:T(8,128)(2,1)}), bf16[8,320,256]{2,1,0:T(8,128)(2,1)S(1)}, u32[]{:S(2)}, u32[]{:S(2)}) %all-to-all-start.6) | async-done | bytes 1310752 | tf_op jit(solution)/shard_map/all_to_all | solution.py:295
  346.4 16.5 %all-gather.16.cloned.1.call-done = bf16[16,320,128]{2,1,0:T(8,128)(2,1)} async-done(((bf16[8,320,128]{2,1,0:T(8,128)(2,1)}), bf16[16,320,128]{2,1,0:T(8,128)(2,1)}) %all-gather.16.cloned.1.call-update) | async-done | bytes 1310736 | tf_op jit(solution)/shard_map/all_gather | solution.py:362
  362.9 6.2 %merge.15 = (bf16[8,320,128]{2,1,0:T(8,128)(2,1)}, f32[8,128]{1,0:T(8,128)}) custom-call(s32[2]{0:T(128)} %pad_add_fusion.refs_0_, s32[32]{0:T(128)} %pad_add_fusion.1.refs_1_, f32[480]{0:T(512)} %mul.52.refs_2_, bf16[8,2,320,128]{3,2,1,0:T(8,128)(2,1)} %copy-done.3, bf16[2,8,320,128]{3,2,1,0:T(8,128)(2,1)} %bitcast.51, f32[8,128]{1,0:T(8,128)} %get-tuple-element.98.refs_5_), custom_call_target="tpu_custom_call" | custom-call | tf_op jit(solution)/shard_map/merge/pallas_call | solution.py:31
  369.1 6.9 %run_chunk.5 = (bf16[1,2560,768]{2,1,0:T(8,128)(2,1)}, bf16[1,2560,768]{2,1,0:T(8,128)(2,1)}, bf16[16,48,256]{2,1,0:T(8,128)(2,1)}, f32[8,128]{1,0:T(8,128)}) custom-call(s32[2]{0:T(128)} %pad_add_fusion.refs_0_, bf16[768,2560]{1,0:T(8,128)(2,1)} %bitcast.39, ...), custom_call_target="tpu_custom_call", output_to_operand_aliasing={{0}: (4, {}), {1}: (5, {})} | custom-call | tf_op jit(solution)/shard_map/run_chunk/pallas_call | solution.py:31
  382.9 6.9 %run_chunk.6 = (bf16[1,2560,768]{2,1,0:T(8,128)(2,1)}, bf16[1,2560,768]{2,1,0:T(8,128)(2,1)}, bf16[16,48,256]{2,1,0:T(8,128)(2,1)}, f32[8,128]{1,0:T(8,128)}) custom-call(s32[2]{0:T(128)} %pad_add_fusion.refs_0_, bf16[768,2560]{1,0:T(8,128)(2,1)} %bitcast.40, ...), custom_call_target="tpu_custom_call", output_to_operand_aliasing={{0}: (4, {}), {1}: (5, {})} | custom-call | tf_op jit(solution)/shard_map/run_chunk/pallas_call | solution.py:31
  398.5 15.6 %collective-permute-done.3.refs_3_ = bf16[2560,128]{1,0:T(8,128)(2,1)S(1)} collective-permute-done((bf16[2560,128]{1,0:T(8,128)(2,1)S(1)}, bf16[2560,128]{1,0:T(8,128)(2,1)S(1)}, u32[]{:S(2)}, u32[]{:S(2)}) %collective-permute-start.3) | collective-permute-done | bytes 655392 | tf_op jit(solution)/shard_map/ppermute | solution.py:374
  414.9 5.4 %run_chunk.7 = (bf16[1,2560,768]{2,1,0:T(8,128)(2,1)}, bf16[1,2560,768]{2,1,0:T(8,128)(2,1)}, bf16[16,48,128]{2,1,0:T(8,128)(2,1)}, f32[8,128]{1,0:T(8,128)}) custom-call(s32[2]{0:T(128)} %pad_add_fusion.refs_0_, bf16[768,2560]{1,0:T(8,128)(2,1)} %bitcast.41, ...), custom_call_target="tpu_custom_call", output_to_operand_aliasing={{0}: (4, {}), {1}: (5, {})} | custom-call | tf_op jit(solution)/shard_map/run_chunk/pallas_call | solution.py:31
  421.3 5.7 %all-to-all-start.9 = ((bf16[16,48,128]{2,1,0:T(8,128)(2,1)}), bf16[16,48,128]{2,1,0:T(8,128)(2,1)S(1)}, u32[]{:S(2)}, u32[]{:S(2)}) async-start(bf16[16,48,128]{2,1,0:T(8,128)(2,1)} %get-tuple-element.124), calls=%async_computation.9 | async-start | bytes 393216 | tf_op jit(solution)/shard_map/all_to_all | solution.py:383
  428.9 7.1 %all-to-all-done.9 = bf16[16,48,128]{2,1,0:T(8,128)(2,1)S(1)} async-done(((bf16[16,48,128]{2,1,0:T(8,128)(2,1)}), bf16[16,48,128]{2,1,0:T(8,128)(2,1)S(1)}, u32[]{:S(2)}, u32[]{:S(2)}) %all-to-all-start.9) | async-done | bytes 196640 | tf_op jit(solution)/shard_map/all_to_all | solution.py:383
  (145 shorter events, 101.6 us)
Async XLA Ops:
  11.4 7.0 %copy-start.20 = (f32[32,20,6]{0,1,2:T(8,128)S(1)}, f32[32,20,6]{0,1,2:T(8,128)}, u32[]{:S(2)}) copy-start(f32[32,20,6]{0,1,2:T(8,128)} %param.12) | copy-start | bytes 46084
  11.4 7.2 %copy-start.21 = (f32[32,20,6]{0,1,2:T(8,128)S(1)}, f32[32,20,6]{0,1,2:T(8,128)}, u32[]{:S(2)}) copy-start(f32[32,20,6]{0,1,2:T(8,128)} %param.13) | copy-start | bytes 46084
  11.4 22.7 %all-to-all-start = ((bf16[8,2,320,128]{3,2,1,0:T(8,128)(2,1)}), bf16[8,2,320,128]{3,2,1,0:T(8,128)(2,1)S(1)}, u32[]{:S(2)}, u32[]{:S(2)}) async-start(bf16[8,2,320,128]{3,2,1,0:T(8,128)(2,1)} %get-tuple-element.64), calls=%async_computation | async-start | bytes 2621440 | tf_op jit(solution)/shard_map/all_to_all | solution.py:295
  16.8 100.6 %all-gather.12.cloned.1.call-start = ((), (), s32[]{:S(2)}) async-start(), calls=%async_computation.11 | async-start | bytes 1966080 | tf_op jit(solution)/shard_map/all_gather | solution.py:362
  40.2 114.6 %all-gather.10.cloned.1.call-start = ((), (), s32[]{:S(2)}) async-start(), calls=%async_computation.10 | async-start | bytes 5570560 | tf_op jit(solution)/shard_map/all_gather | solution.py:340
  40.9 48.9 %all-to-all-start.1 = ((bf16[8,2,320,256]{3,2,1,0:T(8,128)(2,1)}), bf16[8,2,320,256]{3,2,1,0:T(8,128)(2,1)S(1)}, u32[]{:S(2)}, u32[]{:S(2)}) async-start(bf16[8,2,320,256]{3,2,1,0:T(8,128)(2,1)} %get-tuple-element.68), calls=%async_computation.1 | async-start | bytes 5242880 | tf_op jit(solution)/shard_map/all_to_all | solution.py:295
  91.4 69.1 %all-to-all-start.2 = ((bf16[8,2,320,256]{3,2,1,0:T(8,128)(2,1)}), bf16[8,2,320,256]{3,2,1,0:T(8,128)(2,1)S(1)}, u32[]{:S(2)}, u32[]{:S(2)}) async-start(bf16[8,2,320,256]{3,2,1,0:T(8,128)(2,1)} %get-tuple-element.75), calls=%async_computation.2 | async-start | bytes 5242880 | tf_op jit(solution)/shard_map/all_to_all | solution.py:295
  161.9 13.7 %all-to-all-start.4 = ((bf16[8,320,128]{2,1,0:T(8,128)(2,1)}), bf16[8,320,128]{2,1,0:T(8,128)(2,1)S(1)}, u32[]{:S(2)}, u32[]{:S(2)}) async-start(bf16[8,320,128]{2,1,0:T(8,128)(2,1)} %get-tuple-element.80), calls=%async_computation.4 | async-start | bytes 1310720 | tf_op jit(solution)/shard_map/all_to_all | solution.py:295
  165.5 71.0 %all-gather.14.cloned.1.call-start = ((), (), s32[]{:S(2)}) async-start(), calls=%async_computation.12 | async-start | bytes 3932160 | tf_op jit(solution)/shard_map/all_gather | solution.py:362
  175.6 68.0 %all-to-all-start.3 = ((bf16[8,2,320,128]{3,2,1,0:T(8,128)(2,1)}), bf16[8,2,320,128]{3,2,1,0:T(8,128)(2,1)S(1)}, u32[]{:S(2)}, u32[]{:S(2)}) async-start(bf16[8,2,320,128]{3,2,1,0:T(8,128)(2,1)} %get-tuple-element.78), calls=%async_computation.3 | async-start | bytes 2621440 | tf_op jit(solution)/shard_map/all_to_all | solution.py:295
  179.2 125.7 %all-gather.18.cloned.1.call-start = ((), (), s32[]{:S(2)}) async-start(), calls=%async_computation.14 | async-start | bytes 3932160 | tf_op jit(solution)/shard_map/all_gather | solution.py:362
  244.7 34.7 %all-to-all-start.5 = ((bf16[8,320,256]{2,1,0:T(8,128)(2,1)}), bf16[8,320,256]{2,1,0:T(8,128)(2,1)S(1)}, u32[]{:S(2)}, u32[]{:S(2)}) async-start(bf16[8,320,256]{2,1,0:T(8,128)(2,1)} %get-tuple-element.86), calls=%async_computation.5 | async-start | bytes 2621440 | tf_op jit(solution)/shard_map/all_to_all | solution.py:295
  248.4 63.6 %collective-permute-start = (bf16[2560,128]{1,0:T(8,128)(2,1)S(1)}, bf16[2560,128]{1,0:T(8,128)(2,1)S(1)}, u32[]{:S(2)}, u32[]{:S(2)}) collective-permute-start(bf16[2560,128]{1,0:T(8,128)(2,1)S(1)} %copy-done.11), channel_id=1, source_target_pairs={{0,16},{16,0},{1,17},{17,1},{2,18},{18,2},{3,19},{19,3},{4,20},{20... | collective-permute-start | bytes 1966088 | tf_op jit(solution)/shard_map/ppermute | solution.py:374
  318.3 25.5 %all-to-all-start.6 = ((bf16[8,320,256]{2,1,0:T(8,128)(2,1)}), bf16[8,320,256]{2,1,0:T(8,128)(2,1)S(1)}, u32[]{:S(2)}, u32[]{:S(2)}) async-start(bf16[8,320,256]{2,1,0:T(8,128)(2,1)} %get-tuple-element.96), calls=%async_computation.6 | async-start | bytes 2621440 | tf_op jit(solution)/shard_map/all_to_all | solution.py:295
  322.0 40.9 %all-gather.16.cloned.1.call-start = ((), (), s32[]{:S(2)}) async-start(), calls=%async_computation.13 | async-start | bytes 1966080 | tf_op jit(solution)/shard_map/all_gather | solution.py:362
  322.6 46.5 %collective-permute-start.1 = (bf16[2560,256]{1,0:T(8,128)(2,1)S(1)}, bf16[2560,256]{1,0:T(8,128)(2,1)}, u32[]{:S(2)}, u32[]{:S(2)}) collective-permute-start(bf16[2560,256]{1,0:T(8,128)(2,1)S(1)} %copy-done.6), channel_id=1, source_target_pairs={{0,16},{16,0},{1,17},{17,1},{2,18},{18,2},{3,19},{19,3},{4,20},{20... | collective-permute-start | bytes 3932168 | tf_op jit(solution)/shard_map/ppermute | solution.py:374
  344.9 36.9 %collective-permute-start.2 = (bf16[2560,256]{1,0:T(8,128)(2,1)}, bf16[2560,256]{1,0:T(8,128)(2,1)S(1)}, u32[]{:S(2)}, u32[]{:S(2)}) collective-permute-start(bf16[2560,256]{1,0:T(8,128)(2,1)} %get-tuple-element.106.refs_2_), channel_id=1, source_target_pairs={{0,16},{16,0},{1,17},{17,1},{2,18},{18,2},{3,19},{19,3},{4,20},{20... | collective-permute-start | bytes 3932168 | tf_op jit(solution)/shard_map/ppermute | solution.py:374
  376.0 13.8 %all-to-all-start.7 = ((bf16[8,320,128]{2,1,0:T(8,128)(2,1)}), bf16[8,320,128]{2,1,0:T(8,128)(2,1)S(1)}, u32[]{:S(2)}, u32[]{:S(2)}) async-start(bf16[8,320,128]{2,1,0:T(8,128)(2,1)} %get-tuple-element.105), calls=%async_computation.7 | async-start | bytes 1310720 | tf_op jit(solution)/shard_map/all_to_all | solution.py:295
  382.9 7.8 %copy-start.18 = (bf16[16,48,256]{2,1,0:T(8,128)(2,1)S(1)}, bf16[16,48,256]{2,1,0:T(8,128)(2,1)}, u32[]{:S(2)}) copy-start(bf16[16,48,256]{2,1,0:T(8,128)(2,1)} %get-tuple-element.115) | copy-start | bytes 1179652
  382.9 7.8 %copy-start.19 = (bf16[16,48,128]{2,1,0:T(8,128)(2,1)S(1)}, bf16[16,48,128]{2,1,0:T(8,128)(2,1)}, u32[]{:S(2)}) copy-start(bf16[16,48,128]{2,1,0:T(8,128)(2,1)} %get-tuple-element.114) | copy-start | bytes 589828
  392.8 27.5 %all-to-all-start.8 = ((bf16[16,48,640]{2,1,0:T(8,128)(2,1)}), bf16[16,48,640]{2,1,0:T(8,128)(2,1)S(1)}, u32[]{:S(2)}, u32[]{:S(2)}) async-start(bf16[16,48,640]{2,1,0:T(8,128)(2,1)} %get-tuple-element.121), calls=%async_computation.8 | async-start | bytes 1966080 | tf_op jit(solution)/shard_map/all_to_all | solution.py:383
  396.9 17.1 %collective-permute-start.3 = (bf16[2560,128]{1,0:T(8,128)(2,1)S(1)}, bf16[2560,128]{1,0:T(8,128)(2,1)S(1)}, u32[]{:S(2)}, u32[]{:S(2)}) collective-permute-start(bf16[2560,128]{1,0:T(8,128)(2,1)S(1)} %copy-done.9), channel_id=1, source_target_pairs={{0,16},{16,0},{1,17},{17,1},{2,18},{18,2},{3,19},{19,3},{4,20},{20... | collective-permute-start | bytes 1966088 | tf_op jit(solution)/shard_map/ppermute | solution.py:374
  414.9 12.1 %copy-start.13 = (pred[384,768]{1,0:T(32,128)(4,1)S(1)}, pred[384,768]{1,0:T(32,128)(4,1)}, u32[]{:S(2)}) copy-start(pred[384,768]{1,0:T(32,128)(4,1)} %convert_element_type.26) | copy-start | bytes 884740
  421.3 14.7 %all-to-all-start.9 = ((bf16[16,48,128]{2,1,0:T(8,128)(2,1)}), bf16[16,48,128]{2,1,0:T(8,128)(2,1)S(1)}, u32[]{:S(2)}, u32[]{:S(2)}) async-start(bf16[16,48,128]{2,1,0:T(8,128)(2,1)} %get-tuple-element.124), calls=%async_computation.9 | async-start | bytes 393216 | tf_op jit(solution)/shard_map/all_to_all | solution.py:383
  (19 other events, 44.7 us)
Sparse Core Ops, SparseCore 0:
  40.3 38.5 all-gather.11
  81.2 73.5 all-gather.9
  167.8 68.5 all-gather.13
  237.9 67.0 all-gather.17
  324.1 38.7 all-gather.15

commit v10 on v9

--- a/solution.py
+++ b/solution.py
@@ -113,29 +113,36 @@
     return value, token
 
 
-def merge(token, info, slots, factors, rows_of, gathered, start, blocks):
+def first_share(devices):
+    return (5 * devices) // 8
+
+
+def merge(token, info, slots, factors, rows_of, received, start, blocks):
     devices, sources, rows, width = rows_of.shape
     steps, column_blocks = blocks
     step = rows // steps
     first = start // BLOCK
-    base_slot = 0 if gathered is None else devices * sources
+    base_slot = 0 if received is None else devices * sources
+    cut = first_share(devices)
+    shares = (slice(0, cut), slice(cut, devices))
 
     def kernel(info_ref, slots_ref, factors_ref, rows_ref, *rest):
         piece = pl.program_id(0)
-        if gathered is None:
-            out_ref, total = rest
+        if received is None:
+            *outs, total = rest
         else:
-            gathered_ref, out_ref, total, received, sem = rest
+            paired_ref, sent_ref, out_ref, total, landed, sem = rest
 
         @pl.when(piece == 0)
         def _():
-            if gathered is None:
+            if received is None:
                 total[...] = jnp.zeros_like(total)
             else:
-                copy = pltpu.make_async_copy(gathered_ref.at[1 - info_ref[1]], received, sem)
+                copy = pltpu.make_async_copy(paired_ref.at[1 - info_ref[1]], landed, sem)
                 copy.start()
+                total[shares[1]] = sent_ref[...].astype(jnp.float32)
                 copy.wait()
-                total[...] = received[...].astype(jnp.float32)
+                total[shares[0]] = landed[...].astype(jnp.float32)
 
         for number in range(sources):
             source = piece * sources + number
@@ -155,26 +162,33 @@
 
         @pl.when(piece == devices - 1)
         def _():
-            out_ref[...] = total[...].astype(jnp.bfloat16)
-
+            if received is None:
+                for out, share in zip(outs, shares):
+                    out[...] = total[share].astype(jnp.bfloat16)
+            else:
+                out_ref[...] = total[...].astype(jnp.bfloat16)
+
+    def block(count):
+        return pl.BlockSpec((count, rows, width), lambda i: (0, 0, 0))
+
+    counts = (cut, devices - cut) if received is None else (devices,)
     scratch = [pltpu.VMEM((devices, rows, width), jnp.float32)]
-    extra = ()
-    if gathered is not None:
-        scratch += [pltpu.VMEM((devices, rows, width), jnp.bfloat16), pltpu.SemaphoreType.DMA]
-        extra = (gathered,)
-    (merged,), token = step_call(
+    extra, extra_specs = (), []
+    if received is not None:
+        scratch += [pltpu.VMEM((cut, rows, width), jnp.bfloat16), pltpu.SemaphoreType.DMA]
+        extra, extra_specs = tuple(received), [ANY, block(devices - cut)]
+    return step_call(
         kernel,
         token,
         (info, slots, factors, rows_of, *extra),
         [SMEM, SMEM, SMEM, pl.BlockSpec((1, sources, rows, width), lambda i: (i, 0, 0, 0))]
-        + [ANY] * len(extra),
-        [jax.ShapeDtypeStruct((devices, rows, width), jnp.bfloat16)],
-        [pl.BlockSpec((devices, rows, width), lambda i: (0, 0, 0))],
+        + extra_specs,
+        [jax.ShapeDtypeStruct((count, rows, width), jnp.bfloat16) for count in counts],
+        [block(count) for count in counts],
         grid=(devices,),
         scratch_shapes=scratch,
         name="merge",
     )
-    return merged, token
 
 
 def run_chunk(token, info, grouped, own, partner, outputs, start, full, devices):
@@ -289,6 +303,7 @@
 
     by_half = [[part * halfway + i for i in range(halfway)] for part in range(2)]
     pairs = [[i, i + halfway] for i in range(halfway)]
+    across = [(i, (i + halfway) % expert_count) for i in range(expert_count)]
     partners = [(g, g ^ 1) for g in range(group_count)]
 
     def exchange(pieces):
@@ -354,14 +369,18 @@
             (pieces,), token = pack(token, info, quant_gate, quant_up, start, width, halfway)
             gathered[c] = exchange(pieces)
         elif name == "partial":
-            if c == 1:
-                gathered[c], token = hold(token, gathered[c], [placing, picking])
+            if c < 2:
+                earlier = [everyone] if c == 0 else [placing, picking]
+                gathered[c], token = hold(token, gathered[c], earlier)
             partial, token = merge(
                 token, info, slots, factors, gathered[c], None, start, blocks_of_rows
             )
-            received[c] = lax.all_gather(partial, "expert", axis_index_groups=pairs)
+            received[c] = [
+                lax.all_gather(partial[0], "expert", axis_index_groups=pairs),
+                lax.ppermute(partial[1], "expert", across),
+            ]
         elif name == "finish":
-            merged[c], token = merge(
+            (merged[c],), token = merge(
                 token, info, slots, factors, gathered[c], received[c], start, blocks_of_rows
             )
         elif name == "back":

time: 446 us -> 482 us (1.081)
  blocking collectives: 0 us -> 45.9 us
  waiting for transfers between devices: 252 us -> 239 us
    all_gather x4 -> x2, waiting for transfers between devices: 87.3 us -> 28.8 us  [shards(): lax.all_gather(partial[0], 'expert', axis_index_groups=pairs)]
    ppermute x0 -> x4, waiting for transfers between devices: none -> 53.7 us  [shards(): lax.ppermute(partial[1], 'expert', across)]
    all_gather x0 -> x2, blocking collectives: none -> 45.9 us  [shards(): lax.all_gather(partial[0], 'expert', axis_index_groups=pairs)]
    all_to_all x8, waiting for transfers between devices: 106 us -> 79.1 us  [exchange(): lax.all_to_all(pieces, 'expert', 0, 0, tiled=True, axis_index_groups=by_h...]
    all_gather x1, waiting for transfers between devices: 31.2 us -> 52.7 us  [shards(): everyone = lax.all_gather(tokens, 'expert', axis=0, tiled=True)]
    unnamed x51 -> x67, local copies, waits for them, and re-layouts: 13.9 us -> 15.2 us
    pallas_call x27 -> x28, Pallas kernels: 85.3 us -> 85.1 us  [step_call(): pl.pallas_call(ordered, out_shape=[*out_shape, TOKEN], in_specs=[*in_spec...]
  transfers between devices with their start and end apart: 19 -> 21, of which waited for: 12 -> 12; matrix products, arithmetic and copies ran while one was open for 6% -> 6% of each run, Pallas kernels for 16% -> 17%
where the time goes in v10:
time: 482 us; the launch traced here: 480 us
  waiting for transfers between devices  239 us (50%)
  Pallas kernels  85.1 us (18%)
  starting transfers between devices  48.5 us (10%)
  blocking collectives  45.9 us (10%)
  local copies, waits for them, and re-layouts  23.5 us (5%)
  other arithmetic  15.6 us (3%)
  between operations  14.4 us (3%)
  matrix products  7.73 us (2%)
    pallas_call x28, Pallas kernels, step_call(): pl.pallas_call(ordered, out_shape=[*out_shape, TOKEN], in_specs=[*in_spec...  85.1 us
    all_to_all x8, waiting for transfers between devices, exchange(): lax.all_to_all(pieces, 'expert', 0, 0, tiled=True, axis_index_groups=by_h...  79.1 us
    ppermute x4, waiting for transfers between devices, shards(): lax.ppermute(partial[1], 'expert', across)  53.7 us
    all_gather x1, waiting for transfers between devices, shards(): everyone = lax.all_gather(tokens, 'expert', axis=0, tiled=True)  52.7 us
    all_gather x2, blocking collectives, shards(): lax.all_gather(partial[0], 'expert', axis_index_groups=pairs)  45.9 us
    all_to_all x8, starting transfers between devices, exchange(): lax.all_to_all(pieces, 'expert', 0, 0, tiled=True, axis_index_groups=by_h...  30.6 us
    all_gather x2, waiting for transfers between devices, shards(): lax.all_gather(partial[0], 'expert', axis_index_groups=pairs)  28.8 us
    ppermute x4, waiting for transfers between devices, shards(): partner[c] = lax.ppermute(own[c], 'groups', partners)  15.5 us
  transfers between devices with their start and end apart: 21, of which 12 were waited for; matrix products, arithmetic and copies ran while one was open for 6% of the time, Pallas kernels for 17%

profile of v10, /device:TPU:0, one launch (start us, length us, event | category | flops | bytes accessed | tf_op | source)
XLA Modules:
  0.0 479.7 jit_solution(6282902903019008172)
XLA Ops:
  20.6 23.7 %all-to-all-done.refs_0_ = bf16[8,2,320,128]{3,2,1,0:T(8,128)(2,1)S(1)} async-done(((bf16[8,2,320,128]{3,2,1,0:T(8,128)(2,1)}), bf16[8,2,320,128]{3,2,1,0:T(8,128)(2,1)S(1)}, u32[]{:S(2)}, u32[]{:S(2)}) %all-to-all-start) | async-done | bytes 1310752 | tf_op jit(solution)/shard_map/all_to_all | solution.py:310
  54.0 52.7 %all-gather.8.cloned.1.call-done.refs_1_ = bf16[1024,2560]{1,0:T(8,128)(2,1)} async-done(((bf16[64,2560]{1,0:T(8,128)(2,1)}), bf16[1024,2560]{1,0:T(8,128)(2,1)}) %all-gather.8.cloned.1.call-update) | async-done | bytes 5242896 | tf_op jit(solution)/shard_map/all_gather | solution.py:355
  120.7 6.3 %fusion.8 = s32[16,64,16]{2,0,1:T(8,128)S(1)} fusion(s32[16,64,16]{2,0,1:T(8,128)S(1)} %copy.56), kind=kOutput, calls=%fused_computation.58 | output fusion | flops 1032192 | bytes 131072 | tf_op jit(solution)/shard_map/jit(cumsum)/reduce_window_sum | solution.py:281
  138.8 5.6 %convolution_convert_fusion = bf16[16,48,2560]{2,1,0:T(8,128)(2,1)} fusion(bf16[16,64,2560]{2,1,0:T(8,128)(2,1)} %bitcast.42, s32[16,64]{1,0:T(8,128)S(1)} %bitcast.55, pred[16,64]{1,0:T(8,128)(4,1)S(1)} %fusion.5), kind=kOutput, calls=%fused_computation.4 | convolution fusion | flops 253722624 | bytes 9180160 | tf_op jit(solution)/shard_map/jct,jtd->jcd/dot_general | solution.py:356
  144.4 5.9 %merge.9 = (bf16[5,320,256]{2,1,0:T(8,128)(2,1)}, bf16[3,320,256]{2,1,0:T(8,128)(2,1)}, f32[8,128]{1,0:T(8,128)}) custom-call(s32[2]{0:T(128)} %pad_add_fusion.refs_0_, s32[32]{0:T(128)} %pad_add_fusion.1.refs_1_, f32[480]{0:T(512)} %mul.52.refs_2_, bf16[8,2,320,256]{3,2,1,0:T(8,128)(2,1)} %get-tuple-element.80.refs_3_, f32[8,128]{1,0:T(8,128)} %get-tuple-element.81.refs_4_), custom_call_target="tpu_custom_call" | custom-call | tf_op jit(solution)/shard_map/merge/pallas_call | solution.py:31
  150.2 25.4 %all-gather = bf16[10,320,128]{2,1,0:T(8,128)(2,1)} all-gather(bf16[5,320,128]{2,1,0:T(8,128)(2,1)S(1)} %copy-done.20), channel_id=2, replica_groups={{0,8},{1,9},{2,10},{3,11},{4,12},{5,13},{6,14},{7,15},{16,24},{17,25},{..., dimensions={0}, use_global_device_ids=true | all-gather | bytes 1228800 | tf_op jit(solution)/shard_map/all_gather | solution.py:379
  176.3 6.1 %merge.10 = (bf16[8,320,128]{2,1,0:T(8,128)(2,1)}, f32[8,128]{1,0:T(8,128)}) custom-call(s32[2]{0:T(128)} %pad_add_fusion.refs_0_, s32[32]{0:T(128)} %pad_add_fusion.1.refs_1_, f32[480]{0:T(512)} %mul.52.refs_2_, bf16[8,2,320,128]{3,2,1,0:T(8,128)(2,1)} %get-tuple-element.73.refs_3_, bf16[2,5,320,128]{3,2,1,0:T(8,128)(2,1)} %bitcast.49, ...), custom_call_target="tpu_custom_call" | custom-call | tf_op jit(solution)/shard_map/merge/pallas_call | solution.py:31
  190.5 7.2 %all-to-all-done.4 = bf16[8,320,128]{2,1,0:T(8,128)(2,1)S(1)} async-done(((bf16[8,320,128]{2,1,0:T(8,128)(2,1)}), bf16[8,320,128]{2,1,0:T(8,128)(2,1)S(1)}, u32[]{:S(2)}, u32[]{:S(2)}) %all-to-all-start.4) | async-done | bytes 655392 | tf_op jit(solution)/shard_map/all_to_all | solution.py:310
  202.4 5.8 %merge.11 = (bf16[5,320,256]{2,1,0:T(8,128)(2,1)}, bf16[3,320,256]{2,1,0:T(8,128)(2,1)}, f32[8,128]{1,0:T(8,128)}) custom-call(s32[2]{0:T(128)} %pad_add_fusion.refs_0_, s32[32]{0:T(128)} %pad_add_fusion.1.refs_1_, f32[480]{0:T(512)} %mul.52.refs_2_, bf16[8,2,320,256]{3,2,1,0:T(8,128)(2,1)} %copy-done.1, f32[8,128]{1,0:T(8,128)} %get-tuple-element.92.refs_4_), custom_call_target="tpu_custom_call" | custom-call | tf_op jit(solution)/shard_map/merge/pallas_call | solution.py:31
  208.3 39.0 %collective-permute-done.1.refs_5_ = bf16[3,320,256]{2,1,0:T(8,128)(2,1)S(1)} collective-permute-done((bf16[3,320,256]{2,1,0:T(8,128)(2,1)S(1)}, bf16[3,320,256]{2,1,0:T(8,128)(2,1)S(1)}, u32[]{:S(2)}, u32[]{:S(2)}) %collective-permute-start.1) | collective-permute-done | bytes 491552 | tf_op jit(solution)/shard_map/ppermute | solution.py:380
  247.2 15.2 %all-gather.10.cloned.1.call-done = bf16[10,320,256]{2,1,0:T(8,128)(2,1)} async-done(((bf16[5,320,256]{2,1,0:T(8,128)(2,1)}), bf16[10,320,256]{2,1,0:T(8,128)(2,1)}) %all-gather.10.cloned.1.call-update) | async-done | bytes 1638416 | tf_op jit(solution)/shard_map/all_gather | solution.py:379
  262.5 7.0 %merge.12 = (bf16[8,320,256]{2,1,0:T(8,128)(2,1)}, f32[8,128]{1,0:T(8,128)}) custom-call(s32[2]{0:T(128)} %pad_add_fusion.refs_0_, s32[32]{0:T(128)} %pad_add_fusion.1.refs_1_, f32[480]{0:T(512)} %mul.52.refs_2_, bf16[8,2,320,256]{3,2,1,0:T(8,128)(2,1)} %get-tuple-element.80.refs_3_, bf16[2,5,320,256]{3,2,1,0:T(8,128)(2,1)} %bitcast.51, ...), custom_call_target="tpu_custom_call" | custom-call | tf_op jit(solution)/shard_map/merge/pallas_call | solution.py:31
  277.3 25.2 %all-to-all-done.5 = bf16[8,320,256]{2,1,0:T(8,128)(2,1)S(1)} async-done(((bf16[8,320,256]{2,1,0:T(8,128)(2,1)}), bf16[8,320,256]{2,1,0:T(8,128)(2,1)S(1)}, u32[]{:S(2)}, u32[]{:S(2)}) %all-to-all-start.5) | async-done | bytes 1310752 | tf_op jit(solution)/shard_map/all_to_all | solution.py:310
  308.7 14.7 %collective-permute-done.3.refs_5_ = bf16[3,320,256]{2,1,0:T(8,128)(2,1)S(1)} collective-permute-done((bf16[3,320,256]{2,1,0:T(8,128)(2,1)}, bf16[3,320,256]{2,1,0:T(8,128)(2,1)S(1)}, u32[]{:S(2)}, u32[]{:S(2)}) %collective-permute-start.3) | collective-permute-done | bytes 491552 | tf_op jit(solution)/shard_map/ppermute | solution.py:380
  323.4 13.5 %all-gather.12.cloned.1.call-done = bf16[10,320,256]{2,1,0:T(8,128)(2,1)} async-done(((bf16[5,320,256]{2,1,0:T(8,128)(2,1)}), bf16[10,320,256]{2,1,0:T(8,128)(2,1)}) %all-gather.12.cloned.1.call-update) | async-done | bytes 1638416 | tf_op jit(solution)/shard_map/all_gather | solution.py:379
  337.0 7.0 %merge.14 = (bf16[8,320,256]{2,1,0:T(8,128)(2,1)}, f32[8,128]{1,0:T(8,128)}) custom-call(s32[2]{0:T(128)} %pad_add_fusion.refs_0_, s32[32]{0:T(128)} %pad_add_fusion.1.refs_1_, f32[480]{0:T(512)} %mul.52.refs_2_, bf16[8,2,320,256]{3,2,1,0:T(8,128)(2,1)} %copy-done.1, bf16[2,5,320,256]{3,2,1,0:T(8,128)(2,1)} %bitcast.50, bf16[3,320,256]{2,1,0:T(8,128)(2,1)} %copy-done.18, ...), custom_call_target="tpu_custom_call" | custom-call | tf_op jit(solution)/shard_map/merge/pallas_call | solution.py:31
  355.5 20.9 %all-to-all-done.6 = bf16[8,320,256]{2,1,0:T(8,128)(2,1)S(1)} async-done(((bf16[8,320,256]{2,1,0:T(8,128)(2,1)}), bf16[8,320,256]{2,1,0:T(8,128)(2,1)S(1)}, u32[]{:S(2)}, u32[]{:S(2)}) %all-to-all-start.6) | async-done | bytes 1310752 | tf_op jit(solution)/shard_map/all_to_all | solution.py:310
  377.9 20.4 %all-gather.2 = bf16[10,320,128]{2,1,0:T(8,128)(2,1)} all-gather(bf16[5,320,128]{2,1,0:T(8,128)(2,1)S(1)} %copy-done.21), channel_id=4, replica_groups={{0,8},{1,9},{2,10},{3,11},{4,12},{5,13},{6,14},{7,15},{16,24},{17,25},{..., dimensions={0}, use_global_device_ids=true | all-gather | bytes 1228800 | tf_op jit(solution)/shard_map/all_gather | solution.py:379
  399.0 6.1 %merge.15 = (bf16[8,320,128]{2,1,0:T(8,128)(2,1)}, f32[8,128]{1,0:T(8,128)}) custom-call(s32[2]{0:T(128)} %pad_add_fusion.refs_0_, s32[32]{0:T(128)} %pad_add_fusion.1.refs_1_, f32[480]{0:T(512)} %mul.52.refs_2_, bf16[8,2,320,128]{3,2,1,0:T(8,128)(2,1)} %copy-done.3, bf16[2,5,320,128]{3,2,1,0:T(8,128)(2,1)} %bitcast.48, bf16[3,320,128]{2,1,0:T(8,128)(2,1)} %copy-done.24, ...), custom_call_target="tpu_custom_call" | custom-call | tf_op jit(solution)/shard_map/merge/pallas_call | solution.py:31
  405.2 6.9 %run_chunk.5 = (bf16[1,2560,768]{2,1,0:T(8,128)(2,1)}, bf16[1,2560,768]{2,1,0:T(8,128)(2,1)}, bf16[16,48,256]{2,1,0:T(8,128)(2,1)}, f32[8,128]{1,0:T(8,128)}) custom-call(s32[2]{0:T(128)} %pad_add_fusion.refs_0_, bf16[768,2560]{1,0:T(8,128)(2,1)} %bitcast.39, ...), custom_call_target="tpu_custom_call", output_to_operand_aliasing={{0}: (4, {}), {1}: (5, {})} | custom-call | tf_op jit(solution)/shard_map/run_chunk/pallas_call | solution.py:31
  416.8 7.0 %run_chunk.6 = (bf16[1,2560,768]{2,1,0:T(8,128)(2,1)}, bf16[1,2560,768]{2,1,0:T(8,128)(2,1)}, bf16[16,48,256]{2,1,0:T(8,128)(2,1)}, f32[8,128]{1,0:T(8,128)}) custom-call(s32[2]{0:T(128)} %pad_add_fusion.refs_0_, bf16[768,2560]{1,0:T(8,128)(2,1)} %bitcast.40, ...), custom_call_target="tpu_custom_call", output_to_operand_aliasing={{0}: (4, {}), {1}: (5, {})} | custom-call | tf_op jit(solution)/shard_map/run_chunk/pallas_call | solution.py:31
  434.3 15.5 %collective-permute-done.7.refs_3_ = bf16[2560,128]{1,0:T(8,128)(2,1)S(1)} collective-permute-done((bf16[2560,128]{1,0:T(8,128)(2,1)S(1)}, bf16[2560,128]{1,0:T(8,128)(2,1)S(1)}, u32[]{:S(2)}, u32[]{:S(2)}) %collective-permute-start.7) | collective-permute-done | bytes 655392 | tf_op jit(solution)/shard_map/ppermute | solution.py:393
  456.9 5.7 %all-to-all-start.9 = ((bf16[16,48,128]{2,1,0:T(8,128)(2,1)}), bf16[16,48,128]{2,1,0:T(8,128)(2,1)S(1)}, u32[]{:S(2)}, u32[]{:S(2)}) async-start(bf16[16,48,128]{2,1,0:T(8,128)(2,1)} %get-tuple-element.136), calls=%async_computation.9 | async-start | bytes 393216 | tf_op jit(solution)/shard_map/all_to_all | solution.py:402
  464.5 7.2 %all-to-all-done.9 = bf16[16,48,128]{2,1,0:T(8,128)(2,1)S(1)} async-done(((bf16[16,48,128]{2,1,0:T(8,128)(2,1)}), bf16[16,48,128]{2,1,0:T(8,128)(2,1)S(1)}, u32[]{:S(2)}, u32[]{:S(2)}) %all-to-all-start.9) | async-done | bytes 196640 | tf_op jit(solution)/shard_map/all_to_all | solution.py:402
  (166 shorter events, 115.2 us)
Async XLA Ops:
  7.2 99.4 %all-gather.8.cloned.1.call-start = ((), (), s32[]{:S(2)}) async-start(), calls=%async_computation.10 | async-start | bytes 5570560 | tf_op jit(solution)/shard_map/all_gather | solution.py:355
  12.1 32.2 %all-to-all-start = ((bf16[8,2,320,128]{3,2,1,0:T(8,128)(2,1)}), bf16[8,2,320,128]{3,2,1,0:T(8,128)(2,1)S(1)}, u32[]{:S(2)}, u32[]{:S(2)}) async-start(bf16[8,2,320,128]{3,2,1,0:T(8,128)(2,1)} %get-tuple-element.70), calls=%async_computation | async-start | bytes 2621440 | tf_op jit(solution)/shard_map/all_to_all | solution.py:310
  45.4 69.6 %all-to-all-start.1 = ((bf16[8,2,320,256]{3,2,1,0:T(8,128)(2,1)}), bf16[8,2,320,256]{3,2,1,0:T(8,128)(2,1)S(1)}, u32[]{:S(2)}, u32[]{:S(2)}) async-start(bf16[8,2,320,256]{3,2,1,0:T(8,128)(2,1)} %get-tuple-element.77), calls=%async_computation.1 | async-start | bytes 5242880 | tf_op jit(solution)/shard_map/all_to_all | solution.py:310
  116.5 66.0 %all-to-all-start.2 = ((bf16[8,2,320,256]{3,2,1,0:T(8,128)(2,1)}), bf16[8,2,320,256]{3,2,1,0:T(8,128)(2,1)S(1)}, u32[]{:S(2)}, u32[]{:S(2)}) async-start(bf16[8,2,320,256]{3,2,1,0:T(8,128)(2,1)} %get-tuple-element.84), calls=%async_computation.2 | async-start | bytes 5242880 | tf_op jit(solution)/shard_map/all_to_all | solution.py:310
  136.8 38.8 %collective-permute-start = (bf16[3,320,128]{2,1,0:T(8,128)(2,1)}, bf16[3,320,128]{2,1,0:T(8,128)(2,1)S(1)}, u32[]{:S(2)}, u32[]{:S(2)}) collective-permute-start(bf16[3,320,128]{2,1,0:T(8,128)(2,1)} %get-tuple-element.76), channel_id=1, source_target_pairs={{0,8},{1,9},{2,10},{3,11},{4,12},{5,13},{6,14},{7,15},{8,0},{9,1},... | collective-permute-start | bytes 737288 | tf_op jit(solution)/shard_map/ppermute | solution.py:380
  184.0 13.7 %all-to-all-start.4 = ((bf16[8,320,128]{2,1,0:T(8,128)(2,1)}), bf16[8,320,128]{2,1,0:T(8,128)(2,1)S(1)}, u32[]{:S(2)}, u32[]{:S(2)}) async-start(bf16[8,320,128]{2,1,0:T(8,128)(2,1)} %get-tuple-element.90), calls=%async_computation.4 | async-start | bytes 1310720 | tf_op jit(solution)/shard_map/all_to_all | solution.py:310
  197.7 71.8 %all-to-all-start.3 = ((bf16[8,2,320,128]{3,2,1,0:T(8,128)(2,1)}), bf16[8,2,320,128]{3,2,1,0:T(8,128)(2,1)S(1)}, u32[]{:S(2)}, u32[]{:S(2)}) async-start(bf16[8,2,320,128]{3,2,1,0:T(8,128)(2,1)} %get-tuple-element.87), calls=%async_computation.3 | async-start | bytes 2621440 | tf_op jit(solution)/shard_map/all_to_all | solution.py:310
  201.3 61.2 %all-gather.10.cloned.1.call-start = ((), (), s32[]{:S(2)}) async-start(), calls=%async_computation.11 | async-start | bytes 2457600 | tf_op jit(solution)/shard_map/all_gather | solution.py:379
  202.1 45.2 %collective-permute-start.1 = (bf16[3,320,256]{2,1,0:T(8,128)(2,1)S(1)}, bf16[3,320,256]{2,1,0:T(8,128)(2,1)S(1)}, u32[]{:S(2)}, u32[]{:S(2)}) collective-permute-start(bf16[3,320,256]{2,1,0:T(8,128)(2,1)S(1)} %copy-done.30), channel_id=1, source_target_pairs={{0,8},{1,9},{2,10},{3,11},{4,12},{5,13},{6,14},{7,15},{8,0},{9,1},... | collective-permute-start | bytes 1474568 | tf_op jit(solution)/shard_map/ppermute | solution.py:380
  247.2 15.2 %copy-start.19 = (bf16[3,320,256]{2,1,0:T(8,128)(2,1)}, bf16[3,320,256]{2,1,0:T(8,128)(2,1)S(1)}, u32[]{:S(2)}) copy-start(bf16[3,320,256]{2,1,0:T(8,128)(2,1)S(1)} %collective-permute-done.1.refs_5_) | copy-start | bytes 1474564
  270.6 32.0 %all-to-all-start.5 = ((bf16[8,320,256]{2,1,0:T(8,128)(2,1)}), bf16[8,320,256]{2,1,0:T(8,128)(2,1)S(1)}, u32[]{:S(2)}, u32[]{:S(2)}) async-start(bf16[8,320,256]{2,1,0:T(8,128)(2,1)} %get-tuple-element.96), calls=%async_computation.5 | async-start | bytes 2621440 | tf_op jit(solution)/shard_map/all_to_all | solution.py:310
  274.3 62.7 %all-gather.12.cloned.1.call-start = ((), (), s32[]{:S(2)}) async-start(), calls=%async_computation.12 | async-start | bytes 2457600 | tf_op jit(solution)/shard_map/all_gather | solution.py:379
  275.0 69.0 %collective-permute-start.4 = (bf16[2560,128]{1,0:T(8,128)(2,1)S(1)}, bf16[2560,128]{1,0:T(8,128)(2,1)S(1)}, u32[]{:S(2)}, u32[]{:S(2)}) collective-permute-start(bf16[2560,128]{1,0:T(8,128)(2,1)S(1)} %copy-done.11), channel_id=1, source_target_pairs={{0,16},{16,0},{1,17},{17,1},{2,18},{18,2},{3,19},{19,3},{4,20},{20... | collective-permute-start | bytes 1966088 | tf_op jit(solution)/shard_map/ppermute | solution.py:393
  276.7 46.7 %collective-permute-start.3 = (bf16[3,320,256]{2,1,0:T(8,128)(2,1)}, bf16[3,320,256]{2,1,0:T(8,128)(2,1)S(1)}, u32[]{:S(2)}, u32[]{:S(2)}) collective-permute-start(bf16[3,320,256]{2,1,0:T(8,128)(2,1)} %get-tuple-element.102), channel_id=1, source_target_pairs={{0,8},{1,9},{2,10},{3,11},{4,12},{5,13},{6,14},{7,15},{8,0},{9,1},... | collective-permute-start | bytes 1474568 | tf_op jit(solution)/shard_map/ppermute | solution.py:380
  323.4 13.5 %copy-start.18 = (bf16[3,320,256]{2,1,0:T(8,128)(2,1)}, bf16[3,320,256]{2,1,0:T(8,128)(2,1)S(1)}, u32[]{:S(2)}) copy-start(bf16[3,320,256]{2,1,0:T(8,128)(2,1)S(1)} %collective-permute-done.3.refs_5_) | copy-start | bytes 1474564
  350.2 27.7 %copy-start.21 = (bf16[5,320,128]{2,1,0:T(8,128)(2,1)S(1)}, bf16[5,320,128]{2,1,0:T(8,128)(2,1)}, u32[]{:S(2)}) copy-start(bf16[5,320,128]{2,1,0:T(8,128)(2,1)} %get-tuple-element.99) | copy-start | bytes 1228804
  350.2 26.2 %all-to-all-start.6 = ((bf16[8,320,256]{2,1,0:T(8,128)(2,1)}), bf16[8,320,256]{2,1,0:T(8,128)(2,1)S(1)}, u32[]{:S(2)}, u32[]{:S(2)}) async-start(bf16[8,320,256]{2,1,0:T(8,128)(2,1)} %get-tuple-element.108), calls=%async_computation.6 | async-start | bytes 2621440 | tf_op jit(solution)/shard_map/all_to_all | solution.py:310
  353.9 51.3 %collective-permute-start.5 = (bf16[2560,256]{1,0:T(8,128)(2,1)S(1)}, bf16[2560,256]{1,0:T(8,128)(2,1)}, u32[]{:S(2)}, u32[]{:S(2)}) collective-permute-start(bf16[2560,256]{1,0:T(8,128)(2,1)S(1)} %copy-done.6), channel_id=1, source_target_pairs={{0,16},{16,0},{1,17},{17,1},{2,18},{18,2},{3,19},{19,3},{4,20},{20... | collective-permute-start | bytes 3932168 | tf_op jit(solution)/shard_map/ppermute | solution.py:393
  354.4 43.9 %collective-permute-start.2 = (bf16[3,320,128]{2,1,0:T(8,128)(2,1)S(1)}, bf16[3,320,128]{2,1,0:T(8,128)(2,1)S(1)}, u32[]{:S(2)}, u32[]{:S(2)}) collective-permute-start(bf16[3,320,128]{2,1,0:T(8,128)(2,1)S(1)} %copy-done.31), channel_id=1, source_target_pairs={{0,8},{1,9},{2,10},{3,11},{4,12},{5,13},{6,14},{7,15},{8,0},{9,1},... | collective-permute-start | bytes 737288 | tf_op jit(solution)/shard_map/ppermute | solution.py:380
  377.5 38.2 %collective-permute-start.6 = (bf16[2560,256]{1,0:T(8,128)(2,1)}, bf16[2560,256]{1,0:T(8,128)(2,1)S(1)}, u32[]{:S(2)}, u32[]{:S(2)}) collective-permute-start(bf16[2560,256]{1,0:T(8,128)(2,1)} %get-tuple-element.118.refs_2_), channel_id=1, source_target_pairs={{0,16},{16,0},{1,17},{17,1},{2,18},{18,2},{3,19},{19,3},{4,20},{20... | collective-permute-start | bytes 3932168 | tf_op jit(solution)/shard_map/ppermute | solution.py:393
  412.1 13.7 %all-to-all-start.7 = ((bf16[8,320,128]{2,1,0:T(8,128)(2,1)}), bf16[8,320,128]{2,1,0:T(8,128)(2,1)S(1)}, u32[]{:S(2)}, u32[]{:S(2)}) async-start(bf16[8,320,128]{2,1,0:T(8,128)(2,1)} %get-tuple-element.117), calls=%async_computation.7 | async-start | bytes 1310720 | tf_op jit(solution)/shard_map/all_to_all | solution.py:310
  428.8 27.2 %all-to-all-start.8 = ((bf16[16,48,640]{2,1,0:T(8,128)(2,1)}), bf16[16,48,640]{2,1,0:T(8,128)(2,1)S(1)}, u32[]{:S(2)}, u32[]{:S(2)}) async-start(bf16[16,48,640]{2,1,0:T(8,128)(2,1)} %get-tuple-element.133), calls=%async_computation.8 | async-start | bytes 1966080 | tf_op jit(solution)/shard_map/all_to_all | solution.py:402
  432.6 17.1 %collective-permute-start.7 = (bf16[2560,128]{1,0:T(8,128)(2,1)S(1)}, bf16[2560,128]{1,0:T(8,128)(2,1)S(1)}, u32[]{:S(2)}, u32[]{:S(2)}) collective-permute-start(bf16[2560,128]{1,0:T(8,128)(2,1)S(1)} %copy-done.9), channel_id=1, source_target_pairs={{0,16},{16,0},{1,17},{17,1},{2,18},{18,2},{3,19},{19,3},{4,20},{20... | collective-permute-start | bytes 1966088 | tf_op jit(solution)/shard_map/ppermute | solution.py:393
  456.9 14.7 %all-to-all-start.9 = ((bf16[16,48,128]{2,1,0:T(8,128)(2,1)}), bf16[16,48,128]{2,1,0:T(8,128)(2,1)S(1)}, u32[]{:S(2)}, u32[]{:S(2)}) async-start(bf16[16,48,128]{2,1,0:T(8,128)(2,1)} %get-tuple-element.136), calls=%async_computation.9 | async-start | bytes 393216 | tf_op jit(solution)/shard_map/all_to_all | solution.py:402
  (29 other events, 111.6 us)
Sparse Core Ops, SparseCore 0:
  10.3 96.2 all-gather.7
  203.7 58.7 all-gather.9
  276.7 60.2 all-gather.11

commit v11 on v9

--- a/solution.py
+++ b/solution.py
@@ -113,65 +113,45 @@
     return value, token
 
 
-def merge(token, info, slots, factors, rows_of, gathered, start, blocks):
+def merge(token, slots, factors, rows_of, start, blocks):
     devices, sources, rows, width = rows_of.shape
     steps, column_blocks = blocks
     step = rows // steps
     first = start // BLOCK
-    base_slot = 0 if gathered is None else devices * sources
-
-    def kernel(info_ref, slots_ref, factors_ref, rows_ref, *rest):
+
+    def kernel(slots_ref, factors_ref, rows_ref, out_ref, total):
         piece = pl.program_id(0)
-        if gathered is None:
-            out_ref, total = rest
-        else:
-            gathered_ref, out_ref, total, received, sem = rest
 
         @pl.when(piece == 0)
         def _():
-            if gathered is None:
-                total[...] = jnp.zeros_like(total)
-            else:
-                copy = pltpu.make_async_copy(gathered_ref.at[1 - info_ref[1]], received, sem)
-                copy.start()
-                copy.wait()
-                total[...] = received[...].astype(jnp.float32)
+            total[...] = jnp.zeros_like(total)
 
         for number in range(sources):
             source = piece * sources + number
-            slot = slots_ref[base_slot + source]
-
-            @pl.when(slot >= 0)
-            def _():
-                for index in range(steps):
-                    for part in range(width // BLOCK):
-                        base = (source * steps + index) * column_blocks + first
-                        lanes = slice(part * BLOCK, (part + 1) * BLOCK)
-                        place = slice(index * step, (index + 1) * step)
-                        total[slot, place, lanes] += (
-                            rows_ref[0, number, place, lanes].astype(jnp.float32)
-                            * factors_ref[base + part]
-                        )
+            slot = slots_ref[source]
+            for index in range(steps):
+                for part in range(width // BLOCK):
+                    base = (source * steps + index) * column_blocks + first
+                    lanes = slice(part * BLOCK, (part + 1) * BLOCK)
+                    place = slice(index * step, (index + 1) * step)
+                    total[slot, place, lanes] += (
+                        rows_ref[0, number, place, lanes].astype(jnp.float32)
+                        * factors_ref[base + part]
+                    )
 
         @pl.when(piece == devices - 1)
         def _():
             out_ref[...] = total[...].astype(jnp.bfloat16)
 
-    scratch = [pltpu.VMEM((devices, rows, width), jnp.float32)]
-    extra = ()
-    if gathered is not None:
-        scratch += [pltpu.VMEM((devices, rows, width), jnp.bfloat16), pltpu.SemaphoreType.DMA]
-        extra = (gathered,)
     (merged,), token = step_call(
         kernel,
         token,
-        (info, slots, factors, rows_of, *extra),
-        [SMEM, SMEM, SMEM, pl.BlockSpec((1, sources, rows, width), lambda i: (i, 0, 0, 0))]
-        + [ANY] * len(extra),
+        (slots, factors, rows_of),
+        [SMEM, SMEM, pl.BlockSpec((1, sources, rows, width), lambda i: (i, 0, 0, 0))],
         [jax.ShapeDtypeStruct((devices, rows, width), jnp.bfloat16)],
         [pl.BlockSpec((devices, rows, width), lambda i: (0, 0, 0))],
         grid=(devices,),
-        scratch_shapes=scratch,
+        scratch_shapes=[pltpu.VMEM((devices, rows, width), jnp.float32)],
         name="merge",
     )
     return merged, token
@@ -238,25 +218,19 @@
 
 
 def plan(count):
-    order = [("pack", 0)]
-    for chunk in range(count + 1):
+    order = [("pack", 0), ("raw", 0), ("pack", 1), ("raw", 1), ("sum", 0)]
+    for chunk in range(count):
+        if chunk + 2 < count:
+            order.append(("pack", chunk + 2))
+        order.append(("back", chunk))
         if chunk + 1 < count:
-            order.append(("pack", chunk + 1))
-        if chunk >= 2:
-            order.append(("trade", chunk - 2))
-        if chunk < count:
-            order.append(("partial", chunk))
+            order.append(("sum", chunk + 1))
         if chunk >= 1:
-            order.append(("finish", chunk - 1))
-        if chunk >= 3:
-            order.append(("run", chunk - 3))
-        if chunk >= 1:
-            order.append(("back", chunk - 1))
-    order.append(("run", count - 2))
-    order.append(("trade", count - 1))
-    order.append(("give", 0))
-    order.append(("run", count - 1))
-    order.append(("give", 1))
+            order.append(("run", chunk - 1))
+        order.append(("trade", chunk))
+        if chunk + 2 < count:
+            order.append(("raw", chunk + 2))
+    order.extend([("give", 0), ("run", count - 1), ("give", 1)])
     return order
 
 
@@ -269,10 +243,11 @@
 
 
 def chunk_widths(blocks):
-    if blocks < 4:
-        return [1] * blocks
-    middle, odd = divmod(blocks - 2, 2)
-    return [1] + [2] * middle + [1] * odd + [1]
+    widths = []
+    while blocks > 0:
+        widths.append(max(1, (blocks + 1) // 2 if blocks > 3 else blocks - 1))
+        blocks -= widths[-1]
+    return widths
 
 
 def shards(tokens, routes, quant_gate, quant_up, gate_scales, up_scales, cluster_ids, frequency):
@@ -280,35 +255,23 @@
     own_index = lax.axis_index("expert")
     group_count = lax.axis_size("groups")
     half = lax.axis_index("groups") % 2
-    halfway = expert_count // 2
-    side, place = own_index // halfway, own_index % halfway
     depth, full = quant_gate.shape[1:]
     tok_dev = tokens.shape[0]
     top_count = routes.shape[1]
     capacity = min(tok_dev, 2 * tok_dev * top_count // expert_count)
 
-    by_half = [[part * halfway + i for i in range(halfway)] for part in range(2)]
-    pairs = [[i, i + halfway] for i in range(halfway)]
     partners = [(g, g ^ 1) for g in range(group_count)]
 
     def exchange(pieces):
-        return lax.all_to_all(pieces, "expert", 0, 0, tiled=True, axis_index_groups=by_half)
-
-    info = jnp.stack([half, side]).astype(jnp.int32)
-    sources = quant_gate.shape[0]
-    rows = depth // halfway
+        return lax.all_to_all(pieces, "expert", 0, 0, tiled=True)
+
+    info = jnp.stack([half]).astype(jnp.int32)
+    rows = depth // expert_count
     step = math.gcd(rows, BLOCK)
-    held = side * halfway * sources + jnp.arange(halfway * sources, dtype=jnp.int32)
-    target = jnp.take(cluster_ids[:, 0], held)
-    slots = jnp.concatenate(
-        [
-            jnp.where(target // halfway != side, target % halfway, -1),
-            jnp.where(target // halfway == side, target % halfway, -1),
-        ]
-    )
-    weights = jnp.take(cluster_weights(cluster_ids, frequency), held)
-    scales = jnp.take(jnp.where(half == 0, gate_scales, up_scales), held, axis=0)
-    row_blocks = (place * rows + step * jnp.arange(rows // step, dtype=jnp.int32)) // BLOCK
+    slots = cluster_ids[:, 0]
+    weights = cluster_weights(cluster_ids, frequency)
+    scales = jnp.where(half == 0, gate_scales, up_scales)
+    row_blocks = (own_index * rows + step * jnp.arange(rows // step, dtype=jnp.int32)) // BLOCK
     factors = jnp.take(scales, row_blocks, axis=1) * weights[:, None, None]
     blocks_of_rows = factors.shape[1:]
     factors = factors.reshape(-1)
@@ -346,27 +309,23 @@
     ).astype(jnp.bfloat16)
     arrived = lax.all_gather(arrived, "mp", axis=2, tiled=True)
     grouped = arrived.reshape(expert_count * capacity, depth)
-    gathered, received, merged, own, partner, hiddens = ({} for _ in range(6))
+    pieces, gathered, merged, own, partner, hiddens = ({} for _ in range(6))
     outputs, returned, last = (), [], len(widths) - 1
     for name, c in plan(len(widths)):
         start, width = starts[c], widths[c] * BLOCK
         if name == "pack":
-            (pieces,), token = pack(token, info, quant_gate, quant_up, start, width, halfway)
-            gathered[c] = exchange(pieces)
-        elif name == "partial":
-            if c == 1:
-                gathered[c], token = hold(token, gathered[c], [placing, picking])
-            partial, token = merge(
-                token, info, slots, factors, gathered[c], None, start, blocks_of_rows
+            (pieces[c],), token = pack(
+                token, info, quant_gate, quant_up, start, width, expert_count
             )
-            received[c] = lax.all_gather(partial, "expert", axis_index_groups=pairs)
-        elif name == "finish":
-            merged[c], token = merge(
-                token, info, slots, factors, gathered[c], received[c], start, blocks_of_rows
-            )
+        elif name == "raw":
+            if c >= 2:
+                pieces[c], token = hold(token, pieces[c], [])
+            gathered[c] = exchange(pieces[c])
+        elif name == "sum":
+            merged[c], token = merge(token, slots, factors, gathered[c], start, blocks_of_rows)
         elif name == "back":
-            earlier = [gathered[c + 2]] if c + 2 in gathered else []
-            earlier += [grouped] if c == 0 else []
+            earlier = [gathered[c + 1]] if c + 1 in gathered else []
+            earlier += [placing, picking] if c == 0 else [grouped] if c == 1 else []
             merged[c], token = hold(token, merged[c], earlier)
             own[c] = exchange(merged[c])
         elif name == "trade":
@@ -379,9 +338,7 @@
         else:
             batch = [hiddens[i] for i in (range(last) if c == 0 else range(last, last + 1))]
             hidden, token = hold(token, jnp.concatenate(batch, axis=2), returned[:c])
-            returned.append(
-                lax.all_to_all(hidden, "expert", split_axis=0, concat_axis=0, tiled=True)
-            )
+            returned.append(exchange(hidden))
 
     finished = [
         jnp.dot(

time: 446 us -> 446 us (level)
  starting transfers between devices: 47.1 us -> 90 us
  Pallas kernels: 85.3 us -> 58.3 us
  waiting for transfers between devices: 252 us -> 242 us
  local copies, waits for them, and re-layouts: 22.2 us -> 16.9 us
    all_gather x4 -> x0, waiting for transfers between devices: 87.3 us -> none  [shards(): received[c] = lax.all_gather(partial, 'expert', axis_index_groups=pairs)]
    ppermute x4 -> x3, waiting for transfers between devices: 17.8 us -> 74 us  [shards(): partner[c] = lax.ppermute(own[c], 'groups', partners)]
    all_to_all x10 -> x8, waiting for transfers between devices: 114 us -> 167 us  [exchange(): return lax.all_to_all(pieces, 'expert', 0, 0, tiled=True)]
    all_to_all x10 -> x8, starting transfers between devices: 40.6 us -> 85.3 us  [exchange(): return lax.all_to_all(pieces, 'expert', 0, 0, tiled=True)]
    all_gather x1, waiting for transfers between devices: 31.2 us -> 0.02 us  [shards(): everyone = lax.all_gather(tokens, 'expert', axis=0, tiled=True)]
    pallas_call x27 -> x18, Pallas kernels: 85.3 us -> 58.3 us  [step_call(): pl.pallas_call(ordered, out_shape=[*out_shape, TOKEN], in_specs=[*in_spec...]
    unnamed x51 -> x35, local copies, waits for them, and re-layouts: 13.9 us -> 9.57 us
  transfers between devices with their start and end apart: 19 -> 12, of which waited for: 12 -> 8; matrix products, arithmetic and copies ran while one was open for 6% -> 6% of each run, Pallas kernels for 16% -> 12%
where the time goes in v11:
time: 446 us; the launch traced here: 445 us
  waiting for transfers between devices  242 us (54%)
  starting transfers between devices  90 us (20%)
  Pallas kernels  58.3 us (13%)
  local copies, waits for them, and re-layouts  16.9 us (4%)
  other arithmetic  15 us (3%)
  between operations  14.4 us (3%)
  matrix products  7.75 us (2%)
    all_to_all x8, waiting for transfers between devices, exchange(): return lax.all_to_all(pieces, 'expert', 0, 0, tiled=True)  167 us
    all_to_all x8, starting transfers between devices, exchange(): return lax.all_to_all(pieces, 'expert', 0, 0, tiled=True)  85.3 us
    ppermute x3, waiting for transfers between devices, shards(): partner[c] = lax.ppermute(own[c], 'groups', partners)  74 us
    pallas_call x18, Pallas kernels, step_call(): pl.pallas_call(ordered, out_shape=[*out_shape, TOKEN], in_specs=[*in_spec...  58.3 us
    unnamed x35, local copies, waits for them, and re-layouts  9.57 us
  transfers between devices with their start and end apart: 12, of which 8 were waited for; matrix products, arithmetic and copies ran while one was open for 6% of the time, Pallas kernels for 12%

profile of v11, /device:TPU:0, one launch (start us, length us, event | category | flops | bytes accessed | tf_op | source)
XLA Modules:
  0.0 444.5 jit_solution(4801158783192249812)
XLA Ops:
  12.0 7.4 %all-to-all-start = ((bf16[16,2,160,384]{3,2,1,0:T(8,128)(2,1)}), bf16[16,2,160,384]{3,2,1,0:T(8,128)(2,1)}, u32[]{:S(2)}, u32[]{:S(2)}) async-start(bf16[16,2,160,384]{3,2,1,0:T(8,128)(2,1)} %get-tuple-element.44), calls=%async_computation | async-start | bytes 7864320 | tf_op jit(solution)/shard_map/all_to_all | solution.py:266
  22.2 70.3 %all-to-all-done.refs_2_ = bf16[16,2,160,384]{3,2,1,0:T(8,128)(2,1)} async-done(((bf16[16,2,160,384]{3,2,1,0:T(8,128)(2,1)}), bf16[16,2,160,384]{3,2,1,0:T(8,128)(2,1)}, u32[]{:S(2)}, u32[]{:S(2)}) %all-to-all-start) | async-done | bytes 3932192 | tf_op jit(solution)/shard_map/all_to_all | solution.py:266
  92.6 18.7 %all-to-all-start.1 = ((bf16[16,2,160,256]{3,2,1,0:T(8,128)(2,1)}), bf16[16,2,160,256]{3,2,1,0:T(8,128)(2,1)S(1)}, u32[]{:S(2)}, u32[]{:S(2)}) async-start(bf16[16,2,160,256]{3,2,1,0:T(8,128)(2,1)} %get-tuple-element.50), calls=%async_computation.1 | async-start | bytes 5242880 | tf_op jit(solution)/shard_map/all_to_all | solution.py:266
  114.5 6.3 %fusion.7 = s32[16,64,16]{2,0,1:T(8,128)S(1)} fusion(s32[16,64,16]{2,0,1:T(8,128)S(1)} %copy.39), kind=kOutput, calls=%fused_computation.38 | output fusion | flops 1032192 | bytes 131072 | tf_op jit(solution)/shard_map/jit(cumsum)/reduce_window_sum | solution.py:241
  131.6 10.3 %merge.3 = (bf16[16,160,384]{2,1,0:T(8,128)(2,1)}, f32[8,128]{1,0:T(8,128)}) custom-call(s32[32]{0:T(128)} %bitcast.40, f32[960]{0:T(1024)} %mul.47.refs_1_, bf16[16,2,160,384]{3,2,1,0:T(8,128)(2,1)} %all-to-all-done.refs_2_, f32[8,128]{1,0:T(8,128)} %get-tuple-element.46.refs_3_), custom_call_target="tpu_custom_call" | custom-call | tf_op jit(solution)/shard_map/merge/pallas_call | solution.py:31
  144.2 38.7 %all-to-all-done.1.refs_1_.refs_2_ = bf16[16,2,160,256]{3,2,1,0:T(8,128)(2,1)S(1)} async-done(((bf16[16,2,160,256]{3,2,1,0:T(8,128)(2,1)}), bf16[16,2,160,256]{3,2,1,0:T(8,128)(2,1)S(1)}, u32[]{:S(2)}, u32[]{:S(2)}) %all-to-all-start.1) | async-done | bytes 2621472 | tf_op jit(solution)/shard_map/all_to_all | solution.py:266
  184.4 23.5 %all-to-all-start.2 = ((bf16[16,160,384]{2,1,0:T(8,128)(2,1)}), bf16[16,160,384]{2,1,0:T(8,128)(2,1)S(1)}, u32[]{:S(2)}, u32[]{:S(2)}) async-start(bf16[16,160,384]{2,1,0:T(8,128)(2,1)} %get-tuple-element.52), calls=%async_computation.2 | async-start | bytes 3932160 | tf_op jit(solution)/shard_map/all_to_all | solution.py:266
  207.9 9.4 %merge.4 = (bf16[16,160,256]{2,1,0:T(8,128)(2,1)}, f32[8,128]{1,0:T(8,128)}) custom-call(s32[32]{0:T(128)} %bitcast.41, f32[960]{0:T(1024)} %mul.47.refs_1_, bf16[16,2,160,256]{3,2,1,0:T(8,128)(2,1)} %copy-done, f32[8,128]{1,0:T(8,128)} %get-tuple-element.53.refs_3_), custom_call_target="tpu_custom_call" | custom-call | tf_op jit(solution)/shard_map/merge/pallas_call | solution.py:31
  217.3 29.4 %all-to-all-done.2 = bf16[16,160,384]{2,1,0:T(8,128)(2,1)S(1)} async-done(((bf16[16,160,384]{2,1,0:T(8,128)(2,1)}), bf16[16,160,384]{2,1,0:T(8,128)(2,1)S(1)}, u32[]{:S(2)}, u32[]{:S(2)}) %all-to-all-start.2) | async-done | bytes 1966112 | tf_op jit(solution)/shard_map/all_to_all | solution.py:266
  248.0 10.7 %all-to-all-start.3 = ((bf16[16,2,160,128]{3,2,1,0:T(8,128)(2,1)}), bf16[16,2,160,128]{3,2,1,0:T(8,128)(2,1)S(1)}, u32[]{:S(2)}, u32[]{:S(2)}) async-start(bf16[16,2,160,128]{3,2,1,0:T(8,128)(2,1)} %get-tuple-element.56), calls=%async_computation.3 | async-start | bytes 2621440 | tf_op jit(solution)/shard_map/all_to_all | solution.py:266
  258.7 5.6 %convolution_convert_fusion = bf16[16,48,2560]{2,1,0:T(8,128)(2,1)} fusion(bf16[16,64,2560]{2,1,0:T(8,128)(2,1)} %bitcast.34, s32[16,64]{1,0:T(8,128)S(1)} %bitcast.39, pred[16,64]{1,0:T(8,128)(4,1)S(1)} %fusion.5), kind=kOutput, calls=%fused_computation.1 | convolution fusion | flops 253722624 | bytes 9180160 | tf_op jit(solution)/shard_map/jct,jtd->jcd/dot_general | solution.py:304
  264.3 21.8 %all-to-all-done.3.refs_1_.refs_2_ = bf16[16,2,160,128]{3,2,1,0:T(8,128)(2,1)S(1)} async-done(((bf16[16,2,160,128]{3,2,1,0:T(8,128)(2,1)}), bf16[16,2,160,128]{3,2,1,0:T(8,128)(2,1)S(1)}, u32[]{:S(2)}, u32[]{:S(2)}) %all-to-all-start.3) | async-done | bytes 1310752 | tf_op jit(solution)/shard_map/all_to_all | solution.py:266
  287.2 8.1 %all-to-all-start.4 = ((bf16[16,160,256]{2,1,0:T(8,128)(2,1)}), bf16[16,160,256]{2,1,0:T(8,128)(2,1)S(1)}, u32[]{:S(2)}, u32[]{:S(2)}) async-start(bf16[16,160,256]{2,1,0:T(8,128)(2,1)} %get-tuple-element.61), calls=%async_computation.4 | async-start | bytes 2621440 | tf_op jit(solution)/shard_map/all_to_all | solution.py:266
  296.9 8.6 %merge.5 = (bf16[16,160,128]{2,1,0:T(8,128)(2,1)}, f32[8,128]{1,0:T(8,128)}) custom-call(s32[32]{0:T(128)} %bitcast.42, f32[960]{0:T(1024)} %mul.47.refs_1_, bf16[16,2,160,128]{3,2,1,0:T(8,128)(2,1)} %copy-done.4, f32[8,128]{1,0:T(8,128)} %get-tuple-element.59.refs_3_), custom_call_target="tpu_custom_call" | custom-call | tf_op jit(solution)/shard_map/merge/pallas_call | solution.py:31
  305.5 35.1 %collective-permute-done.refs_3_ = bf16[2560,384]{1,0:T(8,128)(2,1)} collective-permute-done((bf16[2560,384]{1,0:T(8,128)(2,1)S(1)}, bf16[2560,384]{1,0:T(8,128)(2,1)}, u32[]{:S(2)}, u32[]{:S(2)}) %collective-permute-start) | collective-permute-done | bytes 1966112 | tf_op jit(solution)/shard_map/ppermute | solution.py:333
  340.7 8.4 %run_chunk.3 = (bf16[1,2560,768]{2,1,0:T(8,128)(2,1)}, bf16[1,2560,768]{2,1,0:T(8,128)(2,1)}, bf16[16,48,384]{2,1,0:T(8,128)(2,1)}, f32[8,128]{1,0:T(8,128)}) custom-call(s32[1]{0:T(128)} %bitcast.refs_0_, bf16[768,2560]{1,0:T(8,128)(2,1)} %bitcast.28, bf16[2560,384]{1,0:T(8,128)(2,1)} %get-tuple-element.62.refs_2_, ...), custom_call_target="tpu_custom_call" | custom-call | tf_op jit(solution)/shard_map/run_chunk/pallas_call | solution.py:31
  351.6 5.7 %all-to-all-start.5 = ((bf16[16,160,128]{2,1,0:T(8,128)(2,1)}), bf16[16,160,128]{2,1,0:T(8,128)(2,1)S(1)}, u32[]{:S(2)}, u32[]{:S(2)}) async-start(bf16[16,160,128]{2,1,0:T(8,128)(2,1)} %get-tuple-element.66), calls=%async_computation.5 | async-start | bytes 1310720 | tf_op jit(solution)/shard_map/all_to_all | solution.py:266
  357.4 23.3 %collective-permute-done.1.refs_3_ = bf16[2560,256]{1,0:T(8,128)(2,1)S(1)} collective-permute-done((bf16[2560,256]{1,0:T(8,128)(2,1)}, bf16[2560,256]{1,0:T(8,128)(2,1)S(1)}, u32[]{:S(2)}, u32[]{:S(2)}) %collective-permute-start.1) | collective-permute-done | bytes 1310752 | tf_op jit(solution)/shard_map/ppermute | solution.py:333
  381.8 6.9 %run_chunk.4 = (bf16[1,2560,768]{2,1,0:T(8,128)(2,1)}, bf16[1,2560,768]{2,1,0:T(8,128)(2,1)}, bf16[16,48,256]{2,1,0:T(8,128)(2,1)}, f32[8,128]{1,0:T(8,128)}) custom-call(s32[1]{0:T(128)} %bitcast.refs_0_, bf16[768,2560]{1,0:T(8,128)(2,1)} %bitcast.29, bf16[2560,256]{1,0:T(8,128)(2,1)} %get-tuple-element.67.refs_2_, ...), custom_call_target="tpu_custom_call", output_to_operand_aliasing={{0}: (4, {}), {1}: (5, {})} | custom-call | tf_op jit(solution)/shard_map/run_chunk/pallas_call | solution.py:31
  391.7 5.4 %all-to-all-start.6 = ((bf16[16,48,640]{2,1,0:T(8,128)(2,1)}), bf16[16,48,640]{2,1,0:T(8,128)(2,1)S(1)}, u32[]{:S(2)}, u32[]{:S(2)}) async-start(bf16[16,48,640]{2,1,0:T(8,128)(2,1)} %get-tuple-element.81), calls=%async_computation.6 | async-start | bytes 1966080 | tf_op jit(solution)/shard_map/all_to_all | solution.py:266
  398.7 15.6 %collective-permute-done.2.refs_3_ = bf16[2560,128]{1,0:T(8,128)(2,1)S(1)} collective-permute-done((bf16[2560,128]{1,0:T(8,128)(2,1)S(1)}, bf16[2560,128]{1,0:T(8,128)(2,1)S(1)}, u32[]{:S(2)}, u32[]{:S(2)}) %collective-permute-start.2) | collective-permute-done | bytes 655392 | tf_op jit(solution)/shard_map/ppermute | solution.py:333
  415.1 5.4 %run_chunk.5 = (bf16[1,2560,768]{2,1,0:T(8,128)(2,1)}, bf16[1,2560,768]{2,1,0:T(8,128)(2,1)}, bf16[16,48,128]{2,1,0:T(8,128)(2,1)}, f32[8,128]{1,0:T(8,128)}) custom-call(s32[1]{0:T(128)} %bitcast.refs_0_, bf16[768,2560]{1,0:T(8,128)(2,1)} %bitcast.30, bf16[2560,128]{1,0:T(8,128)(2,1)} %get-tuple-element.72.refs_2_, ...), custom_call_target="tpu_custom_call", output_to_operand_aliasing={{0}: (4, {}), {1}: (5, {})} | custom-call | tf_op jit(solution)/shard_map/run_chunk/pallas_call | solution.py:31
  421.5 5.7 %all-to-all-start.7 = ((bf16[16,48,128]{2,1,0:T(8,128)(2,1)}), bf16[16,48,128]{2,1,0:T(8,128)(2,1)S(1)}, u32[]{:S(2)}, u32[]{:S(2)}) async-start(bf16[16,48,128]{2,1,0:T(8,128)(2,1)} %get-tuple-element.84), calls=%async_computation.7 | async-start | bytes 393216 | tf_op jit(solution)/shard_map/all_to_all | solution.py:266
  429.0 7.1 %all-to-all-done.7 = bf16[16,48,128]{2,1,0:T(8,128)(2,1)S(1)} async-done(((bf16[16,48,128]{2,1,0:T(8,128)(2,1)}), bf16[16,48,128]{2,1,0:T(8,128)(2,1)S(1)}, u32[]{:S(2)}, u32[]{:S(2)}) %all-to-all-start.7) | async-done | bytes 196640 | tf_op jit(solution)/shard_map/all_to_all | solution.py:266
  (89 shorter events, 42.5 us)
Async XLA Ops:
  12.0 80.6 %all-to-all-start = ((bf16[16,2,160,384]{3,2,1,0:T(8,128)(2,1)}), bf16[16,2,160,384]{3,2,1,0:T(8,128)(2,1)}, u32[]{:S(2)}, u32[]{:S(2)}) async-start(bf16[16,2,160,384]{3,2,1,0:T(8,128)(2,1)} %get-tuple-element.44), calls=%async_computation | async-start | bytes 7864320 | tf_op jit(solution)/shard_map/all_to_all | solution.py:266
  92.5 19.5 %copy-start.15 = (s32[32,1]{0,1:T(1,128)S(1)}, s32[32,1]{0,1:T(1,128)}, u32[]{:S(2)}) copy-start(s32[32,1]{0,1:T(1,128)} %param.14) | copy-start | bytes 388
  92.5 19.5 %copy-start.16 = (f32[32]{0:T(128)S(1)}, f32[32]{0:T(128)}, u32[]{:S(2)}) copy-start(f32[32]{0:T(128)} %param.15) | copy-start | bytes 388
  92.5 19.7 %copy-start.14 = (s32[1024,6]{0,1:T(8,128)S(1)}, s32[1024,6]{0,1:T(8,128)}, u32[]{:S(2)}) copy-start(s32[1024,6]{0,1:T(8,128)} %param.9) | copy-start | bytes 73732
  92.5 20.1 %copy-start.12 = (f32[32,20,6]{0,1,2:T(8,128)S(1)}, f32[32,20,6]{0,1,2:T(8,128)}, u32[]{:S(2)}) copy-start(f32[32,20,6]{0,1,2:T(8,128)} %param.13) | copy-start | bytes 46084
  92.5 20.1 %copy-start.13 = (f32[32,20,6]{0,1,2:T(8,128)S(1)}, f32[32,20,6]{0,1,2:T(8,128)}, u32[]{:S(2)}) copy-start(f32[32,20,6]{0,1,2:T(8,128)} %param.12) | copy-start | bytes 46084
  92.6 90.4 %all-to-all-start.1 = ((bf16[16,2,160,256]{3,2,1,0:T(8,128)(2,1)}), bf16[16,2,160,256]{3,2,1,0:T(8,128)(2,1)S(1)}, u32[]{:S(2)}, u32[]{:S(2)}) async-start(bf16[16,2,160,256]{3,2,1,0:T(8,128)(2,1)} %get-tuple-element.50), calls=%async_computation.1 | async-start | bytes 5242880 | tf_op jit(solution)/shard_map/all_to_all | solution.py:266
  111.3 147.4 %all-gather.2.cloned.1.call-start = ((), (), s32[]{:S(2)}) async-start(), calls=%async_computation.8 | async-start | bytes 5570560 | tf_op jit(solution)/shard_map/all_gather | solution.py:303
  182.9 1.5 copy-start
  184.4 62.3 %all-to-all-start.2 = ((bf16[16,160,384]{2,1,0:T(8,128)(2,1)}), bf16[16,160,384]{2,1,0:T(8,128)(2,1)S(1)}, u32[]{:S(2)}, u32[]{:S(2)}) async-start(bf16[16,160,384]{2,1,0:T(8,128)(2,1)} %get-tuple-element.52), calls=%async_computation.2 | async-start | bytes 3932160 | tf_op jit(solution)/shard_map/all_to_all | solution.py:266
  246.7 1.3 copy-start.1
  248.0 38.1 %all-to-all-start.3 = ((bf16[16,2,160,128]{3,2,1,0:T(8,128)(2,1)}), bf16[16,2,160,128]{3,2,1,0:T(8,128)(2,1)S(1)}, u32[]{:S(2)}, u32[]{:S(2)}) async-start(bf16[16,2,160,128]{3,2,1,0:T(8,128)(2,1)} %get-tuple-element.56), calls=%async_computation.3 | async-start | bytes 2621440 | tf_op jit(solution)/shard_map/all_to_all | solution.py:266
  287.2 8.2 %copy-start.2 = (bf16[2560,384]{1,0:T(8,128)(2,1)S(1)}, bf16[2560,384]{1,0:T(8,128)(2,1)}, u32[]{:S(2)}) copy-start(bf16[2560,384]{1,0:T(8,128)(2,1)} %get-tuple-element.62.refs_2_) | copy-start | bytes 5898244
  287.2 61.9 %all-to-all-start.4 = ((bf16[16,160,256]{2,1,0:T(8,128)(2,1)}), bf16[16,160,256]{2,1,0:T(8,128)(2,1)S(1)}, u32[]{:S(2)}, u32[]{:S(2)}) async-start(bf16[16,160,256]{2,1,0:T(8,128)(2,1)} %get-tuple-element.61), calls=%async_computation.4 | async-start | bytes 2621440 | tf_op jit(solution)/shard_map/all_to_all | solution.py:266
  295.3 45.3 %collective-permute-start = (bf16[2560,384]{1,0:T(8,128)(2,1)S(1)}, bf16[2560,384]{1,0:T(8,128)(2,1)}, u32[]{:S(2)}, u32[]{:S(2)}) collective-permute-start(bf16[2560,384]{1,0:T(8,128)(2,1)S(1)} %copy-done.2), channel_id=1, source_target_pairs={{0,16},{16,0},{1,17},{17,1},{2,18},{18,2},{3,19},{19,3},{4,20},{20... | collective-permute-start | bytes 5898248 | tf_op jit(solution)/shard_map/ppermute | solution.py:333
  350.1 30.5 %collective-permute-start.1 = (bf16[2560,256]{1,0:T(8,128)(2,1)}, bf16[2560,256]{1,0:T(8,128)(2,1)S(1)}, u32[]{:S(2)}, u32[]{:S(2)}) collective-permute-start(bf16[2560,256]{1,0:T(8,128)(2,1)} %get-tuple-element.67.refs_2_), channel_id=1, source_target_pairs={{0,16},{16,0},{1,17},{17,1},{2,18},{18,2},{3,19},{19,3},{4,20},{20... | collective-permute-start | bytes 3932168 | tf_op jit(solution)/shard_map/ppermute | solution.py:333
  351.6 37.1 %all-to-all-start.5 = ((bf16[16,160,128]{2,1,0:T(8,128)(2,1)}), bf16[16,160,128]{2,1,0:T(8,128)(2,1)S(1)}, u32[]{:S(2)}, u32[]{:S(2)}) async-start(bf16[16,160,128]{2,1,0:T(8,128)(2,1)} %get-tuple-element.66), calls=%async_computation.5 | async-start | bytes 1310720 | tf_op jit(solution)/shard_map/all_to_all | solution.py:266
  380.7 1.1 copy-start.9
  381.8 7.8 %copy-start.11 = (bf16[16,48,384]{2,1,0:T(8,128)(2,1)S(1)}, bf16[16,48,384]{2,1,0:T(8,128)(2,1)}, u32[]{:S(2)}) copy-start(bf16[16,48,384]{2,1,0:T(8,128)(2,1)} %get-tuple-element.75) | copy-start | bytes 1769476
  389.6 7.5 %copy-start.6 = (bf16[2560,128]{1,0:T(8,128)(2,1)S(1)}, bf16[2560,128]{1,0:T(8,128)(2,1)}, u32[]{:S(2)}) copy-start(bf16[2560,128]{1,0:T(8,128)(2,1)} %get-tuple-element.72.refs_2_) | copy-start | bytes 1966084
  391.7 28.8 %all-to-all-start.6 = ((bf16[16,48,640]{2,1,0:T(8,128)(2,1)}), bf16[16,48,640]{2,1,0:T(8,128)(2,1)S(1)}, u32[]{:S(2)}, u32[]{:S(2)}) async-start(bf16[16,48,640]{2,1,0:T(8,128)(2,1)} %get-tuple-element.81), calls=%async_computation.6 | async-start | bytes 1966080 | tf_op jit(solution)/shard_map/all_to_all | solution.py:266
  397.1 17.1 %collective-permute-start.2 = (bf16[2560,128]{1,0:T(8,128)(2,1)S(1)}, bf16[2560,128]{1,0:T(8,128)(2,1)S(1)}, u32[]{:S(2)}, u32[]{:S(2)}) collective-permute-start(bf16[2560,128]{1,0:T(8,128)(2,1)S(1)} %copy-done.6), channel_id=1, source_target_pairs={{0,16},{16,0},{1,17},{17,1},{2,18},{18,2},{3,19},{19,3},{4,20},{20... | collective-permute-start | bytes 1966088 | tf_op jit(solution)/shard_map/ppermute | solution.py:333
  415.1 12.1 %copy-start.8 = (pred[384,768]{1,0:T(32,128)(4,1)S(1)}, pred[384,768]{1,0:T(32,128)(4,1)}, u32[]{:S(2)}) copy-start(pred[384,768]{1,0:T(32,128)(4,1)} %convert_element_type.26) | copy-start | bytes 884740
  421.5 14.7 %all-to-all-start.7 = ((bf16[16,48,128]{2,1,0:T(8,128)(2,1)}), bf16[16,48,128]{2,1,0:T(8,128)(2,1)S(1)}, u32[]{:S(2)}, u32[]{:S(2)}) async-start(bf16[16,48,128]{2,1,0:T(8,128)(2,1)} %get-tuple-element.84), calls=%async_computation.7 | async-start | bytes 393216 | tf_op jit(solution)/shard_map/all_to_all | solution.py:266
  (5 other events, 4.8 us)
Sparse Core Ops, SparseCore 0:
  114.4 85.3 all-gather.1

commit v12 on v11

--- a/solution.py
+++ b/solution.py
@@ -9,6 +9,7 @@
 
 D = 2560
 BLOCK = 128
+PLANES = 4
 TOKEN = jax.ShapeDtypeStruct((8, 128), jnp.float32)
 ANY = pl.BlockSpec(memory_space=pl.ANY)
 SMEM = pl.BlockSpec(memory_space=pltpu.SMEM)
@@ -157,10 +158,48 @@
     return merged, token
 
 
-def run_chunk(token, info, grouped, own, partner, outputs, start, full, devices):
+def pair(token, tokens, other):
+    def kernel(tokens_ref, other_ref, out_ref):
+        out_ref[0] = tokens_ref[...]
+        out_ref[1] = other_ref[...]
+
+    (both,), token = step_call(
+        kernel,
+        token,
+        (tokens, other),
+        [VMEM, VMEM],
+        [jax.ShapeDtypeStruct((2,) + tokens.shape, tokens.dtype)],
+        [VMEM],
+        name="pair",
+    )
+    return both, token
+
+
+def line(token, info, both, nearby):
+    _, tok_dev, width = both.shape
+
+    def kernel(info_ref, both_ref, nearby_ref, out_ref):
+        level = info_ref[1]
+        for index, other in enumerate((both_ref, nearby_ref)):
+            out_ref[level ^ index] = other[0]
+            out_ref[level ^ index ^ (PLANES // 2)] = other[1]
+
+    (whole,), token = step_call(
+        kernel,
+        token,
+        (info, both, nearby),
+        [SMEM, VMEM, VMEM],
+        [jax.ShapeDtypeStruct((PLANES, tok_dev, width), both.dtype)],
+        [VMEM],
+        name="line",
+    )
+    return whole, token
+
+
+def run_chunk(token, info, grouped, own, partner, outputs, start, full, blocks):
     depth, width = own.shape
     count = grouped.shape[0]
-    each = count // devices
+    each = count // len(blocks)
     factor = 1.0 / math.sqrt(D)
 
     def kernel(info_ref, grouped_ref, own_ref, partner_ref, *rest):
@@ -195,7 +234,8 @@
         gate_value = values[:, :width] * factor
         up_value = values[:, width:] * factor
         hidden = (gate_value / (1.0 + jnp.exp(-gate_value)) * up_value).astype(jnp.bfloat16)
-        hidden_ref[...] = hidden.reshape(devices, each, width)
+        for index, block in enumerate(blocks):
+            hidden_ref[block] = hidden[index * each : (index + 1) * each]
         for store in stores:
             store.wait()
 
@@ -205,7 +245,7 @@
         token,
         (info, grouped, own, partner, *outputs),
         [SMEM, VMEM, ANY, ANY] + [ANY] * len(outputs),
-        [weights, weights, jax.ShapeDtypeStruct((devices, each, width), jnp.bfloat16)],
+        [weights, weights, jax.ShapeDtypeStruct((len(blocks), each, width), jnp.bfloat16)],
         [ANY, ANY, VMEM],
         scratch_shapes=[
             pltpu.VMEM((depth, 2 * width), jnp.bfloat16),
@@ -217,20 +257,27 @@
     )
 
 
+def first_runs(count):
+    return max(1, count - 2)
+
+
 def plan(count):
-    order = [("pack", 0), ("raw", 0), ("pack", 1), ("raw", 1), ("sum", 0)]
+    cut = first_runs(count)
+    order = [("pack", 0), ("raw", 0), ("pack", 1), ("pair", 0), ("line", 0), ("raw", 1), ("sum", 0)]
     for chunk in range(count):
         if chunk + 2 < count:
             order.append(("pack", chunk + 2))
         order.append(("back", chunk))
         if chunk + 1 < count:
             order.append(("sum", chunk + 1))
-        if chunk >= 1:
-            order.append(("run", chunk - 1))
+        if chunk + 1 == count:
+            order.extend(("run", earlier) for earlier in range(cut))
         order.append(("trade", chunk))
         if chunk + 2 < count:
             order.append(("raw", chunk + 2))
-    order.extend([("give", 0), ("run", count - 1), ("give", 1)])
+    order.append(("give", 0))
+    order.extend(("run", later) for later in range(cut, count))
+    order.append(("give", 1))
     return order
 
 
@@ -260,12 +307,16 @@
     top_count = routes.shape[1]
     capacity = min(tok_dev, 2 * tok_dev * top_count // expert_count)
 
+    plane = expert_count // PLANES
+    by_plane = [[z * plane + p for p in range(plane)] for z in range(PLANES)]
+    across = [(i, (i + expert_count // 2) % expert_count) for i in range(expert_count)]
+    beside = [(i, (i // plane ^ 1) * plane + i % plane) for i in range(expert_count)]
     partners = [(g, g ^ 1) for g in range(group_count)]
 
     def exchange(pieces):
         return lax.all_to_all(pieces, "expert", 0, 0, tiled=True)
 
-    info = jnp.stack([half]).astype(jnp.int32)
+    info = jnp.stack([half, own_index // plane]).astype(jnp.int32)
     rows = depth // expert_count
     step = math.gcd(rows, BLOCK)
     slots = cluster_ids[:, 0]
@@ -279,8 +330,11 @@
     hit_table, position_lookup = route_slots(routes, expert_count, tok_dev)
     positions = jnp.arange(capacity, dtype=jnp.int32)
 
+    blocks = [z * plane + p for p in range(plane) for z in range(PLANES)]
+
     def in_blocks(table):
         column = lax.dynamic_index_in_dim(table, own_index, 2, keepdims=False)
+        column = column.reshape(PLANES, plane, tok_dev).transpose(1, 0, 2)
         return column.reshape(expert_count, 1, tok_dev)
 
     placing = (
@@ -300,32 +354,37 @@
     widths = chunk_widths(full // BLOCK)
     starts = [BLOCK * sum(widths[:chunk]) for chunk in range(len(widths))]
     token = jnp.zeros(TOKEN.shape, TOKEN.dtype)
-    everyone = lax.all_gather(tokens, "expert", axis=0, tiled=True)
-    arrived = jnp.einsum(
-        "jct,jtd->jcd",
-        placing,
-        everyone.reshape(expert_count, tok_dev, everyone.shape[1]),
-        preferred_element_type=jnp.float32,
-    ).astype(jnp.bfloat16)
-    arrived = lax.all_gather(arrived, "mp", axis=2, tiled=True)
-    grouped = arrived.reshape(expert_count * capacity, depth)
+    opposite = lax.ppermute(tokens, "expert", across)
     pieces, gathered, merged, own, partner, hiddens = ({} for _ in range(6))
     outputs, returned, last = (), [], len(widths) - 1
+    cut = first_runs(len(widths))
     for name, c in plan(len(widths)):
         start, width = starts[c], widths[c] * BLOCK
         if name == "pack":
             (pieces[c],), token = pack(
                 token, info, quant_gate, quant_up, start, width, expert_count
             )
+        elif name == "pair":
+            both, token = pair(token, tokens, opposite)
+            nearby = lax.ppermute(both, "expert", beside)
+        elif name == "line":
+            whole, token = line(token, info, both, nearby)
+            everyone = lax.all_gather(whole, "expert", axis=0, tiled=True, axis_index_groups=by_plane)
+            arrived = jnp.einsum(
+                "jct,jtd->jcd", placing, everyone, preferred_element_type=jnp.float32
+            ).astype(jnp.bfloat16)
+            arrived = lax.all_gather(arrived, "mp", axis=2, tiled=True)
+            grouped = arrived.reshape(expert_count * capacity, depth)
         elif name == "raw":
-            if c >= 2:
-                pieces[c], token = hold(token, pieces[c], [])
+            if c >= 1:
+                pieces[c], token = hold(token, pieces[c], [gathered[0]] if c == 1 else [])
             gathered[c] = exchange(pieces[c])
         elif name == "sum":
             merged[c], token = merge(token, slots, factors, gathered[c], start, blocks_of_rows)
         elif name == "back":
             earlier = [gathered[c + 1]] if c + 1 in gathered else []
             earlier += [placing, picking] if c == 0 else [grouped] if c == 1 else []
+            earlier += [partner[c - 1]] if 0 < c < last else []
             merged[c], token = hold(token, merged[c], earlier)
             own[c] = exchange(merged[c])
         elif name == "trade":
@@ -333,10 +392,10 @@
             partner[c] = lax.ppermute(own[c], "groups", partners)
         elif name == "run":
             (*outputs, hiddens[c]), token = run_chunk(
-                token, info, grouped, own[c], partner[c], outputs, start, full, expert_count
+                token, info, grouped, own[c], partner[c], outputs, start, full, blocks
             )
         else:
-            batch = [hiddens[i] for i in (range(last) if c == 0 else range(last, last + 1))]
+            batch = [hiddens[i] for i in (range(cut) if c == 0 else range(cut, last + 1))]
             hidden, token = hold(token, jnp.concatenate(batch, axis=2), returned[:c])
             returned.append(exchange(hidden))
 

time: 446 us -> 441 us (0.989)
  starting transfers between devices: 90 us -> 67.3 us
  waiting for transfers between devices: 242 us -> 252 us
  Pallas kernels: 58.3 us -> 64.9 us
    ppermute x0 -> x2, waiting for transfers between devices: none -> 113 us  [the longest x1 96.1 us: shards(): opposite = lax.ppermute(tokens, 'expert', across)]
    all_to_all x8, waiting for transfers between devices: 167 us -> 87 us  [exchange(): return lax.all_to_all(pieces, 'expert', 0, 0, tiled=True)]
    all_to_all x8, starting transfers between devices: 85.3 us -> 59.8 us  [exchange(): return lax.all_to_all(pieces, 'expert', 0, 0, tiled=True)]
    ppermute x3, waiting for transfers between devices: 74 us -> 51.7 us  [shards(): partner[c] = lax.ppermute(own[c], 'groups', partners)]
    pallas_call x18 -> x21, Pallas kernels: 58.3 us -> 64.9 us  [step_call(): pl.pallas_call(ordered, out_shape=[*out_shape, TOKEN], in_specs=[*in_spec...]
    unnamed x35 -> x41, local copies, waits for them, and re-layouts: 9.57 us -> 11.9 us
  transfers between devices with their start and end apart: 12 -> 14, of which waited for: 8 -> 10; matrix products, arithmetic and copies ran while one was open for 6% -> 6% of each run, Pallas kernels for 12% -> 14%
where the time goes in v12:
time: 441 us; the launch traced here: 439 us
  waiting for transfers between devices  252 us (57%)
  starting transfers between devices  67.3 us (15%)
  Pallas kernels  64.9 us (15%)
  local copies, waits for them, and re-layouts  18.5 us (4%)
  other arithmetic  14.5 us (3%)
  between operations  14.4 us (3%)
  matrix products  7.65 us (2%)
    ppermute x1, waiting for transfers between devices, shards(): opposite = lax.ppermute(tokens, 'expert', across)  96.1 us
    all_to_all x8, waiting for transfers between devices, exchange(): return lax.all_to_all(pieces, 'expert', 0, 0, tiled=True)  87 us
    pallas_call x21, Pallas kernels, step_call(): pl.pallas_call(ordered, out_shape=[*out_shape, TOKEN], in_specs=[*in_spec...  64.9 us
    all_to_all x8, starting transfers between devices, exchange(): return lax.all_to_all(pieces, 'expert', 0, 0, tiled=True)  59.8 us
    ppermute x3, waiting for transfers between devices, shards(): partner[c] = lax.ppermute(own[c], 'groups', partners)  51.7 us
    ppermute x1, waiting for transfers between devices, shards(): nearby = lax.ppermute(both, 'expert', beside)  16.5 us
    unnamed x41, local copies, waits for them, and re-layouts  11.9 us
  transfers between devices with their start and end apart: 14, of which 10 were waited for; matrix products, arithmetic and copies ran while one was open for 6% of the time, Pallas kernels for 14%

profile of v12, /device:TPU:0, one launch (start us, length us, event | category | flops | bytes accessed | tf_op | source)
XLA Modules:
  0.0 438.8 jit_solution(3552101696125308947)
XLA Ops:
  13.2 7.6 %all-to-all-start = ((bf16[16,2,160,384]{3,2,1,0:T(8,128)(2,1)}), bf16[16,2,160,384]{3,2,1,0:T(8,128)(2,1)}, u32[]{:S(2)}, u32[]{:S(2)}) async-start(bf16[16,2,160,384]{3,2,1,0:T(8,128)(2,1)} %get-tuple-element.55), calls=%async_computation | async-start | bytes 7864320 | tf_op jit(solution)/shard_map/all_to_all | solution.py:317
  27.1 96.1 %collective-permute-done.refs_1_ = bf16[64,2560]{1,0:T(8,128)(2,1)S(1)} collective-permute-done((bf16[64,2560]{1,0:T(8,128)(2,1)S(1)}, bf16[64,2560]{1,0:T(8,128)(2,1)S(1)}, u32[]{:S(2)}, u32[]{:S(2)}) %collective-permute-start) | collective-permute-done | bytes 327712 | tf_op jit(solution)/shard_map/ppermute | solution.py:357
  125.9 16.5 %collective-permute-done.1.refs_2_ = bf16[2,64,2560]{2,1,0:T(8,128)(2,1)S(1)} collective-permute-done((bf16[2,64,2560]{2,1,0:T(8,128)(2,1)}, bf16[2,64,2560]{2,1,0:T(8,128)(2,1)S(1)}, u32[]{:S(2)}, u32[]{:S(2)}) %collective-permute-start.1) | collective-permute-done | bytes 655392 | tf_op jit(solution)/shard_map/ppermute | solution.py:369
  152.5 6.3 %fusion.6 = s32[16,64,16]{2,0,1:T(8,128)S(1)} fusion(s32[16,64,16]{2,0,1:T(8,128)S(1)} %copy.64), kind=kOutput, calls=%fused_computation.38 | output fusion | flops 1032192 | bytes 131072 | tf_op jit(solution)/shard_map/jit(cumsum)/reduce_window_sum | solution.py:288
  168.5 10.3 %merge.3 = (bf16[16,160,384]{2,1,0:T(8,128)(2,1)}, f32[8,128]{1,0:T(8,128)}) custom-call(s32[32]{0:T(128)} %bitcast.47, f32[960]{0:T(1024)} %mul.47.refs_1_, bf16[16,2,160,384]{3,2,1,0:T(8,128)(2,1)} %all-to-all-done.refs_1_.refs_2_, f32[8,128]{1,0:T(8,128)} %get-tuple-element.58.refs_3_), custom_call_target="tpu_custom_call" | custom-call | tf_op jit(solution)/shard_map/merge/pallas_call | solution.py:32
  181.8 18.2 %all-to-all-done.1.refs_1_.refs_2_ = bf16[16,2,160,256]{3,2,1,0:T(8,128)(2,1)S(1)} async-done(((bf16[16,2,160,256]{3,2,1,0:T(8,128)(2,1)}), bf16[16,2,160,256]{3,2,1,0:T(8,128)(2,1)S(1)}, u32[]{:S(2)}, u32[]{:S(2)}) %all-to-all-start.1) | async-done | bytes 2621472 | tf_op jit(solution)/shard_map/all_to_all | solution.py:317
  201.6 13.2 %all-to-all-start.2 = ((bf16[16,160,384]{2,1,0:T(8,128)(2,1)}), bf16[16,160,384]{2,1,0:T(8,128)(2,1)S(1)}, u32[]{:S(2)}, u32[]{:S(2)}) async-start(bf16[16,160,384]{2,1,0:T(8,128)(2,1)} %get-tuple-element.64), calls=%async_computation.2 | async-start | bytes 3932160 | tf_op jit(solution)/shard_map/all_to_all | solution.py:317
  214.8 9.4 %merge.4 = (bf16[16,160,256]{2,1,0:T(8,128)(2,1)}, f32[8,128]{1,0:T(8,128)}) custom-call(s32[32]{0:T(128)} %bitcast.48, f32[960]{0:T(1024)} %mul.47.refs_1_, bf16[16,2,160,256]{3,2,1,0:T(8,128)(2,1)} %copy-done, f32[8,128]{1,0:T(8,128)} %get-tuple-element.65.refs_3_), custom_call_target="tpu_custom_call" | custom-call | tf_op jit(solution)/shard_map/merge/pallas_call | solution.py:32
  224.2 29.4 %all-to-all-done.2 = bf16[16,160,384]{2,1,0:T(8,128)(2,1)S(1)} async-done(((bf16[16,160,384]{2,1,0:T(8,128)(2,1)}), bf16[16,160,384]{2,1,0:T(8,128)(2,1)S(1)}, u32[]{:S(2)}, u32[]{:S(2)}) %all-to-all-start.2) | async-done | bytes 1966112 | tf_op jit(solution)/shard_map/all_to_all | solution.py:317
  254.9 10.8 %all-to-all-start.3 = ((bf16[16,2,160,128]{3,2,1,0:T(8,128)(2,1)}), bf16[16,2,160,128]{3,2,1,0:T(8,128)(2,1)S(1)}, u32[]{:S(2)}, u32[]{:S(2)}) async-start(bf16[16,2,160,128]{3,2,1,0:T(8,128)(2,1)} %get-tuple-element.68), calls=%async_computation.3 | async-start | bytes 2621440 | tf_op jit(solution)/shard_map/all_to_all | solution.py:317
  267.3 5.5 %convolution_convert_fusion = bf16[16,48,2560]{2,1,0:T(8,128)(2,1)} fusion(bf16[16,64,2560]{2,1,0:T(8,128)(2,1)} %all-gather.2.cloned.1.call-done, s32[16,64]{1,0:T(8,128)S(1)} %bitcast.43, pred[16,64]{1,0:T(8,128)(4,1)S(1)} %bitcast.46), kind=kOutput, calls=%fused_computation.1 | convolution fusion | flops 253722624 | bytes 9180160 | tf_op jit(solution)/shard_map/jct,jtd->jcd/dot_general | solution.py:373
  272.9 38.2 %collective-permute-done.2.refs_3_ = bf16[2560,384]{1,0:T(8,128)(2,1)} collective-permute-done((bf16[2560,384]{1,0:T(8,128)(2,1)S(1)}, bf16[2560,384]{1,0:T(8,128)(2,1)}, u32[]{:S(2)}, u32[]{:S(2)}) %collective-permute-start.2) | collective-permute-done | bytes 1966112 | tf_op jit(solution)/shard_map/ppermute | solution.py:392
  312.1 5.7 %all-to-all-start.4 = ((bf16[16,160,256]{2,1,0:T(8,128)(2,1)}), bf16[16,160,256]{2,1,0:T(8,128)(2,1)S(1)}, u32[]{:S(2)}, u32[]{:S(2)}) async-start(bf16[16,160,256]{2,1,0:T(8,128)(2,1)} %get-tuple-element.74), calls=%async_computation.4 | async-start | bytes 2621440 | tf_op jit(solution)/shard_map/all_to_all | solution.py:317
  317.9 8.6 %merge.5 = (bf16[16,160,128]{2,1,0:T(8,128)(2,1)}, f32[8,128]{1,0:T(8,128)}) custom-call(s32[32]{0:T(128)} %bitcast.49, f32[960]{0:T(1024)} %mul.47.refs_1_, bf16[16,2,160,128]{3,2,1,0:T(8,128)(2,1)} %copy-done.4, f32[8,128]{1,0:T(8,128)} %get-tuple-element.72.refs_3_), custom_call_target="tpu_custom_call" | custom-call | tf_op jit(solution)/shard_map/merge/pallas_call | solution.py:32
  326.5 18.8 %all-to-all-done.4 = bf16[16,160,256]{2,1,0:T(8,128)(2,1)S(1)} async-done(((bf16[16,160,256]{2,1,0:T(8,128)(2,1)}), bf16[16,160,256]{2,1,0:T(8,128)(2,1)S(1)}, u32[]{:S(2)}, u32[]{:S(2)}) %all-to-all-start.4) | async-done | bytes 1310752 | tf_op jit(solution)/shard_map/all_to_all | solution.py:317
  346.4 8.0 %all-to-all-start.5 = ((bf16[16,160,128]{2,1,0:T(8,128)(2,1)}), bf16[16,160,128]{2,1,0:T(8,128)(2,1)S(1)}, u32[]{:S(2)}, u32[]{:S(2)}) async-start(bf16[16,160,128]{2,1,0:T(8,128)(2,1)} %get-tuple-element.77), calls=%async_computation.5 | async-start | bytes 1310720 | tf_op jit(solution)/shard_map/all_to_all | solution.py:317
  356.0 8.4 %run_chunk.3 = (bf16[1,2560,768]{2,1,0:T(8,128)(2,1)}, bf16[1,2560,768]{2,1,0:T(8,128)(2,1)}, bf16[16,48,384]{2,1,0:T(8,128)(2,1)}, f32[8,128]{1,0:T(8,128)}) custom-call(s32[2]{0:T(128)} %pad_add_fusion.refs_0_, bf16[768,2560]{1,0:T(8,128)(2,1)} %bitcast.33, bf16[2560,384]{1,0:T(8,128)(2,1)} %get-tuple-element.70.refs_2_, ...), custom_call_target="tpu_custom_call" | custom-call | tf_op jit(solution)/shard_map/run_chunk/pallas_call | solution.py:32
  364.4 6.6 %all-to-all-done.5 = bf16[16,160,128]{2,1,0:T(8,128)(2,1)S(1)} async-done(((bf16[16,160,128]{2,1,0:T(8,128)(2,1)}), bf16[16,160,128]{2,1,0:T(8,128)(2,1)S(1)}, u32[]{:S(2)}, u32[]{:S(2)}) %all-to-all-start.5) | async-done | bytes 655392 | tf_op jit(solution)/shard_map/all_to_all | solution.py:317
  378.2 8.1 %collective-permute-done.4.refs_3_ = bf16[2560,256]{1,0:T(8,128)(2,1)S(1)} collective-permute-done((bf16[2560,256]{1,0:T(8,128)(2,1)}, bf16[2560,256]{1,0:T(8,128)(2,1)S(1)}, u32[]{:S(2)}, u32[]{:S(2)}) %collective-permute-start.4) | collective-permute-done | bytes 1310752 | tf_op jit(solution)/shard_map/ppermute | solution.py:392
  387.4 6.9 %run_chunk.4 = (bf16[1,2560,768]{2,1,0:T(8,128)(2,1)}, bf16[1,2560,768]{2,1,0:T(8,128)(2,1)}, bf16[16,48,256]{2,1,0:T(8,128)(2,1)}, f32[8,128]{1,0:T(8,128)}) custom-call(s32[2]{0:T(128)} %pad_add_fusion.refs_0_, bf16[768,2560]{1,0:T(8,128)(2,1)} %bitcast.34, ...), custom_call_target="tpu_custom_call", output_to_operand_aliasing={{0}: (4, {}), {1}: (5, {})} | custom-call | tf_op jit(solution)/shard_map/run_chunk/pallas_call | solution.py:32
  394.3 5.4 %collective-permute-done.3.refs_3_ = bf16[2560,128]{1,0:T(8,128)(2,1)S(1)} collective-permute-done((bf16[2560,128]{1,0:T(8,128)(2,1)}, bf16[2560,128]{1,0:T(8,128)(2,1)S(1)}, u32[]{:S(2)}, u32[]{:S(2)}) %collective-permute-start.3) | collective-permute-done | bytes 655392 | tf_op jit(solution)/shard_map/ppermute | solution.py:392
  400.6 5.4 %run_chunk.5 = (bf16[1,2560,768]{2,1,0:T(8,128)(2,1)}, bf16[1,2560,768]{2,1,0:T(8,128)(2,1)}, bf16[16,48,128]{2,1,0:T(8,128)(2,1)}, f32[8,128]{1,0:T(8,128)}) custom-call(s32[2]{0:T(128)} %pad_add_fusion.refs_0_, bf16[768,2560]{1,0:T(8,128)(2,1)} %bitcast.35, ...), custom_call_target="tpu_custom_call", output_to_operand_aliasing={{0}: (4, {}), {1}: (5, {})} | custom-call | tf_op jit(solution)/shard_map/run_chunk/pallas_call | solution.py:32
  408.7 5.7 %all-to-all-start.7 = ((bf16[16,48,384]{2,1,0:T(8,128)(2,1)}), bf16[16,48,384]{2,1,0:T(8,128)(2,1)S(1)}, u32[]{:S(2)}, u32[]{:S(2)}) async-start(bf16[16,48,384]{2,1,0:T(8,128)(2,1)} %get-tuple-element.96), calls=%async_computation.7 | async-start | bytes 1179648 | tf_op jit(solution)/shard_map/all_to_all | solution.py:317
  416.1 13.9 %all-to-all-done.7 = bf16[16,48,384]{2,1,0:T(8,128)(2,1)S(1)} async-done(((bf16[16,48,384]{2,1,0:T(8,128)(2,1)}), bf16[16,48,384]{2,1,0:T(8,128)(2,1)S(1)}, u32[]{:S(2)}, u32[]{:S(2)}) %all-to-all-start.7) | async-done | bytes 589856 | tf_op jit(solution)/shard_map/all_to_all | solution.py:317
  (106 shorter events, 61.2 us)
Async XLA Ops:
  13.2 7.6 %copy-start.13 = (bf16[64,2560]{1,0:T(8,128)(2,1)S(1)}, bf16[64,2560]{1,0:T(8,128)(2,1)}, u32[]{:S(2)}) copy-start(bf16[64,2560]{1,0:T(8,128)(2,1)} %refs_0_.1) | copy-start | bytes 983044
  13.2 132.5 %all-to-all-start = ((bf16[16,2,160,384]{3,2,1,0:T(8,128)(2,1)}), bf16[16,2,160,384]{3,2,1,0:T(8,128)(2,1)}, u32[]{:S(2)}, u32[]{:S(2)}) async-start(bf16[16,2,160,384]{3,2,1,0:T(8,128)(2,1)} %get-tuple-element.55), calls=%async_computation | async-start | bytes 7864320 | tf_op jit(solution)/shard_map/all_to_all | solution.py:317
  20.8 102.4 %collective-permute-start = (bf16[64,2560]{1,0:T(8,128)(2,1)S(1)}, bf16[64,2560]{1,0:T(8,128)(2,1)S(1)}, u32[]{:S(2)}, u32[]{:S(2)}) collective-permute-start(bf16[64,2560]{1,0:T(8,128)(2,1)S(1)} %copy-done.13), channel_id=1, source_target_pairs={{0,8},{1,9},{2,10},{3,11},{4,12},{5,13},{6,14},{7,15},{8,0},{9,1},... | collective-permute-start | bytes 983048 | tf_op jit(solution)/shard_map/ppermute | solution.py:357
  125.9 16.5 %collective-permute-start.1 = (bf16[2,64,2560]{2,1,0:T(8,128)(2,1)}, bf16[2,64,2560]{2,1,0:T(8,128)(2,1)S(1)}, u32[]{:S(2)}, u32[]{:S(2)}) collective-permute-start(bf16[2,64,2560]{2,1,0:T(8,128)(2,1)} %get-tuple-element.52.refs_1_), channel_id=1, source_target_pairs={{0,4},{1,5},{2,6},{3,7},{4,0},{5,1},{6,2},{7,3},{8,12},{9,13},{10,... | collective-permute-start | bytes 1966088 | tf_op jit(solution)/shard_map/ppermute | solution.py:369
  145.8 4.0 copy-start.17
  145.8 4.2 copy-start.18
  145.8 4.2 copy-start.19
  145.8 5.1 %copy-start.15 = (f32[32,20,6]{0,1,2:T(8,128)S(1)}, f32[32,20,6]{0,1,2:T(8,128)}, u32[]{:S(2)}) copy-start(f32[32,20,6]{0,1,2:T(8,128)} %param.13) | copy-start | bytes 46084
  145.8 5.1 %copy-start.16 = (f32[32,20,6]{0,1,2:T(8,128)S(1)}, f32[32,20,6]{0,1,2:T(8,128)}, u32[]{:S(2)}) copy-start(f32[32,20,6]{0,1,2:T(8,128)} %param.12) | copy-start | bytes 46084
  145.8 54.3 %all-to-all-start.1 = ((bf16[16,2,160,256]{3,2,1,0:T(8,128)(2,1)}), bf16[16,2,160,256]{3,2,1,0:T(8,128)(2,1)S(1)}, u32[]{:S(2)}, u32[]{:S(2)}) async-start(bf16[16,2,160,256]{3,2,1,0:T(8,128)(2,1)} %get-tuple-element.62), calls=%async_computation.1 | async-start | bytes 5242880 | tf_op jit(solution)/shard_map/all_to_all | solution.py:317
  149.7 117.6 %all-gather.2.cloned.1.call-start = ((), (), s32[]{:S(2)}) async-start(), calls=%async_computation.8 | async-start | bytes 6553600 | tf_op jit(solution)/shard_map/all_gather | solution.py:372
  200.1 1.5 copy-start
  201.6 52.1 %all-to-all-start.2 = ((bf16[16,160,384]{2,1,0:T(8,128)(2,1)}), bf16[16,160,384]{2,1,0:T(8,128)(2,1)S(1)}, u32[]{:S(2)}, u32[]{:S(2)}) async-start(bf16[16,160,384]{2,1,0:T(8,128)(2,1)} %get-tuple-element.64), calls=%async_computation.2 | async-start | bytes 3932160 | tf_op jit(solution)/shard_map/all_to_all | solution.py:317
  254.9 10.8 %copy-start.2 = (bf16[2560,384]{1,0:T(8,128)(2,1)S(1)}, bf16[2560,384]{1,0:T(8,128)(2,1)}, u32[]{:S(2)}) copy-start(bf16[2560,384]{1,0:T(8,128)(2,1)} %get-tuple-element.70.refs_2_) | copy-start | bytes 5898244
  254.9 56.2 %all-to-all-start.3 = ((bf16[16,2,160,128]{3,2,1,0:T(8,128)(2,1)}), bf16[16,2,160,128]{3,2,1,0:T(8,128)(2,1)S(1)}, u32[]{:S(2)}, u32[]{:S(2)}) async-start(bf16[16,2,160,128]{3,2,1,0:T(8,128)(2,1)} %get-tuple-element.68), calls=%async_computation.3 | async-start | bytes 2621440 | tf_op jit(solution)/shard_map/all_to_all | solution.py:317
  265.7 45.3 %collective-permute-start.2 = (bf16[2560,384]{1,0:T(8,128)(2,1)S(1)}, bf16[2560,384]{1,0:T(8,128)(2,1)}, u32[]{:S(2)}, u32[]{:S(2)}) collective-permute-start(bf16[2560,384]{1,0:T(8,128)(2,1)S(1)} %copy-done.2), channel_id=1, source_target_pairs={{0,16},{16,0},{1,17},{17,1},{2,18},{18,2},{3,19},{19,3},{4,20},{20... | collective-permute-start | bytes 5898248 | tf_op jit(solution)/shard_map/ppermute | solution.py:392
  312.1 33.1 %all-to-all-start.4 = ((bf16[16,160,256]{2,1,0:T(8,128)(2,1)}), bf16[16,160,256]{2,1,0:T(8,128)(2,1)S(1)}, u32[]{:S(2)}, u32[]{:S(2)}) async-start(bf16[16,160,256]{2,1,0:T(8,128)(2,1)} %get-tuple-element.74), calls=%async_computation.4 | async-start | bytes 2621440 | tf_op jit(solution)/shard_map/all_to_all | solution.py:317
  346.4 24.6 %all-to-all-start.5 = ((bf16[16,160,128]{2,1,0:T(8,128)(2,1)}), bf16[16,160,128]{2,1,0:T(8,128)(2,1)S(1)}, u32[]{:S(2)}, u32[]{:S(2)}) async-start(bf16[16,160,128]{2,1,0:T(8,128)(2,1)} %get-tuple-element.77), calls=%async_computation.5 | async-start | bytes 1310720 | tf_op jit(solution)/shard_map/all_to_all | solution.py:317
  354.4 31.9 %collective-permute-start.4 = (bf16[2560,256]{1,0:T(8,128)(2,1)}, bf16[2560,256]{1,0:T(8,128)(2,1)S(1)}, u32[]{:S(2)}, u32[]{:S(2)}) collective-permute-start(bf16[2560,256]{1,0:T(8,128)(2,1)} %get-tuple-element.81.refs_2_), channel_id=1, source_target_pairs={{0,16},{16,0},{1,17},{17,1},{2,18},{18,2},{3,19},{19,3},{4,20},{20... | collective-permute-start | bytes 3932168 | tf_op jit(solution)/shard_map/ppermute | solution.py:392
  371.8 36.1 %all-to-all-start.6 = ((bf16[16,48,384]{2,1,0:T(8,128)(2,1)}), bf16[16,48,384]{2,1,0:T(8,128)(2,1)S(1)}, u32[]{:S(2)}, u32[]{:S(2)}) async-start(bf16[16,48,384]{2,1,0:T(8,128)(2,1)} %get-tuple-element.92), calls=%async_computation.6 | async-start | bytes 1179648 | tf_op jit(solution)/shard_map/all_to_all | solution.py:317
  376.6 23.1 %collective-permute-start.3 = (bf16[2560,128]{1,0:T(8,128)(2,1)}, bf16[2560,128]{1,0:T(8,128)(2,1)S(1)}, u32[]{:S(2)}, u32[]{:S(2)}) collective-permute-start(bf16[2560,128]{1,0:T(8,128)(2,1)} %get-tuple-element.80.refs_2_), channel_id=1, source_target_pairs={{0,16},{16,0},{1,17},{17,1},{2,18},{18,2},{3,19},{19,3},{4,20},{20... | collective-permute-start | bytes 1966088 | tf_op jit(solution)/shard_map/ppermute | solution.py:392
  400.6 5.4 %copy-start.12 = (bf16[16,48,256]{2,1,0:T(8,128)(2,1)S(1)}, bf16[16,48,256]{2,1,0:T(8,128)(2,1)}, u32[]{:S(2)}) copy-start(bf16[16,48,256]{2,1,0:T(8,128)(2,1)} %get-tuple-element.93) | copy-start | bytes 1179652
  406.0 8.5 %copy-start.9 = (pred[384,768]{1,0:T(32,128)(4,1)S(1)}, pred[384,768]{1,0:T(32,128)(4,1)}, u32[]{:S(2)}) copy-start(pred[384,768]{1,0:T(32,128)(4,1)} %convert_element_type.26) | copy-start | bytes 884740
  408.7 21.3 %all-to-all-start.7 = ((bf16[16,48,384]{2,1,0:T(8,128)(2,1)}), bf16[16,48,384]{2,1,0:T(8,128)(2,1)S(1)}, u32[]{:S(2)}, u32[]{:S(2)}) async-start(bf16[16,48,384]{2,1,0:T(8,128)(2,1)} %get-tuple-element.96), calls=%async_computation.7 | async-start | bytes 1179648 | tf_op jit(solution)/shard_map/all_to_all | solution.py:317
  (10 other events, 9.5 us)
Sparse Core Ops, SparseCore 0:
  152.1 58.4 all-gather.1

commit v13 on v12

--- a/solution.py
+++ b/solution.py
@@ -258,18 +258,22 @@
 
 
 def first_runs(count):
-    return max(1, count - 2)
+    return max(1, count - 1)
 
 
 def plan(count):
     cut = first_runs(count)
-    order = [("pack", 0), ("raw", 0), ("pack", 1), ("pair", 0), ("line", 0), ("raw", 1), ("sum", 0)]
+    order = [("pack", 0), ("raw", 0), ("pack", 1), ("raw", 1), ("sum", 0)]
     for chunk in range(count):
         if chunk + 2 < count:
             order.append(("pack", chunk + 2))
+        if chunk == 0:
+            order.append(("pair", 0))
         order.append(("back", chunk))
         if chunk + 1 < count:
             order.append(("sum", chunk + 1))
+        if chunk == 0:
+            order.append(("line", 0))
         if chunk + 1 == count:
             order.extend(("run", earlier) for earlier in range(cut))
         order.append(("trade", chunk))
@@ -290,11 +294,9 @@
 
 
 def chunk_widths(blocks):
-    widths = []
-    while blocks > 0:
-        widths.append(max(1, (blocks + 1) // 2 if blocks > 3 else blocks - 1))
-        blocks -= widths[-1]
-    return widths
+    first = max(1, blocks // 2)
+    second = max(1, blocks // 6)
+    return [width for width in (first, second, blocks - first - second) if width > 0]
 
 
 def shards(tokens, routes, quant_gate, quant_up, gate_scales, up_scales, cluster_ids, frequency):
@@ -383,7 +385,7 @@
             merged[c], token = merge(token, slots, factors, gathered[c], start, blocks_of_rows)
         elif name == "back":
             earlier = [gathered[c + 1]] if c + 1 in gathered else []
-            earlier += [placing, picking] if c == 0 else [grouped] if c == 1 else []
+            earlier += [placing, picking] if c == 0 else [grouped] if c == last else []
             earlier += [partner[c - 1]] if 0 < c < last else []
             merged[c], token = hold(token, merged[c], earlier)
             own[c] = exchange(merged[c])

time: 441 us -> 408 us (0.925)
  waiting for transfers between devices: 252 us -> 212 us
  starting transfers between devices: 67.3 us -> 79.2 us
    ppermute x1, waiting for transfers between devices: 96.1 us -> 0.01 us  [shards(): opposite = lax.ppermute(tokens, 'expert', across)]
    ppermute x3, waiting for transfers between devices: 51.7 us -> 80.8 us  [shards(): partner[c] = lax.ppermute(own[c], 'groups', partners)]
    ppermute x1, waiting for transfers between devices: 16.5 us -> 38.2 us  [shards(): nearby = lax.ppermute(both, 'expert', beside)]
    all_to_all x8, starting transfers between devices: 59.8 us -> 69.6 us  [exchange(): return lax.all_to_all(pieces, 'expert', 0, 0, tiled=True)]
    all_to_all x8, waiting for transfers between devices: 87 us -> 93.1 us  [exchange(): return lax.all_to_all(pieces, 'expert', 0, 0, tiled=True)]
    unnamed x41 -> x35, local copies, waits for them, and re-layouts: 11.9 us -> 9.67 us
  transfers between devices with their start and end apart: 14 -> 14, of which waited for: 10 -> 9; matrix products, arithmetic and copies ran while one was open for 6% -> 6% of each run, Pallas kernels for 14% -> 15%
where the time goes in v13:
time: 408 us; the launch traced here: 406 us
  waiting for transfers between devices  212 us (52%)
  starting transfers between devices  79.2 us (19%)
  Pallas kernels  64.9 us (16%)
  between operations  14.5 us (4%)
  local copies, waits for them, and re-layouts  14.4 us (4%)
  other arithmetic  13.7 us (3%)
  matrix products  7.55 us (2%)
    all_to_all x8, waiting for transfers between devices, exchange(): return lax.all_to_all(pieces, 'expert', 0, 0, tiled=True)  93.1 us
    ppermute x3, waiting for transfers between devices, shards(): partner[c] = lax.ppermute(own[c], 'groups', partners)  80.8 us
    all_to_all x8, starting transfers between devices, exchange(): return lax.all_to_all(pieces, 'expert', 0, 0, tiled=True)  69.6 us
    pallas_call x21, Pallas kernels, step_call(): pl.pallas_call(ordered, out_shape=[*out_shape, TOKEN], in_specs=[*in_spec...  64.9 us
    ppermute x1, waiting for transfers between devices, shards(): nearby = lax.ppermute(both, 'expert', beside)  38.2 us
    unnamed x35, local copies, waits for them, and re-layouts  9.67 us
  transfers between devices with their start and end apart: 14, of which 9 were waited for; matrix products, arithmetic and copies ran while one was open for 6% of the time, Pallas kernels for 15%

profile of v13, /device:TPU:0, one launch (start us, length us, event | category | flops | bytes accessed | tf_op | source)
XLA Modules:
  0.0 406.4 jit_solution(12680346564539014236)
XLA Ops:
  8.4 4.8 %pack.3 = (bf16[16,2,160,384]{3,2,1,0:T(8,128)(2,1)}, f32[8,128]{1,0:T(8,128)}) custom-call(s32[2]{0:T(128)} %pad_add_fusion.refs_0_, bf16[2,2560,768]{2,1,0:T(8,128)(2,1)} %refs_1_.5, bf16[2,2560,768]{2,1,0:T(8,128)(2,1)} %refs_2_.5, f32[8,128]{1,0:T(8,128)} %broadcast_in_dim.40.refs_3_), custom_call_target="tpu_custom_call" | custom-call | tf_op jit(solution)/shard_map/pack/pallas_call | solution.py:32
  13.3 7.6 %all-to-all-start = ((bf16[16,2,160,384]{3,2,1,0:T(8,128)(2,1)}), bf16[16,2,160,384]{3,2,1,0:T(8,128)(2,1)}, u32[]{:S(2)}, u32[]{:S(2)}) async-start(bf16[16,2,160,384]{3,2,1,0:T(8,128)(2,1)} %get-tuple-element.50), calls=%async_computation | async-start | bytes 7864320 | tf_op jit(solution)/shard_map/all_to_all | solution.py:319
  27.1 73.8 %all-to-all-done.refs_1_.refs_2_ = bf16[16,2,160,384]{3,2,1,0:T(8,128)(2,1)} async-done(((bf16[16,2,160,384]{3,2,1,0:T(8,128)(2,1)}), bf16[16,2,160,384]{3,2,1,0:T(8,128)(2,1)}, u32[]{:S(2)}, u32[]{:S(2)}) %all-to-all-start) | async-done | bytes 3932192 | tf_op jit(solution)/shard_map/all_to_all | solution.py:319
  101.0 19.1 %all-to-all-start.1 = ((bf16[16,2,160,128]{3,2,1,0:T(8,128)(2,1)}), bf16[16,2,160,128]{3,2,1,0:T(8,128)(2,1)S(1)}, u32[]{:S(2)}, u32[]{:S(2)}) async-start(bf16[16,2,160,128]{3,2,1,0:T(8,128)(2,1)} %get-tuple-element.58), calls=%async_computation.1 | async-start | bytes 2621440 | tf_op jit(solution)/shard_map/all_to_all | solution.py:319
  122.1 6.3 %fusion.6 = s32[16,64,16]{2,0,1:T(8,128)S(1)} fusion(s32[16,64,16]{2,0,1:T(8,128)S(1)} %copy.65), kind=kOutput, calls=%fused_computation.38 | output fusion | flops 1032192 | bytes 131072 | tf_op jit(solution)/shard_map/jit(cumsum)/reduce_window_sum | solution.py:292
  135.1 10.2 %merge.3 = (bf16[16,160,384]{2,1,0:T(8,128)(2,1)}, f32[8,128]{1,0:T(8,128)}) custom-call(s32[32]{0:T(128)} %bitcast.47, f32[960]{0:T(1024)} %mul.47.refs_1_, bf16[16,2,160,384]{3,2,1,0:T(8,128)(2,1)} %all-to-all-done.refs_1_.refs_2_, f32[8,128]{1,0:T(8,128)} %get-tuple-element.54.refs_3_), custom_call_target="tpu_custom_call" | custom-call | tf_op jit(solution)/shard_map/merge/pallas_call | solution.py:32
  151.9 6.1 %all-to-all-start.2 = ((bf16[16,160,384]{2,1,0:T(8,128)(2,1)}), bf16[16,160,384]{2,1,0:T(8,128)(2,1)S(1)}, u32[]{:S(2)}, u32[]{:S(2)}) async-start(bf16[16,160,384]{2,1,0:T(8,128)(2,1)} %get-tuple-element.65), calls=%async_computation.2 | async-start | bytes 3932160 | tf_op jit(solution)/shard_map/all_to_all | solution.py:319
  160.1 8.6 %merge.4 = (bf16[16,160,128]{2,1,0:T(8,128)(2,1)}, f32[8,128]{1,0:T(8,128)}) custom-call(s32[32]{0:T(128)} %bitcast.48, f32[960]{0:T(1024)} %mul.47.refs_1_, bf16[16,2,160,128]{3,2,1,0:T(8,128)(2,1)} %copy-done.2, f32[8,128]{1,0:T(8,128)} %get-tuple-element.61.refs_3_), custom_call_target="tpu_custom_call" | custom-call | tf_op jit(solution)/shard_map/merge/pallas_call | solution.py:32
  168.7 38.2 %collective-permute-done.1.refs_2_ = bf16[2,64,2560]{2,1,0:T(8,128)(2,1)} collective-permute-done((bf16[2,64,2560]{2,1,0:T(8,128)(2,1)S(1)}, bf16[2,64,2560]{2,1,0:T(8,128)(2,1)}, u32[]{:S(2)}, u32[]{:S(2)}) %collective-permute-start.1) | collective-permute-done | bytes 655392 | tf_op jit(solution)/shard_map/ppermute | solution.py:371
  210.9 5.0 %all-to-all-start.3 = ((bf16[16,2,160,256]{3,2,1,0:T(8,128)(2,1)}), bf16[16,2,160,256]{3,2,1,0:T(8,128)(2,1)S(1)}, u32[]{:S(2)}, u32[]{:S(2)}) async-start(bf16[16,2,160,256]{3,2,1,0:T(8,128)(2,1)} %get-tuple-element.68), calls=%async_computation.3 | async-start | bytes 5242880 | tf_op jit(solution)/shard_map/all_to_all | solution.py:319
  217.4 43.9 %collective-permute-done.2.refs_2_.refs_3_ = bf16[2560,384]{1,0:T(8,128)(2,1)} collective-permute-done((bf16[2560,384]{1,0:T(8,128)(2,1)}, bf16[2560,384]{1,0:T(8,128)(2,1)}, u32[]{:S(2)}, u32[]{:S(2)}) %collective-permute-start.2) | collective-permute-done | bytes 1966112 | tf_op jit(solution)/shard_map/ppermute | solution.py:394
  261.3 5.0 %all-to-all-done.3.refs_1_.refs_2_ = bf16[16,2,160,256]{3,2,1,0:T(8,128)(2,1)S(1)} async-done(((bf16[16,2,160,256]{3,2,1,0:T(8,128)(2,1)}), bf16[16,2,160,256]{3,2,1,0:T(8,128)(2,1)S(1)}, u32[]{:S(2)}, u32[]{:S(2)}) %all-to-all-start.3) | async-done | bytes 2621472 | tf_op jit(solution)/shard_map/all_to_all | solution.py:319
  267.8 13.2 %all-to-all-start.4 = ((bf16[16,160,128]{2,1,0:T(8,128)(2,1)}), bf16[16,160,128]{2,1,0:T(8,128)(2,1)S(1)}, u32[]{:S(2)}, u32[]{:S(2)}) async-start(bf16[16,160,128]{2,1,0:T(8,128)(2,1)} %get-tuple-element.74), calls=%async_computation.4 | async-start | bytes 1310720 | tf_op jit(solution)/shard_map/all_to_all | solution.py:319
  281.0 5.6 %convolution_convert_fusion = bf16[16,48,2560]{2,1,0:T(8,128)(2,1)} fusion(bf16[16,64,2560]{2,1,0:T(8,128)(2,1)} %all-gather.2.cloned.1.call-done, s32[16,64]{1,0:T(8,128)S(1)} %bitcast.43, pred[16,64]{1,0:T(8,128)(4,1)S(1)} %bitcast.46), kind=kOutput, calls=%fused_computation.1 | convolution fusion | flops 253722624 | bytes 9180160 | tf_op jit(solution)/shard_map/jct,jtd->jcd/dot_general | solution.py:375
  286.6 9.5 %merge.5 = (bf16[16,160,256]{2,1,0:T(8,128)(2,1)}, f32[8,128]{1,0:T(8,128)}) custom-call(s32[32]{0:T(128)} %bitcast.49, f32[960]{0:T(1024)} %mul.47.refs_1_, bf16[16,2,160,256]{3,2,1,0:T(8,128)(2,1)} %copy-done, f32[8,128]{1,0:T(8,128)} %get-tuple-element.72.refs_3_), custom_call_target="tpu_custom_call" | custom-call | tf_op jit(solution)/shard_map/merge/pallas_call | solution.py:32
  298.5 4.9 %all-to-all-start.5 = ((bf16[16,160,256]{2,1,0:T(8,128)(2,1)}), bf16[16,160,256]{2,1,0:T(8,128)(2,1)S(1)}, u32[]{:S(2)}, u32[]{:S(2)}) async-start(bf16[16,160,256]{2,1,0:T(8,128)(2,1)} %get-tuple-element.77), calls=%async_computation.5 | async-start | bytes 2621440 | tf_op jit(solution)/shard_map/all_to_all | solution.py:319
  305.0 8.4 %run_chunk.3 = (bf16[1,2560,768]{2,1,0:T(8,128)(2,1)}, bf16[1,2560,768]{2,1,0:T(8,128)(2,1)}, bf16[16,48,384]{2,1,0:T(8,128)(2,1)}, f32[8,128]{1,0:T(8,128)}) custom-call(s32[2]{0:T(128)} %pad_add_fusion.refs_0_, bf16[768,2560]{1,0:T(8,128)(2,1)} %bitcast.33, bf16[2560,384]{1,0:T(8,128)(2,1)} %get-tuple-element.70.refs_2_, ...), custom_call_target="tpu_custom_call" | custom-call | tf_op jit(solution)/shard_map/run_chunk/pallas_call | solution.py:32
  313.4 7.1 %collective-permute-done.3.refs_3_ = bf16[2560,128]{1,0:T(8,128)(2,1)S(1)} collective-permute-done((bf16[2560,128]{1,0:T(8,128)(2,1)S(1)}, bf16[2560,128]{1,0:T(8,128)(2,1)S(1)}, u32[]{:S(2)}, u32[]{:S(2)}) %collective-permute-start.3) | collective-permute-done | bytes 655392 | tf_op jit(solution)/shard_map/ppermute | solution.py:394
  321.4 5.4 %run_chunk.4 = (bf16[1,2560,768]{2,1,0:T(8,128)(2,1)}, bf16[1,2560,768]{2,1,0:T(8,128)(2,1)}, bf16[16,48,128]{2,1,0:T(8,128)(2,1)}, f32[8,128]{1,0:T(8,128)}) custom-call(s32[2]{0:T(128)} %pad_add_fusion.refs_0_, bf16[768,2560]{1,0:T(8,128)(2,1)} %bitcast.34, ...), custom_call_target="tpu_custom_call", output_to_operand_aliasing={{0}: (4, {}), {1}: (5, {})} | custom-call | tf_op jit(solution)/shard_map/run_chunk/pallas_call | solution.py:32
  331.8 8.0 %all-to-all-start.6 = ((bf16[16,48,512]{2,1,0:T(8,128)(2,1)}), bf16[16,48,512]{2,1,0:T(8,128)(2,1)S(1)}, u32[]{:S(2)}, u32[]{:S(2)}) async-start(bf16[16,48,512]{2,1,0:T(8,128)(2,1)} %get-tuple-element.93), calls=%async_computation.6 | async-start | bytes 1572864 | tf_op jit(solution)/shard_map/all_to_all | solution.py:319
  341.4 29.7 %collective-permute-done.4.refs_3_ = bf16[2560,256]{1,0:T(8,128)(2,1)S(1)} collective-permute-done((bf16[2560,256]{1,0:T(8,128)(2,1)}, bf16[2560,256]{1,0:T(8,128)(2,1)S(1)}, u32[]{:S(2)}, u32[]{:S(2)}) %collective-permute-start.4) | collective-permute-done | bytes 1310752 | tf_op jit(solution)/shard_map/ppermute | solution.py:394
  372.3 6.9 %run_chunk.5 = (bf16[1,2560,768]{2,1,0:T(8,128)(2,1)}, bf16[1,2560,768]{2,1,0:T(8,128)(2,1)}, bf16[16,48,256]{2,1,0:T(8,128)(2,1)}, f32[8,128]{1,0:T(8,128)}) custom-call(s32[2]{0:T(128)} %pad_add_fusion.refs_0_, bf16[768,2560]{1,0:T(8,128)(2,1)} %bitcast.35, ...), custom_call_target="tpu_custom_call", output_to_operand_aliasing={{0}: (4, {}), {1}: (5, {})} | custom-call | tf_op jit(solution)/shard_map/run_chunk/pallas_call | solution.py:32
  380.1 5.7 %all-to-all-start.7 = ((bf16[16,48,256]{2,1,0:T(8,128)(2,1)}), bf16[16,48,256]{2,1,0:T(8,128)(2,1)S(1)}, u32[]{:S(2)}, u32[]{:S(2)}) async-start(bf16[16,48,256]{2,1,0:T(8,128)(2,1)} %get-tuple-element.96), calls=%async_computation.7 | async-start | bytes 786432 | tf_op jit(solution)/shard_map/all_to_all | solution.py:319
  387.4 10.6 %all-to-all-done.7 = bf16[16,48,256]{2,1,0:T(8,128)(2,1)S(1)} async-done(((bf16[16,48,256]{2,1,0:T(8,128)(2,1)}), bf16[16,48,256]{2,1,0:T(8,128)(2,1)S(1)}, u32[]{:S(2)}, u32[]{:S(2)}) %all-to-all-start.7) | async-done | bytes 393248 | tf_op jit(solution)/shard_map/all_to_all | solution.py:319
  (99 shorter events, 48.1 us)
Async XLA Ops:
  13.3 7.6 %copy-start.11 = (bf16[64,2560]{1,0:T(8,128)(2,1)S(1)}, bf16[64,2560]{1,0:T(8,128)(2,1)}, u32[]{:S(2)}) copy-start(bf16[64,2560]{1,0:T(8,128)(2,1)} %refs_0_.1) | copy-start | bytes 983044
  13.3 87.7 %all-to-all-start = ((bf16[16,2,160,384]{3,2,1,0:T(8,128)(2,1)}), bf16[16,2,160,384]{3,2,1,0:T(8,128)(2,1)}, u32[]{:S(2)}, u32[]{:S(2)}) async-start(bf16[16,2,160,384]{3,2,1,0:T(8,128)(2,1)} %get-tuple-element.50), calls=%async_computation | async-start | bytes 7864320 | tf_op jit(solution)/shard_map/all_to_all | solution.py:319
  20.9 128.0 %collective-permute-start = (bf16[64,2560]{1,0:T(8,128)(2,1)S(1)}, bf16[64,2560]{1,0:T(8,128)(2,1)}, u32[]{:S(2)}, u32[]{:S(2)}) collective-permute-start(bf16[64,2560]{1,0:T(8,128)(2,1)S(1)} %copy-done.11), channel_id=1, source_target_pairs={{0,8},{1,9},{2,10},{3,11},{4,12},{5,13},{6,14},{7,15},{8,0},{9,1},... | collective-permute-start | bytes 983048 | tf_op jit(solution)/shard_map/ppermute | solution.py:359
  23.7 3.2 copy-start.15
  23.7 3.2 copy-start.16
  101.0 19.1 %copy-start.12 = (f32[32,20,6]{0,1,2:T(8,128)S(1)}, f32[32,20,6]{0,1,2:T(8,128)}, u32[]{:S(2)}) copy-start(f32[32,20,6]{0,1,2:T(8,128)} %param.13) | copy-start | bytes 46084
  101.0 19.1 %copy-start.13 = (f32[32,20,6]{0,1,2:T(8,128)S(1)}, f32[32,20,6]{0,1,2:T(8,128)}, u32[]{:S(2)}) copy-start(f32[32,20,6]{0,1,2:T(8,128)} %param.12) | copy-start | bytes 46084
  101.0 20.7 %copy-start.14 = (s32[1024,6]{0,1:T(8,128)S(1)}, s32[1024,6]{0,1:T(8,128)}, u32[]{:S(2)}) copy-start(s32[1024,6]{0,1:T(8,128)} %param.9) | copy-start | bytes 73732
  101.0 49.8 %all-to-all-start.1 = ((bf16[16,2,160,128]{3,2,1,0:T(8,128)(2,1)}), bf16[16,2,160,128]{3,2,1,0:T(8,128)(2,1)S(1)}, u32[]{:S(2)}, u32[]{:S(2)}) async-start(bf16[16,2,160,128]{3,2,1,0:T(8,128)(2,1)} %get-tuple-element.58), calls=%async_computation.1 | async-start | bytes 2621440 | tf_op jit(solution)/shard_map/all_to_all | solution.py:319
  151.9 6.2 %copy-start.9 = (bf16[2,64,2560]{2,1,0:T(8,128)(2,1)S(1)}, bf16[2,64,2560]{2,1,0:T(8,128)(2,1)}, u32[]{:S(2)}) copy-start(bf16[2,64,2560]{2,1,0:T(8,128)(2,1)} %get-tuple-element.57.refs_1_) | copy-start | bytes 1966084
  151.9 57.5 %all-to-all-start.2 = ((bf16[16,160,384]{2,1,0:T(8,128)(2,1)}), bf16[16,160,384]{2,1,0:T(8,128)(2,1)S(1)}, u32[]{:S(2)}, u32[]{:S(2)}) async-start(bf16[16,160,384]{2,1,0:T(8,128)(2,1)} %get-tuple-element.65), calls=%async_computation.2 | async-start | bytes 3932160 | tf_op jit(solution)/shard_map/all_to_all | solution.py:319
  158.1 123.0 %all-gather.2.cloned.1.call-start = ((), (), s32[]{:S(2)}) async-start(), calls=%async_computation.8 | async-start | bytes 6553600 | tf_op jit(solution)/shard_map/all_gather | solution.py:374
  158.1 48.8 %collective-permute-start.1 = (bf16[2,64,2560]{2,1,0:T(8,128)(2,1)S(1)}, bf16[2,64,2560]{2,1,0:T(8,128)(2,1)}, u32[]{:S(2)}, u32[]{:S(2)}) collective-permute-start(bf16[2,64,2560]{2,1,0:T(8,128)(2,1)S(1)} %copy-done.9), channel_id=1, source_target_pairs={{0,4},{1,5},{2,6},{3,7},{4,0},{5,1},{6,2},{7,3},{8,12},{9,13},{10,... | collective-permute-start | bytes 1966088 | tf_op jit(solution)/shard_map/ppermute | solution.py:371
  210.9 55.4 %all-to-all-start.3 = ((bf16[16,2,160,256]{3,2,1,0:T(8,128)(2,1)}), bf16[16,2,160,256]{3,2,1,0:T(8,128)(2,1)S(1)}, u32[]{:S(2)}, u32[]{:S(2)}) async-start(bf16[16,2,160,256]{3,2,1,0:T(8,128)(2,1)} %get-tuple-element.68), calls=%async_computation.3 | async-start | bytes 5242880 | tf_op jit(solution)/shard_map/all_to_all | solution.py:319
  215.8 45.5 %collective-permute-start.2 = (bf16[2560,384]{1,0:T(8,128)(2,1)}, bf16[2560,384]{1,0:T(8,128)(2,1)}, u32[]{:S(2)}, u32[]{:S(2)}) collective-permute-start(bf16[2560,384]{1,0:T(8,128)(2,1)} %get-tuple-element.70.refs_2_), channel_id=1, source_target_pairs={{0,16},{16,0},{1,17},{17,1},{2,18},{18,2},{3,19},{19,3},{4,20},{20... | collective-permute-start | bytes 5898248 | tf_op jit(solution)/shard_map/ppermute | solution.py:394
  266.3 1.5 copy-start
  267.8 29.8 %all-to-all-start.4 = ((bf16[16,160,128]{2,1,0:T(8,128)(2,1)}), bf16[16,160,128]{2,1,0:T(8,128)(2,1)S(1)}, u32[]{:S(2)}, u32[]{:S(2)}) async-start(bf16[16,160,128]{2,1,0:T(8,128)(2,1)} %get-tuple-element.74), calls=%async_computation.4 | async-start | bytes 1310720 | tf_op jit(solution)/shard_map/all_to_all | solution.py:319
  298.5 4.9 %copy-start.5 = (bf16[2560,128]{1,0:T(8,128)(2,1)S(1)}, bf16[2560,128]{1,0:T(8,128)(2,1)}, u32[]{:S(2)}) copy-start(bf16[2560,128]{1,0:T(8,128)(2,1)} %get-tuple-element.78.refs_2_) | copy-start | bytes 1966084
  298.5 32.3 %all-to-all-start.5 = ((bf16[16,160,256]{2,1,0:T(8,128)(2,1)}), bf16[16,160,256]{2,1,0:T(8,128)(2,1)S(1)}, u32[]{:S(2)}, u32[]{:S(2)}) async-start(bf16[16,160,256]{2,1,0:T(8,128)(2,1)} %get-tuple-element.77), calls=%async_computation.5 | async-start | bytes 2621440 | tf_op jit(solution)/shard_map/all_to_all | solution.py:319
  303.4 17.1 %collective-permute-start.3 = (bf16[2560,128]{1,0:T(8,128)(2,1)S(1)}, bf16[2560,128]{1,0:T(8,128)(2,1)S(1)}, u32[]{:S(2)}, u32[]{:S(2)}) collective-permute-start(bf16[2560,128]{1,0:T(8,128)(2,1)S(1)} %copy-done.5), channel_id=1, source_target_pairs={{0,16},{16,0},{1,17},{17,1},{2,18},{18,2},{3,19},{19,3},{4,20},{20... | collective-permute-start | bytes 1966088 | tf_op jit(solution)/shard_map/ppermute | solution.py:394
  321.4 5.4 %copy-start.10 = (bf16[16,48,384]{2,1,0:T(8,128)(2,1)S(1)}, bf16[16,48,384]{2,1,0:T(8,128)(2,1)}, u32[]{:S(2)}) copy-start(bf16[16,48,384]{2,1,0:T(8,128)(2,1)} %get-tuple-element.87) | copy-start | bytes 1769476
  331.8 47.3 %all-to-all-start.6 = ((bf16[16,48,512]{2,1,0:T(8,128)(2,1)}), bf16[16,48,512]{2,1,0:T(8,128)(2,1)S(1)}, u32[]{:S(2)}, u32[]{:S(2)}) async-start(bf16[16,48,512]{2,1,0:T(8,128)(2,1)} %get-tuple-element.93), calls=%async_computation.6 | async-start | bytes 1572864 | tf_op jit(solution)/shard_map/all_to_all | solution.py:319
  339.9 31.3 %collective-permute-start.4 = (bf16[2560,256]{1,0:T(8,128)(2,1)}, bf16[2560,256]{1,0:T(8,128)(2,1)S(1)}, u32[]{:S(2)}, u32[]{:S(2)}) collective-permute-start(bf16[2560,256]{1,0:T(8,128)(2,1)} %get-tuple-element.84.refs_2_), channel_id=1, source_target_pairs={{0,16},{16,0},{1,17},{17,1},{2,18},{18,2},{3,19},{19,3},{4,20},{20... | collective-permute-start | bytes 3932168 | tf_op jit(solution)/shard_map/ppermute | solution.py:394
  380.1 17.9 %all-to-all-start.7 = ((bf16[16,48,256]{2,1,0:T(8,128)(2,1)}), bf16[16,48,256]{2,1,0:T(8,128)(2,1)S(1)}, u32[]{:S(2)}, u32[]{:S(2)}) async-start(bf16[16,48,256]{2,1,0:T(8,128)(2,1)} %get-tuple-element.96), calls=%async_computation.7 | async-start | bytes 786432 | tf_op jit(solution)/shard_map/all_to_all | solution.py:319
  (7 other events, 7.2 us)
Sparse Core Ops, SparseCore 0:
  209.6 67.1 all-gather.1

commit v14 on v13

--- a/solution.py
+++ b/solution.py
@@ -276,7 +276,6 @@
             order.append(("line", 0))
         if chunk + 1 == count:
             order.extend(("run", earlier) for earlier in range(cut))
-        order.append(("trade", chunk))
         if chunk + 2 < count:
             order.append(("raw", chunk + 2))
     order.append(("give", 0))
@@ -294,9 +293,7 @@
 
 
 def chunk_widths(blocks):
-    first = max(1, blocks // 2)
-    second = max(1, blocks // 6)
-    return [width for width in (first, second, blocks - first - second) if width > 0]
+    return [max(1, blocks - 2)] + [1] * min(2, blocks - 1)
 
 
 def shards(tokens, routes, quant_gate, quant_up, gate_scales, up_scales, cluster_ids, frequency):
@@ -378,19 +375,17 @@
             arrived = lax.all_gather(arrived, "mp", axis=2, tiled=True)
             grouped = arrived.reshape(expert_count * capacity, depth)
         elif name == "raw":
-            if c >= 1:
-                pieces[c], token = hold(token, pieces[c], [gathered[0]] if c == 1 else [])
+            if c == 1:
+                pieces[c], token = hold(token, pieces[c], [gathered[0], placing, picking])
+            elif c >= 2:
+                pieces[c], token = hold(token, pieces[c], [own[c - 2]])
             gathered[c] = exchange(pieces[c])
         elif name == "sum":
             merged[c], token = merge(token, slots, factors, gathered[c], start, blocks_of_rows)
         elif name == "back":
-            earlier = [gathered[c + 1]] if c + 1 in gathered else []
-            earlier += [placing, picking] if c == 0 else [grouped] if c == last else []
-            earlier += [partner[c - 1]] if 0 < c < last else []
-            merged[c], token = hold(token, merged[c], earlier)
-            own[c] = exchange(merged[c])
-        elif name == "trade":
-            own[c], token = hold(token, own[c].reshape(depth, width), [])
+            if 0 < c < last:
+                merged[c], token = hold(token, merged[c], [gathered[c + 1]])
+            own[c] = exchange(merged[c]).reshape(depth, width)
             partner[c] = lax.ppermute(own[c], "groups", partners)
         elif name == "run":
             (*outputs, hiddens[c]), token = run_chunk(

time: 408 us -> 418 us (1.025)
  waiting for transfers between devices: 212 us -> 227 us
    ppermute x1, waiting for transfers between devices: 0.01 us -> 68.4 us  [shards(): opposite = lax.ppermute(tokens, 'expert', across)]
    ppermute x3, waiting for transfers between devices: 80.8 us -> 15.8 us  [shards(): partner[c] = lax.ppermute(own[c], 'groups', partners)]
    all_to_all x8, waiting for transfers between devices: 93.1 us -> 135 us  [exchange(): return lax.all_to_all(pieces, 'expert', 0, 0, tiled=True)]
    ppermute x1, waiting for transfers between devices: 38.2 us -> 8 us  [shards(): nearby = lax.ppermute(both, 'expert', beside)]
    unnamed x35 -> x33, local copies, waits for them, and re-layouts: 9.67 us -> 7.88 us
    pallas_call x21 -> x16, Pallas kernels: 64.9 us -> 65 us  [step_call(): pl.pallas_call(ordered, out_shape=[*out_shape, TOKEN], in_specs=[*in_spec...]
  transfers between devices with their start and end apart: 14 -> 14, of which waited for: 9 -> 8; matrix products, arithmetic and copies ran while one was open for 6% -> 6% of each run, Pallas kernels for 15% -> 14%
where the time goes in v14:
time: 418 us; the launch traced here: 416 us
  waiting for transfers between devices  227 us (54%)
  starting transfers between devices  75.1 us (18%)
  Pallas kernels  65 us (16%)
  between operations  14.4 us (3%)
  other arithmetic  13.7 us (3%)
  local copies, waits for them, and re-layouts  12.6 us (3%)
  matrix products  7.74 us (2%)
    all_to_all x8, waiting for transfers between devices, exchange(): return lax.all_to_all(pieces, 'expert', 0, 0, tiled=True)  135 us
    ppermute x1, waiting for transfers between devices, shards(): opposite = lax.ppermute(tokens, 'expert', across)  68.4 us
    all_to_all x8, starting transfers between devices, exchange(): return lax.all_to_all(pieces, 'expert', 0, 0, tiled=True)  67.7 us
    pallas_call x16, Pallas kernels, step_call(): pl.pallas_call(ordered, out_shape=[*out_shape, TOKEN], in_specs=[*in_spec...  65 us
    ppermute x3, waiting for transfers between devices, shards(): partner[c] = lax.ppermute(own[c], 'groups', partners)  15.8 us
  transfers between devices with their start and end apart: 14, of which 8 were waited for; matrix products, arithmetic and copies ran while one was open for 6% of the time, Pallas kernels for 14%

profile of v14, /device:TPU:0, one launch (start us, length us, event | category | flops | bytes accessed | tf_op | source)
XLA Modules:
  0.0 415.9 jit_solution(6689085381270738371)
XLA Ops:
  8.3 5.6 %pack.3 = (bf16[16,2,160,512]{3,2,1,0:T(8,128)(2,1)}, f32[8,128]{1,0:T(8,128)}) custom-call(s32[2]{0:T(128)} %pad_add_fusion.refs_0_, bf16[2,2560,768]{2,1,0:T(8,128)(2,1)} %refs_1_.5, bf16[2,2560,768]{2,1,0:T(8,128)(2,1)} %refs_2_.5, f32[8,128]{1,0:T(8,128)} %broadcast_in_dim.40.refs_3_), custom_call_target="tpu_custom_call" | custom-call | tf_op jit(solution)/shard_map/pack/pallas_call | solution.py:32
  14.0 7.4 %all-to-all-start = ((bf16[16,2,160,512]{3,2,1,0:T(8,128)(2,1)}), bf16[16,2,160,512]{3,2,1,0:T(8,128)(2,1)}, u32[]{:S(2)}, u32[]{:S(2)}) async-start(bf16[16,2,160,512]{3,2,1,0:T(8,128)(2,1)} %get-tuple-element.40), calls=%async_computation | async-start | bytes 10485760 | tf_op jit(solution)/shard_map/all_to_all | solution.py:316
  25.0 6.3 %fusion.6 = s32[16,64,16]{2,0,1:T(8,128)S(1)} fusion(s32[16,64,16]{2,0,1:T(8,128)S(1)} %copy.60), kind=kOutput, calls=%fused_computation.38 | output fusion | flops 1032192 | bytes 131072 | tf_op jit(solution)/shard_map/jit(cumsum)/reduce_window_sum | solution.py:291
  38.0 79.4 %all-to-all-done.refs_1_.refs_2_ = bf16[16,2,160,512]{3,2,1,0:T(8,128)(2,1)} async-done(((bf16[16,2,160,512]{3,2,1,0:T(8,128)(2,1)}), bf16[16,2,160,512]{3,2,1,0:T(8,128)(2,1)}, u32[]{:S(2)}, u32[]{:S(2)}) %all-to-all-start) | async-done | bytes 5242912 | tf_op jit(solution)/shard_map/all_to_all | solution.py:316
  117.4 24.0 %all-to-all-start.1 = ((bf16[16,2,160,128]{3,2,1,0:T(8,128)(2,1)}), bf16[16,2,160,128]{3,2,1,0:T(8,128)(2,1)S(1)}, u32[]{:S(2)}, u32[]{:S(2)}) async-start(bf16[16,2,160,128]{3,2,1,0:T(8,128)(2,1)} %get-tuple-element.48), calls=%async_computation.1 | async-start | bytes 2621440 | tf_op jit(solution)/shard_map/all_to_all | solution.py:316
  143.2 10.9 %merge.3 = (bf16[16,160,512]{2,1,0:T(8,128)(2,1)}, f32[8,128]{1,0:T(8,128)}) custom-call(s32[32]{0:T(128)} %bitcast.50, f32[960]{0:T(1024)} %mul.47.refs_1_, bf16[16,2,160,512]{3,2,1,0:T(8,128)(2,1)} %all-to-all-done.refs_1_.refs_2_, f32[8,128]{1,0:T(8,128)} %get-tuple-element.44.refs_3_), custom_call_target="tpu_custom_call" | custom-call | tf_op jit(solution)/shard_map/merge/pallas_call | solution.py:32
  154.2 14.7 %all-to-all-done.1.refs_2_ = bf16[16,2,160,128]{3,2,1,0:T(8,128)(2,1)S(1)} async-done(((bf16[16,2,160,128]{3,2,1,0:T(8,128)(2,1)}), bf16[16,2,160,128]{3,2,1,0:T(8,128)(2,1)S(1)}, u32[]{:S(2)}, u32[]{:S(2)}) %all-to-all-start.1) | async-done | bytes 1310752 | tf_op jit(solution)/shard_map/all_to_all | solution.py:316
  169.9 8.0 %all-to-all-start.2 = ((bf16[16,160,512]{2,1,0:T(8,128)(2,1)}), bf16[16,160,512]{2,1,0:T(8,128)(2,1)S(1)}, u32[]{:S(2)}, u32[]{:S(2)}) async-start(bf16[16,160,512]{2,1,0:T(8,128)(2,1)} %get-tuple-element.53), calls=%async_computation.2 | async-start | bytes 5242880 | tf_op jit(solution)/shard_map/all_to_all | solution.py:316
  183.9 68.4 %collective-permute-done.refs_1_ = bf16[64,2560]{1,0:T(8,128)(2,1)S(1)} collective-permute-done((bf16[64,2560]{1,0:T(8,128)(2,1)S(1)}, bf16[64,2560]{1,0:T(8,128)(2,1)S(1)}, u32[]{:S(2)}, u32[]{:S(2)}) %collective-permute-start) | collective-permute-done | bytes 327712 | tf_op jit(solution)/shard_map/ppermute | solution.py:356
  255.0 8.6 %merge.4 = (bf16[16,160,128]{2,1,0:T(8,128)(2,1)}, f32[8,128]{1,0:T(8,128)}) custom-call(s32[32]{0:T(128)} %bitcast.51, f32[960]{0:T(1024)} %mul.47.refs_1_, bf16[16,2,160,128]{3,2,1,0:T(8,128)(2,1)} %copy-done.2, f32[8,128]{1,0:T(8,128)} %get-tuple-element.49.refs_3_), custom_call_target="tpu_custom_call" | custom-call | tf_op jit(solution)/shard_map/merge/pallas_call | solution.py:32
  263.6 8.0 %collective-permute-done.1.refs_2_ = bf16[2,64,2560]{2,1,0:T(8,128)(2,1)} collective-permute-done((bf16[2,64,2560]{2,1,0:T(8,128)(2,1)}, bf16[2,64,2560]{2,1,0:T(8,128)(2,1)}, u32[]{:S(2)}, u32[]{:S(2)}) %collective-permute-start.1) | collective-permute-done | bytes 655392 | tf_op jit(solution)/shard_map/ppermute | solution.py:368
  280.8 25.9 %all-to-all-done.3.refs_1_.refs_2_ = bf16[16,2,160,128]{3,2,1,0:T(8,128)(2,1)S(1)} async-done(((bf16[16,2,160,128]{3,2,1,0:T(8,128)(2,1)}), bf16[16,2,160,128]{3,2,1,0:T(8,128)(2,1)S(1)}, u32[]{:S(2)}, u32[]{:S(2)}) %all-to-all-start.3) | async-done | bytes 1310752 | tf_op jit(solution)/shard_map/all_to_all | solution.py:316
  307.8 8.1 %all-to-all-start.5 = ((bf16[16,160,128]{2,1,0:T(8,128)(2,1)}), bf16[16,160,128]{2,1,0:T(8,128)(2,1)S(1)}, u32[]{:S(2)}, u32[]{:S(2)}) async-start(bf16[16,160,128]{2,1,0:T(8,128)(2,1)} %get-tuple-element.60), calls=%async_computation.5 | async-start | bytes 1310720 | tf_op jit(solution)/shard_map/all_to_all | solution.py:316
  315.8 8.7 %merge.5 = (bf16[16,160,128]{2,1,0:T(8,128)(2,1)}, f32[8,128]{1,0:T(8,128)}) custom-call(s32[32]{0:T(128)} %bitcast.52, f32[960]{0:T(1024)} %mul.47.refs_1_, bf16[16,2,160,128]{3,2,1,0:T(8,128)(2,1)} %copy-done.1, f32[8,128]{1,0:T(8,128)} %get-tuple-element.58.refs_3_), custom_call_target="tpu_custom_call" | custom-call | tf_op jit(solution)/shard_map/merge/pallas_call | solution.py:32
  324.5 7.9 %all-to-all-done.5 = bf16[16,160,128]{2,1,0:T(8,128)(2,1)S(1)} async-done(((bf16[16,160,128]{2,1,0:T(8,128)(2,1)}), bf16[16,160,128]{2,1,0:T(8,128)(2,1)S(1)}, u32[]{:S(2)}, u32[]{:S(2)}) %all-to-all-start.5) | async-done | bytes 655392 | tf_op jit(solution)/shard_map/all_to_all | solution.py:316
  332.5 4.8 %all-to-all-start.4 = ((bf16[16,160,128]{2,1,0:T(8,128)(2,1)}), bf16[16,160,128]{2,1,0:T(8,128)(2,1)S(1)}, u32[]{:S(2)}, u32[]{:S(2)}) async-start(bf16[16,160,128]{2,1,0:T(8,128)(2,1)} %get-tuple-element.59), calls=%async_computation.4 | async-start | bytes 1310720 | tf_op jit(solution)/shard_map/all_to_all | solution.py:316
  338.8 5.6 %convolution_convert_fusion = bf16[16,48,2560]{2,1,0:T(8,128)(2,1)} fusion(bf16[16,64,2560]{2,1,0:T(8,128)(2,1)} %all-gather.2.cloned.1.call-done, s32[16,64]{1,0:T(8,128)S(1)} %bitcast.46, pred[16,64]{1,0:T(8,128)(4,1)S(1)} %bitcast.49), kind=kOutput, calls=%fused_computation.1 | convolution fusion | flops 253722624 | bytes 9180160 | tf_op jit(solution)/shard_map/jct,jtd->jcd/dot_general | solution.py:372
  344.4 9.9 %run_chunk.3 = (bf16[1,2560,768]{2,1,0:T(8,128)(2,1)}, bf16[1,2560,768]{2,1,0:T(8,128)(2,1)}, bf16[16,48,512]{2,1,0:T(8,128)(2,1)}, f32[8,128]{1,0:T(8,128)}) custom-call(s32[2]{0:T(128)} %pad_add_fusion.refs_0_, bf16[768,2560]{1,0:T(8,128)(2,1)} %bitcast.32, bf16[2560,512]{1,0:T(8,128)(2,1)} %bitcast.37, bf16[2560,512]{1,0:T(8,128)(2,1)} %collective-permute-done.4.refs_3_, ...), custom_call_target="tpu_custom_call" | custom-call | tf_op jit(solution)/shard_map/run_chunk/pallas_call | solution.py:32
  355.2 5.4 %run_chunk.4 = (bf16[1,2560,768]{2,1,0:T(8,128)(2,1)}, bf16[1,2560,768]{2,1,0:T(8,128)(2,1)}, bf16[16,48,128]{2,1,0:T(8,128)(2,1)}, f32[8,128]{1,0:T(8,128)}) custom-call(s32[2]{0:T(128)} %pad_add_fusion.refs_0_, bf16[768,2560]{1,0:T(8,128)(2,1)} %bitcast.33, bf16[2560,128]{1,0:T(8,128)(2,1)} %bitcast.42, ...), custom_call_target="tpu_custom_call", output_to_operand_aliasing={{0}: (4, {}), {1}: (5, {})} | custom-call | tf_op jit(solution)/shard_map/run_chunk/pallas_call | solution.py:32
  362.6 6.0 %all-to-all-start.6 = ((bf16[16,48,640]{2,1,0:T(8,128)(2,1)}), bf16[16,48,640]{2,1,0:T(8,128)(2,1)S(1)}, u32[]{:S(2)}, u32[]{:S(2)}) async-start(bf16[16,48,640]{2,1,0:T(8,128)(2,1)} %get-tuple-element.73), calls=%async_computation.6 | async-start | bytes 1966080 | tf_op jit(solution)/shard_map/all_to_all | solution.py:316
  369.9 15.7 %collective-permute-done.2.refs_3_ = bf16[2560,128]{1,0:T(8,128)(2,1)S(1)} collective-permute-done((bf16[2560,128]{1,0:T(8,128)(2,1)S(1)}, bf16[2560,128]{1,0:T(8,128)(2,1)S(1)}, u32[]{:S(2)}, u32[]{:S(2)}) %collective-permute-start.2) | collective-permute-done | bytes 655392 | tf_op jit(solution)/shard_map/ppermute | solution.py:389
  386.5 5.3 %run_chunk.5 = (bf16[1,2560,768]{2,1,0:T(8,128)(2,1)}, bf16[1,2560,768]{2,1,0:T(8,128)(2,1)}, bf16[16,48,128]{2,1,0:T(8,128)(2,1)}, f32[8,128]{1,0:T(8,128)}) custom-call(s32[2]{0:T(128)} %pad_add_fusion.refs_0_, bf16[768,2560]{1,0:T(8,128)(2,1)} %bitcast.34, bf16[2560,128]{1,0:T(8,128)(2,1)} %bitcast.40, ...), custom_call_target="tpu_custom_call", output_to_operand_aliasing={{0}: (4, {}), {1}: (5, {})} | custom-call | tf_op jit(solution)/shard_map/run_chunk/pallas_call | solution.py:32
  392.8 5.7 %all-to-all-start.7 = ((bf16[16,48,128]{2,1,0:T(8,128)(2,1)}), bf16[16,48,128]{2,1,0:T(8,128)(2,1)S(1)}, u32[]{:S(2)}, u32[]{:S(2)}) async-start(bf16[16,48,128]{2,1,0:T(8,128)(2,1)} %get-tuple-element.76), calls=%async_computation.7 | async-start | bytes 393216 | tf_op jit(solution)/shard_map/all_to_all | solution.py:316
  400.3 7.2 %all-to-all-done.7 = bf16[16,48,128]{2,1,0:T(8,128)(2,1)S(1)} async-done(((bf16[16,48,128]{2,1,0:T(8,128)(2,1)}), bf16[16,48,128]{2,1,0:T(8,128)(2,1)S(1)}, u32[]{:S(2)}, u32[]{:S(2)}) %all-to-all-start.7) | async-done | bytes 196640 | tf_op jit(solution)/shard_map/all_to_all | solution.py:316
  (92 shorter events, 43.9 us)
Async XLA Ops:
  14.0 103.4 %all-to-all-start = ((bf16[16,2,160,512]{3,2,1,0:T(8,128)(2,1)}), bf16[16,2,160,512]{3,2,1,0:T(8,128)(2,1)}, u32[]{:S(2)}, u32[]{:S(2)}) async-start(bf16[16,2,160,512]{3,2,1,0:T(8,128)(2,1)} %get-tuple-element.40), calls=%async_computation | async-start | bytes 10485760 | tf_op jit(solution)/shard_map/all_to_all | solution.py:316
  21.4 3.2 copy-start.13
  117.4 24.0 %copy-start.14 = (s32[32,1]{0,1:T(1,128)S(1)}, s32[32,1]{0,1:T(1,128)}, u32[]{:S(2)}) copy-start(s32[32,1]{0,1:T(1,128)} %param.14) | copy-start | bytes 388
  117.4 24.0 %copy-start.15 = (f32[32]{0:T(128)S(1)}, f32[32]{0:T(128)}, u32[]{:S(2)}) copy-start(f32[32]{0:T(128)} %param.15) | copy-start | bytes 388
  117.4 24.3 %copy-start.11 = (f32[32,20,6]{0,1,2:T(8,128)S(1)}, f32[32,20,6]{0,1,2:T(8,128)}, u32[]{:S(2)}) copy-start(f32[32,20,6]{0,1,2:T(8,128)} %param.13) | copy-start | bytes 46084
  117.4 24.3 %copy-start.12 = (f32[32,20,6]{0,1,2:T(8,128)S(1)}, f32[32,20,6]{0,1,2:T(8,128)}, u32[]{:S(2)}) copy-start(f32[32,20,6]{0,1,2:T(8,128)} %param.12) | copy-start | bytes 46084
  117.4 51.4 %all-to-all-start.1 = ((bf16[16,2,160,128]{3,2,1,0:T(8,128)(2,1)}), bf16[16,2,160,128]{3,2,1,0:T(8,128)(2,1)S(1)}, u32[]{:S(2)}, u32[]{:S(2)}) async-start(bf16[16,2,160,128]{3,2,1,0:T(8,128)(2,1)} %get-tuple-element.48), calls=%async_computation.1 | async-start | bytes 2621440 | tf_op jit(solution)/shard_map/all_to_all | solution.py:316
  154.2 23.8 %copy-start.9 = (bf16[64,2560]{1,0:T(8,128)(2,1)S(1)}, bf16[64,2560]{1,0:T(8,128)(2,1)}, u32[]{:S(2)}) copy-start(bf16[64,2560]{1,0:T(8,128)(2,1)} %refs_0_.1) | copy-start | bytes 983044
  169.9 104.2 %all-to-all-start.2 = ((bf16[16,160,512]{2,1,0:T(8,128)(2,1)}), bf16[16,160,512]{2,1,0:T(8,128)(2,1)S(1)}, u32[]{:S(2)}, u32[]{:S(2)}) async-start(bf16[16,160,512]{2,1,0:T(8,128)(2,1)} %get-tuple-element.53), calls=%async_computation.2 | async-start | bytes 5242880 | tf_op jit(solution)/shard_map/all_to_all | solution.py:316
  177.9 160.9 %all-gather.2.cloned.1.call-start = ((), (), s32[]{:S(2)}) async-start(), calls=%async_computation.8 | async-start | bytes 6553600 | tf_op jit(solution)/shard_map/all_gather | solution.py:371
  178.0 74.3 %collective-permute-start = (bf16[64,2560]{1,0:T(8,128)(2,1)S(1)}, bf16[64,2560]{1,0:T(8,128)(2,1)S(1)}, u32[]{:S(2)}, u32[]{:S(2)}) collective-permute-start(bf16[64,2560]{1,0:T(8,128)(2,1)S(1)} %copy-done.9), channel_id=1, source_target_pairs={{0,8},{1,9},{2,10},{3,11},{4,12},{5,13},{6,14},{7,15},{8,0},{9,1},... | collective-permute-start | bytes 983048 | tf_op jit(solution)/shard_map/ppermute | solution.py:356
  255.0 16.6 %collective-permute-start.1 = (bf16[2,64,2560]{2,1,0:T(8,128)(2,1)}, bf16[2,64,2560]{2,1,0:T(8,128)(2,1)}, u32[]{:S(2)}, u32[]{:S(2)}) collective-permute-start(bf16[2,64,2560]{2,1,0:T(8,128)(2,1)} %get-tuple-element.47.refs_1_), channel_id=1, source_target_pairs={{0,4},{1,5},{2,6},{3,7},{4,0},{5,1},{6,2},{7,3},{8,12},{9,13},{10,... | collective-permute-start | bytes 1966088 | tf_op jit(solution)/shard_map/ppermute | solution.py:368
  274.1 1.5 copy-start
  275.6 31.2 %all-to-all-start.3 = ((bf16[16,2,160,128]{3,2,1,0:T(8,128)(2,1)}), bf16[16,2,160,128]{3,2,1,0:T(8,128)(2,1)S(1)}, u32[]{:S(2)}, u32[]{:S(2)}) async-start(bf16[16,2,160,128]{3,2,1,0:T(8,128)(2,1)} %get-tuple-element.55), calls=%async_computation.3 | async-start | bytes 2621440 | tf_op jit(solution)/shard_map/all_to_all | solution.py:316
  279.3 65.1 %collective-permute-start.4 = (bf16[2560,512]{1,0:T(8,128)(2,1)}, bf16[2560,512]{1,0:T(8,128)(2,1)}, u32[]{:S(2)}, u32[]{:S(2)}) collective-permute-start(bf16[2560,512]{1,0:T(8,128)(2,1)} %bitcast.36), channel_id=1, source_target_pairs={{0,16},{16,0},{1,17},{17,1},{2,18},{18,2},{3,19},{19,3},{4,20},{20... | collective-permute-start | bytes 7864328 | tf_op jit(solution)/shard_map/ppermute | solution.py:389
  307.8 24.7 %all-to-all-start.5 = ((bf16[16,160,128]{2,1,0:T(8,128)(2,1)}), bf16[16,160,128]{2,1,0:T(8,128)(2,1)S(1)}, u32[]{:S(2)}, u32[]{:S(2)}) async-start(bf16[16,160,128]{2,1,0:T(8,128)(2,1)} %get-tuple-element.60), calls=%async_computation.5 | async-start | bytes 1310720 | tf_op jit(solution)/shard_map/all_to_all | solution.py:316
  332.5 12.0 %copy-start.5 = (bf16[16,160,128]{2,1,0:T(8,128)(2,1)}, bf16[16,160,128]{2,1,0:T(8,128)(2,1)S(1)}, u32[]{:S(2)}) copy-start(bf16[16,160,128]{2,1,0:T(8,128)(2,1)S(1)} %all-to-all-done.5) | copy-start | bytes 1966084
  332.5 30.1 %all-to-all-start.4 = ((bf16[16,160,128]{2,1,0:T(8,128)(2,1)}), bf16[16,160,128]{2,1,0:T(8,128)(2,1)S(1)}, u32[]{:S(2)}, u32[]{:S(2)}) async-start(bf16[16,160,128]{2,1,0:T(8,128)(2,1)} %get-tuple-element.59), calls=%async_computation.4 | async-start | bytes 1310720 | tf_op jit(solution)/shard_map/all_to_all | solution.py:316
  337.2 17.1 %collective-permute-start.3 = (bf16[2560,128]{1,0:T(8,128)(2,1)S(1)}, bf16[2560,128]{1,0:T(8,128)(2,1)S(1)}, u32[]{:S(2)}, u32[]{:S(2)}) collective-permute-start(bf16[2560,128]{1,0:T(8,128)(2,1)S(1)} %bitcast.41), channel_id=1, source_target_pairs={{0,16},{16,0},{1,17},{17,1},{2,18},{18,2},{3,19},{19,3},{4,20},{20... | collective-permute-start | bytes 1966088 | tf_op jit(solution)/shard_map/ppermute | solution.py:389
  355.2 5.4 %copy-start.6 = (bf16[16,48,512]{2,1,0:T(8,128)(2,1)S(1)}, bf16[16,48,512]{2,1,0:T(8,128)(2,1)}, u32[]{:S(2)}) copy-start(bf16[16,48,512]{2,1,0:T(8,128)(2,1)} %get-tuple-element.67) | copy-start | bytes 2359300
  362.6 23.0 %copy-start.4 = (bf16[16,160,128]{2,1,0:T(8,128)(2,1)}, bf16[16,160,128]{2,1,0:T(8,128)(2,1)S(1)}, u32[]{:S(2)}) copy-start(bf16[16,160,128]{2,1,0:T(8,128)(2,1)S(1)} %all-to-all-done.4) | copy-start | bytes 1966084
  362.6 29.2 %all-to-all-start.6 = ((bf16[16,48,640]{2,1,0:T(8,128)(2,1)}), bf16[16,48,640]{2,1,0:T(8,128)(2,1)S(1)}, u32[]{:S(2)}, u32[]{:S(2)}) async-start(bf16[16,48,640]{2,1,0:T(8,128)(2,1)} %get-tuple-element.73), calls=%async_computation.6 | async-start | bytes 1966080 | tf_op jit(solution)/shard_map/all_to_all | solution.py:316
  368.6 17.0 %collective-permute-start.2 = (bf16[2560,128]{1,0:T(8,128)(2,1)S(1)}, bf16[2560,128]{1,0:T(8,128)(2,1)S(1)}, u32[]{:S(2)}, u32[]{:S(2)}) collective-permute-start(bf16[2560,128]{1,0:T(8,128)(2,1)S(1)} %bitcast.39), channel_id=1, source_target_pairs={{0,16},{16,0},{1,17},{17,1},{2,18},{18,2},{3,19},{19,3},{4,20},{20... | collective-permute-start | bytes 1966088 | tf_op jit(solution)/shard_map/ppermute | solution.py:389
  392.8 14.8 %all-to-all-start.7 = ((bf16[16,48,128]{2,1,0:T(8,128)(2,1)}), bf16[16,48,128]{2,1,0:T(8,128)(2,1)S(1)}, u32[]{:S(2)}, u32[]{:S(2)}) async-start(bf16[16,48,128]{2,1,0:T(8,128)(2,1)} %get-tuple-element.76), calls=%async_computation.7 | async-start | bytes 393216 | tf_op jit(solution)/shard_map/all_to_all | solution.py:316
  (6 other events, 5.5 us)
Sparse Core Ops, SparseCore 0:
  274.2 57.1 all-gather.1

commit v15 on v14

--- a/solution.py
+++ b/solution.py
@@ -263,17 +263,15 @@
 
 def plan(count):
     cut = first_runs(count)
-    order = [("pack", 0), ("raw", 0), ("pack", 1), ("raw", 1), ("sum", 0)]
+    order = [("pack", 0), ("raw", 0), ("pack", 1), ("raw", 1), ("pair", 0), ("sum", 0)]
     for chunk in range(count):
         if chunk + 2 < count:
             order.append(("pack", chunk + 2))
         if chunk == 0:
-            order.append(("pair", 0))
+            order.append(("line", 0))
         order.append(("back", chunk))
         if chunk + 1 < count:
             order.append(("sum", chunk + 1))
-        if chunk == 0:
-            order.append(("line", 0))
         if chunk + 1 == count:
             order.extend(("run", earlier) for earlier in range(cut))
         if chunk + 2 < count:
@@ -378,12 +376,12 @@
             if c == 1:
                 pieces[c], token = hold(token, pieces[c], [gathered[0], placing, picking])
             elif c >= 2:
-                pieces[c], token = hold(token, pieces[c], [own[c - 2]])
+                pieces[c], token = hold(token, pieces[c], [own[c - 2], grouped])
             gathered[c] = exchange(pieces[c])
         elif name == "sum":
             merged[c], token = merge(token, slots, factors, gathered[c], start, blocks_of_rows)
         elif name == "back":
-            if 0 < c < last:
+            if c < last:
                 merged[c], token = hold(token, merged[c], [gathered[c + 1]])
             own[c] = exchange(merged[c]).reshape(depth, width)
             partner[c] = lax.ppermute(own[c], "groups", partners)

time: 418 us -> 417 us (level)
  blocking collectives: 0 us -> 35.1 us
  starting transfers between devices: 75.1 us -> 56.8 us
  waiting for transfers between devices: 227 us -> 210 us
    ppermute x1, waiting for transfers between devices: 68.4 us -> 27.6 us  [shards(): opposite = lax.ppermute(tokens, 'expert', across)]
    all_to_all x0 -> x1, blocking collectives: none -> 35.1 us  [exchange(): return lax.all_to_all(pieces, 'expert', 0, 0, tiled=True)]
    all_gather x1, waiting for transfers between devices: 0.01 us -> 21.5 us  [shards(): lax.all_gather(whole, 'expert', axis=0, tiled=True, axis_index_groups=by_...]
    all_to_all x8 -> x7, starting transfers between devices: 67.7 us -> 49.2 us  [exchange(): return lax.all_to_all(pieces, 'expert', 0, 0, tiled=True)]
    ppermute x1, waiting for transfers between devices: 8 us -> 0.79 us  [shards(): nearby = lax.ppermute(both, 'expert', beside)]
    ppermute x3, waiting for transfers between devices: 15.8 us -> 21.1 us  [shards(): partner[c] = lax.ppermute(own[c], 'groups', partners)]
    all_to_all x8 -> x7, waiting for transfers between devices: 135 us -> 139 us  [exchange(): return lax.all_to_all(pieces, 'expert', 0, 0, tiled=True)]
    pallas_call x16 -> x17, Pallas kernels: 65 us -> 65.2 us  [step_call(): pl.pallas_call(ordered, out_shape=[*out_shape, TOKEN], in_specs=[*in_spec...]
  transfers between devices with their start and end apart: 14 -> 13, of which waited for: 8 -> 10; matrix products, arithmetic and copies ran while one was open for 6% -> 6% of each run, Pallas kernels for 14% -> 13%
where the time goes in v15:
time: 417 us; the launch traced here: 415 us
  waiting for transfers between devices  210 us (50%)
  Pallas kernels  65.2 us (16%)
  starting transfers between devices  56.8 us (14%)
  blocking collectives  35.1 us (8%)
  between operations  14.4 us (3%)
  other arithmetic  13.8 us (3%)
  local copies, waits for them, and re-layouts  12.4 us (3%)
  matrix products  7.74 us (2%)
    all_to_all x7, waiting for transfers between devices, exchange(): return lax.all_to_all(pieces, 'expert', 0, 0, tiled=True)  139 us
    pallas_call x17, Pallas kernels, step_call(): pl.pallas_call(ordered, out_shape=[*out_shape, TOKEN], in_specs=[*in_spec...  65.2 us
    all_to_all x7, starting transfers between devices, exchange(): return lax.all_to_all(pieces, 'expert', 0, 0, tiled=True)  49.2 us
    all_to_all x1, blocking collectives, exchange(): return lax.all_to_all(pieces, 'expert', 0, 0, tiled=True)  35.1 us
    ppermute x1, waiting for transfers between devices, shards(): opposite = lax.ppermute(tokens, 'expert', across)  27.6 us
    all_gather x1, waiting for transfers between devices, shards(): lax.all_gather(whole, 'expert', axis=0, tiled=True, axis_index_groups=by_...  21.5 us
    ppermute x3, waiting for transfers between devices, shards(): partner[c] = lax.ppermute(own[c], 'groups', partners)  21.1 us
  transfers between devices with their start and end apart: 13, of which 10 were waited for; matrix products, arithmetic and copies ran while one was open for 6% of the time, Pallas kernels for 13%

profile of v15, /device:TPU:0, one launch (start us, length us, event | category | flops | bytes accessed | tf_op | source)
XLA Modules:
  0.0 415.2 jit_solution(1832086330732230803)
XLA Ops:
  8.4 5.6 %pack.3 = (bf16[16,2,160,512]{3,2,1,0:T(8,128)(2,1)}, f32[8,128]{1,0:T(8,128)}) custom-call(s32[2]{0:T(128)} %pad_add_fusion.refs_0_, bf16[2,2560,768]{2,1,0:T(8,128)(2,1)} %refs_1_.5, bf16[2,2560,768]{2,1,0:T(8,128)(2,1)} %refs_2_.5, f32[8,128]{1,0:T(8,128)} %broadcast_in_dim.38.refs_3_), custom_call_target="tpu_custom_call" | custom-call | tf_op jit(solution)/shard_map/pack/pallas_call | solution.py:32
  14.1 7.6 %all-to-all-start = ((bf16[16,2,160,512]{3,2,1,0:T(8,128)(2,1)}), bf16[16,2,160,512]{3,2,1,0:T(8,128)(2,1)}, u32[]{:S(2)}, u32[]{:S(2)}) async-start(bf16[16,2,160,512]{3,2,1,0:T(8,128)(2,1)} %get-tuple-element.44), calls=%async_computation | async-start | bytes 10485760 | tf_op jit(solution)/shard_map/all_to_all | solution.py:314
  28.2 6.3 %fusion.6 = s32[16,64,16]{2,0,1:T(8,128)S(1)} fusion(s32[16,64,16]{2,0,1:T(8,128)S(1)} %copy.61), kind=kOutput, calls=%fused_computation.38 | output fusion | flops 1032192 | bytes 131072 | tf_op jit(solution)/shard_map/jit(cumsum)/reduce_window_sum | solution.py:289
  41.4 83.2 %all-to-all-done.refs_1_.refs_2_ = bf16[16,2,160,512]{3,2,1,0:T(8,128)(2,1)} async-done(((bf16[16,2,160,512]{3,2,1,0:T(8,128)(2,1)}), bf16[16,2,160,512]{3,2,1,0:T(8,128)(2,1)}, u32[]{:S(2)}, u32[]{:S(2)}) %all-to-all-start) | async-done | bytes 5242912 | tf_op jit(solution)/shard_map/all_to_all | solution.py:314
  124.6 27.6 %collective-permute-done.refs_1_ = bf16[64,2560]{1,0:T(8,128)(2,1)S(1)} collective-permute-done((bf16[64,2560]{1,0:T(8,128)(2,1)S(1)}, bf16[64,2560]{1,0:T(8,128)(2,1)S(1)}, u32[]{:S(2)}, u32[]{:S(2)}) %collective-permute-start) | collective-permute-done | bytes 327712 | tf_op jit(solution)/shard_map/ppermute | solution.py:354
  156.4 10.9 %merge.3 = (bf16[16,160,512]{2,1,0:T(8,128)(2,1)}, f32[8,128]{1,0:T(8,128)}) custom-call(s32[32]{0:T(128)} %bitcast.51, f32[960]{0:T(1024)} %mul.48.refs_1_, bf16[16,2,160,512]{3,2,1,0:T(8,128)(2,1)} %all-to-all-done.refs_1_.refs_2_, f32[8,128]{1,0:T(8,128)} %get-tuple-element.48.refs_3_), custom_call_target="tpu_custom_call" | custom-call | tf_op jit(solution)/shard_map/merge/pallas_call | solution.py:32
  174.8 35.1 %all_to_all.40.refs_1_.refs_2_ = bf16[16,2,160,128]{3,2,1,0:T(8,128)(2,1)} all-to-all(bf16[16,2,160,128]{3,2,1,0:T(8,128)(2,1)S(1)} %copy-done.2), channel_id=1, replica_groups=mesh['groups'=2,'expert'=16,'mp'=1] {'expert'}, dimensions={0} | all-to-all | bytes 2621440 | tf_op jit(solution)/shard_map/all_to_all | solution.py:314
  213.8 8.6 %merge.4 = (bf16[16,160,128]{2,1,0:T(8,128)(2,1)}, f32[8,128]{1,0:T(8,128)}) custom-call(s32[32]{0:T(128)} %bitcast.52, f32[960]{0:T(1024)} %mul.48.refs_1_, bf16[16,2,160,128]{3,2,1,0:T(8,128)(2,1)} %all_to_all.40.refs_1_.refs_2_, f32[8,128]{1,0:T(8,128)} %get-tuple-element.57.refs_3_), custom_call_target="tpu_custom_call" | custom-call | tf_op jit(solution)/shard_map/merge/pallas_call | solution.py:32
  222.5 21.5 %all-gather.2.cloned.1.call-done = bf16[16,64,2560]{2,1,0:T(8,128)(2,1)} async-done(((bf16[4,64,2560]{2,1,0:T(8,128)(2,1)}), bf16[16,64,2560]{2,1,0:T(8,128)(2,1)}) %all-gather.2.cloned.1.call-update) | async-done | bytes 5242896 | tf_op jit(solution)/shard_map/all_gather | solution.py:369
  243.9 5.6 %convolution_convert_fusion = bf16[16,48,2560]{2,1,0:T(8,128)(2,1)} fusion(bf16[16,64,2560]{2,1,0:T(8,128)(2,1)} %all-gather.2.cloned.1.call-done, s32[16,64]{1,0:T(8,128)S(1)} %bitcast.47, pred[16,64]{1,0:T(8,128)(4,1)S(1)} %bitcast.50), kind=kOutput, calls=%fused_computation.1 | convolution fusion | flops 253722624 | bytes 9180160 | tf_op jit(solution)/shard_map/jct,jtd->jcd/dot_general | solution.py:370
  249.5 14.6 %all-to-all-done.2 = bf16[16,160,512]{2,1,0:T(8,128)(2,1)S(1)} async-done(((bf16[16,160,512]{2,1,0:T(8,128)(2,1)}), bf16[16,160,512]{2,1,0:T(8,128)(2,1)S(1)}, u32[]{:S(2)}, u32[]{:S(2)}) %all-to-all-start.2) | async-done | bytes 2621472 | tf_op jit(solution)/shard_map/all_to_all | solution.py:314
  265.6 13.4 %all-to-all-start.3 = ((bf16[16,2,160,128]{3,2,1,0:T(8,128)(2,1)}), bf16[16,2,160,128]{3,2,1,0:T(8,128)(2,1)S(1)}, u32[]{:S(2)}, u32[]{:S(2)}) async-start(bf16[16,2,160,128]{3,2,1,0:T(8,128)(2,1)} %get-tuple-element.59), calls=%async_computation.3 | async-start | bytes 2621440 | tf_op jit(solution)/shard_map/all_to_all | solution.py:314
  280.5 25.8 %all-to-all-done.3.refs_1_.refs_2_ = bf16[16,2,160,128]{3,2,1,0:T(8,128)(2,1)S(1)} async-done(((bf16[16,2,160,128]{3,2,1,0:T(8,128)(2,1)}), bf16[16,2,160,128]{3,2,1,0:T(8,128)(2,1)S(1)}, u32[]{:S(2)}, u32[]{:S(2)}) %all-to-all-start.3) | async-done | bytes 1310752 | tf_op jit(solution)/shard_map/all_to_all | solution.py:314
  307.4 8.0 %all-to-all-start.5 = ((bf16[16,160,128]{2,1,0:T(8,128)(2,1)}), bf16[16,160,128]{2,1,0:T(8,128)(2,1)S(1)}, u32[]{:S(2)}, u32[]{:S(2)}) async-start(bf16[16,160,128]{2,1,0:T(8,128)(2,1)} %get-tuple-element.64), calls=%async_computation.5 | async-start | bytes 1310720 | tf_op jit(solution)/shard_map/all_to_all | solution.py:314
  315.4 8.6 %merge.5 = (bf16[16,160,128]{2,1,0:T(8,128)(2,1)}, f32[8,128]{1,0:T(8,128)}) custom-call(s32[32]{0:T(128)} %bitcast.53, f32[960]{0:T(1024)} %mul.48.refs_1_, bf16[16,2,160,128]{3,2,1,0:T(8,128)(2,1)} %copy-done.1, f32[8,128]{1,0:T(8,128)} %get-tuple-element.62.refs_3_), custom_call_target="tpu_custom_call" | custom-call | tf_op jit(solution)/shard_map/merge/pallas_call | solution.py:32
  324.1 8.0 %all-to-all-done.5 = bf16[16,160,128]{2,1,0:T(8,128)(2,1)S(1)} async-done(((bf16[16,160,128]{2,1,0:T(8,128)(2,1)}), bf16[16,160,128]{2,1,0:T(8,128)(2,1)S(1)}, u32[]{:S(2)}, u32[]{:S(2)}) %all-to-all-start.5) | async-done | bytes 655392 | tf_op jit(solution)/shard_map/all_to_all | solution.py:314
  338.5 9.9 %run_chunk.3 = (bf16[1,2560,768]{2,1,0:T(8,128)(2,1)}, bf16[1,2560,768]{2,1,0:T(8,128)(2,1)}, bf16[16,48,512]{2,1,0:T(8,128)(2,1)}, f32[8,128]{1,0:T(8,128)}) custom-call(s32[2]{0:T(128)} %pad_add_fusion.refs_0_, bf16[768,2560]{1,0:T(8,128)(2,1)} %bitcast.33, bf16[2560,512]{1,0:T(8,128)(2,1)} %bitcast.38, bf16[2560,512]{1,0:T(8,128)(2,1)} %collective-permute-done.4.refs_3_, ...), custom_call_target="tpu_custom_call" | custom-call | tf_op jit(solution)/shard_map/run_chunk/pallas_call | solution.py:32
  348.4 5.6 %collective-permute-done.3.refs_3_ = bf16[2560,128]{1,0:T(8,128)(2,1)S(1)} collective-permute-done((bf16[2560,128]{1,0:T(8,128)(2,1)S(1)}, bf16[2560,128]{1,0:T(8,128)(2,1)S(1)}, u32[]{:S(2)}, u32[]{:S(2)}) %collective-permute-start.3) | collective-permute-done | bytes 655392 | tf_op jit(solution)/shard_map/ppermute | solution.py:387
  354.8 5.4 %run_chunk.4 = (bf16[1,2560,768]{2,1,0:T(8,128)(2,1)}, bf16[1,2560,768]{2,1,0:T(8,128)(2,1)}, bf16[16,48,128]{2,1,0:T(8,128)(2,1)}, f32[8,128]{1,0:T(8,128)}) custom-call(s32[2]{0:T(128)} %pad_add_fusion.refs_0_, bf16[768,2560]{1,0:T(8,128)(2,1)} %bitcast.34, bf16[2560,128]{1,0:T(8,128)(2,1)} %bitcast.43, ...), custom_call_target="tpu_custom_call", output_to_operand_aliasing={{0}: (4, {}), {1}: (5, {})} | custom-call | tf_op jit(solution)/shard_map/run_chunk/pallas_call | solution.py:32
  362.2 5.7 %all-to-all-start.6 = ((bf16[16,48,640]{2,1,0:T(8,128)(2,1)}), bf16[16,48,640]{2,1,0:T(8,128)(2,1)S(1)}, u32[]{:S(2)}, u32[]{:S(2)}) async-start(bf16[16,48,640]{2,1,0:T(8,128)(2,1)} %get-tuple-element.77), calls=%async_computation.6 | async-start | bytes 1966080 | tf_op jit(solution)/shard_map/all_to_all | solution.py:314
  369.5 15.5 %collective-permute-done.2.refs_3_ = bf16[2560,128]{1,0:T(8,128)(2,1)S(1)} collective-permute-done((bf16[2560,128]{1,0:T(8,128)(2,1)S(1)}, bf16[2560,128]{1,0:T(8,128)(2,1)S(1)}, u32[]{:S(2)}, u32[]{:S(2)}) %collective-permute-start.2) | collective-permute-done | bytes 655392 | tf_op jit(solution)/shard_map/ppermute | solution.py:387
  385.8 5.3 %run_chunk.5 = (bf16[1,2560,768]{2,1,0:T(8,128)(2,1)}, bf16[1,2560,768]{2,1,0:T(8,128)(2,1)}, bf16[16,48,128]{2,1,0:T(8,128)(2,1)}, f32[8,128]{1,0:T(8,128)}) custom-call(s32[2]{0:T(128)} %pad_add_fusion.refs_0_, bf16[768,2560]{1,0:T(8,128)(2,1)} %bitcast.35, bf16[2560,128]{1,0:T(8,128)(2,1)} %bitcast.41, ...), custom_call_target="tpu_custom_call", output_to_operand_aliasing={{0}: (4, {}), {1}: (5, {})} | custom-call | tf_op jit(solution)/shard_map/run_chunk/pallas_call | solution.py:32
  392.1 5.7 %all-to-all-start.7 = ((bf16[16,48,128]{2,1,0:T(8,128)(2,1)}), bf16[16,48,128]{2,1,0:T(8,128)(2,1)S(1)}, u32[]{:S(2)}, u32[]{:S(2)}) async-start(bf16[16,48,128]{2,1,0:T(8,128)(2,1)} %get-tuple-element.80), calls=%async_computation.7 | async-start | bytes 393216 | tf_op jit(solution)/shard_map/all_to_all | solution.py:314
  399.7 7.2 %all-to-all-done.7 = bf16[16,48,128]{2,1,0:T(8,128)(2,1)S(1)} async-done(((bf16[16,48,128]{2,1,0:T(8,128)(2,1)}), bf16[16,48,128]{2,1,0:T(8,128)(2,1)S(1)}, u32[]{:S(2)}, u32[]{:S(2)}) %all-to-all-start.7) | async-done | bytes 196640 | tf_op jit(solution)/shard_map/all_to_all | solution.py:314
  (94 shorter events, 50.0 us)
Async XLA Ops:
  14.1 7.6 %copy-start.10 = (bf16[64,2560]{1,0:T(8,128)(2,1)S(1)}, bf16[64,2560]{1,0:T(8,128)(2,1)}, u32[]{:S(2)}) copy-start(bf16[64,2560]{1,0:T(8,128)(2,1)} %refs_0_.1) | copy-start | bytes 983044
  14.1 110.5 %all-to-all-start = ((bf16[16,2,160,512]{3,2,1,0:T(8,128)(2,1)}), bf16[16,2,160,512]{3,2,1,0:T(8,128)(2,1)}, u32[]{:S(2)}, u32[]{:S(2)}) async-start(bf16[16,2,160,512]{3,2,1,0:T(8,128)(2,1)} %get-tuple-element.44), calls=%async_computation | async-start | bytes 10485760 | tf_op jit(solution)/shard_map/all_to_all | solution.py:314
  21.7 222.3 %all-gather.2.cloned.1.call-start = ((), (), s32[]{:S(2)}) async-start(), calls=%async_computation.8 | async-start | bytes 6553600 | tf_op jit(solution)/shard_map/all_gather | solution.py:369
  21.7 130.5 %collective-permute-start = (bf16[64,2560]{1,0:T(8,128)(2,1)S(1)}, bf16[64,2560]{1,0:T(8,128)(2,1)S(1)}, u32[]{:S(2)}, u32[]{:S(2)}) collective-permute-start(bf16[64,2560]{1,0:T(8,128)(2,1)S(1)} %copy-done.10), channel_id=1, source_target_pairs={{0,8},{1,9},{2,10},{3,11},{4,12},{5,13},{6,14},{7,15},{8,0},{9,1},... | collective-permute-start | bytes 983048 | tf_op jit(solution)/shard_map/ppermute | solution.py:354
  24.6 3.2 copy-start.14
  28.2 12.2 %copy-start.15 = (s32[32,1]{0,1:T(1,128)S(1)}, s32[32,1]{0,1:T(1,128)}, u32[]{:S(2)}) copy-start(s32[32,1]{0,1:T(1,128)} %param.14) | copy-start | bytes 388
  28.2 12.2 %copy-start.16 = (f32[32]{0:T(128)S(1)}, f32[32]{0:T(128)}, u32[]{:S(2)}) copy-start(f32[32]{0:T(128)} %param.15) | copy-start | bytes 388
  124.6 30.2 %copy-start.12 = (f32[32,20,6]{0,1,2:T(8,128)S(1)}, f32[32,20,6]{0,1,2:T(8,128)}, u32[]{:S(2)}) copy-start(f32[32,20,6]{0,1,2:T(8,128)} %param.13) | copy-start | bytes 46084
  124.6 30.2 %copy-start.13 = (f32[32,20,6]{0,1,2:T(8,128)S(1)}, f32[32,20,6]{0,1,2:T(8,128)}, u32[]{:S(2)}) copy-start(f32[32,20,6]{0,1,2:T(8,128)} %param.12) | copy-start | bytes 46084
  154.8 16.5 %collective-permute-start.1 = (bf16[2,64,2560]{2,1,0:T(8,128)(2,1)}, bf16[2,64,2560]{2,1,0:T(8,128)(2,1)S(1)}, u32[]{:S(2)}, u32[]{:S(2)}) collective-permute-start(bf16[2,64,2560]{2,1,0:T(8,128)(2,1)} %get-tuple-element.47.refs_1_), channel_id=1, source_target_pairs={{0,4},{1,5},{2,6},{3,7},{4,0},{5,1},{6,2},{7,3},{8,12},{9,13},{10,... | collective-permute-start | bytes 1966088 | tf_op jit(solution)/shard_map/ppermute | solution.py:366
  167.4 7.4 %copy-start.2 = (bf16[16,2,160,128]{3,2,1,0:T(8,128)(2,1)S(1)}, bf16[16,2,160,128]{3,2,1,0:T(8,128)(2,1)}, u32[]{:S(2)}) copy-start(bf16[16,2,160,128]{3,2,1,0:T(8,128)(2,1)} %get-tuple-element.54) | copy-start | bytes 3932164
  209.8 54.3 %all-to-all-start.2 = ((bf16[16,160,512]{2,1,0:T(8,128)(2,1)}), bf16[16,160,512]{2,1,0:T(8,128)(2,1)S(1)}, u32[]{:S(2)}, u32[]{:S(2)}) async-start(bf16[16,160,512]{2,1,0:T(8,128)(2,1)} %get-tuple-element.56), calls=%async_computation.2 | async-start | bytes 5242880 | tf_op jit(solution)/shard_map/all_to_all | solution.py:314
  264.1 1.5 copy-start
  265.6 40.8 %all-to-all-start.3 = ((bf16[16,2,160,128]{3,2,1,0:T(8,128)(2,1)}), bf16[16,2,160,128]{3,2,1,0:T(8,128)(2,1)S(1)}, u32[]{:S(2)}, u32[]{:S(2)}) async-start(bf16[16,2,160,128]{3,2,1,0:T(8,128)(2,1)} %get-tuple-element.59), calls=%async_computation.3 | async-start | bytes 2621440 | tf_op jit(solution)/shard_map/all_to_all | solution.py:314
  279.0 59.5 %collective-permute-start.4 = (bf16[2560,512]{1,0:T(8,128)(2,1)}, bf16[2560,512]{1,0:T(8,128)(2,1)}, u32[]{:S(2)}, u32[]{:S(2)}) collective-permute-start(bf16[2560,512]{1,0:T(8,128)(2,1)} %bitcast.37), channel_id=1, source_target_pairs={{0,16},{16,0},{1,17},{17,1},{2,18},{18,2},{3,19},{19,3},{4,20},{20... | collective-permute-start | bytes 7864328 | tf_op jit(solution)/shard_map/ppermute | solution.py:387
  307.4 24.6 %all-to-all-start.5 = ((bf16[16,160,128]{2,1,0:T(8,128)(2,1)}), bf16[16,160,128]{2,1,0:T(8,128)(2,1)S(1)}, u32[]{:S(2)}, u32[]{:S(2)}) async-start(bf16[16,160,128]{2,1,0:T(8,128)(2,1)} %get-tuple-element.64), calls=%async_computation.5 | async-start | bytes 1310720 | tf_op jit(solution)/shard_map/all_to_all | solution.py:314
  332.1 16.3 %copy-start.5 = (bf16[16,160,128]{2,1,0:T(8,128)(2,1)}, bf16[16,160,128]{2,1,0:T(8,128)(2,1)S(1)}, u32[]{:S(2)}) copy-start(bf16[16,160,128]{2,1,0:T(8,128)(2,1)S(1)} %all-to-all-done.5) | copy-start | bytes 1966084
  332.1 30.1 %all-to-all-start.4 = ((bf16[16,160,128]{2,1,0:T(8,128)(2,1)}), bf16[16,160,128]{2,1,0:T(8,128)(2,1)S(1)}, u32[]{:S(2)}, u32[]{:S(2)}) async-start(bf16[16,160,128]{2,1,0:T(8,128)(2,1)} %get-tuple-element.63), calls=%async_computation.4 | async-start | bytes 1310720 | tf_op jit(solution)/shard_map/all_to_all | solution.py:314
  336.8 17.1 %collective-permute-start.3 = (bf16[2560,128]{1,0:T(8,128)(2,1)S(1)}, bf16[2560,128]{1,0:T(8,128)(2,1)S(1)}, u32[]{:S(2)}, u32[]{:S(2)}) collective-permute-start(bf16[2560,128]{1,0:T(8,128)(2,1)S(1)} %bitcast.42), channel_id=1, source_target_pairs={{0,16},{16,0},{1,17},{17,1},{2,18},{18,2},{3,19},{19,3},{4,20},{20... | collective-permute-start | bytes 1966088 | tf_op jit(solution)/shard_map/ppermute | solution.py:387
  354.8 5.4 %copy-start.6 = (bf16[16,48,512]{2,1,0:T(8,128)(2,1)S(1)}, bf16[16,48,512]{2,1,0:T(8,128)(2,1)}, u32[]{:S(2)}) copy-start(bf16[16,48,512]{2,1,0:T(8,128)(2,1)} %get-tuple-element.71) | copy-start | bytes 2359300
  362.2 22.8 %copy-start.4 = (bf16[16,160,128]{2,1,0:T(8,128)(2,1)}, bf16[16,160,128]{2,1,0:T(8,128)(2,1)S(1)}, u32[]{:S(2)}) copy-start(bf16[16,160,128]{2,1,0:T(8,128)(2,1)S(1)} %all-to-all-done.4) | copy-start | bytes 1966084
  362.2 28.9 %all-to-all-start.6 = ((bf16[16,48,640]{2,1,0:T(8,128)(2,1)}), bf16[16,48,640]{2,1,0:T(8,128)(2,1)S(1)}, u32[]{:S(2)}, u32[]{:S(2)}) async-start(bf16[16,48,640]{2,1,0:T(8,128)(2,1)} %get-tuple-element.77), calls=%async_computation.6 | async-start | bytes 1966080 | tf_op jit(solution)/shard_map/all_to_all | solution.py:314
  367.9 17.0 %collective-permute-start.2 = (bf16[2560,128]{1,0:T(8,128)(2,1)S(1)}, bf16[2560,128]{1,0:T(8,128)(2,1)S(1)}, u32[]{:S(2)}, u32[]{:S(2)}) collective-permute-start(bf16[2560,128]{1,0:T(8,128)(2,1)S(1)} %bitcast.40), channel_id=1, source_target_pairs={{0,16},{16,0},{1,17},{17,1},{2,18},{18,2},{3,19},{19,3},{4,20},{20... | collective-permute-start | bytes 1966088 | tf_op jit(solution)/shard_map/ppermute | solution.py:387
  392.1 14.7 %all-to-all-start.7 = ((bf16[16,48,128]{2,1,0:T(8,128)(2,1)}), bf16[16,48,128]{2,1,0:T(8,128)(2,1)S(1)}, u32[]{:S(2)}, u32[]{:S(2)}) async-start(bf16[16,48,128]{2,1,0:T(8,128)(2,1)} %get-tuple-element.80), calls=%async_computation.7 | async-start | bytes 393216 | tf_op jit(solution)/shard_map/all_to_all | solution.py:314
  (6 other events, 5.3 us)
Sparse Core Ops, SparseCore 0:
  174.9 69.0 all-gather.1

commit v16 on v14

--- a/solution.py
+++ b/solution.py
@@ -383,7 +383,7 @@
         elif name == "sum":
             merged[c], token = merge(token, slots, factors, gathered[c], start, blocks_of_rows)
         elif name == "back":
-            if 0 < c < last:
+            if c < last:
                 merged[c], token = hold(token, merged[c], [gathered[c + 1]])
             own[c] = exchange(merged[c]).reshape(depth, width)
             partner[c] = lax.ppermute(own[c], "groups", partners)

time: 418 us -> 402 us (0.962)
  waiting for transfers between devices: 227 us -> 213 us
    ppermute x1, waiting for transfers between devices: 68.4 us -> 27.6 us  [shards(): opposite = lax.ppermute(tokens, 'expert', across)]
    ppermute x1, waiting for transfers between devices: 8 us -> 48.8 us  [shards(): nearby = lax.ppermute(both, 'expert', beside)]
    all_to_all x8, waiting for transfers between devices: 135 us -> 120 us  [exchange(): return lax.all_to_all(pieces, 'expert', 0, 0, tiled=True)]
    pallas_call x16 -> x17, Pallas kernels: 65 us -> 65 us  [step_call(): pl.pallas_call(ordered, out_shape=[*out_shape, TOKEN], in_specs=[*in_spec...]
  transfers between devices with their start and end apart: 14 -> 14, of which waited for: 8 -> 7; matrix products, arithmetic and copies ran while one was open for 6% -> 6% of each run, Pallas kernels for 14% -> 15%
where the time goes in v16:
time: 402 us; the launch traced here: 400 us
  waiting for transfers between devices  213 us (53%)
  starting transfers between devices  74 us (18%)
  Pallas kernels  65 us (16%)
  between operations  14.4 us (4%)
  other arithmetic  13.9 us (3%)
  local copies, waits for them, and re-layouts  12.6 us (3%)
  matrix products  7.75 us (2%)
    all_to_all x8, waiting for transfers between devices, exchange(): return lax.all_to_all(pieces, 'expert', 0, 0, tiled=True)  120 us
    pallas_call x17, Pallas kernels, step_call(): pl.pallas_call(ordered, out_shape=[*out_shape, TOKEN], in_specs=[*in_spec...  65 us
    all_to_all x8, starting transfers between devices, exchange(): return lax.all_to_all(pieces, 'expert', 0, 0, tiled=True)  64.7 us
    ppermute x1, waiting for transfers between devices, shards(): nearby = lax.ppermute(both, 'expert', beside)  48.8 us
    ppermute x1, waiting for transfers between devices, shards(): opposite = lax.ppermute(tokens, 'expert', across)  27.6 us
    ppermute x3, waiting for transfers between devices, shards(): partner[c] = lax.ppermute(own[c], 'groups', partners)  15.8 us
  transfers between devices with their start and end apart: 14, of which 7 were waited for; matrix products, arithmetic and copies ran while one was open for 6% of the time, Pallas kernels for 15%

profile of v16, /device:TPU:0, one launch (start us, length us, event | category | flops | bytes accessed | tf_op | source)
XLA Modules:
  0.0 400.2 jit_solution(15038999846065051544)
XLA Ops:
  8.4 5.6 %pack.3 = (bf16[16,2,160,512]{3,2,1,0:T(8,128)(2,1)}, f32[8,128]{1,0:T(8,128)}) custom-call(s32[2]{0:T(128)} %pad_add_fusion.refs_0_, bf16[2,2560,768]{2,1,0:T(8,128)(2,1)} %refs_1_.5, bf16[2,2560,768]{2,1,0:T(8,128)(2,1)} %refs_2_.5, f32[8,128]{1,0:T(8,128)} %broadcast_in_dim.40.refs_3_), custom_call_target="tpu_custom_call" | custom-call | tf_op jit(solution)/shard_map/pack/pallas_call | solution.py:32
  14.1 7.4 %all-to-all-start = ((bf16[16,2,160,512]{3,2,1,0:T(8,128)(2,1)}), bf16[16,2,160,512]{3,2,1,0:T(8,128)(2,1)}, u32[]{:S(2)}, u32[]{:S(2)}) async-start(bf16[16,2,160,512]{3,2,1,0:T(8,128)(2,1)} %get-tuple-element.42), calls=%async_computation | async-start | bytes 10485760 | tf_op jit(solution)/shard_map/all_to_all | solution.py:316
  25.1 6.3 %fusion.6 = s32[16,64,16]{2,0,1:T(8,128)S(1)} fusion(s32[16,64,16]{2,0,1:T(8,128)S(1)} %copy.61), kind=kOutput, calls=%fused_computation.38 | output fusion | flops 1032192 | bytes 131072 | tf_op jit(solution)/shard_map/jit(cumsum)/reduce_window_sum | solution.py:291
  38.1 79.4 %all-to-all-done.refs_1_.refs_2_ = bf16[16,2,160,512]{3,2,1,0:T(8,128)(2,1)} async-done(((bf16[16,2,160,512]{3,2,1,0:T(8,128)(2,1)}), bf16[16,2,160,512]{3,2,1,0:T(8,128)(2,1)}, u32[]{:S(2)}, u32[]{:S(2)}) %all-to-all-start) | async-done | bytes 5242912 | tf_op jit(solution)/shard_map/all_to_all | solution.py:316
  117.5 24.0 %all-to-all-start.1 = ((bf16[16,2,160,128]{3,2,1,0:T(8,128)(2,1)}), bf16[16,2,160,128]{3,2,1,0:T(8,128)(2,1)S(1)}, u32[]{:S(2)}, u32[]{:S(2)}) async-start(bf16[16,2,160,128]{3,2,1,0:T(8,128)(2,1)} %get-tuple-element.50), calls=%async_computation.1 | async-start | bytes 2621440 | tf_op jit(solution)/shard_map/all_to_all | solution.py:316
  146.2 10.9 %merge.3 = (bf16[16,160,512]{2,1,0:T(8,128)(2,1)}, f32[8,128]{1,0:T(8,128)}) custom-call(s32[32]{0:T(128)} %bitcast.50, f32[960]{0:T(1024)} %mul.47.refs_1_, bf16[16,2,160,512]{3,2,1,0:T(8,128)(2,1)} %all-to-all-done.refs_1_.refs_2_, f32[8,128]{1,0:T(8,128)} %get-tuple-element.46.refs_3_), custom_call_target="tpu_custom_call" | custom-call | tf_op jit(solution)/shard_map/merge/pallas_call | solution.py:32
  160.2 27.6 %collective-permute-done.refs_1_ = bf16[64,2560]{1,0:T(8,128)(2,1)S(1)} collective-permute-done((bf16[64,2560]{1,0:T(8,128)(2,1)S(1)}, bf16[64,2560]{1,0:T(8,128)(2,1)S(1)}, u32[]{:S(2)}, u32[]{:S(2)}) %collective-permute-start) | collective-permute-done | bytes 327712 | tf_op jit(solution)/shard_map/ppermute | solution.py:356
  191.5 3.7 all-to-all-start.2
  197.2 8.6 %merge.4 = (bf16[16,160,128]{2,1,0:T(8,128)(2,1)}, f32[8,128]{1,0:T(8,128)}) custom-call(s32[32]{0:T(128)} %bitcast.51, f32[960]{0:T(1024)} %mul.47.refs_1_, bf16[16,2,160,128]{3,2,1,0:T(8,128)(2,1)} %copy-done.1, f32[8,128]{1,0:T(8,128)} %get-tuple-element.53.refs_3_), custom_call_target="tpu_custom_call" | custom-call | tf_op jit(solution)/shard_map/merge/pallas_call | solution.py:32
  205.8 48.8 %collective-permute-done.1.refs_2_ = bf16[2,64,2560]{2,1,0:T(8,128)(2,1)} collective-permute-done((bf16[2,64,2560]{2,1,0:T(8,128)(2,1)}, bf16[2,64,2560]{2,1,0:T(8,128)(2,1)}, u32[]{:S(2)}, u32[]{:S(2)}) %collective-permute-start.1) | collective-permute-done | bytes 655392 | tf_op jit(solution)/shard_map/ppermute | solution.py:368
  258.6 5.0 %all-to-all-start.3 = ((bf16[16,2,160,128]{3,2,1,0:T(8,128)(2,1)}), bf16[16,2,160,128]{3,2,1,0:T(8,128)(2,1)S(1)}, u32[]{:S(2)}, u32[]{:S(2)}) async-start(bf16[16,2,160,128]{3,2,1,0:T(8,128)(2,1)} %get-tuple-element.59), calls=%async_computation.3 | async-start | bytes 2621440 | tf_op jit(solution)/shard_map/all_to_all | solution.py:316
  265.1 25.9 %all-to-all-done.3.refs_1_.refs_2_ = bf16[16,2,160,128]{3,2,1,0:T(8,128)(2,1)S(1)} async-done(((bf16[16,2,160,128]{3,2,1,0:T(8,128)(2,1)}), bf16[16,2,160,128]{3,2,1,0:T(8,128)(2,1)S(1)}, u32[]{:S(2)}, u32[]{:S(2)}) %all-to-all-start.3) | async-done | bytes 1310752 | tf_op jit(solution)/shard_map/all_to_all | solution.py:316
  292.1 8.0 %all-to-all-start.5 = ((bf16[16,160,128]{2,1,0:T(8,128)(2,1)}), bf16[16,160,128]{2,1,0:T(8,128)(2,1)S(1)}, u32[]{:S(2)}, u32[]{:S(2)}) async-start(bf16[16,160,128]{2,1,0:T(8,128)(2,1)} %get-tuple-element.64), calls=%async_computation.5 | async-start | bytes 1310720 | tf_op jit(solution)/shard_map/all_to_all | solution.py:316
  300.1 8.7 %merge.5 = (bf16[16,160,128]{2,1,0:T(8,128)(2,1)}, f32[8,128]{1,0:T(8,128)}) custom-call(s32[32]{0:T(128)} %bitcast.52, f32[960]{0:T(1024)} %mul.47.refs_1_, bf16[16,2,160,128]{3,2,1,0:T(8,128)(2,1)} %copy-done.2, f32[8,128]{1,0:T(8,128)} %get-tuple-element.62.refs_3_), custom_call_target="tpu_custom_call" | custom-call | tf_op jit(solution)/shard_map/merge/pallas_call | solution.py:32
  308.8 7.9 %all-to-all-done.5 = bf16[16,160,128]{2,1,0:T(8,128)(2,1)S(1)} async-done(((bf16[16,160,128]{2,1,0:T(8,128)(2,1)}), bf16[16,160,128]{2,1,0:T(8,128)(2,1)S(1)}, u32[]{:S(2)}, u32[]{:S(2)}) %all-to-all-start.5) | async-done | bytes 655392 | tf_op jit(solution)/shard_map/all_to_all | solution.py:316
  316.7 4.8 %all-to-all-start.4 = ((bf16[16,160,128]{2,1,0:T(8,128)(2,1)}), bf16[16,160,128]{2,1,0:T(8,128)(2,1)S(1)}, u32[]{:S(2)}, u32[]{:S(2)}) async-start(bf16[16,160,128]{2,1,0:T(8,128)(2,1)} %get-tuple-element.63), calls=%async_computation.4 | async-start | bytes 1310720 | tf_op jit(solution)/shard_map/all_to_all | solution.py:316
  323.1 5.6 %convolution_convert_fusion = bf16[16,48,2560]{2,1,0:T(8,128)(2,1)} fusion(bf16[16,64,2560]{2,1,0:T(8,128)(2,1)} %all-gather.2.cloned.1.call-done, s32[16,64]{1,0:T(8,128)S(1)} %bitcast.46, pred[16,64]{1,0:T(8,128)(4,1)S(1)} %bitcast.49), kind=kOutput, calls=%fused_computation.1 | convolution fusion | flops 253722624 | bytes 9180160 | tf_op jit(solution)/shard_map/jct,jtd->jcd/dot_general | solution.py:372
  328.7 9.9 %run_chunk.3 = (bf16[1,2560,768]{2,1,0:T(8,128)(2,1)}, bf16[1,2560,768]{2,1,0:T(8,128)(2,1)}, bf16[16,48,512]{2,1,0:T(8,128)(2,1)}, f32[8,128]{1,0:T(8,128)}) custom-call(s32[2]{0:T(128)} %pad_add_fusion.refs_0_, bf16[768,2560]{1,0:T(8,128)(2,1)} %bitcast.32, bf16[2560,512]{1,0:T(8,128)(2,1)} %bitcast.37, bf16[2560,512]{1,0:T(8,128)(2,1)} %collective-permute-done.4.refs_3_, ...), custom_call_target="tpu_custom_call" | custom-call | tf_op jit(solution)/shard_map/run_chunk/pallas_call | solution.py:32
  339.5 5.4 %run_chunk.4 = (bf16[1,2560,768]{2,1,0:T(8,128)(2,1)}, bf16[1,2560,768]{2,1,0:T(8,128)(2,1)}, bf16[16,48,128]{2,1,0:T(8,128)(2,1)}, f32[8,128]{1,0:T(8,128)}) custom-call(s32[2]{0:T(128)} %pad_add_fusion.refs_0_, bf16[768,2560]{1,0:T(8,128)(2,1)} %bitcast.33, bf16[2560,128]{1,0:T(8,128)(2,1)} %bitcast.42, ...), custom_call_target="tpu_custom_call", output_to_operand_aliasing={{0}: (4, {}), {1}: (5, {})} | custom-call | tf_op jit(solution)/shard_map/run_chunk/pallas_call | solution.py:32
  346.9 6.0 %all-to-all-start.6 = ((bf16[16,48,640]{2,1,0:T(8,128)(2,1)}), bf16[16,48,640]{2,1,0:T(8,128)(2,1)S(1)}, u32[]{:S(2)}, u32[]{:S(2)}) async-start(bf16[16,48,640]{2,1,0:T(8,128)(2,1)} %get-tuple-element.77), calls=%async_computation.6 | async-start | bytes 1966080 | tf_op jit(solution)/shard_map/all_to_all | solution.py:316
  354.2 15.7 %collective-permute-done.2.refs_3_ = bf16[2560,128]{1,0:T(8,128)(2,1)S(1)} collective-permute-done((bf16[2560,128]{1,0:T(8,128)(2,1)S(1)}, bf16[2560,128]{1,0:T(8,128)(2,1)S(1)}, u32[]{:S(2)}, u32[]{:S(2)}) %collective-permute-start.2) | collective-permute-done | bytes 655392 | tf_op jit(solution)/shard_map/ppermute | solution.py:389
  370.8 5.3 %run_chunk.5 = (bf16[1,2560,768]{2,1,0:T(8,128)(2,1)}, bf16[1,2560,768]{2,1,0:T(8,128)(2,1)}, bf16[16,48,128]{2,1,0:T(8,128)(2,1)}, f32[8,128]{1,0:T(8,128)}) custom-call(s32[2]{0:T(128)} %pad_add_fusion.refs_0_, bf16[768,2560]{1,0:T(8,128)(2,1)} %bitcast.34, bf16[2560,128]{1,0:T(8,128)(2,1)} %bitcast.40, ...), custom_call_target="tpu_custom_call", output_to_operand_aliasing={{0}: (4, {}), {1}: (5, {})} | custom-call | tf_op jit(solution)/shard_map/run_chunk/pallas_call | solution.py:32
  377.1 5.8 %all-to-all-start.7 = ((bf16[16,48,128]{2,1,0:T(8,128)(2,1)}), bf16[16,48,128]{2,1,0:T(8,128)(2,1)S(1)}, u32[]{:S(2)}, u32[]{:S(2)}) async-start(bf16[16,48,128]{2,1,0:T(8,128)(2,1)} %get-tuple-element.80), calls=%async_computation.7 | async-start | bytes 393216 | tf_op jit(solution)/shard_map/all_to_all | solution.py:316
  384.7 7.2 %all-to-all-done.7 = bf16[16,48,128]{2,1,0:T(8,128)(2,1)S(1)} async-done(((bf16[16,48,128]{2,1,0:T(8,128)(2,1)}), bf16[16,48,128]{2,1,0:T(8,128)(2,1)S(1)}, u32[]{:S(2)}, u32[]{:S(2)}) %all-to-all-start.7) | async-done | bytes 196640 | tf_op jit(solution)/shard_map/all_to_all | solution.py:316
  (93 shorter events, 42.3 us)
Async XLA Ops:
  14.1 103.4 %all-to-all-start = ((bf16[16,2,160,512]{3,2,1,0:T(8,128)(2,1)}), bf16[16,2,160,512]{3,2,1,0:T(8,128)(2,1)}, u32[]{:S(2)}, u32[]{:S(2)}) async-start(bf16[16,2,160,512]{3,2,1,0:T(8,128)(2,1)} %get-tuple-element.42), calls=%async_computation | async-start | bytes 10485760 | tf_op jit(solution)/shard_map/all_to_all | solution.py:316
  21.5 3.2 copy-start.13
  117.5 24.0 %copy-start.9 = (bf16[64,2560]{1,0:T(8,128)(2,1)S(1)}, bf16[64,2560]{1,0:T(8,128)(2,1)}, u32[]{:S(2)}) copy-start(bf16[64,2560]{1,0:T(8,128)(2,1)} %refs_0_.1) | copy-start | bytes 983044
  117.5 26.9 %copy-start.14 = (s32[32,1]{0,1:T(1,128)S(1)}, s32[32,1]{0,1:T(1,128)}, u32[]{:S(2)}) copy-start(s32[32,1]{0,1:T(1,128)} %param.14) | copy-start | bytes 388
  117.5 26.9 %copy-start.15 = (f32[32]{0:T(128)S(1)}, f32[32]{0:T(128)}, u32[]{:S(2)}) copy-start(f32[32]{0:T(128)} %param.15) | copy-start | bytes 388
  117.5 27.2 %copy-start.11 = (f32[32,20,6]{0,1,2:T(8,128)S(1)}, f32[32,20,6]{0,1,2:T(8,128)}, u32[]{:S(2)}) copy-start(f32[32,20,6]{0,1,2:T(8,128)} %param.13) | copy-start | bytes 46084
  117.5 27.2 %copy-start.12 = (f32[32,20,6]{0,1,2:T(8,128)S(1)}, f32[32,20,6]{0,1,2:T(8,128)}, u32[]{:S(2)}) copy-start(f32[32,20,6]{0,1,2:T(8,128)} %param.12) | copy-start | bytes 46084
  117.5 72.9 %all-to-all-start.1 = ((bf16[16,2,160,128]{3,2,1,0:T(8,128)(2,1)}), bf16[16,2,160,128]{3,2,1,0:T(8,128)(2,1)S(1)}, u32[]{:S(2)}, u32[]{:S(2)}) async-start(bf16[16,2,160,128]{3,2,1,0:T(8,128)(2,1)} %get-tuple-element.50), calls=%async_computation.1 | async-start | bytes 2621440 | tf_op jit(solution)/shard_map/all_to_all | solution.py:316
  141.5 46.2 %collective-permute-start = (bf16[64,2560]{1,0:T(8,128)(2,1)S(1)}, bf16[64,2560]{1,0:T(8,128)(2,1)S(1)}, u32[]{:S(2)}, u32[]{:S(2)}) collective-permute-start(bf16[64,2560]{1,0:T(8,128)(2,1)S(1)} %copy-done.9), channel_id=1, source_target_pairs={{0,8},{1,9},{2,10},{3,11},{4,12},{5,13},{6,14},{7,15},{8,0},{9,1},... | collective-permute-start | bytes 983048 | tf_op jit(solution)/shard_map/ppermute | solution.py:356
  191.5 65.6 %all-to-all-start.2 = ((bf16[16,160,512]{2,1,0:T(8,128)(2,1)}), bf16[16,160,512]{2,1,0:T(8,128)(2,1)S(1)}, u32[]{:S(2)}, u32[]{:S(2)}) async-start(bf16[16,160,512]{2,1,0:T(8,128)(2,1)} %get-tuple-element.57), calls=%async_computation.2 | async-start | bytes 5242880 | tf_op jit(solution)/shard_map/all_to_all | solution.py:316
  195.2 127.9 %all-gather.2.cloned.1.call-start = ((), (), s32[]{:S(2)}) async-start(), calls=%async_computation.8 | async-start | bytes 6553600 | tf_op jit(solution)/shard_map/all_gather | solution.py:371
  195.3 59.3 %collective-permute-start.1 = (bf16[2,64,2560]{2,1,0:T(8,128)(2,1)}, bf16[2,64,2560]{2,1,0:T(8,128)(2,1)}, u32[]{:S(2)}, u32[]{:S(2)}) collective-permute-start(bf16[2,64,2560]{2,1,0:T(8,128)(2,1)} %get-tuple-element.49.refs_1_), channel_id=1, source_target_pairs={{0,4},{1,5},{2,6},{3,7},{4,0},{5,1},{6,2},{7,3},{8,12},{9,13},{10,... | collective-permute-start | bytes 1966088 | tf_op jit(solution)/shard_map/ppermute | solution.py:368
  257.1 1.5 copy-start
  258.6 32.5 %all-to-all-start.3 = ((bf16[16,2,160,128]{3,2,1,0:T(8,128)(2,1)}), bf16[16,2,160,128]{3,2,1,0:T(8,128)(2,1)S(1)}, u32[]{:S(2)}, u32[]{:S(2)}) async-start(bf16[16,2,160,128]{3,2,1,0:T(8,128)(2,1)} %get-tuple-element.59), calls=%async_computation.3 | async-start | bytes 2621440 | tf_op jit(solution)/shard_map/all_to_all | solution.py:316
  263.5 65.2 %collective-permute-start.4 = (bf16[2560,512]{1,0:T(8,128)(2,1)}, bf16[2560,512]{1,0:T(8,128)(2,1)}, u32[]{:S(2)}, u32[]{:S(2)}) collective-permute-start(bf16[2560,512]{1,0:T(8,128)(2,1)} %bitcast.36), channel_id=1, source_target_pairs={{0,16},{16,0},{1,17},{17,1},{2,18},{18,2},{3,19},{19,3},{4,20},{20... | collective-permute-start | bytes 7864328 | tf_op jit(solution)/shard_map/ppermute | solution.py:389
  292.1 24.7 %all-to-all-start.5 = ((bf16[16,160,128]{2,1,0:T(8,128)(2,1)}), bf16[16,160,128]{2,1,0:T(8,128)(2,1)S(1)}, u32[]{:S(2)}, u32[]{:S(2)}) async-start(bf16[16,160,128]{2,1,0:T(8,128)(2,1)} %get-tuple-element.64), calls=%async_computation.5 | async-start | bytes 1310720 | tf_op jit(solution)/shard_map/all_to_all | solution.py:316
  316.7 12.0 %copy-start.5 = (bf16[16,160,128]{2,1,0:T(8,128)(2,1)}, bf16[16,160,128]{2,1,0:T(8,128)(2,1)S(1)}, u32[]{:S(2)}) copy-start(bf16[16,160,128]{2,1,0:T(8,128)(2,1)S(1)} %all-to-all-done.5) | copy-start | bytes 1966084
  316.7 30.2 %all-to-all-start.4 = ((bf16[16,160,128]{2,1,0:T(8,128)(2,1)}), bf16[16,160,128]{2,1,0:T(8,128)(2,1)S(1)}, u32[]{:S(2)}, u32[]{:S(2)}) async-start(bf16[16,160,128]{2,1,0:T(8,128)(2,1)} %get-tuple-element.63), calls=%async_computation.4 | async-start | bytes 1310720 | tf_op jit(solution)/shard_map/all_to_all | solution.py:316
  321.5 17.1 %collective-permute-start.3 = (bf16[2560,128]{1,0:T(8,128)(2,1)S(1)}, bf16[2560,128]{1,0:T(8,128)(2,1)S(1)}, u32[]{:S(2)}, u32[]{:S(2)}) collective-permute-start(bf16[2560,128]{1,0:T(8,128)(2,1)S(1)} %bitcast.41), channel_id=1, source_target_pairs={{0,16},{16,0},{1,17},{17,1},{2,18},{18,2},{3,19},{19,3},{4,20},{20... | collective-permute-start | bytes 1966088 | tf_op jit(solution)/shard_map/ppermute | solution.py:389
  339.5 5.4 %copy-start.6 = (bf16[16,48,512]{2,1,0:T(8,128)(2,1)S(1)}, bf16[16,48,512]{2,1,0:T(8,128)(2,1)}, u32[]{:S(2)}) copy-start(bf16[16,48,512]{2,1,0:T(8,128)(2,1)} %get-tuple-element.71) | copy-start | bytes 2359300
  346.9 23.0 %copy-start.4 = (bf16[16,160,128]{2,1,0:T(8,128)(2,1)}, bf16[16,160,128]{2,1,0:T(8,128)(2,1)S(1)}, u32[]{:S(2)}) copy-start(bf16[16,160,128]{2,1,0:T(8,128)(2,1)S(1)} %all-to-all-done.4) | copy-start | bytes 1966084
  346.9 29.2 %all-to-all-start.6 = ((bf16[16,48,640]{2,1,0:T(8,128)(2,1)}), bf16[16,48,640]{2,1,0:T(8,128)(2,1)S(1)}, u32[]{:S(2)}, u32[]{:S(2)}) async-start(bf16[16,48,640]{2,1,0:T(8,128)(2,1)} %get-tuple-element.77), calls=%async_computation.6 | async-start | bytes 1966080 | tf_op jit(solution)/shard_map/all_to_all | solution.py:316
  352.9 17.0 %collective-permute-start.2 = (bf16[2560,128]{1,0:T(8,128)(2,1)S(1)}, bf16[2560,128]{1,0:T(8,128)(2,1)S(1)}, u32[]{:S(2)}, u32[]{:S(2)}) collective-permute-start(bf16[2560,128]{1,0:T(8,128)(2,1)S(1)} %bitcast.39), channel_id=1, source_target_pairs={{0,16},{16,0},{1,17},{17,1},{2,18},{18,2},{3,19},{19,3},{4,20},{20... | collective-permute-start | bytes 1966088 | tf_op jit(solution)/shard_map/ppermute | solution.py:389
  377.1 14.8 %all-to-all-start.7 = ((bf16[16,48,128]{2,1,0:T(8,128)(2,1)}), bf16[16,48,128]{2,1,0:T(8,128)(2,1)S(1)}, u32[]{:S(2)}, u32[]{:S(2)}) async-start(bf16[16,48,128]{2,1,0:T(8,128)(2,1)} %get-tuple-element.80), calls=%async_computation.7 | async-start | bytes 393216 | tf_op jit(solution)/shard_map/all_to_all | solution.py:316
  (6 other events, 5.5 us)
Sparse Core Ops, SparseCore 0:
  257.2 58.4 all-gather.1

commit v17 on v16

--- a/solution.py
+++ b/solution.py
@@ -375,9 +375,11 @@
             arrived = lax.all_gather(arrived, "mp", axis=2, tiled=True)
             grouped = arrived.reshape(expert_count * capacity, depth)
         elif name == "raw":
-            if c == 1:
+            if c == 0:
+                pieces[c], token = hold(token, pieces[c], [opposite])
+            elif c == 1:
                 pieces[c], token = hold(token, pieces[c], [gathered[0], placing, picking])
-            elif c >= 2:
+            else:
                 pieces[c], token = hold(token, pieces[c], [own[c - 2]])
             gathered[c] = exchange(pieces[c])
         elif name == "sum":

time: 402 us -> 397 us (0.988)
  waiting for transfers between devices: 213 us -> 203 us
  starting transfers between devices: 74 us -> 78.1 us
    ppermute x1, waiting for transfers between devices: 27.6 us -> 8.05 us  [shards(): opposite = lax.ppermute(tokens, 'expert', across)]
    all_to_all x8, waiting for transfers between devices: 120 us -> 130 us  [exchange(): return lax.all_to_all(pieces, 'expert', 0, 0, tiled=True)]
    pallas_call x17 -> x18, Pallas kernels: 65 us -> 64.9 us  [step_call(): pl.pallas_call(ordered, out_shape=[*out_shape, TOKEN], in_specs=[*in_spec...]
  transfers between devices with their start and end apart: 14 -> 14, of which waited for: 7 -> 9; matrix products, arithmetic and copies ran while one was open for 6% -> 7% of each run, Pallas kernels for 15% -> 16%
where the time goes in v17:
time: 397 us; the launch traced here: 394 us
  waiting for transfers between devices  203 us (51%)
  starting transfers between devices  78.1 us (20%)
  Pallas kernels  64.9 us (16%)
  between operations  14.4 us (4%)
  other arithmetic  13.9 us (4%)
  local copies, waits for them, and re-layouts  12.6 us (3%)
  matrix products  7.74 us (2%)
    all_to_all x8, waiting for transfers between devices, exchange(): return lax.all_to_all(pieces, 'expert', 0, 0, tiled=True)  130 us
    all_to_all x8, starting transfers between devices, exchange(): return lax.all_to_all(pieces, 'expert', 0, 0, tiled=True)  67.5 us
    pallas_call x18, Pallas kernels, step_call(): pl.pallas_call(ordered, out_shape=[*out_shape, TOKEN], in_specs=[*in_spec...  64.9 us
    ppermute x1, waiting for transfers between devices, shards(): nearby = lax.ppermute(both, 'expert', beside)  48.8 us
    ppermute x3, waiting for transfers between devices, shards(): partner[c] = lax.ppermute(own[c], 'groups', partners)  15.8 us
    ppermute x1, waiting for transfers between devices, shards(): opposite = lax.ppermute(tokens, 'expert', across)  8.05 us
  transfers between devices with their start and end apart: 14, of which 9 were waited for; matrix products, arithmetic and copies ran while one was open for 7% of the time, Pallas kernels for 16%

profile of v17, /device:TPU:0, one launch (start us, length us, event | category | flops | bytes accessed | tf_op | source)
XLA Modules:
  0.0 394.4 jit_solution(8296895925337576105)
XLA Ops:
  12.5 5.6 %pack.3 = (bf16[16,2,160,512]{3,2,1,0:T(8,128)(2,1)}, f32[8,128]{1,0:T(8,128)}) custom-call(s32[2]{0:T(128)} %pad_add_fusion.refs_0_, bf16[2,2560,768]{2,1,0:T(8,128)(2,1)} %refs_1_.5, bf16[2,2560,768]{2,1,0:T(8,128)(2,1)} %refs_2_.5, f32[8,128]{1,0:T(8,128)} %broadcast_in_dim.40.refs_3_), custom_call_target="tpu_custom_call" | custom-call | tf_op jit(solution)/shard_map/pack/pallas_call | solution.py:32
  18.2 8.0 %collective-permute-done.refs_1_ = bf16[64,2560]{1,0:T(8,128)(2,1)S(1)} collective-permute-done((bf16[64,2560]{1,0:T(8,128)(2,1)}, bf16[64,2560]{1,0:T(8,128)(2,1)S(1)}, u32[]{:S(2)}, u32[]{:S(2)}) %collective-permute-start) | collective-permute-done | bytes 327712 | tf_op jit(solution)/shard_map/ppermute | solution.py:356
  26.9 6.0 %all-to-all-start = ((bf16[16,2,160,512]{3,2,1,0:T(8,128)(2,1)}), bf16[16,2,160,512]{3,2,1,0:T(8,128)(2,1)}, u32[]{:S(2)}, u32[]{:S(2)}) async-start(bf16[16,2,160,512]{3,2,1,0:T(8,128)(2,1)} %get-tuple-element.46), calls=%async_computation | async-start | bytes 10485760 | tf_op jit(solution)/shard_map/all_to_all | solution.py:316
  33.4 6.3 %fusion.6 = s32[16,64,16]{2,0,1:T(8,128)S(1)} fusion(s32[16,64,16]{2,0,1:T(8,128)S(1)} %copy.62), kind=kOutput, calls=%fused_computation.38 | output fusion | flops 1032192 | bytes 131072 | tf_op jit(solution)/shard_map/jit(cumsum)/reduce_window_sum | solution.py:291
  49.4 79.5 %all-to-all-done.refs_1_.refs_2_ = bf16[16,2,160,512]{3,2,1,0:T(8,128)(2,1)} async-done(((bf16[16,2,160,512]{3,2,1,0:T(8,128)(2,1)}), bf16[16,2,160,512]{3,2,1,0:T(8,128)(2,1)}, u32[]{:S(2)}, u32[]{:S(2)}) %all-to-all-start) | async-done | bytes 5242912 | tf_op jit(solution)/shard_map/all_to_all | solution.py:316
  128.9 24.0 %all-to-all-start.1 = ((bf16[16,2,160,128]{3,2,1,0:T(8,128)(2,1)}), bf16[16,2,160,128]{3,2,1,0:T(8,128)(2,1)S(1)}, u32[]{:S(2)}, u32[]{:S(2)}) async-start(bf16[16,2,160,128]{3,2,1,0:T(8,128)(2,1)} %get-tuple-element.54), calls=%async_computation.1 | async-start | bytes 2621440 | tf_op jit(solution)/shard_map/all_to_all | solution.py:316
  154.8 10.9 %merge.3 = (bf16[16,160,512]{2,1,0:T(8,128)(2,1)}, f32[8,128]{1,0:T(8,128)}) custom-call(s32[32]{0:T(128)} %bitcast.50, f32[960]{0:T(1024)} %mul.47.refs_1_, bf16[16,2,160,512]{3,2,1,0:T(8,128)(2,1)} %all-to-all-done.refs_1_.refs_2_, f32[8,128]{1,0:T(8,128)} %get-tuple-element.50.refs_3_), custom_call_target="tpu_custom_call" | custom-call | tf_op jit(solution)/shard_map/merge/pallas_call | solution.py:32
  170.7 9.7 %all-to-all-done.1.refs_1_.refs_2_ = bf16[16,2,160,128]{3,2,1,0:T(8,128)(2,1)S(1)} async-done(((bf16[16,2,160,128]{3,2,1,0:T(8,128)(2,1)}), bf16[16,2,160,128]{3,2,1,0:T(8,128)(2,1)S(1)}, u32[]{:S(2)}, u32[]{:S(2)}) %all-to-all-start.1) | async-done | bytes 1310752 | tf_op jit(solution)/shard_map/all_to_all | solution.py:316
  181.4 8.0 %all-to-all-start.2 = ((bf16[16,160,512]{2,1,0:T(8,128)(2,1)}), bf16[16,160,512]{2,1,0:T(8,128)(2,1)S(1)}, u32[]{:S(2)}, u32[]{:S(2)}) async-start(bf16[16,160,512]{2,1,0:T(8,128)(2,1)} %get-tuple-element.61), calls=%async_computation.2 | async-start | bytes 5242880 | tf_op jit(solution)/shard_map/all_to_all | solution.py:316
  191.5 8.6 %merge.4 = (bf16[16,160,128]{2,1,0:T(8,128)(2,1)}, f32[8,128]{1,0:T(8,128)}) custom-call(s32[32]{0:T(128)} %bitcast.51, f32[960]{0:T(1024)} %mul.47.refs_1_, bf16[16,2,160,128]{3,2,1,0:T(8,128)(2,1)} %copy-done.1, f32[8,128]{1,0:T(8,128)} %get-tuple-element.57.refs_3_), custom_call_target="tpu_custom_call" | custom-call | tf_op jit(solution)/shard_map/merge/pallas_call | solution.py:32
  200.1 48.8 %collective-permute-done.1.refs_2_ = bf16[2,64,2560]{2,1,0:T(8,128)(2,1)} collective-permute-done((bf16[2,64,2560]{2,1,0:T(8,128)(2,1)}, bf16[2,64,2560]{2,1,0:T(8,128)(2,1)}, u32[]{:S(2)}, u32[]{:S(2)}) %collective-permute-start.1) | collective-permute-done | bytes 655392 | tf_op jit(solution)/shard_map/ppermute | solution.py:368
  252.8 5.0 %all-to-all-start.3 = ((bf16[16,2,160,128]{3,2,1,0:T(8,128)(2,1)}), bf16[16,2,160,128]{3,2,1,0:T(8,128)(2,1)S(1)}, u32[]{:S(2)}, u32[]{:S(2)}) async-start(bf16[16,2,160,128]{3,2,1,0:T(8,128)(2,1)} %get-tuple-element.63), calls=%async_computation.3 | async-start | bytes 2621440 | tf_op jit(solution)/shard_map/all_to_all | solution.py:316
  259.3 26.0 %all-to-all-done.3.refs_1_.refs_2_ = bf16[16,2,160,128]{3,2,1,0:T(8,128)(2,1)S(1)} async-done(((bf16[16,2,160,128]{3,2,1,0:T(8,128)(2,1)}), bf16[16,2,160,128]{3,2,1,0:T(8,128)(2,1)S(1)}, u32[]{:S(2)}, u32[]{:S(2)}) %all-to-all-start.3) | async-done | bytes 1310752 | tf_op jit(solution)/shard_map/all_to_all | solution.py:316
  286.3 8.0 %all-to-all-start.5 = ((bf16[16,160,128]{2,1,0:T(8,128)(2,1)}), bf16[16,160,128]{2,1,0:T(8,128)(2,1)S(1)}, u32[]{:S(2)}, u32[]{:S(2)}) async-start(bf16[16,160,128]{2,1,0:T(8,128)(2,1)} %get-tuple-element.68), calls=%async_computation.5 | async-start | bytes 1310720 | tf_op jit(solution)/shard_map/all_to_all | solution.py:316
  294.4 8.7 %merge.5 = (bf16[16,160,128]{2,1,0:T(8,128)(2,1)}, f32[8,128]{1,0:T(8,128)}) custom-call(s32[32]{0:T(128)} %bitcast.52, f32[960]{0:T(1024)} %mul.47.refs_1_, bf16[16,2,160,128]{3,2,1,0:T(8,128)(2,1)} %copy-done.2, f32[8,128]{1,0:T(8,128)} %get-tuple-element.66.refs_3_), custom_call_target="tpu_custom_call" | custom-call | tf_op jit(solution)/shard_map/merge/pallas_call | solution.py:32
  303.1 7.9 %all-to-all-done.5 = bf16[16,160,128]{2,1,0:T(8,128)(2,1)S(1)} async-done(((bf16[16,160,128]{2,1,0:T(8,128)(2,1)}), bf16[16,160,128]{2,1,0:T(8,128)(2,1)S(1)}, u32[]{:S(2)}, u32[]{:S(2)}) %all-to-all-start.5) | async-done | bytes 655392 | tf_op jit(solution)/shard_map/all_to_all | solution.py:316
  317.3 5.6 %convolution_convert_fusion = bf16[16,48,2560]{2,1,0:T(8,128)(2,1)} fusion(bf16[16,64,2560]{2,1,0:T(8,128)(2,1)} %all-gather.2.cloned.1.call-done, s32[16,64]{1,0:T(8,128)S(1)} %bitcast.46, pred[16,64]{1,0:T(8,128)(4,1)S(1)} %bitcast.49), kind=kOutput, calls=%fused_computation.1 | convolution fusion | flops 253722624 | bytes 9180160 | tf_op jit(solution)/shard_map/jct,jtd->jcd/dot_general | solution.py:372
  322.9 9.9 %run_chunk.3 = (bf16[1,2560,768]{2,1,0:T(8,128)(2,1)}, bf16[1,2560,768]{2,1,0:T(8,128)(2,1)}, bf16[16,48,512]{2,1,0:T(8,128)(2,1)}, f32[8,128]{1,0:T(8,128)}) custom-call(s32[2]{0:T(128)} %pad_add_fusion.refs_0_, bf16[768,2560]{1,0:T(8,128)(2,1)} %bitcast.32, bf16[2560,512]{1,0:T(8,128)(2,1)} %bitcast.37, bf16[2560,512]{1,0:T(8,128)(2,1)} %collective-permute-done.4.refs_3_, ...), custom_call_target="tpu_custom_call" | custom-call | tf_op jit(solution)/shard_map/run_chunk/pallas_call | solution.py:32
  333.8 5.4 %run_chunk.4 = (bf16[1,2560,768]{2,1,0:T(8,128)(2,1)}, bf16[1,2560,768]{2,1,0:T(8,128)(2,1)}, bf16[16,48,128]{2,1,0:T(8,128)(2,1)}, f32[8,128]{1,0:T(8,128)}) custom-call(s32[2]{0:T(128)} %pad_add_fusion.refs_0_, bf16[768,2560]{1,0:T(8,128)(2,1)} %bitcast.33, bf16[2560,128]{1,0:T(8,128)(2,1)} %bitcast.42, ...), custom_call_target="tpu_custom_call", output_to_operand_aliasing={{0}: (4, {}), {1}: (5, {})} | custom-call | tf_op jit(solution)/shard_map/run_chunk/pallas_call | solution.py:32
  341.2 6.0 %all-to-all-start.6 = ((bf16[16,48,640]{2,1,0:T(8,128)(2,1)}), bf16[16,48,640]{2,1,0:T(8,128)(2,1)S(1)}, u32[]{:S(2)}, u32[]{:S(2)}) async-start(bf16[16,48,640]{2,1,0:T(8,128)(2,1)} %get-tuple-element.81), calls=%async_computation.6 | async-start | bytes 1966080 | tf_op jit(solution)/shard_map/all_to_all | solution.py:316
  348.4 15.7 %collective-permute-done.2.refs_3_ = bf16[2560,128]{1,0:T(8,128)(2,1)S(1)} collective-permute-done((bf16[2560,128]{1,0:T(8,128)(2,1)S(1)}, bf16[2560,128]{1,0:T(8,128)(2,1)S(1)}, u32[]{:S(2)}, u32[]{:S(2)}) %collective-permute-start.2) | collective-permute-done | bytes 655392 | tf_op jit(solution)/shard_map/ppermute | solution.py:391
  365.0 5.3 %run_chunk.5 = (bf16[1,2560,768]{2,1,0:T(8,128)(2,1)}, bf16[1,2560,768]{2,1,0:T(8,128)(2,1)}, bf16[16,48,128]{2,1,0:T(8,128)(2,1)}, f32[8,128]{1,0:T(8,128)}) custom-call(s32[2]{0:T(128)} %pad_add_fusion.refs_0_, bf16[768,2560]{1,0:T(8,128)(2,1)} %bitcast.34, bf16[2560,128]{1,0:T(8,128)(2,1)} %bitcast.40, ...), custom_call_target="tpu_custom_call", output_to_operand_aliasing={{0}: (4, {}), {1}: (5, {})} | custom-call | tf_op jit(solution)/shard_map/run_chunk/pallas_call | solution.py:32
  371.3 5.7 %all-to-all-start.7 = ((bf16[16,48,128]{2,1,0:T(8,128)(2,1)}), bf16[16,48,128]{2,1,0:T(8,128)(2,1)S(1)}, u32[]{:S(2)}, u32[]{:S(2)}) async-start(bf16[16,48,128]{2,1,0:T(8,128)(2,1)} %get-tuple-element.84), calls=%async_computation.7 | async-start | bytes 393216 | tf_op jit(solution)/shard_map/all_to_all | solution.py:316
  378.9 7.2 %all-to-all-done.7 = bf16[16,48,128]{2,1,0:T(8,128)(2,1)S(1)} async-done(((bf16[16,48,128]{2,1,0:T(8,128)(2,1)}), bf16[16,48,128]{2,1,0:T(8,128)(2,1)S(1)}, u32[]{:S(2)}, u32[]{:S(2)}) %all-to-all-start.7) | async-done | bytes 196640 | tf_op jit(solution)/shard_map/all_to_all | solution.py:316
  (92 shorter events, 48.1 us)
Async XLA Ops:
  7.2 19.0 %collective-permute-start = (bf16[64,2560]{1,0:T(8,128)(2,1)}, bf16[64,2560]{1,0:T(8,128)(2,1)S(1)}, u32[]{:S(2)}, u32[]{:S(2)}) collective-permute-start(bf16[64,2560]{1,0:T(8,128)(2,1)} %refs_0_.1), channel_id=1, source_target_pairs={{0,8},{1,9},{2,10},{3,11},{4,12},{5,13},{6,14},{7,15},{8,0},{9,1},... | collective-permute-start | bytes 983048 | tf_op jit(solution)/shard_map/ppermute | solution.py:356
  26.9 6.1 %copy-start.12 = (s32[1024,6]{0,1:T(8,128)S(1)}, s32[1024,6]{0,1:T(8,128)}, u32[]{:S(2)}) copy-start(s32[1024,6]{0,1:T(8,128)} %param.9) | copy-start | bytes 73732
  26.9 102.0 %all-to-all-start = ((bf16[16,2,160,512]{3,2,1,0:T(8,128)(2,1)}), bf16[16,2,160,512]{3,2,1,0:T(8,128)(2,1)}, u32[]{:S(2)}, u32[]{:S(2)}) async-start(bf16[16,2,160,512]{3,2,1,0:T(8,128)(2,1)} %get-tuple-element.46), calls=%async_computation | async-start | bytes 10485760 | tf_op jit(solution)/shard_map/all_to_all | solution.py:316
  128.9 24.0 %copy-start.13 = (s32[32,1]{0,1:T(1,128)S(1)}, s32[32,1]{0,1:T(1,128)}, u32[]{:S(2)}) copy-start(s32[32,1]{0,1:T(1,128)} %param.14) | copy-start | bytes 388
  128.9 24.0 %copy-start.14 = (f32[32]{0:T(128)S(1)}, f32[32]{0:T(128)}, u32[]{:S(2)}) copy-start(f32[32]{0:T(128)} %param.15) | copy-start | bytes 388
  128.9 24.3 %copy-start.10 = (f32[32,20,6]{0,1,2:T(8,128)S(1)}, f32[32,20,6]{0,1,2:T(8,128)}, u32[]{:S(2)}) copy-start(f32[32,20,6]{0,1,2:T(8,128)} %param.13) | copy-start | bytes 46084
  128.9 24.3 %copy-start.11 = (f32[32,20,6]{0,1,2:T(8,128)S(1)}, f32[32,20,6]{0,1,2:T(8,128)}, u32[]{:S(2)}) copy-start(f32[32,20,6]{0,1,2:T(8,128)} %param.12) | copy-start | bytes 46084
  128.9 51.4 %all-to-all-start.1 = ((bf16[16,2,160,128]{3,2,1,0:T(8,128)(2,1)}), bf16[16,2,160,128]{3,2,1,0:T(8,128)(2,1)S(1)}, u32[]{:S(2)}, u32[]{:S(2)}) async-start(bf16[16,2,160,128]{3,2,1,0:T(8,128)(2,1)} %get-tuple-element.54), calls=%async_computation.1 | async-start | bytes 2621440 | tf_op jit(solution)/shard_map/all_to_all | solution.py:316
  180.4 1.1 copy-start.1
  181.4 69.9 %all-to-all-start.2 = ((bf16[16,160,512]{2,1,0:T(8,128)(2,1)}), bf16[16,160,512]{2,1,0:T(8,128)(2,1)S(1)}, u32[]{:S(2)}, u32[]{:S(2)}) async-start(bf16[16,160,512]{2,1,0:T(8,128)(2,1)} %get-tuple-element.61), calls=%async_computation.2 | async-start | bytes 5242880 | tf_op jit(solution)/shard_map/all_to_all | solution.py:316
  189.4 127.9 %all-gather.2.cloned.1.call-start = ((), (), s32[]{:S(2)}) async-start(), calls=%async_computation.8 | async-start | bytes 6553600 | tf_op jit(solution)/shard_map/all_gather | solution.py:371
  189.5 59.4 %collective-permute-start.1 = (bf16[2,64,2560]{2,1,0:T(8,128)(2,1)}, bf16[2,64,2560]{2,1,0:T(8,128)(2,1)}, u32[]{:S(2)}, u32[]{:S(2)}) collective-permute-start(bf16[2,64,2560]{2,1,0:T(8,128)(2,1)} %get-tuple-element.53.refs_1_), channel_id=1, source_target_pairs={{0,4},{1,5},{2,6},{3,7},{4,0},{5,1},{6,2},{7,3},{8,12},{9,13},{10,... | collective-permute-start | bytes 1966088 | tf_op jit(solution)/shard_map/ppermute | solution.py:368
  251.3 1.5 copy-start
  252.8 32.5 %all-to-all-start.3 = ((bf16[16,2,160,128]{3,2,1,0:T(8,128)(2,1)}), bf16[16,2,160,128]{3,2,1,0:T(8,128)(2,1)S(1)}, u32[]{:S(2)}, u32[]{:S(2)}) async-start(bf16[16,2,160,128]{3,2,1,0:T(8,128)(2,1)} %get-tuple-element.63), calls=%async_computation.3 | async-start | bytes 2621440 | tf_op jit(solution)/shard_map/all_to_all | solution.py:316
  257.8 65.2 %collective-permute-start.4 = (bf16[2560,512]{1,0:T(8,128)(2,1)}, bf16[2560,512]{1,0:T(8,128)(2,1)}, u32[]{:S(2)}, u32[]{:S(2)}) collective-permute-start(bf16[2560,512]{1,0:T(8,128)(2,1)} %bitcast.36), channel_id=1, source_target_pairs={{0,16},{16,0},{1,17},{17,1},{2,18},{18,2},{3,19},{19,3},{4,20},{20... | collective-permute-start | bytes 7864328 | tf_op jit(solution)/shard_map/ppermute | solution.py:391
  286.3 24.7 %all-to-all-start.5 = ((bf16[16,160,128]{2,1,0:T(8,128)(2,1)}), bf16[16,160,128]{2,1,0:T(8,128)(2,1)S(1)}, u32[]{:S(2)}, u32[]{:S(2)}) async-start(bf16[16,160,128]{2,1,0:T(8,128)(2,1)} %get-tuple-element.68), calls=%async_computation.5 | async-start | bytes 1310720 | tf_op jit(solution)/shard_map/all_to_all | solution.py:316
  311.0 11.9 %copy-start.5 = (bf16[16,160,128]{2,1,0:T(8,128)(2,1)}, bf16[16,160,128]{2,1,0:T(8,128)(2,1)S(1)}, u32[]{:S(2)}) copy-start(bf16[16,160,128]{2,1,0:T(8,128)(2,1)S(1)} %all-to-all-done.5) | copy-start | bytes 1966084
  311.0 30.2 %all-to-all-start.4 = ((bf16[16,160,128]{2,1,0:T(8,128)(2,1)}), bf16[16,160,128]{2,1,0:T(8,128)(2,1)S(1)}, u32[]{:S(2)}, u32[]{:S(2)}) async-start(bf16[16,160,128]{2,1,0:T(8,128)(2,1)} %get-tuple-element.67), calls=%async_computation.4 | async-start | bytes 1310720 | tf_op jit(solution)/shard_map/all_to_all | solution.py:316
  315.8 17.1 %collective-permute-start.3 = (bf16[2560,128]{1,0:T(8,128)(2,1)S(1)}, bf16[2560,128]{1,0:T(8,128)(2,1)S(1)}, u32[]{:S(2)}, u32[]{:S(2)}) collective-permute-start(bf16[2560,128]{1,0:T(8,128)(2,1)S(1)} %bitcast.41), channel_id=1, source_target_pairs={{0,16},{16,0},{1,17},{17,1},{2,18},{18,2},{3,19},{19,3},{4,20},{20... | collective-permute-start | bytes 1966088 | tf_op jit(solution)/shard_map/ppermute | solution.py:391
  333.8 5.4 %copy-start.7 = (bf16[16,48,512]{2,1,0:T(8,128)(2,1)S(1)}, bf16[16,48,512]{2,1,0:T(8,128)(2,1)}, u32[]{:S(2)}) copy-start(bf16[16,48,512]{2,1,0:T(8,128)(2,1)} %get-tuple-element.75) | copy-start | bytes 2359300
  341.2 23.0 %copy-start.4 = (bf16[16,160,128]{2,1,0:T(8,128)(2,1)}, bf16[16,160,128]{2,1,0:T(8,128)(2,1)S(1)}, u32[]{:S(2)}) copy-start(bf16[16,160,128]{2,1,0:T(8,128)(2,1)S(1)} %all-to-all-done.4) | copy-start | bytes 1966084
  341.2 29.2 %all-to-all-start.6 = ((bf16[16,48,640]{2,1,0:T(8,128)(2,1)}), bf16[16,48,640]{2,1,0:T(8,128)(2,1)S(1)}, u32[]{:S(2)}, u32[]{:S(2)}) async-start(bf16[16,48,640]{2,1,0:T(8,128)(2,1)} %get-tuple-element.81), calls=%async_computation.6 | async-start | bytes 1966080 | tf_op jit(solution)/shard_map/all_to_all | solution.py:316
  347.1 17.0 %collective-permute-start.2 = (bf16[2560,128]{1,0:T(8,128)(2,1)S(1)}, bf16[2560,128]{1,0:T(8,128)(2,1)S(1)}, u32[]{:S(2)}, u32[]{:S(2)}) collective-permute-start(bf16[2560,128]{1,0:T(8,128)(2,1)S(1)} %bitcast.39), channel_id=1, source_target_pairs={{0,16},{16,0},{1,17},{17,1},{2,18},{18,2},{3,19},{19,3},{4,20},{20... | collective-permute-start | bytes 1966088 | tf_op jit(solution)/shard_map/ppermute | solution.py:391
  371.3 14.8 %all-to-all-start.7 = ((bf16[16,48,128]{2,1,0:T(8,128)(2,1)}), bf16[16,48,128]{2,1,0:T(8,128)(2,1)S(1)}, u32[]{:S(2)}, u32[]{:S(2)}) async-start(bf16[16,48,128]{2,1,0:T(8,128)(2,1)} %get-tuple-element.84), calls=%async_computation.7 | async-start | bytes 393216 | tf_op jit(solution)/shard_map/all_to_all | solution.py:316
  (5 other events, 4.4 us)
Sparse Core Ops, SparseCore 0:
  251.4 58.4 all-gather.1

commit v18 on v17

--- a/solution.py
+++ b/solution.py
@@ -98,6 +98,10 @@
 
 
 def hold(token, value, earlier):
+    earlier = [
+        part[(slice(0, 1),) * (part.ndim - 2) + (slice(0, 16), slice(0, 128))] for part in earlier
+    ]
+
     def kernel(*refs):
         pass
 

time: 397 us -> 397 us (level)
    slice x0 -> x6, local copies, waits for them, and re-layouts: none -> 5 us  [hold(): part[(slice(0, 1),) * (part.ndim - 2) + (slice(0, 16), slice(0, 128))]]
    unnamed x31, local copies, waits for them, and re-layouts: 7.86 us -> 3.2 us
where the time goes in v18:
time: 397 us; the launch traced here: 395 us
  waiting for transfers between devices  204 us (51%)
  starting transfers between devices  77.9 us (20%)
  Pallas kernels  65 us (16%)
  between operations  14.5 us (4%)
  other arithmetic  13.4 us (3%)
  local copies, waits for them, and re-layouts  13.3 us (3%)
  matrix products  6.54 us (2%)
    all_to_all x8, waiting for transfers between devices, exchange(): return lax.all_to_all(pieces, 'expert', 0, 0, tiled=True)  132 us
    all_to_all x8, starting transfers between devices, exchange(): return lax.all_to_all(pieces, 'expert', 0, 0, tiled=True)  67.1 us
    pallas_call x18, Pallas kernels, step_call(): pl.pallas_call(ordered, out_shape=[*out_shape, TOKEN], in_specs=[*in_spec...  65 us
    ppermute x1, waiting for transfers between devices, shards(): nearby = lax.ppermute(both, 'expert', beside)  48.7 us
    ppermute x3, waiting for transfers between devices, shards(): partner[c] = lax.ppermute(own[c], 'groups', partners)  15.9 us
    ppermute x1, waiting for transfers between devices, shards(): opposite = lax.ppermute(tokens, 'expert', across)  8.08 us
  transfers between devices with their start and end apart: 14, of which 9 were waited for; matrix products, arithmetic and copies ran while one was open for 7% of the time, Pallas kernels for 16%

profile of v18, /device:TPU:0, one launch (start us, length us, event | category | flops | bytes accessed | tf_op | source)
XLA Modules:
  0.0 394.7 jit_solution(2309234392144767223)
XLA Ops:
  12.5 5.6 %pack.3 = (bf16[16,2,160,512]{3,2,1,0:T(8,128)(2,1)}, f32[8,128]{1,0:T(8,128)}) custom-call(s32[2]{0:T(128)} %pad_add_fusion.refs_0_, bf16[2,2560,768]{2,1,0:T(8,128)(2,1)} %refs_1_.5, bf16[2,2560,768]{2,1,0:T(8,128)(2,1)} %refs_2_.5, f32[8,128]{1,0:T(8,128)} %broadcast_in_dim.40.refs_3_), custom_call_target="tpu_custom_call" | custom-call | tf_op jit(solution)/shard_map/pack/pallas_call | solution.py:32
  18.1 8.1 %collective-permute-done.refs_1_ = bf16[64,2560]{1,0:T(8,128)(2,1)S(1)} collective-permute-done((bf16[64,2560]{1,0:T(8,128)(2,1)}, bf16[64,2560]{1,0:T(8,128)(2,1)S(1)}, u32[]{:S(2)}, u32[]{:S(2)}) %collective-permute-start) | collective-permute-done | bytes 327712 | tf_op jit(solution)/shard_map/ppermute | solution.py:360
  26.9 5.9 %all-to-all-start = ((bf16[16,2,160,512]{3,2,1,0:T(8,128)(2,1)}), bf16[16,2,160,512]{3,2,1,0:T(8,128)(2,1)}, u32[]{:S(2)}, u32[]{:S(2)}) async-start(bf16[16,2,160,512]{3,2,1,0:T(8,128)(2,1)} %get-tuple-element.46), calls=%async_computation | async-start | bytes 10485760 | tf_op jit(solution)/shard_map/all_to_all | solution.py:320
  33.3 6.3 %fusion.3 = s32[16,64,16]{2,0,1:T(8,128)S(1)} fusion(s32[16,64,16]{2,0,1:T(8,128)S(1)} %copy.62), kind=kOutput, calls=%fused_computation.37 | output fusion | flops 1032192 | bytes 131072 | tf_op jit(solution)/shard_map/jit(cumsum)/reduce_window_sum | solution.py:295
  49.3 79.5 %all-to-all-done.refs_2_ = bf16[16,2,160,512]{3,2,1,0:T(8,128)(2,1)} async-done(((bf16[16,2,160,512]{3,2,1,0:T(8,128)(2,1)}), bf16[16,2,160,512]{3,2,1,0:T(8,128)(2,1)}, u32[]{:S(2)}, u32[]{:S(2)}) %all-to-all-start) | async-done | bytes 5242912 | tf_op jit(solution)/shard_map/all_to_all | solution.py:320
  130.1 23.9 %all-to-all-start.1 = ((bf16[16,2,160,128]{3,2,1,0:T(8,128)(2,1)}), bf16[16,2,160,128]{3,2,1,0:T(8,128)(2,1)S(1)}, u32[]{:S(2)}, u32[]{:S(2)}) async-start(bf16[16,2,160,128]{3,2,1,0:T(8,128)(2,1)} %get-tuple-element.54), calls=%async_computation.1 | async-start | bytes 2621440 | tf_op jit(solution)/shard_map/all_to_all | solution.py:320
  155.8 10.9 %merge.3 = (bf16[16,160,512]{2,1,0:T(8,128)(2,1)}, f32[8,128]{1,0:T(8,128)}) custom-call(s32[32]{0:T(128)} %bitcast.50, f32[960]{0:T(1024)} %mul.47.refs_1_, bf16[16,2,160,512]{3,2,1,0:T(8,128)(2,1)} %all-to-all-done.refs_2_, f32[8,128]{1,0:T(8,128)} %get-tuple-element.50.refs_3_), custom_call_target="tpu_custom_call" | custom-call | tf_op jit(solution)/shard_map/merge/pallas_call | solution.py:32
  171.6 9.7 %all-to-all-done.1.refs_2_ = bf16[16,2,160,128]{3,2,1,0:T(8,128)(2,1)S(1)} async-done(((bf16[16,2,160,128]{3,2,1,0:T(8,128)(2,1)}), bf16[16,2,160,128]{3,2,1,0:T(8,128)(2,1)S(1)}, u32[]{:S(2)}, u32[]{:S(2)}) %all-to-all-start.1) | async-done | bytes 1310752 | tf_op jit(solution)/shard_map/all_to_all | solution.py:320
  182.4 8.0 %all-to-all-start.2 = ((bf16[16,160,512]{2,1,0:T(8,128)(2,1)}), bf16[16,160,512]{2,1,0:T(8,128)(2,1)S(1)}, u32[]{:S(2)}, u32[]{:S(2)}) async-start(bf16[16,160,512]{2,1,0:T(8,128)(2,1)} %get-tuple-element.61), calls=%async_computation.2 | async-start | bytes 5242880 | tf_op jit(solution)/shard_map/all_to_all | solution.py:320
  192.5 8.7 %merge.4 = (bf16[16,160,128]{2,1,0:T(8,128)(2,1)}, f32[8,128]{1,0:T(8,128)}) custom-call(s32[32]{0:T(128)} %bitcast.51, f32[960]{0:T(1024)} %mul.47.refs_1_, bf16[16,2,160,128]{3,2,1,0:T(8,128)(2,1)} %copy-done.1, f32[8,128]{1,0:T(8,128)} %get-tuple-element.57.refs_3_), custom_call_target="tpu_custom_call" | custom-call | tf_op jit(solution)/shard_map/merge/pallas_call | solution.py:32
  201.1 48.7 %collective-permute-done.1.refs_2_ = bf16[2,64,2560]{2,1,0:T(8,128)(2,1)} collective-permute-done((bf16[2,64,2560]{2,1,0:T(8,128)(2,1)S(1)}, bf16[2,64,2560]{2,1,0:T(8,128)(2,1)}, u32[]{:S(2)}, u32[]{:S(2)}) %collective-permute-start.1) | collective-permute-done | bytes 655392 | tf_op jit(solution)/shard_map/ppermute | solution.py:372
  252.9 5.0 %all-to-all-start.3 = ((bf16[16,2,160,128]{3,2,1,0:T(8,128)(2,1)}), bf16[16,2,160,128]{3,2,1,0:T(8,128)(2,1)}, u32[]{:S(2)}, u32[]{:S(2)}) async-start(bf16[16,2,160,128]{3,2,1,0:T(8,128)(2,1)} %get-tuple-element.63), calls=%async_computation.3 | async-start | bytes 2621440 | tf_op jit(solution)/shard_map/all_to_all | solution.py:320
  259.5 26.0 %all-to-all-done.3.refs_2_ = bf16[16,2,160,128]{3,2,1,0:T(8,128)(2,1)} async-done(((bf16[16,2,160,128]{3,2,1,0:T(8,128)(2,1)}), bf16[16,2,160,128]{3,2,1,0:T(8,128)(2,1)}, u32[]{:S(2)}, u32[]{:S(2)}) %all-to-all-start.3) | async-done | bytes 1310752 | tf_op jit(solution)/shard_map/all_to_all | solution.py:320
  286.8 8.0 %all-to-all-start.5 = ((bf16[16,160,128]{2,1,0:T(8,128)(2,1)}), bf16[16,160,128]{2,1,0:T(8,128)(2,1)S(1)}, u32[]{:S(2)}, u32[]{:S(2)}) async-start(bf16[16,160,128]{2,1,0:T(8,128)(2,1)} %get-tuple-element.68), calls=%async_computation.5 | async-start | bytes 1310720 | tf_op jit(solution)/shard_map/all_to_all | solution.py:320
  294.8 8.7 %merge.5 = (bf16[16,160,128]{2,1,0:T(8,128)(2,1)}, f32[8,128]{1,0:T(8,128)}) custom-call(s32[32]{0:T(128)} %bitcast.52, f32[960]{0:T(1024)} %mul.47.refs_1_, bf16[16,2,160,128]{3,2,1,0:T(8,128)(2,1)} %all-to-all-done.3.refs_2_, f32[8,128]{1,0:T(8,128)} %get-tuple-element.66.refs_3_), custom_call_target="tpu_custom_call" | custom-call | tf_op jit(solution)/shard_map/merge/pallas_call | solution.py:32
  303.5 7.9 %all-to-all-done.5 = bf16[16,160,128]{2,1,0:T(8,128)(2,1)S(1)} async-done(((bf16[16,160,128]{2,1,0:T(8,128)(2,1)}), bf16[16,160,128]{2,1,0:T(8,128)(2,1)S(1)}, u32[]{:S(2)}, u32[]{:S(2)}) %all-to-all-start.5) | async-done | bytes 655392 | tf_op jit(solution)/shard_map/all_to_all | solution.py:320
  318.7 5.6 %convolution_convert_fusion = bf16[16,48,2560]{2,1,0:T(8,128)(2,1)} fusion(bf16[16,64,2560]{2,1,0:T(8,128)(2,1)} %all-gather.2.cloned.1.call-done, s32[16,64]{1,0:T(8,128)S(1)} %bitcast.46, pred[16,64]{1,0:T(8,128)(4,1)S(1)} %bitcast.49), kind=kOutput, calls=%fused_computation.1 | convolution fusion | flops 253722624 | bytes 9180160 | tf_op jit(solution)/shard_map/jct,jtd->jcd/dot_general | solution.py:376
  324.3 9.9 %run_chunk.3 = (bf16[1,2560,768]{2,1,0:T(8,128)(2,1)}, bf16[1,2560,768]{2,1,0:T(8,128)(2,1)}, bf16[16,48,512]{2,1,0:T(8,128)(2,1)}, f32[8,128]{1,0:T(8,128)}) custom-call(s32[2]{0:T(128)} %pad_add_fusion.refs_0_, bf16[768,2560]{1,0:T(8,128)(2,1)} %bitcast.32, bf16[2560,512]{1,0:T(8,128)(2,1)} %bitcast.37, bf16[2560,512]{1,0:T(8,128)(2,1)} %collective-permute-done.4.refs_3_, ...), custom_call_target="tpu_custom_call" | custom-call | tf_op jit(solution)/shard_map/run_chunk/pallas_call | solution.py:32
  334.6 5.4 %run_chunk.4 = (bf16[1,2560,768]{2,1,0:T(8,128)(2,1)}, bf16[1,2560,768]{2,1,0:T(8,128)(2,1)}, bf16[16,48,128]{2,1,0:T(8,128)(2,1)}, f32[8,128]{1,0:T(8,128)}) custom-call(s32[2]{0:T(128)} %pad_add_fusion.refs_0_, bf16[768,2560]{1,0:T(8,128)(2,1)} %bitcast.33, bf16[2560,128]{1,0:T(8,128)(2,1)} %bitcast.41, ...), custom_call_target="tpu_custom_call", output_to_operand_aliasing={{0}: (4, {}), {1}: (5, {})} | custom-call | tf_op jit(solution)/shard_map/run_chunk/pallas_call | solution.py:32
  342.0 5.7 %all-to-all-start.6 = ((bf16[16,48,640]{2,1,0:T(8,128)(2,1)}), bf16[16,48,640]{2,1,0:T(8,128)(2,1)S(1)}, u32[]{:S(2)}, u32[]{:S(2)}) async-start(bf16[16,48,640]{2,1,0:T(8,128)(2,1)} %get-tuple-element.81), calls=%async_computation.6 | async-start | bytes 1966080 | tf_op jit(solution)/shard_map/all_to_all | solution.py:320
  349.3 15.5 %collective-permute-done.2.refs_3_ = bf16[2560,128]{1,0:T(8,128)(2,1)S(1)} collective-permute-done((bf16[2560,128]{1,0:T(8,128)(2,1)S(1)}, bf16[2560,128]{1,0:T(8,128)(2,1)S(1)}, u32[]{:S(2)}, u32[]{:S(2)}) %collective-permute-start.2) | collective-permute-done | bytes 655392 | tf_op jit(solution)/shard_map/ppermute | solution.py:395
  365.6 5.4 %run_chunk.5 = (bf16[1,2560,768]{2,1,0:T(8,128)(2,1)}, bf16[1,2560,768]{2,1,0:T(8,128)(2,1)}, bf16[16,48,128]{2,1,0:T(8,128)(2,1)}, f32[8,128]{1,0:T(8,128)}) custom-call(s32[2]{0:T(128)} %pad_add_fusion.refs_0_, bf16[768,2560]{1,0:T(8,128)(2,1)} %bitcast.34, bf16[2560,128]{1,0:T(8,128)(2,1)} %bitcast.39, ...), custom_call_target="tpu_custom_call", output_to_operand_aliasing={{0}: (4, {}), {1}: (5, {})} | custom-call | tf_op jit(solution)/shard_map/run_chunk/pallas_call | solution.py:32
  371.6 5.7 %all-to-all-start.7 = ((bf16[16,48,128]{2,1,0:T(8,128)(2,1)}), bf16[16,48,128]{2,1,0:T(8,128)(2,1)S(1)}, u32[]{:S(2)}, u32[]{:S(2)}) async-start(bf16[16,48,128]{2,1,0:T(8,128)(2,1)} %get-tuple-element.84), calls=%async_computation.7 | async-start | bytes 393216 | tf_op jit(solution)/shard_map/all_to_all | solution.py:320
  378.0 8.3 %all-to-all-done.7 = bf16[16,48,128]{2,1,0:T(8,128)(2,1)S(1)} async-done(((bf16[16,48,128]{2,1,0:T(8,128)(2,1)}), bf16[16,48,128]{2,1,0:T(8,128)(2,1)S(1)}, u32[]{:S(2)}, u32[]{:S(2)}) %all-to-all-start.7) | async-done | bytes 196640 | tf_op jit(solution)/shard_map/all_to_all | solution.py:320
  (99 shorter events, 47.7 us)
Async XLA Ops:
  7.2 19.0 %collective-permute-start = (bf16[64,2560]{1,0:T(8,128)(2,1)}, bf16[64,2560]{1,0:T(8,128)(2,1)S(1)}, u32[]{:S(2)}, u32[]{:S(2)}) collective-permute-start(bf16[64,2560]{1,0:T(8,128)(2,1)} %refs_0_.1), channel_id=1, source_target_pairs={{0,8},{1,9},{2,10},{3,11},{4,12},{5,13},{6,14},{7,15},{8,0},{9,1},... | collective-permute-start | bytes 983048 | tf_op jit(solution)/shard_map/ppermute | solution.py:360
  26.8 6.0 %copy-start.12 = (s32[1024,6]{0,1:T(8,128)S(1)}, s32[1024,6]{0,1:T(8,128)}, u32[]{:S(2)}) copy-start(s32[1024,6]{0,1:T(8,128)} %param.9) | copy-start | bytes 73732
  26.9 101.9 %all-to-all-start = ((bf16[16,2,160,512]{3,2,1,0:T(8,128)(2,1)}), bf16[16,2,160,512]{3,2,1,0:T(8,128)(2,1)}, u32[]{:S(2)}, u32[]{:S(2)}) async-start(bf16[16,2,160,512]{3,2,1,0:T(8,128)(2,1)} %get-tuple-element.46), calls=%async_computation | async-start | bytes 10485760 | tf_op jit(solution)/shard_map/all_to_all | solution.py:320
  49.2 104.7 %copy-start.13 = (s32[32,1]{0,1:T(1,128)S(1)}, s32[32,1]{0,1:T(1,128)}, u32[]{:S(2)}) copy-start(s32[32,1]{0,1:T(1,128)} %param.14) | copy-start | bytes 388
  49.2 104.7 %copy-start.14 = (f32[32]{0:T(128)S(1)}, f32[32]{0:T(128)}, u32[]{:S(2)}) copy-start(f32[32]{0:T(128)} %param.15) | copy-start | bytes 388
  49.3 104.9 %copy-start.10 = (f32[32,20,6]{0,1,2:T(8,128)S(1)}, f32[32,20,6]{0,1,2:T(8,128)}, u32[]{:S(2)}) copy-start(f32[32,20,6]{0,1,2:T(8,128)} %param.13) | copy-start | bytes 46084
  49.3 104.9 %copy-start.11 = (f32[32,20,6]{0,1,2:T(8,128)S(1)}, f32[32,20,6]{0,1,2:T(8,128)}, u32[]{:S(2)}) copy-start(f32[32,20,6]{0,1,2:T(8,128)} %param.12) | copy-start | bytes 46084
  130.1 51.3 %all-to-all-start.1 = ((bf16[16,2,160,128]{3,2,1,0:T(8,128)(2,1)}), bf16[16,2,160,128]{3,2,1,0:T(8,128)(2,1)S(1)}, u32[]{:S(2)}, u32[]{:S(2)}) async-start(bf16[16,2,160,128]{3,2,1,0:T(8,128)(2,1)} %get-tuple-element.54), calls=%async_computation.1 | async-start | bytes 2621440 | tf_op jit(solution)/shard_map/all_to_all | solution.py:320
  182.0 8.5 %copy-start.6 = (bf16[2,64,2560]{2,1,0:T(8,128)(2,1)S(1)}, bf16[2,64,2560]{2,1,0:T(8,128)(2,1)}, u32[]{:S(2)}) copy-start(bf16[2,64,2560]{2,1,0:T(8,128)(2,1)} %get-tuple-element.53.refs_1_) | copy-start | bytes 1966084
  182.4 69.9 %all-to-all-start.2 = ((bf16[16,160,512]{2,1,0:T(8,128)(2,1)}), bf16[16,160,512]{2,1,0:T(8,128)(2,1)S(1)}, u32[]{:S(2)}, u32[]{:S(2)}) async-start(bf16[16,160,512]{2,1,0:T(8,128)(2,1)} %get-tuple-element.61), calls=%async_computation.2 | async-start | bytes 5242880 | tf_op jit(solution)/shard_map/all_to_all | solution.py:320
  190.4 128.3 %all-gather.2.cloned.1.call-start = ((), (), s32[]{:S(2)}) async-start(), calls=%async_computation.8 | async-start | bytes 6553600 | tf_op jit(solution)/shard_map/all_gather | solution.py:375
  190.5 59.4 %collective-permute-start.1 = (bf16[2,64,2560]{2,1,0:T(8,128)(2,1)S(1)}, bf16[2,64,2560]{2,1,0:T(8,128)(2,1)}, u32[]{:S(2)}, u32[]{:S(2)}) collective-permute-start(bf16[2,64,2560]{2,1,0:T(8,128)(2,1)S(1)} %copy-done.6), channel_id=1, source_target_pairs={{0,4},{1,5},{2,6},{3,7},{4,0},{5,1},{6,2},{7,3},{8,12},{9,13},{10,... | collective-permute-start | bytes 1966088 | tf_op jit(solution)/shard_map/ppermute | solution.py:372
  252.3 60.0 %copy-start = (bf16[16,160,512]{2,1,0:T(8,128)(2,1)}, bf16[16,160,512]{2,1,0:T(8,128)(2,1)S(1)}, u32[]{:S(2)}) copy-start(bf16[16,160,512]{2,1,0:T(8,128)(2,1)S(1)} %all-to-all-done.2) | copy-start | bytes 7864324
  252.9 32.6 %all-to-all-start.3 = ((bf16[16,2,160,128]{3,2,1,0:T(8,128)(2,1)}), bf16[16,2,160,128]{3,2,1,0:T(8,128)(2,1)}, u32[]{:S(2)}, u32[]{:S(2)}) async-start(bf16[16,2,160,128]{3,2,1,0:T(8,128)(2,1)} %get-tuple-element.63), calls=%async_computation.3 | async-start | bytes 2621440 | tf_op jit(solution)/shard_map/all_to_all | solution.py:320
  257.9 66.3 %collective-permute-start.4 = (bf16[2560,512]{1,0:T(8,128)(2,1)S(1)}, bf16[2560,512]{1,0:T(8,128)(2,1)}, u32[]{:S(2)}, u32[]{:S(2)}) collective-permute-start(bf16[2560,512]{1,0:T(8,128)(2,1)S(1)} %bitcast.36), channel_id=1, source_target_pairs={{0,16},{16,0},{1,17},{17,1},{2,18},{18,2},{3,19},{19,3},{4,20},{20... | collective-permute-start | bytes 7864328 | tf_op jit(solution)/shard_map/ppermute | solution.py:395
  286.8 24.7 %all-to-all-start.5 = ((bf16[16,160,128]{2,1,0:T(8,128)(2,1)}), bf16[16,160,128]{2,1,0:T(8,128)(2,1)S(1)}, u32[]{:S(2)}, u32[]{:S(2)}) async-start(bf16[16,160,128]{2,1,0:T(8,128)(2,1)} %get-tuple-element.68), calls=%async_computation.5 | async-start | bytes 1310720 | tf_op jit(solution)/shard_map/all_to_all | solution.py:320
  312.3 29.6 %all-to-all-start.4 = ((bf16[16,160,128]{2,1,0:T(8,128)(2,1)}), bf16[16,160,128]{2,1,0:T(8,128)(2,1)S(1)}, u32[]{:S(2)}, u32[]{:S(2)}) async-start(bf16[16,160,128]{2,1,0:T(8,128)(2,1)} %get-tuple-element.67), calls=%async_computation.4 | async-start | bytes 1310720 | tf_op jit(solution)/shard_map/all_to_all | solution.py:320
  317.1 17.4 %collective-permute-start.3 = (bf16[2560,128]{1,0:T(8,128)(2,1)}, bf16[2560,128]{1,0:T(8,128)(2,1)}, u32[]{:S(2)}, u32[]{:S(2)}) collective-permute-start(bf16[2560,128]{1,0:T(8,128)(2,1)} %bitcast.40), channel_id=1, source_target_pairs={{0,16},{16,0},{1,17},{17,1},{2,18},{18,2},{3,19},{19,3},{4,20},{20... | collective-permute-start | bytes 1966088 | tf_op jit(solution)/shard_map/ppermute | solution.py:395
  334.6 5.4 %copy-start.4 = (bf16[16,48,512]{2,1,0:T(8,128)(2,1)S(1)}, bf16[16,48,512]{2,1,0:T(8,128)(2,1)}, u32[]{:S(2)}) copy-start(bf16[16,48,512]{2,1,0:T(8,128)(2,1)} %get-tuple-element.75) | copy-start | bytes 2359300
  342.0 22.8 %copy-start.2 = (bf16[16,160,128]{2,1,0:T(8,128)(2,1)}, bf16[16,160,128]{2,1,0:T(8,128)(2,1)S(1)}, u32[]{:S(2)}) copy-start(bf16[16,160,128]{2,1,0:T(8,128)(2,1)S(1)} %all-to-all-done.4) | copy-start | bytes 1966084
  342.0 29.0 %all-to-all-start.6 = ((bf16[16,48,640]{2,1,0:T(8,128)(2,1)}), bf16[16,48,640]{2,1,0:T(8,128)(2,1)S(1)}, u32[]{:S(2)}, u32[]{:S(2)}) async-start(bf16[16,48,640]{2,1,0:T(8,128)(2,1)} %get-tuple-element.81), calls=%async_computation.6 | async-start | bytes 1966080 | tf_op jit(solution)/shard_map/all_to_all | solution.py:320
  347.7 17.0 %collective-permute-start.2 = (bf16[2560,128]{1,0:T(8,128)(2,1)S(1)}, bf16[2560,128]{1,0:T(8,128)(2,1)S(1)}, u32[]{:S(2)}, u32[]{:S(2)}) collective-permute-start(bf16[2560,128]{1,0:T(8,128)(2,1)S(1)} %bitcast.38), channel_id=1, source_target_pairs={{0,16},{16,0},{1,17},{17,1},{2,18},{18,2},{3,19},{19,3},{4,20},{20... | collective-permute-start | bytes 1966088 | tf_op jit(solution)/shard_map/ppermute | solution.py:395
  365.6 11.7 %copy-start.9 = (pred[384,768]{1,0:T(8,128)(4,1)S(1)}, pred[384,768]{1,0:T(8,128)(4,1)}, u32[]{:S(2)}) copy-start(pred[384,768]{1,0:T(8,128)(4,1)} %copy-done.8) | copy-start | bytes 884740
  371.6 14.8 %all-to-all-start.7 = ((bf16[16,48,128]{2,1,0:T(8,128)(2,1)}), bf16[16,48,128]{2,1,0:T(8,128)(2,1)S(1)}, u32[]{:S(2)}, u32[]{:S(2)}) async-start(bf16[16,48,128]{2,1,0:T(8,128)(2,1)} %get-tuple-element.84), calls=%async_computation.7 | async-start | bytes 393216 | tf_op jit(solution)/shard_map/all_to_all | solution.py:320
  (5 other events, 8.3 us)
Sparse Core Ops, SparseCore 0:
  252.4 57.6 all-gather.1

commit v19 on v17

--- a/solution.py
+++ b/solution.py
@@ -196,14 +196,18 @@
     return whole, token
 
 
-def run_chunk(token, info, grouped, own, partner, outputs, start, full, blocks):
+def run_chunk(token, info, grouped, own, partner, outputs, start, full, blocks, sent):
+    begun, sent_width, sent_start = sent
+    outputs = (*outputs, *begun)
+    given = len(outputs)
+    place_of = [0, 1, 2] if len(outputs) == 3 else [0, 1] if given == 2 and not begun else [2][:given]
     depth, width = own.shape
     count = grouped.shape[0]
     each = count // len(blocks)
     factor = 1.0 / math.sqrt(D)
 
     def kernel(info_ref, grouped_ref, own_ref, partner_ref, *rest):
-        gate_out, up_out, hidden_ref, whole, in_sems, out_sems = rest[len(outputs) :]
+        gate_out, up_out, hidden_out, whole, hidden_ref, in_sems, out_sems = rest[given:]
         halves = [whole.at[:, pl.ds(index * width, width)] for index in range(2)]
 
         def fill(*sources):
@@ -236,6 +240,11 @@
         hidden = (gate_value / (1.0 + jnp.exp(-gate_value)) * up_value).astype(jnp.bfloat16)
         for index, block in enumerate(blocks):
             hidden_ref[block] = hidden[index * each : (index + 1) * each]
+        back = pltpu.make_async_copy(
+            hidden_ref, hidden_out.at[:, :, pl.ds(sent_start, width)], out_sems.at[2]
+        )
+        back.start()
+        back.wait()
         for store in stores:
             store.wait()
 
@@ -245,14 +254,15 @@
         token,
         (info, grouped, own, partner, *outputs),
         [SMEM, VMEM, ANY, ANY] + [ANY] * len(outputs),
-        [weights, weights, jax.ShapeDtypeStruct((len(blocks), each, width), jnp.bfloat16)],
-        [ANY, ANY, VMEM],
+        [weights, weights, jax.ShapeDtypeStruct((len(blocks), each, sent_width), jnp.bfloat16)],
+        [ANY, ANY, ANY],
         scratch_shapes=[
             pltpu.VMEM((depth, 2 * width), jnp.bfloat16),
+            pltpu.VMEM((len(blocks), each, width), jnp.bfloat16),
             pltpu.SemaphoreType.DMA((2,)),
-            pltpu.SemaphoreType.DMA((2,)),
+            pltpu.SemaphoreType.DMA((3,)),
         ],
-        input_output_aliases={4 + index: index for index in range(len(outputs))},
+        input_output_aliases={4 + index: place for index, place in enumerate(place_of)},
         name="run_chunk",
     )
 
@@ -390,12 +400,14 @@
             own[c] = exchange(merged[c]).reshape(depth, width)
             partner[c] = lax.ppermute(own[c], "groups", partners)
         elif name == "run":
-            (*outputs, hiddens[c]), token = run_chunk(
-                token, info, grouped, own[c], partner[c], outputs, start, full, blocks
+            batch = 0 if c < cut else 1
+            base = starts[cut] if batch else 0
+            sent = ([hiddens[batch]] if batch in hiddens else [], (full if batch else starts[cut]) - base, start - base)
+            (*outputs, hiddens[batch]), token = run_chunk(
+                token, info, grouped, own[c], partner[c], outputs, start, full, blocks, sent
             )
         else:
-            batch = [hiddens[i] for i in (range(cut) if c == 0 else range(cut, last + 1))]
-            hidden, token = hold(token, jnp.concatenate(batch, axis=2), returned[:c])
+            hidden, token = hold(token, hiddens[c], returned[:c])
             returned.append(exchange(hidden))
 
     finished = [

time: 397 us -> 395 us (level)
  transfers between devices with their start and end apart: 14 -> 14, of which waited for: 9 -> 9; matrix products, arithmetic and copies ran while one was open for 7% -> 6% of each run, Pallas kernels for 16% -> 17%
where the time goes in v19:
time: 395 us; the launch traced here: 392 us
  waiting for transfers between devices  203 us (51%)
  starting transfers between devices  78.1 us (20%)
  Pallas kernels  64.8 us (16%)
  between operations  14.4 us (4%)
  local copies, waits for them, and re-layouts  12.6 us (3%)
  other arithmetic  11.9 us (3%)
  matrix products  7.75 us (2%)
    all_to_all x8, waiting for transfers between devices, exchange(): return lax.all_to_all(pieces, 'expert', 0, 0, tiled=True)  130 us
    all_to_all x8, starting transfers between devices, exchange(): return lax.all_to_all(pieces, 'expert', 0, 0, tiled=True)  67.5 us
    pallas_call x18, Pallas kernels, step_call(): pl.pallas_call(ordered, out_shape=[*out_shape, TOKEN], in_specs=[*in_spec...  64.8 us
    ppermute x1, waiting for transfers between devices, shards(): nearby = lax.ppermute(both, 'expert', beside)  48.8 us
    ppermute x3, waiting for transfers between devices, shards(): partner[c] = lax.ppermute(own[c], 'groups', partners)  15.8 us
    ppermute x1, waiting for transfers between devices, shards(): opposite = lax.ppermute(tokens, 'expert', across)  8.06 us
  transfers between devices with their start and end apart: 14, of which 9 were waited for; matrix products, arithmetic and copies ran while one was open for 6% of the time, Pallas kernels for 17%

profile of v19, /device:TPU:0, one launch (start us, length us, event | category | flops | bytes accessed | tf_op | source)
XLA Modules:
  0.0 392.4 jit_solution(6836259492944354851)
XLA Ops:
  12.5 5.6 %pack.3 = (bf16[16,2,160,512]{3,2,1,0:T(8,128)(2,1)}, f32[8,128]{1,0:T(8,128)}) custom-call(s32[2]{0:T(128)} %pad_add_fusion.refs_0_, bf16[2,2560,768]{2,1,0:T(8,128)(2,1)} %refs_1_.5, bf16[2,2560,768]{2,1,0:T(8,128)(2,1)} %refs_2_.5, f32[8,128]{1,0:T(8,128)} %broadcast_in_dim.40.refs_3_), custom_call_target="tpu_custom_call" | custom-call | tf_op jit(solution)/shard_map/pack/pallas_call | solution.py:32
  18.1 8.1 %collective-permute-done.refs_1_ = bf16[64,2560]{1,0:T(8,128)(2,1)S(1)} collective-permute-done((bf16[64,2560]{1,0:T(8,128)(2,1)}, bf16[64,2560]{1,0:T(8,128)(2,1)S(1)}, u32[]{:S(2)}, u32[]{:S(2)}) %collective-permute-start) | collective-permute-done | bytes 327712 | tf_op jit(solution)/shard_map/ppermute | solution.py:366
  26.9 6.0 %all-to-all-start = ((bf16[16,2,160,512]{3,2,1,0:T(8,128)(2,1)}), bf16[16,2,160,512]{3,2,1,0:T(8,128)(2,1)}, u32[]{:S(2)}, u32[]{:S(2)}) async-start(bf16[16,2,160,512]{3,2,1,0:T(8,128)(2,1)} %get-tuple-element.46), calls=%async_computation | async-start | bytes 10485760 | tf_op jit(solution)/shard_map/all_to_all | solution.py:326
  33.4 6.3 %fusion.6 = s32[16,64,16]{2,0,1:T(8,128)S(1)} fusion(s32[16,64,16]{2,0,1:T(8,128)S(1)} %copy.63), kind=kOutput, calls=%fused_computation.37 | output fusion | flops 1032192 | bytes 131072 | tf_op jit(solution)/shard_map/jit(cumsum)/reduce_window_sum | solution.py:301
  49.4 79.5 %all-to-all-done.refs_1_.refs_2_ = bf16[16,2,160,512]{3,2,1,0:T(8,128)(2,1)} async-done(((bf16[16,2,160,512]{3,2,1,0:T(8,128)(2,1)}), bf16[16,2,160,512]{3,2,1,0:T(8,128)(2,1)}, u32[]{:S(2)}, u32[]{:S(2)}) %all-to-all-start) | async-done | bytes 5242912 | tf_op jit(solution)/shard_map/all_to_all | solution.py:326
  129.0 24.0 %all-to-all-start.1 = ((bf16[16,2,160,128]{3,2,1,0:T(8,128)(2,1)}), bf16[16,2,160,128]{3,2,1,0:T(8,128)(2,1)S(1)}, u32[]{:S(2)}, u32[]{:S(2)}) async-start(bf16[16,2,160,128]{3,2,1,0:T(8,128)(2,1)} %get-tuple-element.54), calls=%async_computation.1 | async-start | bytes 2621440 | tf_op jit(solution)/shard_map/all_to_all | solution.py:326
  154.8 10.9 %merge.3 = (bf16[16,160,512]{2,1,0:T(8,128)(2,1)}, f32[8,128]{1,0:T(8,128)}) custom-call(s32[32]{0:T(128)} %bitcast.50, f32[960]{0:T(1024)} %mul.47.refs_1_, bf16[16,2,160,512]{3,2,1,0:T(8,128)(2,1)} %all-to-all-done.refs_1_.refs_2_, f32[8,128]{1,0:T(8,128)} %get-tuple-element.50.refs_3_), custom_call_target="tpu_custom_call" | custom-call | tf_op jit(solution)/shard_map/merge/pallas_call | solution.py:32
  170.7 9.7 %all-to-all-done.1.refs_1_.refs_2_ = bf16[16,2,160,128]{3,2,1,0:T(8,128)(2,1)S(1)} async-done(((bf16[16,2,160,128]{3,2,1,0:T(8,128)(2,1)}), bf16[16,2,160,128]{3,2,1,0:T(8,128)(2,1)S(1)}, u32[]{:S(2)}, u32[]{:S(2)}) %all-to-all-start.1) | async-done | bytes 1310752 | tf_op jit(solution)/shard_map/all_to_all | solution.py:326
  181.4 8.0 %all-to-all-start.2 = ((bf16[16,160,512]{2,1,0:T(8,128)(2,1)}), bf16[16,160,512]{2,1,0:T(8,128)(2,1)S(1)}, u32[]{:S(2)}, u32[]{:S(2)}) async-start(bf16[16,160,512]{2,1,0:T(8,128)(2,1)} %get-tuple-element.61), calls=%async_computation.2 | async-start | bytes 5242880 | tf_op jit(solution)/shard_map/all_to_all | solution.py:326
  191.5 8.6 %merge.4 = (bf16[16,160,128]{2,1,0:T(8,128)(2,1)}, f32[8,128]{1,0:T(8,128)}) custom-call(s32[32]{0:T(128)} %bitcast.51, f32[960]{0:T(1024)} %mul.47.refs_1_, bf16[16,2,160,128]{3,2,1,0:T(8,128)(2,1)} %copy-done.1, f32[8,128]{1,0:T(8,128)} %get-tuple-element.57.refs_3_), custom_call_target="tpu_custom_call" | custom-call | tf_op jit(solution)/shard_map/merge/pallas_call | solution.py:32
  200.1 48.8 %collective-permute-done.1.refs_2_ = bf16[2,64,2560]{2,1,0:T(8,128)(2,1)} collective-permute-done((bf16[2,64,2560]{2,1,0:T(8,128)(2,1)}, bf16[2,64,2560]{2,1,0:T(8,128)(2,1)}, u32[]{:S(2)}, u32[]{:S(2)}) %collective-permute-start.1) | collective-permute-done | bytes 655392 | tf_op jit(solution)/shard_map/ppermute | solution.py:378
  252.8 5.0 %all-to-all-start.3 = ((bf16[16,2,160,128]{3,2,1,0:T(8,128)(2,1)}), bf16[16,2,160,128]{3,2,1,0:T(8,128)(2,1)S(1)}, u32[]{:S(2)}, u32[]{:S(2)}) async-start(bf16[16,2,160,128]{3,2,1,0:T(8,128)(2,1)} %get-tuple-element.63), calls=%async_computation.3 | async-start | bytes 2621440 | tf_op jit(solution)/shard_map/all_to_all | solution.py:326
  259.3 26.0 %all-to-all-done.3.refs_1_.refs_2_ = bf16[16,2,160,128]{3,2,1,0:T(8,128)(2,1)S(1)} async-done(((bf16[16,2,160,128]{3,2,1,0:T(8,128)(2,1)}), bf16[16,2,160,128]{3,2,1,0:T(8,128)(2,1)S(1)}, u32[]{:S(2)}, u32[]{:S(2)}) %all-to-all-start.3) | async-done | bytes 1310752 | tf_op jit(solution)/shard_map/all_to_all | solution.py:326
  286.3 8.0 %all-to-all-start.5 = ((bf16[16,160,128]{2,1,0:T(8,128)(2,1)}), bf16[16,160,128]{2,1,0:T(8,128)(2,1)S(1)}, u32[]{:S(2)}, u32[]{:S(2)}) async-start(bf16[16,160,128]{2,1,0:T(8,128)(2,1)} %get-tuple-element.68), calls=%async_computation.5 | async-start | bytes 1310720 | tf_op jit(solution)/shard_map/all_to_all | solution.py:326
  294.4 8.7 %merge.5 = (bf16[16,160,128]{2,1,0:T(8,128)(2,1)}, f32[8,128]{1,0:T(8,128)}) custom-call(s32[32]{0:T(128)} %bitcast.52, f32[960]{0:T(1024)} %mul.47.refs_1_, bf16[16,2,160,128]{3,2,1,0:T(8,128)(2,1)} %copy-done.2, f32[8,128]{1,0:T(8,128)} %get-tuple-element.66.refs_3_), custom_call_target="tpu_custom_call" | custom-call | tf_op jit(solution)/shard_map/merge/pallas_call | solution.py:32
  303.0 7.9 %all-to-all-done.5 = bf16[16,160,128]{2,1,0:T(8,128)(2,1)S(1)} async-done(((bf16[16,160,128]{2,1,0:T(8,128)(2,1)}), bf16[16,160,128]{2,1,0:T(8,128)(2,1)S(1)}, u32[]{:S(2)}, u32[]{:S(2)}) %all-to-all-start.5) | async-done | bytes 655392 | tf_op jit(solution)/shard_map/all_to_all | solution.py:326
  317.3 5.6 %convolution_convert_fusion = bf16[16,48,2560]{2,1,0:T(8,128)(2,1)} fusion(bf16[16,64,2560]{2,1,0:T(8,128)(2,1)} %all-gather.2.cloned.1.call-done, s32[16,64]{1,0:T(8,128)S(1)} %bitcast.46, pred[16,64]{1,0:T(8,128)(4,1)S(1)} %bitcast.49), kind=kOutput, calls=%fused_computation.1 | convolution fusion | flops 253722624 | bytes 9180160 | tf_op jit(solution)/shard_map/jct,jtd->jcd/dot_general | solution.py:382
  322.9 9.9 %run_chunk.3 = (bf16[1,2560,768]{2,1,0:T(8,128)(2,1)}, bf16[1,2560,768]{2,1,0:T(8,128)(2,1)}, bf16[16,48,640]{2,1,0:T(8,128)(2,1)}, f32[8,128]{1,0:T(8,128)}) custom-call(s32[2]{0:T(128)} %pad_add_fusion.refs_0_, bf16[768,2560]{1,0:T(8,128)(2,1)} %bitcast.32, bf16[2560,512]{1,0:T(8,128)(2,1)} %bitcast.37, bf16[2560,512]{1,0:T(8,128)(2,1)} %collective-permute-done.4.refs_3_, ...), custom_call_target="tpu_custom_call" | custom-call | tf_op jit(solution)/shard_map/run_chunk/pallas_call | solution.py:32
  333.8 5.4 %run_chunk.4 = (bf16[1,2560,768]{2,1,0:T(8,128)(2,1)}, bf16[1,2560,768]{2,1,0:T(8,128)(2,1)}, bf16[16,48,640]{2,1,0:T(8,128)(2,1)}, f32[8,128]{1,0:T(8,128)}) custom-call(s32[2]{0:T(128)} %pad_add_fusion.refs_0_, bf16[768,2560]{1,0:T(8,128)(2,1)} %bitcast.33, bf16[2560,128]{1,0:T(8,128)(2,1)} %bitcast.42, ...), custom_call_target="tpu_custom_call", output_to_operand_aliasing={{0}: (4, {}), {1}: (5, {}), {2}: (6, {})} | custom-call | tf_op jit(solution)/shard_map/run_chunk/pallas_call | solution.py:32
  339.2 6.0 %all-to-all-start.6 = ((bf16[16,48,640]{2,1,0:T(8,128)(2,1)}), bf16[16,48,640]{2,1,0:T(8,128)(2,1)S(1)}, u32[]{:S(2)}, u32[]{:S(2)}) async-start(bf16[16,48,640]{2,1,0:T(8,128)(2,1)} %get-tuple-element.81), calls=%async_computation.6 | async-start | bytes 1966080 | tf_op jit(solution)/shard_map/all_to_all | solution.py:326
  346.5 15.7 %collective-permute-done.2.refs_3_ = bf16[2560,128]{1,0:T(8,128)(2,1)S(1)} collective-permute-done((bf16[2560,128]{1,0:T(8,128)(2,1)S(1)}, bf16[2560,128]{1,0:T(8,128)(2,1)S(1)}, u32[]{:S(2)}, u32[]{:S(2)}) %collective-permute-start.2) | collective-permute-done | bytes 655392 | tf_op jit(solution)/shard_map/ppermute | solution.py:401
  363.0 5.3 %run_chunk.5 = (bf16[1,2560,768]{2,1,0:T(8,128)(2,1)}, bf16[1,2560,768]{2,1,0:T(8,128)(2,1)}, bf16[16,48,128]{2,1,0:T(8,128)(2,1)}, f32[8,128]{1,0:T(8,128)}) custom-call(s32[2]{0:T(128)} %pad_add_fusion.refs_0_, bf16[768,2560]{1,0:T(8,128)(2,1)} %bitcast.34, bf16[2560,128]{1,0:T(8,128)(2,1)} %bitcast.40, ...), custom_call_target="tpu_custom_call", output_to_operand_aliasing={{0}: (4, {}), {1}: (5, {})} | custom-call | tf_op jit(solution)/shard_map/run_chunk/pallas_call | solution.py:32
  369.3 5.7 %all-to-all-start.7 = ((bf16[16,48,128]{2,1,0:T(8,128)(2,1)}), bf16[16,48,128]{2,1,0:T(8,128)(2,1)S(1)}, u32[]{:S(2)}, u32[]{:S(2)}) async-start(bf16[16,48,128]{2,1,0:T(8,128)(2,1)} %get-tuple-element.84), calls=%async_computation.7 | async-start | bytes 393216 | tf_op jit(solution)/shard_map/all_to_all | solution.py:326
  376.9 7.2 %all-to-all-done.7 = bf16[16,48,128]{2,1,0:T(8,128)(2,1)S(1)} async-done(((bf16[16,48,128]{2,1,0:T(8,128)(2,1)}), bf16[16,48,128]{2,1,0:T(8,128)(2,1)S(1)}, u32[]{:S(2)}, u32[]{:S(2)}) %all-to-all-start.7) | async-done | bytes 196640 | tf_op jit(solution)/shard_map/all_to_all | solution.py:326
  (89 shorter events, 46.1 us)
Async XLA Ops:
  7.2 19.0 %collective-permute-start = (bf16[64,2560]{1,0:T(8,128)(2,1)}, bf16[64,2560]{1,0:T(8,128)(2,1)S(1)}, u32[]{:S(2)}, u32[]{:S(2)}) collective-permute-start(bf16[64,2560]{1,0:T(8,128)(2,1)} %refs_0_.1), channel_id=1, source_target_pairs={{0,8},{1,9},{2,10},{3,11},{4,12},{5,13},{6,14},{7,15},{8,0},{9,1},... | collective-permute-start | bytes 983048 | tf_op jit(solution)/shard_map/ppermute | solution.py:366
  26.9 6.1 %copy-start.11 = (s32[1024,6]{0,1:T(8,128)S(1)}, s32[1024,6]{0,1:T(8,128)}, u32[]{:S(2)}) copy-start(s32[1024,6]{0,1:T(8,128)} %param.9) | copy-start | bytes 73732
  26.9 102.0 %all-to-all-start = ((bf16[16,2,160,512]{3,2,1,0:T(8,128)(2,1)}), bf16[16,2,160,512]{3,2,1,0:T(8,128)(2,1)}, u32[]{:S(2)}, u32[]{:S(2)}) async-start(bf16[16,2,160,512]{3,2,1,0:T(8,128)(2,1)} %get-tuple-element.46), calls=%async_computation | async-start | bytes 10485760 | tf_op jit(solution)/shard_map/all_to_all | solution.py:326
  128.9 24.0 %copy-start.12 = (s32[32,1]{0,1:T(1,128)S(1)}, s32[32,1]{0,1:T(1,128)}, u32[]{:S(2)}) copy-start(s32[32,1]{0,1:T(1,128)} %param.14) | copy-start | bytes 388
  128.9 24.0 %copy-start.13 = (f32[32]{0:T(128)S(1)}, f32[32]{0:T(128)}, u32[]{:S(2)}) copy-start(f32[32]{0:T(128)} %param.15) | copy-start | bytes 388
  128.9 24.3 %copy-start.9 = (f32[32,20,6]{0,1,2:T(8,128)S(1)}, f32[32,20,6]{0,1,2:T(8,128)}, u32[]{:S(2)}) copy-start(f32[32,20,6]{0,1,2:T(8,128)} %param.13) | copy-start | bytes 46084
  128.9 24.3 %copy-start.10 = (f32[32,20,6]{0,1,2:T(8,128)S(1)}, f32[32,20,6]{0,1,2:T(8,128)}, u32[]{:S(2)}) copy-start(f32[32,20,6]{0,1,2:T(8,128)} %param.12) | copy-start | bytes 46084
  129.0 51.4 %all-to-all-start.1 = ((bf16[16,2,160,128]{3,2,1,0:T(8,128)(2,1)}), bf16[16,2,160,128]{3,2,1,0:T(8,128)(2,1)S(1)}, u32[]{:S(2)}, u32[]{:S(2)}) async-start(bf16[16,2,160,128]{3,2,1,0:T(8,128)(2,1)} %get-tuple-element.54), calls=%async_computation.1 | async-start | bytes 2621440 | tf_op jit(solution)/shard_map/all_to_all | solution.py:326
  180.4 1.1 copy-start.1
  181.4 69.9 %all-to-all-start.2 = ((bf16[16,160,512]{2,1,0:T(8,128)(2,1)}), bf16[16,160,512]{2,1,0:T(8,128)(2,1)S(1)}, u32[]{:S(2)}, u32[]{:S(2)}) async-start(bf16[16,160,512]{2,1,0:T(8,128)(2,1)} %get-tuple-element.61), calls=%async_computation.2 | async-start | bytes 5242880 | tf_op jit(solution)/shard_map/all_to_all | solution.py:326
  189.4 127.9 %all-gather.2.cloned.1.call-start = ((), (), s32[]{:S(2)}) async-start(), calls=%async_computation.8 | async-start | bytes 6553600 | tf_op jit(solution)/shard_map/all_gather | solution.py:381
  189.5 59.4 %collective-permute-start.1 = (bf16[2,64,2560]{2,1,0:T(8,128)(2,1)}, bf16[2,64,2560]{2,1,0:T(8,128)(2,1)}, u32[]{:S(2)}, u32[]{:S(2)}) collective-permute-start(bf16[2,64,2560]{2,1,0:T(8,128)(2,1)} %get-tuple-element.53.refs_1_), channel_id=1, source_target_pairs={{0,4},{1,5},{2,6},{3,7},{4,0},{5,1},{6,2},{7,3},{8,12},{9,13},{10,... | collective-permute-start | bytes 1966088 | tf_op jit(solution)/shard_map/ppermute | solution.py:378
  251.3 1.5 copy-start
  252.8 32.5 %all-to-all-start.3 = ((bf16[16,2,160,128]{3,2,1,0:T(8,128)(2,1)}), bf16[16,2,160,128]{3,2,1,0:T(8,128)(2,1)S(1)}, u32[]{:S(2)}, u32[]{:S(2)}) async-start(bf16[16,2,160,128]{3,2,1,0:T(8,128)(2,1)} %get-tuple-element.63), calls=%async_computation.3 | async-start | bytes 2621440 | tf_op jit(solution)/shard_map/all_to_all | solution.py:326
  257.8 65.2 %collective-permute-start.4 = (bf16[2560,512]{1,0:T(8,128)(2,1)}, bf16[2560,512]{1,0:T(8,128)(2,1)}, u32[]{:S(2)}, u32[]{:S(2)}) collective-permute-start(bf16[2560,512]{1,0:T(8,128)(2,1)} %bitcast.36), channel_id=1, source_target_pairs={{0,16},{16,0},{1,17},{17,1},{2,18},{18,2},{3,19},{19,3},{4,20},{20... | collective-permute-start | bytes 7864328 | tf_op jit(solution)/shard_map/ppermute | solution.py:401
  285.3 1.1 copy-start.2
  286.3 24.7 %all-to-all-start.5 = ((bf16[16,160,128]{2,1,0:T(8,128)(2,1)}), bf16[16,160,128]{2,1,0:T(8,128)(2,1)S(1)}, u32[]{:S(2)}, u32[]{:S(2)}) async-start(bf16[16,160,128]{2,1,0:T(8,128)(2,1)} %get-tuple-element.68), calls=%async_computation.5 | async-start | bytes 1310720 | tf_op jit(solution)/shard_map/all_to_all | solution.py:326
  311.0 12.0 %copy-start.5 = (bf16[16,160,128]{2,1,0:T(8,128)(2,1)}, bf16[16,160,128]{2,1,0:T(8,128)(2,1)S(1)}, u32[]{:S(2)}) copy-start(bf16[16,160,128]{2,1,0:T(8,128)(2,1)S(1)} %all-to-all-done.5) | copy-start | bytes 1966084
  311.0 28.2 %all-to-all-start.4 = ((bf16[16,160,128]{2,1,0:T(8,128)(2,1)}), bf16[16,160,128]{2,1,0:T(8,128)(2,1)S(1)}, u32[]{:S(2)}, u32[]{:S(2)}) async-start(bf16[16,160,128]{2,1,0:T(8,128)(2,1)} %get-tuple-element.67), calls=%async_computation.4 | async-start | bytes 1310720 | tf_op jit(solution)/shard_map/all_to_all | solution.py:326
  315.8 17.1 %collective-permute-start.3 = (bf16[2560,128]{1,0:T(8,128)(2,1)S(1)}, bf16[2560,128]{1,0:T(8,128)(2,1)S(1)}, u32[]{:S(2)}, u32[]{:S(2)}) collective-permute-start(bf16[2560,128]{1,0:T(8,128)(2,1)S(1)} %bitcast.41), channel_id=1, source_target_pairs={{0,16},{16,0},{1,17},{17,1},{2,18},{18,2},{3,19},{19,3},{4,20},{20... | collective-permute-start | bytes 1966088 | tf_op jit(solution)/shard_map/ppermute | solution.py:401
  339.2 23.0 %copy-start.4 = (bf16[16,160,128]{2,1,0:T(8,128)(2,1)}, bf16[16,160,128]{2,1,0:T(8,128)(2,1)S(1)}, u32[]{:S(2)}) copy-start(bf16[16,160,128]{2,1,0:T(8,128)(2,1)S(1)} %all-to-all-done.4) | copy-start | bytes 1966084
  339.2 29.2 %all-to-all-start.6 = ((bf16[16,48,640]{2,1,0:T(8,128)(2,1)}), bf16[16,48,640]{2,1,0:T(8,128)(2,1)S(1)}, u32[]{:S(2)}, u32[]{:S(2)}) async-start(bf16[16,48,640]{2,1,0:T(8,128)(2,1)} %get-tuple-element.81), calls=%async_computation.6 | async-start | bytes 1966080 | tf_op jit(solution)/shard_map/all_to_all | solution.py:326
  345.1 17.0 %collective-permute-start.2 = (bf16[2560,128]{1,0:T(8,128)(2,1)S(1)}, bf16[2560,128]{1,0:T(8,128)(2,1)S(1)}, u32[]{:S(2)}, u32[]{:S(2)}) collective-permute-start(bf16[2560,128]{1,0:T(8,128)(2,1)S(1)} %bitcast.39), channel_id=1, source_target_pairs={{0,16},{16,0},{1,17},{17,1},{2,18},{18,2},{3,19},{19,3},{4,20},{20... | collective-permute-start | bytes 1966088 | tf_op jit(solution)/shard_map/ppermute | solution.py:401
  369.3 14.7 %all-to-all-start.7 = ((bf16[16,48,128]{2,1,0:T(8,128)(2,1)}), bf16[16,48,128]{2,1,0:T(8,128)(2,1)S(1)}, u32[]{:S(2)}, u32[]{:S(2)}) async-start(bf16[16,48,128]{2,1,0:T(8,128)(2,1)} %get-tuple-element.84), calls=%async_computation.7 | async-start | bytes 393216 | tf_op jit(solution)/shard_map/all_to_all | solution.py:326
  (4 other events, 3.4 us)
Sparse Core Ops, SparseCore 0:
  251.4 58.4 all-gather.1

commit v20 on v19

--- a/solution.py
+++ b/solution.py
@@ -95,6 +95,10 @@
         ],
         name="pack",
     )
+
+
+def corner(part):
+    return part[(slice(0, 1),) * (part.ndim - 2) + (slice(0, 16), slice(0, 128))]
 
 
 def hold(token, value, earlier):
@@ -390,13 +394,15 @@
             elif c == 1:
                 pieces[c], token = hold(token, pieces[c], [gathered[0], placing, picking])
             else:
-                pieces[c], token = hold(token, pieces[c], [own[c - 2]])
+                pieces[c], token = hold(token, pieces[c], [corner(own[c - 2])])
             gathered[c] = exchange(pieces[c])
         elif name == "sum":
             merged[c], token = merge(token, slots, factors, gathered[c], start, blocks_of_rows)
         elif name == "back":
             if c < last:
-                merged[c], token = hold(token, merged[c], [gathered[c + 1]])
+                merged[c], token = hold(
+                    token, merged[c], [gathered[c + 1] if c else corner(gathered[c + 1])]
+                )
             own[c] = exchange(merged[c]).reshape(depth, width)
             partner[c] = lax.ppermute(own[c], "groups", partners)
         elif name == "run":
@@ -407,7 +413,7 @@
                 token, info, grouped, own[c], partner[c], outputs, start, full, blocks, sent
             )
         else:
-            hidden, token = hold(token, hiddens[c], returned[:c])
+            hidden, token = hold(token, hiddens[c], [corner(part) for part in returned[:c]])
             returned.append(exchange(hidden))
 
     finished = [

time: 395 us -> 394 us (level)
  transfers between devices with their start and end apart: 14 -> 14, of which waited for: 9 -> 8; matrix products, arithmetic and copies ran while one was open for 6% -> 6% of each run, Pallas kernels for 17% -> 17%
where the time goes in v20:
time: 394 us; the launch traced here: 392 us
  waiting for transfers between devices  204 us (52%)
  starting transfers between devices  78.1 us (20%)
  Pallas kernels  64.9 us (16%)
  between operations  14.4 us (4%)
  local copies, waits for them, and re-layouts  12.2 us (3%)
  other arithmetic  11.8 us (3%)
  matrix products  6.55 us (2%)
    all_to_all x8, waiting for transfers between devices, exchange(): return lax.all_to_all(pieces, 'expert', 0, 0, tiled=True)  131 us
    all_to_all x8, starting transfers between devices, exchange(): return lax.all_to_all(pieces, 'expert', 0, 0, tiled=True)  67.6 us
    pallas_call x18, Pallas kernels, step_call(): pl.pallas_call(ordered, out_shape=[*out_shape, TOKEN], in_specs=[*in_spec...  64.9 us
    ppermute x1, waiting for transfers between devices, shards(): nearby = lax.ppermute(both, 'expert', beside)  48.8 us
    ppermute x3, waiting for transfers between devices, shards(): partner[c] = lax.ppermute(own[c], 'groups', partners)  15.8 us
    ppermute x1, waiting for transfers between devices, shards(): opposite = lax.ppermute(tokens, 'expert', across)  8.15 us
  transfers between devices with their start and end apart: 14, of which 8 were waited for; matrix products, arithmetic and copies ran while one was open for 6% of the time, Pallas kernels for 17%

profile of v20, /device:TPU:0, one launch (start us, length us, event | category | flops | bytes accessed | tf_op | source)
XLA Modules:
  0.0 392.1 jit_solution(2318366331148987650)
XLA Ops:
  12.4 5.6 %pack.3 = (bf16[16,2,160,512]{3,2,1,0:T(8,128)(2,1)}, f32[8,128]{1,0:T(8,128)}) custom-call(s32[2]{0:T(128)} %pad_add_fusion.refs_0_, bf16[2,2560,768]{2,1,0:T(8,128)(2,1)} %refs_1_.5, bf16[2,2560,768]{2,1,0:T(8,128)(2,1)} %refs_2_.5, f32[8,128]{1,0:T(8,128)} %broadcast_in_dim.40.refs_3_), custom_call_target="tpu_custom_call" | custom-call | tf_op jit(solution)/shard_map/pack/pallas_call | solution.py:32
  18.1 8.2 %collective-permute-done.refs_1_ = bf16[64,2560]{1,0:T(8,128)(2,1)S(1)} collective-permute-done((bf16[64,2560]{1,0:T(8,128)(2,1)}, bf16[64,2560]{1,0:T(8,128)(2,1)S(1)}, u32[]{:S(2)}, u32[]{:S(2)}) %collective-permute-start) | collective-permute-done | bytes 327712 | tf_op jit(solution)/shard_map/ppermute | solution.py:370
  26.9 6.0 %all-to-all-start = ((bf16[16,2,160,512]{3,2,1,0:T(8,128)(2,1)}), bf16[16,2,160,512]{3,2,1,0:T(8,128)(2,1)}, u32[]{:S(2)}, u32[]{:S(2)}) async-start(bf16[16,2,160,512]{3,2,1,0:T(8,128)(2,1)} %get-tuple-element.46), calls=%async_computation | async-start | bytes 10485760 | tf_op jit(solution)/shard_map/all_to_all | solution.py:330
  33.4 6.3 %fusion.6 = s32[16,64,16]{2,0,1:T(8,128)S(1)} fusion(s32[16,64,16]{2,0,1:T(8,128)S(1)} %copy.63), kind=kOutput, calls=%fused_computation.37 | output fusion | flops 1032192 | bytes 131072 | tf_op jit(solution)/shard_map/jit(cumsum)/reduce_window_sum | solution.py:305
  49.4 79.5 %all-to-all-done.refs_1_.refs_2_ = bf16[16,2,160,512]{3,2,1,0:T(8,128)(2,1)} async-done(((bf16[16,2,160,512]{3,2,1,0:T(8,128)(2,1)}), bf16[16,2,160,512]{3,2,1,0:T(8,128)(2,1)}, u32[]{:S(2)}, u32[]{:S(2)}) %all-to-all-start) | async-done | bytes 5242912 | tf_op jit(solution)/shard_map/all_to_all | solution.py:330
  129.0 24.0 %all-to-all-start.1 = ((bf16[16,2,160,128]{3,2,1,0:T(8,128)(2,1)}), bf16[16,2,160,128]{3,2,1,0:T(8,128)(2,1)S(1)}, u32[]{:S(2)}, u32[]{:S(2)}) async-start(bf16[16,2,160,128]{3,2,1,0:T(8,128)(2,1)} %get-tuple-element.54), calls=%async_computation.1 | async-start | bytes 2621440 | tf_op jit(solution)/shard_map/all_to_all | solution.py:330
  154.8 10.9 %merge.3 = (bf16[16,160,512]{2,1,0:T(8,128)(2,1)}, f32[8,128]{1,0:T(8,128)}) custom-call(s32[32]{0:T(128)} %bitcast.50, f32[960]{0:T(1024)} %mul.47.refs_1_, bf16[16,2,160,512]{3,2,1,0:T(8,128)(2,1)} %all-to-all-done.refs_1_.refs_2_, f32[8,128]{1,0:T(8,128)} %get-tuple-element.50.refs_3_), custom_call_target="tpu_custom_call" | custom-call | tf_op jit(solution)/shard_map/merge/pallas_call | solution.py:32
  170.7 9.7 %all-to-all-done.1.refs_2_ = bf16[16,2,160,128]{3,2,1,0:T(8,128)(2,1)S(1)} async-done(((bf16[16,2,160,128]{3,2,1,0:T(8,128)(2,1)}), bf16[16,2,160,128]{3,2,1,0:T(8,128)(2,1)S(1)}, u32[]{:S(2)}, u32[]{:S(2)}) %all-to-all-start.1) | async-done | bytes 1310752 | tf_op jit(solution)/shard_map/all_to_all | solution.py:330
  181.4 8.0 %all-to-all-start.2 = ((bf16[16,160,512]{2,1,0:T(8,128)(2,1)}), bf16[16,160,512]{2,1,0:T(8,128)(2,1)S(1)}, u32[]{:S(2)}, u32[]{:S(2)}) async-start(bf16[16,160,512]{2,1,0:T(8,128)(2,1)} %get-tuple-element.61), calls=%async_computation.2 | async-start | bytes 5242880 | tf_op jit(solution)/shard_map/all_to_all | solution.py:330
  191.5 8.6 %merge.4 = (bf16[16,160,128]{2,1,0:T(8,128)(2,1)}, f32[8,128]{1,0:T(8,128)}) custom-call(s32[32]{0:T(128)} %bitcast.51, f32[960]{0:T(1024)} %mul.47.refs_1_, bf16[16,2,160,128]{3,2,1,0:T(8,128)(2,1)} %copy-done.2, f32[8,128]{1,0:T(8,128)} %get-tuple-element.57.refs_3_), custom_call_target="tpu_custom_call" | custom-call | tf_op jit(solution)/shard_map/merge/pallas_call | solution.py:32
  200.1 48.8 %collective-permute-done.1.refs_2_ = bf16[2,64,2560]{2,1,0:T(8,128)(2,1)} collective-permute-done((bf16[2,64,2560]{2,1,0:T(8,128)(2,1)}, bf16[2,64,2560]{2,1,0:T(8,128)(2,1)}, u32[]{:S(2)}, u32[]{:S(2)}) %collective-permute-start.1) | collective-permute-done | bytes 655392 | tf_op jit(solution)/shard_map/ppermute | solution.py:382
  252.8 5.0 %all-to-all-start.3 = ((bf16[16,2,160,128]{3,2,1,0:T(8,128)(2,1)}), bf16[16,2,160,128]{3,2,1,0:T(8,128)(2,1)S(1)}, u32[]{:S(2)}, u32[]{:S(2)}) async-start(bf16[16,2,160,128]{3,2,1,0:T(8,128)(2,1)} %get-tuple-element.63), calls=%async_computation.3 | async-start | bytes 2621440 | tf_op jit(solution)/shard_map/all_to_all | solution.py:330
  259.3 26.0 %all-to-all-done.3.refs_1_.refs_2_ = bf16[16,2,160,128]{3,2,1,0:T(8,128)(2,1)S(1)} async-done(((bf16[16,2,160,128]{3,2,1,0:T(8,128)(2,1)}), bf16[16,2,160,128]{3,2,1,0:T(8,128)(2,1)S(1)}, u32[]{:S(2)}, u32[]{:S(2)}) %all-to-all-start.3) | async-done | bytes 1310752 | tf_op jit(solution)/shard_map/all_to_all | solution.py:330
  286.3 8.0 %all-to-all-start.5 = ((bf16[16,160,128]{2,1,0:T(8,128)(2,1)}), bf16[16,160,128]{2,1,0:T(8,128)(2,1)S(1)}, u32[]{:S(2)}, u32[]{:S(2)}) async-start(bf16[16,160,128]{2,1,0:T(8,128)(2,1)} %get-tuple-element.68), calls=%async_computation.5 | async-start | bytes 1310720 | tf_op jit(solution)/shard_map/all_to_all | solution.py:330
  294.4 8.7 %merge.5 = (bf16[16,160,128]{2,1,0:T(8,128)(2,1)}, f32[8,128]{1,0:T(8,128)}) custom-call(s32[32]{0:T(128)} %bitcast.52, f32[960]{0:T(1024)} %mul.47.refs_1_, bf16[16,2,160,128]{3,2,1,0:T(8,128)(2,1)} %copy-done, f32[8,128]{1,0:T(8,128)} %get-tuple-element.66.refs_3_), custom_call_target="tpu_custom_call" | custom-call | tf_op jit(solution)/shard_map/merge/pallas_call | solution.py:32
  303.0 7.9 %all-to-all-done.5 = bf16[16,160,128]{2,1,0:T(8,128)(2,1)S(1)} async-done(((bf16[16,160,128]{2,1,0:T(8,128)(2,1)}), bf16[16,160,128]{2,1,0:T(8,128)(2,1)S(1)}, u32[]{:S(2)}, u32[]{:S(2)}) %all-to-all-start.5) | async-done | bytes 655392 | tf_op jit(solution)/shard_map/all_to_all | solution.py:330
  317.3 5.6 %convolution_convert_fusion = bf16[16,48,2560]{2,1,0:T(8,128)(2,1)} fusion(bf16[16,64,2560]{2,1,0:T(8,128)(2,1)} %all-gather.2.cloned.1.call-done, s32[16,64]{1,0:T(8,128)S(1)} %bitcast.46, pred[16,64]{1,0:T(8,128)(4,1)S(1)} %bitcast.49), kind=kOutput, calls=%fused_computation.1 | convolution fusion | flops 253722624 | bytes 9180160 | tf_op jit(solution)/shard_map/jct,jtd->jcd/dot_general | solution.py:386
  323.0 9.9 %run_chunk.3 = (bf16[1,2560,768]{2,1,0:T(8,128)(2,1)}, bf16[1,2560,768]{2,1,0:T(8,128)(2,1)}, bf16[16,48,640]{2,1,0:T(8,128)(2,1)}, f32[8,128]{1,0:T(8,128)}) custom-call(s32[2]{0:T(128)} %pad_add_fusion.refs_0_, bf16[768,2560]{1,0:T(8,128)(2,1)} %bitcast.32, bf16[2560,512]{1,0:T(8,128)(2,1)} %bitcast.37, bf16[2560,512]{1,0:T(8,128)(2,1)} %collective-permute-done.4.refs_3_, ...), custom_call_target="tpu_custom_call" | custom-call | tf_op jit(solution)/shard_map/run_chunk/pallas_call | solution.py:32
  333.8 5.4 %run_chunk.4 = (bf16[1,2560,768]{2,1,0:T(8,128)(2,1)}, bf16[1,2560,768]{2,1,0:T(8,128)(2,1)}, bf16[16,48,640]{2,1,0:T(8,128)(2,1)}, f32[8,128]{1,0:T(8,128)}) custom-call(s32[2]{0:T(128)} %pad_add_fusion.refs_0_, bf16[768,2560]{1,0:T(8,128)(2,1)} %bitcast.33, bf16[2560,128]{1,0:T(8,128)(2,1)} %bitcast.41, ...), custom_call_target="tpu_custom_call", output_to_operand_aliasing={{0}: (4, {}), {1}: (5, {}), {2}: (6, {})} | custom-call | tf_op jit(solution)/shard_map/run_chunk/pallas_call | solution.py:32
  339.2 6.0 %all-to-all-start.6 = ((bf16[16,48,640]{2,1,0:T(8,128)(2,1)}), bf16[16,48,640]{2,1,0:T(8,128)(2,1)S(1)}, u32[]{:S(2)}, u32[]{:S(2)}) async-start(bf16[16,48,640]{2,1,0:T(8,128)(2,1)} %get-tuple-element.81), calls=%async_computation.6 | async-start | bytes 1966080 | tf_op jit(solution)/shard_map/all_to_all | solution.py:330
  346.5 15.8 %collective-permute-done.2.refs_3_ = bf16[2560,128]{1,0:T(8,128)(2,1)S(1)} collective-permute-done((bf16[2560,128]{1,0:T(8,128)(2,1)S(1)}, bf16[2560,128]{1,0:T(8,128)(2,1)S(1)}, u32[]{:S(2)}, u32[]{:S(2)}) %collective-permute-start.2) | collective-permute-done | bytes 655392 | tf_op jit(solution)/shard_map/ppermute | solution.py:407
  363.0 5.3 %run_chunk.5 = (bf16[1,2560,768]{2,1,0:T(8,128)(2,1)}, bf16[1,2560,768]{2,1,0:T(8,128)(2,1)}, bf16[16,48,128]{2,1,0:T(8,128)(2,1)}, f32[8,128]{1,0:T(8,128)}) custom-call(s32[2]{0:T(128)} %pad_add_fusion.refs_0_, bf16[768,2560]{1,0:T(8,128)(2,1)} %bitcast.34, bf16[2560,128]{1,0:T(8,128)(2,1)} %bitcast.39, ...), custom_call_target="tpu_custom_call", output_to_operand_aliasing={{0}: (4, {}), {1}: (5, {})} | custom-call | tf_op jit(solution)/shard_map/run_chunk/pallas_call | solution.py:32
  369.0 5.7 %all-to-all-start.7 = ((bf16[16,48,128]{2,1,0:T(8,128)(2,1)}), bf16[16,48,128]{2,1,0:T(8,128)(2,1)S(1)}, u32[]{:S(2)}, u32[]{:S(2)}) async-start(bf16[16,48,128]{2,1,0:T(8,128)(2,1)} %get-tuple-element.84), calls=%async_computation.7 | async-start | bytes 393216 | tf_op jit(solution)/shard_map/all_to_all | solution.py:330
  375.4 8.4 %all-to-all-done.7 = bf16[16,48,128]{2,1,0:T(8,128)(2,1)S(1)} async-done(((bf16[16,48,128]{2,1,0:T(8,128)(2,1)}), bf16[16,48,128]{2,1,0:T(8,128)(2,1)S(1)}, u32[]{:S(2)}, u32[]{:S(2)}) %all-to-all-start.7) | async-done | bytes 196640 | tf_op jit(solution)/shard_map/all_to_all | solution.py:330
  (90 shorter events, 44.4 us)
Async XLA Ops:
  7.2 19.0 %collective-permute-start = (bf16[64,2560]{1,0:T(8,128)(2,1)}, bf16[64,2560]{1,0:T(8,128)(2,1)S(1)}, u32[]{:S(2)}, u32[]{:S(2)}) collective-permute-start(bf16[64,2560]{1,0:T(8,128)(2,1)} %refs_0_.1), channel_id=1, source_target_pairs={{0,8},{1,9},{2,10},{3,11},{4,12},{5,13},{6,14},{7,15},{8,0},{9,1},... | collective-permute-start | bytes 983048 | tf_op jit(solution)/shard_map/ppermute | solution.py:370
  26.9 6.1 %copy-start.10 = (s32[1024,6]{0,1:T(8,128)S(1)}, s32[1024,6]{0,1:T(8,128)}, u32[]{:S(2)}) copy-start(s32[1024,6]{0,1:T(8,128)} %param.9) | copy-start | bytes 73732
  26.9 102.0 %all-to-all-start = ((bf16[16,2,160,512]{3,2,1,0:T(8,128)(2,1)}), bf16[16,2,160,512]{3,2,1,0:T(8,128)(2,1)}, u32[]{:S(2)}, u32[]{:S(2)}) async-start(bf16[16,2,160,512]{3,2,1,0:T(8,128)(2,1)} %get-tuple-element.46), calls=%async_computation | async-start | bytes 10485760 | tf_op jit(solution)/shard_map/all_to_all | solution.py:330
  128.9 24.0 %copy-start.11 = (s32[32,1]{0,1:T(1,128)S(1)}, s32[32,1]{0,1:T(1,128)}, u32[]{:S(2)}) copy-start(s32[32,1]{0,1:T(1,128)} %param.14) | copy-start | bytes 388
  128.9 24.0 %copy-start.12 = (f32[32]{0:T(128)S(1)}, f32[32]{0:T(128)}, u32[]{:S(2)}) copy-start(f32[32]{0:T(128)} %param.15) | copy-start | bytes 388
  128.9 24.3 %copy-start.8 = (f32[32,20,6]{0,1,2:T(8,128)S(1)}, f32[32,20,6]{0,1,2:T(8,128)}, u32[]{:S(2)}) copy-start(f32[32,20,6]{0,1,2:T(8,128)} %param.13) | copy-start | bytes 46084
  128.9 24.3 %copy-start.9 = (f32[32,20,6]{0,1,2:T(8,128)S(1)}, f32[32,20,6]{0,1,2:T(8,128)}, u32[]{:S(2)}) copy-start(f32[32,20,6]{0,1,2:T(8,128)} %param.12) | copy-start | bytes 46084
  129.0 51.4 %all-to-all-start.1 = ((bf16[16,2,160,128]{3,2,1,0:T(8,128)(2,1)}), bf16[16,2,160,128]{3,2,1,0:T(8,128)(2,1)S(1)}, u32[]{:S(2)}, u32[]{:S(2)}) async-start(bf16[16,2,160,128]{3,2,1,0:T(8,128)(2,1)} %get-tuple-element.54), calls=%async_computation.1 | async-start | bytes 2621440 | tf_op jit(solution)/shard_map/all_to_all | solution.py:330
  180.4 1.1 copy-start.2
  181.4 69.9 %all-to-all-start.2 = ((bf16[16,160,512]{2,1,0:T(8,128)(2,1)}), bf16[16,160,512]{2,1,0:T(8,128)(2,1)S(1)}, u32[]{:S(2)}, u32[]{:S(2)}) async-start(bf16[16,160,512]{2,1,0:T(8,128)(2,1)} %get-tuple-element.61), calls=%async_computation.2 | async-start | bytes 5242880 | tf_op jit(solution)/shard_map/all_to_all | solution.py:330
  189.5 127.9 %all-gather.2.cloned.1.call-start = ((), (), s32[]{:S(2)}) async-start(), calls=%async_computation.8 | async-start | bytes 6553600 | tf_op jit(solution)/shard_map/all_gather | solution.py:385
  189.5 59.4 %collective-permute-start.1 = (bf16[2,64,2560]{2,1,0:T(8,128)(2,1)}, bf16[2,64,2560]{2,1,0:T(8,128)(2,1)}, u32[]{:S(2)}, u32[]{:S(2)}) collective-permute-start(bf16[2,64,2560]{2,1,0:T(8,128)(2,1)} %get-tuple-element.53.refs_1_), channel_id=1, source_target_pairs={{0,4},{1,5},{2,6},{3,7},{4,0},{5,1},{6,2},{7,3},{8,12},{9,13},{10,... | collective-permute-start | bytes 1966088 | tf_op jit(solution)/shard_map/ppermute | solution.py:382
  251.3 1.5 copy-start.1
  252.8 32.5 %all-to-all-start.3 = ((bf16[16,2,160,128]{3,2,1,0:T(8,128)(2,1)}), bf16[16,2,160,128]{3,2,1,0:T(8,128)(2,1)S(1)}, u32[]{:S(2)}, u32[]{:S(2)}) async-start(bf16[16,2,160,128]{3,2,1,0:T(8,128)(2,1)} %get-tuple-element.63), calls=%async_computation.3 | async-start | bytes 2621440 | tf_op jit(solution)/shard_map/all_to_all | solution.py:330
  257.8 65.2 %collective-permute-start.4 = (bf16[2560,512]{1,0:T(8,128)(2,1)}, bf16[2560,512]{1,0:T(8,128)(2,1)}, u32[]{:S(2)}, u32[]{:S(2)}) collective-permute-start(bf16[2560,512]{1,0:T(8,128)(2,1)} %bitcast.36), channel_id=1, source_target_pairs={{0,16},{16,0},{1,17},{17,1},{2,18},{18,2},{3,19},{19,3},{4,20},{20... | collective-permute-start | bytes 7864328 | tf_op jit(solution)/shard_map/ppermute | solution.py:407
  285.3 1.1 copy-start
  286.3 24.7 %all-to-all-start.5 = ((bf16[16,160,128]{2,1,0:T(8,128)(2,1)}), bf16[16,160,128]{2,1,0:T(8,128)(2,1)S(1)}, u32[]{:S(2)}, u32[]{:S(2)}) async-start(bf16[16,160,128]{2,1,0:T(8,128)(2,1)} %get-tuple-element.68), calls=%async_computation.5 | async-start | bytes 1310720 | tf_op jit(solution)/shard_map/all_to_all | solution.py:330
  311.0 12.0 %copy-start.4 = (bf16[16,160,128]{2,1,0:T(8,128)(2,1)}, bf16[16,160,128]{2,1,0:T(8,128)(2,1)S(1)}, u32[]{:S(2)}) copy-start(bf16[16,160,128]{2,1,0:T(8,128)(2,1)S(1)} %all-to-all-done.5) | copy-start | bytes 1966084
  311.0 28.1 %all-to-all-start.4 = ((bf16[16,160,128]{2,1,0:T(8,128)(2,1)}), bf16[16,160,128]{2,1,0:T(8,128)(2,1)S(1)}, u32[]{:S(2)}, u32[]{:S(2)}) async-start(bf16[16,160,128]{2,1,0:T(8,128)(2,1)} %get-tuple-element.67), calls=%async_computation.4 | async-start | bytes 1310720 | tf_op jit(solution)/shard_map/all_to_all | solution.py:330
  315.8 17.1 %collective-permute-start.3 = (bf16[2560,128]{1,0:T(8,128)(2,1)S(1)}, bf16[2560,128]{1,0:T(8,128)(2,1)S(1)}, u32[]{:S(2)}, u32[]{:S(2)}) collective-permute-start(bf16[2560,128]{1,0:T(8,128)(2,1)S(1)} %bitcast.40), channel_id=1, source_target_pairs={{0,16},{16,0},{1,17},{17,1},{2,18},{18,2},{3,19},{19,3},{4,20},{20... | collective-permute-start | bytes 1966088 | tf_op jit(solution)/shard_map/ppermute | solution.py:407
  339.1 23.1 %copy-start.3 = (bf16[16,160,128]{2,1,0:T(8,128)(2,1)}, bf16[16,160,128]{2,1,0:T(8,128)(2,1)S(1)}, u32[]{:S(2)}) copy-start(bf16[16,160,128]{2,1,0:T(8,128)(2,1)S(1)} %all-to-all-done.4) | copy-start | bytes 1966084
  339.2 29.2 %all-to-all-start.6 = ((bf16[16,48,640]{2,1,0:T(8,128)(2,1)}), bf16[16,48,640]{2,1,0:T(8,128)(2,1)S(1)}, u32[]{:S(2)}, u32[]{:S(2)}) async-start(bf16[16,48,640]{2,1,0:T(8,128)(2,1)} %get-tuple-element.81), calls=%async_computation.6 | async-start | bytes 1966080 | tf_op jit(solution)/shard_map/all_to_all | solution.py:330
  345.2 17.0 %collective-permute-start.2 = (bf16[2560,128]{1,0:T(8,128)(2,1)S(1)}, bf16[2560,128]{1,0:T(8,128)(2,1)S(1)}, u32[]{:S(2)}, u32[]{:S(2)}) collective-permute-start(bf16[2560,128]{1,0:T(8,128)(2,1)S(1)} %bitcast.38), channel_id=1, source_target_pairs={{0,16},{16,0},{1,17},{17,1},{2,18},{18,2},{3,19},{19,3},{4,20},{20... | collective-permute-start | bytes 1966088 | tf_op jit(solution)/shard_map/ppermute | solution.py:407
  369.0 14.8 %all-to-all-start.7 = ((bf16[16,48,128]{2,1,0:T(8,128)(2,1)}), bf16[16,48,128]{2,1,0:T(8,128)(2,1)S(1)}, u32[]{:S(2)}, u32[]{:S(2)}) async-start(bf16[16,48,128]{2,1,0:T(8,128)(2,1)} %get-tuple-element.84), calls=%async_computation.7 | async-start | bytes 393216 | tf_op jit(solution)/shard_map/all_to_all | solution.py:330
  (3 other events, 2.4 us)
Sparse Core Ops, SparseCore 0:
  251.4 58.4 all-gather.1
